TPU v7x, 32 devices: a whole 2x2x4 slice. The times are simulated.
32 devices in a mesh: seq: 8 (over y, x, core), head: 4 (over z).
Axes of the slice: x: 2, y: 2, z: 4, core: 2. Of those that a mesh axis runs over, the one named last changes fastest.
Arguments:
- mixer_input: bfloat16 [4096, 8192], P('seq', 'head'), may hold values from -0.54 to 0.54
- output_grad: bfloat16 [4096, 8192], P('seq', 'head'), may hold values from -6.5 to 6.5
- input_map: bfloat16 [4096, 128], P('seq'), may hold values from -1 to 1
- output_map: bfloat16 [4096, 128], P('seq'), may hold values from -1 to 1
- decays: float32 [128, 4096], P('head', 'seq'), may hold values from 0.25 to 1
Outputs:
- input_grad: bfloat16 [4096, 8192], P('seq', 'head')
- input_map_grad: float32 [4096, 128], P(('seq', 'head'))
- output_map_grad: float32 [4096, 128], P(('seq', 'head'))
All inputs are finite; a program needn't handle non-finite values.
Results may differ from a plain program's by a relative error of at most 0.0012.
Values sent between devices are 32-bit elements; how exact they have to be, the bound alone decides.
No kernel may reach another device: no remote copies, remote signals or barrier semaphores. Data moves between devices by JAX's collectives and lax.ppermute only.
A program may use at most 128 MiB of HBM per device.

v0:
```python
import functools

import jax
import jax.numpy as jnp
from jax import lax
from jax.experimental import pallas as pl
from jax.experimental.pallas import tpu as pltpu
from jax.sharding import PartitionSpec as P

P_SIZE = 64
N = 128
SUB = 64
TILE = 256
EXTRA = 8
PARAMS = pltpu.CompilerParams(vmem_limit_bytes=56 * 1024 * 1024)
F32 = jnp.float32
BF16 = jnp.bfloat16

NN = (((1,), (0,)), ((), ()))
NT = (((1,), (1,)), ((), ()))


def dot(a, b, dims=NN):
    return lax.dot_general(a, b, dims, preferred_element_type=F32)


def halves(v):
    hi = v.astype(BF16)
    return hi, (v - hi.astype(F32)).astype(BF16)


def dot21(pair, b, dims=NN):
    return dot(pair[0], b, dims) + dot(pair[1], b, dims)


def dot12(a, pair, dims=NN):
    return dot(a, pair[0], dims) + dot(a, pair[1], dims)


def dot22(p, q, dims=NN):
    return dot(p[0], q[0], dims) + (dot(p[0], q[1], dims) + dot(p[1], q[0], dims))


def thirds(v):
    hi = v.astype(BF16)
    rest = v - hi.astype(F32)
    mid = rest.astype(BF16)
    return hi, mid, (rest - mid.astype(F32)).astype(BF16)


def packed_thirds(v, heads):
    hi, mid, lo = thirds(v)
    group = lax.broadcasted_iota(jnp.int32, v.shape, 1) // heads
    picked = jnp.where(group == 0, hi.astype(F32), jnp.where(group == 1, mid.astype(F32), lo.astype(F32)))
    return picked.astype(BF16)


def spread(heads, first, width):
    rows = lax.broadcasted_iota(jnp.int32, (3 * heads, width), 0)
    columns = lax.broadcasted_iota(jnp.int32, (3 * heads, width), 1)
    return (rows % heads == first + columns // P_SIZE).astype(F32).astype(BF16)


def stacked(*parts):
    return jnp.concatenate(parts, axis=0)


def transposed(v):
    return v.astype(F32).T.astype(BF16)


def summed_logs(table, logs3):
    return dot(table, logs3[0], NT) + (dot(table, logs3[1], NT) + dot(table, logs3[2], NT))


def log_parts(decays):
    logs = jnp.log(decays)
    return tuple(jnp.concatenate([part.astype(F32)] * 3, axis=0).astype(BF16) for part in thirds(logs))


def device_factors(decays, pre_ref, suf_ref):
    heads, local = decays.shape
    logs3 = log_parts(decays)
    rows = lax.broadcasted_iota(jnp.int32, (local, local), 0)
    columns = lax.broadcasted_iota(jnp.int32, (local, local), 1)
    upto = (columns <= rows).astype(F32).astype(BF16)
    after = (columns > rows).astype(F32).astype(BF16)
    pre_ref[...] = packed_thirds(jnp.exp(summed_logs(upto, logs3)), heads)
    suf_ref[...] = packed_thirds(jnp.exp(summed_logs(after, logs3)), heads)


def totals_kernel(heads, count, pick_ref, x_ref, dy_ref, b_ref, c_ref, *refs):
    if len(refs) == 6:
        decays_ref, out_ref, pre_ref, suf_ref, bt_ref, ct_ref = refs
    else:
        pre_ref, suf_ref, out_ref, bt_ref, ct_ref = refs
        decays_ref = None
    step = pl.program_id(0)

    @pl.when(step == 0)
    def _():
        bt_ref[...] = transposed(b_ref[...])
        ct_ref[...] = transposed(c_ref[...])
        if decays_ref is not None:
            device_factors(decays_ref[...], pre_ref, suf_ref)

    tile = x_ref.shape[1]
    table = spread(heads, (pick_ref[0] * count + step) * (tile // P_SIZE), tile)
    before = dot(pre_ref[...], table)
    after = dot(suf_ref[...], table)
    ended = before[before.shape[0] - 1 :, :]
    out_ref[0, :N, :] = dot12(bt_ref[...], halves(x_ref[...].astype(F32) * after))
    out_ref[1, :N, :] = dot12(ct_ref[...], halves(dy_ref[...].astype(F32) * before))
    out_ref[0, N:, :] = jnp.broadcast_to(ended, (EXTRA, tile))
    out_ref[1, N:, :] = jnp.broadcast_to(ended, (EXTRA, tile))


def totals(half, x, dy, b, c, decays=None, pre=None, suf=None):
    local, width = x.shape
    heads = width // P_SIZE
    count = width // 2 // TILE
    whole = lambda a: pl.BlockSpec(a.shape, lambda j, pick: (0, 0))
    column = pl.BlockSpec((local, TILE), lambda j, pick: (0, pick[0] * count + j))
    factor = jax.ShapeDtypeStruct((local, 3 * heads), BF16)
    rest = (pre, suf) if decays is None else (decays,)
    out_specs = [pl.BlockSpec((2, N + EXTRA, TILE), lambda j, pick: (0, 0, j))]
    out_shape = [jax.ShapeDtypeStruct((2, N + EXTRA, width // 2), F32)]
    if decays is not None:
        out_specs += [whole(factor), whole(factor)]
        out_shape += [factor, factor]
    return pl.pallas_call(
        functools.partial(totals_kernel, heads, count),
        grid_spec=pltpu.PrefetchScalarGridSpec(
            num_scalar_prefetch=1,
            grid=(count,),
            in_specs=[column, column, whole(b), whole(c)] + [whole(a) for a in rest],
            out_specs=out_specs,
            scratch_shapes=[pltpu.VMEM((N, local), BF16), pltpu.VMEM((N, local), BF16)],
        ),
        out_shape=out_shape,
        compiler_params=PARAMS,
        name="state_totals",
        cost_estimate=pl.CostEstimate(flops=8 * local * N * width // 2, bytes_accessed=4 * local * width, transcendentals=0),
    )(half, x, dy, b, c, *rest)


def ordered(core, mine, recv):
    return jnp.where(core == 0, mine, recv), jnp.where(core == 0, recv, mine)


def chip_kernel(chips, place_ref, mine_ref, recv_ref, *out_refs):
    core, chip = place_ref[0], place_ref[1]
    early, late = ordered(core, mine_ref[0], recv_ref[0])
    early_decay, late_decay = early[N : N + 1], late[N : N + 1]
    both = jnp.broadcast_to(early_decay * late_decay, (EXTRA, early.shape[1]))
    state = late_decay * early[:N] + late[:N]
    early, late = ordered(core, mine_ref[1], recv_ref[1])
    grad = early[:N] + early_decay * late[:N]
    for r, out_ref in enumerate(out_refs, 1):
        out_ref[:N, :] = jnp.where(chip + r < chips, state, grad)
        out_ref[N:, :] = both


def chip_totals(chips, place, mine, recv):
    width = mine.shape[2]
    tile = min(512, width)
    block = pl.BlockSpec((2, N + EXTRA, tile), lambda j, pick: (0, 0, j))
    out = pl.BlockSpec((N + EXTRA, tile), lambda j, pick: (0, j))
    shape = jax.ShapeDtypeStruct((N + EXTRA, width), F32)
    return pl.pallas_call(
        functools.partial(chip_kernel, chips),
        grid_spec=pltpu.PrefetchScalarGridSpec(
            num_scalar_prefetch=1, grid=(width // tile,), in_specs=[block, block], out_specs=[out] * (chips - 1)
        ),
        out_shape=[shape] * (chips - 1),
        compiler_params=PARAMS,
        name="chip_totals",
        cost_estimate=pl.CostEstimate(flops=6 * N * width, bytes_accessed=24 * N * width, transcendentals=0),
    )(place, mine, recv)


def carried_kernel(chips, place_ref, mine_ref, recv_ref, *refs):
    others, (own_ref, peer_ref) = refs[:-2], refs[-2:]
    core, chip = place_ref[0], place_ref[1]
    state = grad = jnp.zeros((N, own_ref.shape[2]), F32)
    state_weight = grad_weight = jnp.ones((1, own_ref.shape[2]), F32)
    for r, ref in enumerate(others, 1):
        earlier = chip >= r
        state = jnp.where(earlier, state + state_weight * ref[:N, :], state)
        state_weight = state_weight * ref[N : N + 1, :]
    for r in range(1, chips):
        later = chip + r < chips
        ref = others[chips - r - 1]
        grad = jnp.where(later, grad + grad_weight * ref[:N, :], grad)
        grad_weight = grad_weight * ref[N : N + 1, :]
    early, late = ordered(core, mine_ref[0], recv_ref[0])
    at_late = early[N : N + 1] * state + early[:N]
    own_ref[0] = jnp.where(core == 0, state, at_late)
    peer_ref[0] = jnp.where(core == 0, at_late, state)
    early, late = ordered(core, mine_ref[1], recv_ref[1])
    at_early = late[:N] + late[N : N + 1] * grad
    own_ref[1] = jnp.where(core == 0, at_early, grad)
    peer_ref[1] = jnp.where(core == 0, grad, at_early)


def carried(chips, place, mine, recv, others):
    width = mine.shape[2]
    tile = min(512, width)
    pair = pl.BlockSpec((2, N + EXTRA, tile), lambda j, pick: (0, 0, j))
    other = pl.BlockSpec((N + EXTRA, tile), lambda j, pick: (0, j))
    out = pl.BlockSpec((2, N, tile), lambda j, pick: (0, 0, j))
    shape = jax.ShapeDtypeStruct((2, N, width), F32)
    return pl.pallas_call(
        functools.partial(carried_kernel, chips),
        grid_spec=pltpu.PrefetchScalarGridSpec(
            num_scalar_prefetch=1,
            grid=(width // tile,),
            in_specs=[pair, pair] + [other] * len(others),
            out_specs=(out, out),
        ),
        out_shape=(shape, shape),
        compiler_params=PARAMS,
        name="carried_in",
        cost_estimate=pl.CostEstimate(flops=20 * N * width, bytes_accessed=44 * N * width, transcendentals=0),
    )(place, mine, recv, *others)


def local_kernel(
    heads, x_ref, dy_ref, b_ref, c_ref, decays_ref, part_ref, out_ref, map_ref,
    lift_ref, drop_ref, rows_ref, sums_ref, scores_ref, twice_ref, bt_ref, ct_ref, dys_ref, xs_ref,
):
    local, tile = x_ref.shape
    chunks = local // SUB
    step = pl.program_id(0)

    @pl.when(step == 0)
    def _():
        logs3 = log_parts(decays_ref[...])
        rows = lax.broadcasted_iota(jnp.int32, (local, local), 0)
        columns = lax.broadcasted_iota(jnp.int32, (local, local), 1)
        middle = (rows // SUB) * SUB + SUB // 2
        same = rows // SUB == columns // SUB
        later = same & (columns > middle) & (columns <= rows)
        sooner = same & (columns > rows) & (columns <= middle)
        signed = (later.astype(F32) - sooner.astype(F32)).astype(BF16)
        offset = summed_logs(signed, logs3)
        lift_ref[...] = packed_thirds(jnp.exp(offset), heads)
        drop_ref[...] = packed_thirds(jnp.exp(-offset), heads)
        chunk = lax.broadcasted_iota(jnp.int32, (2 * chunks, local), 0)
        token = lax.broadcasted_iota(jnp.int32, (2 * chunks, local), 1)
        inside = (token // SUB) == (chunk % chunks)
        first = token % SUB <= SUB // 2
        taken = inside & (first == (chunk < chunks))
        rows_ref[...] = packed_thirds(jnp.exp(summed_logs(taken.astype(F32).astype(BF16), logs3)), heads)
        sums_ref[...] = jnp.zeros(sums_ref.shape, F32)
        map_ref[...] = jnp.zeros(map_ref.shape, F32)
        twice_ref[:, :N] = b_ref[...]
        twice_ref[:, N:] = b_ref[...]
        sooner = lax.broadcasted_iota(jnp.int32, (SUB, SUB), 0) <= lax.broadcasted_iota(jnp.int32, (SUB, SUB), 1)
        for k in range(chunks):
            at = pl.ds(k * SUB, SUB)
            hi, lo = halves(jnp.where(sooner, dot(b_ref[at, :], c_ref[at, :], NT), 0.0))
            scores_ref[at, :SUB] = hi
            scores_ref[at, SUB : 2 * SUB] = lo
            scores_ref[at, 2 * SUB :] = hi
            bt_ref[k] = transposed(stacked(b_ref[at, :], b_ref[at, :]))
            ct_ref[k] = transposed(stacked(c_ref[at, :], c_ref[at, :]))

    table = spread(heads, step * (tile // P_SIZE), tile)
    dys_ref[0], dys_ref[1] = halves(dy_ref[...].astype(F32) * dot(lift_ref[...], table))
    drop = dot(drop_ref[...], table)
    xs_ref[0], xs_ref[1] = halves(x_ref[...].astype(F32) * drop)
    row = dot(rows_ref[...], table)

    state = None
    for k in range(chunks):
        at = pl.ds(k * SUB, SUB)
        dys, xs = (dys_ref[0, at, :], dys_ref[1, at, :]), (xs_ref[0, at, :], xs_ref[1, at, :])
        to_middle, to_end = row[k : k + 1], row[chunks + k : chunks + k + 1]
        if state is None:
            against = xs
        else:
            scaled = halves(state * to_middle)
            against = stacked(scaled[0], xs[0]), stacked(scaled[1], xs[1])
        both = dot(stacked(*dys), against[0], NT)
        summed = both[:SUB] + (both[SUB:] + dot(dys[0], against[1], NT))
        if state is None:
            sums_ref[at, N:] += summed
        else:
            sums_ref[at, :] += summed
        if k < chunks - 1:
            gained = to_end * dot(bt_ref[k], stacked(*xs))
            state = gained if state is None else (to_middle * to_end) * state + gained
    grad = None
    for k in reversed(range(chunks)):
        at = pl.ds(k * SUB, SUB)
        dys, xs = (dys_ref[0, at, :], dys_ref[1, at, :]), (xs_ref[0, at, :], xs_ref[1, at, :])
        to_middle, to_end = row[k : k + 1], row[chunks + k : chunks + k + 1]
        summed = dot(scores_ref[at, :], stacked(dys[0], dys[0], dys[1]))
        if grad is not None:
            scaled = halves(grad * to_end)
            summed = summed + dot(twice_ref[at, :], stacked(*scaled))
            both = dot(stacked(*xs), scaled[0], NT)
            map_ref[at, :] += both[:SUB] + (both[SUB:] + dot(xs[0], scaled[1], NT))
        part_ref[at, :] = drop[k * SUB : (k + 1) * SUB] * summed
        if k > 0:
            gained = to_middle * dot(ct_ref[k], stacked(*dys))
            grad = gained if grad is None else (to_middle * to_end) * grad + gained

    @pl.when(step == pl.num_programs(0) - 1)
    def _():
        causal = lax.broadcasted_iota(jnp.int32, (SUB, SUB), 0) >= lax.broadcasted_iota(jnp.int32, (SUB, SUB), 1)
        for k in range(chunks):
            at = pl.ds(k * SUB, SUB)
            mixed = jnp.where(causal, sums_ref[at, N:], 0.0)
            out_ref[at, :] = sums_ref[at, :N] + dot21(halves(mixed), b_ref[at, :])
            map_ref[at, :] += dot21(halves(mixed.T), c_ref[at, :])


def local_part(x, dy, b, c, decays):
    local, width = x.shape
    heads = width // P_SIZE
    count = width // TILE
    chunks = local // SUB
    whole = lambda a: pl.BlockSpec(a.shape, lambda j: (0, 0))
    column = pl.BlockSpec((local, TILE), lambda j: (0, j))
    tokens = pl.BlockSpec((local, N), lambda j: (0, 0))
    return pl.pallas_call(
        functools.partial(local_kernel, heads),
        grid=(count,),
        in_specs=[column, column, whole(b), whole(c), whole(decays)],
        out_specs=(column, tokens, tokens),
        out_shape=(
            jax.ShapeDtypeStruct((local, width), F32),
            jax.ShapeDtypeStruct((local, N), F32),
            jax.ShapeDtypeStruct((local, N), F32),
        ),
        scratch_shapes=[
            pltpu.VMEM((local, 3 * heads), BF16),
            pltpu.VMEM((local, 3 * heads), BF16),
            pltpu.VMEM((2 * chunks, 3 * heads), BF16),
            pltpu.VMEM((local, N + SUB), F32),
            pltpu.VMEM((local, 3 * SUB), BF16),
            pltpu.VMEM((local, 2 * N), BF16),
            pltpu.VMEM((chunks, N, 2 * SUB), BF16),
            pltpu.VMEM((chunks, N, 2 * SUB), BF16),
            pltpu.VMEM((2, local, TILE), BF16),
            pltpu.VMEM((2, local, TILE), BF16),
        ],
        compiler_params=PARAMS,
        name="local_part",
        cost_estimate=pl.CostEstimate(flops=40 * local * N * width, bytes_accessed=8 * local * width, transcendentals=0),
    )(x, dy, b, c, decays)


def map_kernel(heads, count, ranks, pick_ref, x_ref, dy_ref, pre_ref, suf_ref, carry_ref, out_before_ref, map_before_ref, *refs):
    messages, (out_ref, map_ref) = refs[:-2], refs[-2:]
    step = pl.program_id(0)
    tile = dy_ref.shape[1]

    @pl.when(step == 0)
    def _():
        out_ref[...] = out_before_ref[...]
        map_ref[...] = map_before_ref[...]

    table = spread(heads, (pick_ref[0] * count + step) * (tile // P_SIZE), tile)
    scaled = halves(dy_ref[...].astype(F32) * dot(pre_ref[...], table))
    out_ref[...] += dot22(scaled, halves(carry_ref[0]), NT)
    scaled = halves(x_ref[...].astype(F32) * dot(suf_ref[...], table))
    map_ref[...] += dot22(scaled, halves(carry_ref[1]), NT)

    if messages:

        @pl.when(step == count - 1)
        def _():
            rows = messages[0].shape[1]
            for r, message in enumerate(messages):
                at = pl.ds(pl.multiple_of(((pick_ref[1] + r) % ranks) * rows, rows), rows)
                message[0] = out_ref[at, :]
                message[1] = map_ref[at, :]


def map_terms(pick, x, dy, pre, suf, carry, out_before, map_before, ranks=0):
    local, width = dy.shape
    heads = width // P_SIZE
    count = width // 2 // TILE
    whole = lambda a: pl.BlockSpec(a.shape, lambda j, pick: (0,) * len(a.shape))
    tokens = jax.ShapeDtypeStruct((local, N), F32)
    column = pl.BlockSpec((local, TILE), lambda j, pick: (0, pick[0] * count + j))
    if ranks:
        out_shape = [jax.ShapeDtypeStruct((2, local // ranks, N), F32)] * ranks
        scratch = [pltpu.VMEM((local, N), F32), pltpu.VMEM((local, N), F32)]
    else:
        out_shape, scratch = [tokens, tokens], []
    return pl.pallas_call(
        functools.partial(map_kernel, heads, count, ranks),
        grid_spec=pltpu.PrefetchScalarGridSpec(
            num_scalar_prefetch=1,
            grid=(count,),
            in_specs=[
                column,
                column,
                whole(pre),
                whole(suf),
                pl.BlockSpec((2, N, TILE), lambda j, pick: (0, 0, j)),
                whole(tokens),
                whole(tokens),
            ],
            out_specs=[whole(shape) for shape in out_shape],
            scratch_shapes=scratch,
        ),
        out_shape=out_shape,
        compiler_params=PARAMS,
        name="map_terms",
        cost_estimate=pl.CostEstimate(flops=12 * local * N * width // 2, bytes_accessed=4 * local * width, transcendentals=0),
    )(pick, x, dy, pre, suf, carry, out_before, map_before)


def input_kernel(heads, count, pick_ref, part_ref, suf_ref, b_ref, own_ref, other_ref, input_ref):
    tile = part_ref.shape[1]
    step = pl.program_id(0)
    after = dot(suf_ref[...], spread(heads, step * (tile // P_SIZE), tile))
    grad = jnp.where(step // count == pick_ref[0], own_ref[0], other_ref[0])
    input_ref[...] = (part_ref[...] + after * dot12(b_ref[...], halves(grad))).astype(BF16)


def input_terms(core, part, suf, b, own, other):
    local, width = part.shape
    heads = width // P_SIZE
    count = width // 2 // TILE
    whole = lambda a: pl.BlockSpec(a.shape, lambda j, pick: (0, 0))
    column = pl.BlockSpec((local, TILE), lambda j, pick: (0, j))
    carry = pl.BlockSpec((1, N, TILE), lambda j, pick: (1, 0, j % count))
    return pl.pallas_call(
        functools.partial(input_kernel, heads, count),
        grid_spec=pltpu.PrefetchScalarGridSpec(
            num_scalar_prefetch=1,
            grid=(2 * count,),
            in_specs=[column, whole(suf), whole(b), carry, carry],
            out_specs=column,
        ),
        out_shape=jax.ShapeDtypeStruct((local, width), BF16),
        compiler_params=PARAMS,
        name="input_terms",
        cost_estimate=pl.CostEstimate(flops=4 * local * N * width, bytes_accessed=8 * local * width, transcendentals=0),
    )(core, part, suf, b, own, other)


def swap_cores(v, length):
    return lax.ppermute(v, "seq", [(i, i ^ 1) for i in range(length)])


def turned(v, axis, length, by):
    return lax.ppermute(v, axis, [(i, (i + by) % length) for i in range(length)])


def per_device(mixer_input, output_grad, input_map, output_map, decays):
    length, ranks = lax.axis_size("seq"), lax.axis_size("head")
    chips = length // 2
    index, rank = lax.axis_index("seq"), lax.axis_index("head")
    core, chip = index % 2, index // 2
    place = jnp.stack([core, chip]).astype(jnp.int32)
    here = jnp.stack([core, rank]).astype(jnp.int32)
    there = jnp.stack([1 - core, rank]).astype(jnp.int32)
    sent, pre, suf = totals(there, mixer_input, output_grad, input_map, output_map, decays=decays)
    recv = swap_cores(sent, length)
    (mine,) = totals(here, mixer_input, output_grad, input_map, output_map, pre=pre, suf=suf)
    messages = chip_totals(chips, place, mine, recv)
    others = [turned(message, "seq", length, 2 * r) for r, message in enumerate(messages, 1)]
    part, out_part, map_part = local_part(mixer_input, output_grad, input_map, output_map, decays)
    others, part, out_part, map_part = lax.optimization_barrier((others, part, out_part, map_part))
    own, peer = carried(chips, place, mine, recv, others)
    other = swap_cores(peer, length)
    out_part, map_part = map_terms(here, mixer_input, output_grad, pre, suf, own, out_part, map_part)
    shares = map_terms(there, mixer_input, output_grad, pre, suf, other, out_part, map_part, ranks)
    total = shares[0]
    own, other, shares = lax.optimization_barrier((own, other, shares))
    for r in range(1, ranks):
        total = total + turned(shares[r], "head", ranks, r)
    input_grad = input_terms(place, part, suf, input_map, own, other)
    return input_grad, total[1], total[0]


def solution(mesh):
    in_specs = (
        P("seq", "head"),
        P("seq", "head"),
        P("seq", None),
        P("seq", None),
        P("head", "seq"),
    )
    out_specs = (P("seq", "head"), P(("seq", "head"), None), P(("seq", "head"), None))
    return jax.shard_map(
        per_device, mesh=mesh, in_specs=in_specs, out_specs=out_specs, check_vma=False
    )
```

profile of v0, /device:TPU:11, one launch (start us, length us, event | category | flops | bytes accessed | tf_op | source)
XLA Modules:
  0.0 82.9 jit_solution(12506443010674586826)
XLA Ops:
  0.6 0.6 pad_add_fusion.1.pick_ref
  1.3 6.5 %state_totals.2 = (f32[2,136,1024]{2,1,0:T(8,128)}, bf16[512,96]{1,0:T(8,128)(2,1)}, bf16[512,96]{1,0:T(8,128)(2,1)}) custom-call(s32[2]{0:T(128)} %pad_add_fusion.1.pick_ref, bf16[512,2048]{1,0:T(8,128)(2,1)} %x_ref.9, bf16[512,2048]{1,0:T(8,128)(2,1)} %dy_ref.9, bf16[512,128]{1,0:T(8,128)(2,1)} %b_ref.7, bf16[512,128]{1,0:T(8,128)(2,1)} %c_ref.5, ...), custom_call_target="tpu_custom_call" | custom-call | flops 536870912 | bytes 4194304 | tf_op jit(solution)/shard_map/state_totals/pallas_call | solution.py:131
  7.8 0.7 collective-permute-start
  8.5 0.7 pad_add_fusion
  9.1 5.7 %state_totals.3.mine_ref = f32[2,136,1024]{2,1,0:T(8,128)} custom-call(s32[2]{0:T(128)} %get-tuple-element.62.pick_ref, bf16[512,2048]{1,0:T(8,128)(2,1)} %x_ref.9, bf16[512,2048]{1,0:T(8,128)(2,1)} %dy_ref.9, bf16[512,128]{1,0:T(8,128)(2,1)} %b_ref.7, bf16[512,128]{1,0:T(8,128)(2,1)} %c_ref.5, bf16[512,96]{1,0:T(8,128)(2,1)} %get-tuple-element.31.refs_0_.pre_ref, ...), custom_call_target="tpu_custom_call" | custom-call | flops 536870912 | bytes 4194304 | tf_op jit(solution)/shard_map/state_totals/pallas_call | solution.py:131
  14.9 1.0 %copy-done = f32[2,136,1024]{2,1,0:T(8,128)} copy-done((f32[2,136,1024]{2,1,0:T(8,128)}, f32[2,136,1024]{2,1,0:T(8,128)S(1)}, u32[]{:S(2)}) %copy-start) | copy-done | bytes 1114136
  15.8 3.3 %chip_totals.1 = (f32[136,1024]{1,0:T(8,128)}, f32[136,1024]{1,0:T(8,128)}, f32[136,1024]{1,0:T(8,128)}) custom-call(s32[2]{0:T(128)} %get-tuple-element.61.place_ref.pick_ref, f32[2,136,1024]{2,1,0:T(8,128)} %state_totals.3.mine_ref, f32[2,136,1024]{2,1,0:T(8,128)} %copy-done), custom_call_target="tpu_custom_call" | custom-call | flops 786432 | bytes 3145728 | tf_op jit(solution)/shard_map/chip_totals/pallas_call | solution.py:170
  19.1 1.2 %collective-permute-start.1 = (f32[136,1024]{1,0:T(8,128)}, f32[136,1024]{1,0:T(8,128)S(1)}, u32[]{:S(2)}, u32[]{:S(2)}) collective-permute-start(f32[136,1024]{1,0:T(8,128)} %get-tuple-element.34), channel_id=1, source_target_pairs={{0,8},{4,12},{8,16},{12,20},{16,24},{20,28},{24,0},{28,4},{1,9},{5... | collective-permute-start | bytes 1671176 | tf_op jit(solution)/shard_map/ppermute | solution.py:454
  20.5 1.3 %collective-permute-start.3 = (f32[136,1024]{1,0:T(8,128)}, f32[136,1024]{1,0:T(8,128)S(1)}, u32[]{:S(2)}, u32[]{:S(2)}) collective-permute-start(f32[136,1024]{1,0:T(8,128)} %get-tuple-element.36), channel_id=1, source_target_pairs={{0,24},{4,28},{8,0},{12,4},{16,8},{20,12},{24,16},{28,20},{1,25},{... | collective-permute-start | bytes 1671176 | tf_op jit(solution)/shard_map/ppermute | solution.py:454
  21.8 25.2 %local_part.1 = (f32[512,2048]{1,0:T(8,128)}, f32[512,128]{1,0:T(8,128)}, f32[512,128]{1,0:T(8,128)}) custom-call(bf16[512,2048]{1,0:T(8,128)(2,1)} %x_ref.9, bf16[512,2048]{1,0:T(8,128)(2,1)} %dy_ref.9, bf16[512,128]{1,0:T(8,128)(2,1)} %b_ref.7, bf16[512,128]{1,0:T(8,128)(2,1)} %c_ref.5, f32[32,512]{1,0:T(8,128)} %decays_ref.1), custom_call_target="tpu_custom_call" | custom-call | flops 5368709120 | bytes 8388608 | tf_op jit(solution)/shard_map/local_part/pallas_call | solution.py:328
  47.1 0.8 copy-done.2
  47.8 0.3 copy-done.3
  48.3 4.0 %carried_in.1 = (f32[2,128,1024]{2,1,0:T(8,128)}, f32[2,128,1024]{2,1,0:T(8,128)}) custom-call(s32[2]{0:T(128)} %get-tuple-element.61.place_ref.pick_ref, f32[2,136,1024]{2,1,0:T(8,128)} %state_totals.3.mine_ref, f32[2,136,1024]{2,1,0:T(8,128)} %copy-done, f32[136,1024]{1,0:T(8,128)} %copy-done.2, f32[136,1024]{1,0:T(8,128)} %copy-done.3, f32[136,1024]{1,0:T(8,128)} %copy-done.4), custom_call_target="tpu_custom_call" | custom-call | flops 2621440 | bytes 5767168 | tf_op jit(solution)/shard_map/carried_in/pallas_call | solution.py:213
  52.3 0.9 %collective-permute-start.4 = (f32[2,128,1024]{2,1,0:T(8,128)}, f32[2,128,1024]{2,1,0:T(8,128)S(1)}, u32[]{:S(2)}, u32[]{:S(2)}) collective-permute-start(f32[2,128,1024]{2,1,0:T(8,128)} %get-tuple-element.45), channel_id=1, source_target_pairs={{0,4},{4,0},{8,12},{12,8},{16,20},{20,16},{24,28},{28,24},{1,5},{5... | collective-permute-start | bytes 3145736 | tf_op jit(solution)/shard_map/ppermute | solution.py:450
  53.1 6.5 %map_terms.2 = (f32[512,128]{1,0:T(8,128)}, f32[512,128]{1,0:T(8,128)}) custom-call(s32[2]{0:T(128)} %get-tuple-element.62.pick_ref, bf16[512,2048]{1,0:T(8,128)(2,1)} %x_ref.9, bf16[512,2048]{1,0:T(8,128)(2,1)} %dy_ref.9, bf16[512,96]{1,0:T(8,128)(2,1)} %get-tuple-element.31.refs_0_.pre_ref, bf16[512,96]{1,0:T(8,128)(2,1)} %get-tuple-element.32.refs_1_.suf_ref, ...), custom_call_target="tpu_custom_call" | custom-call | flops 805306368 | bytes 4194304 | tf_op jit(solution)/shard_map/map_terms/pallas_call | solution.py:395
  59.6 1.0 %copy-done.1 = f32[2,128,1024]{2,1,0:T(8,128)} copy-done((f32[2,128,1024]{2,1,0:T(8,128)}, f32[2,128,1024]{2,1,0:T(8,128)S(1)}, u32[]{:S(2)}) %copy-start.1) | copy-done | bytes 1048600
  60.6 6.6 %map_terms.3 = (f32[2,128,128]{2,1,0:T(8,128)}, f32[2,128,128]{2,1,0:T(8,128)}, f32[2,128,128]{2,1,0:T(8,128)}, f32[2,128,128]{2,1,0:T(8,128)}) custom-call(s32[2]{0:T(128)} %pad_add_fusion.1.pick_ref, bf16[512,2048]{1,0:T(8,128)(2,1)} %x_ref.9, bf16[512,2048]{1,0:T(8,128)(2,1)} %dy_ref.9, bf16[512,96]{1,0:T(8,128)(2,1)} %get-tuple-element.31.refs_0_.pre_ref, ...), custom_call_target="tpu_custom_call" | custom-call | flops 805306368 | bytes 4194304 | tf_op jit(solution)/shard_map/map_terms/pallas_call | solution.py:395
  67.2 1.3 %collective-permute-start.5 = (f32[2,128,128]{2,1,0:T(8,128)}, f32[2,128,128]{2,1,0:T(8,128)S(1)}, u32[]{:S(2)}, u32[]{:S(2)}) collective-permute-start(f32[2,128,128]{2,1,0:T(8,128)} %get-tuple-element.56), channel_id=1, source_target_pairs={{0,1},{1,2},{2,3},{3,0},{4,5},{5,6},{6,7},{7,4},{8,9},{9,10},{10,1... | collective-permute-start | bytes 393224 | tf_op jit(solution)/shard_map/ppermute | solution.py:454
  68.5 1.1 %collective-permute-start.6 = (f32[2,128,128]{2,1,0:T(8,128)}, f32[2,128,128]{2,1,0:T(8,128)S(1)}, u32[]{:S(2)}, u32[]{:S(2)}) collective-permute-start(f32[2,128,128]{2,1,0:T(8,128)} %get-tuple-element.57), channel_id=1, source_target_pairs={{0,2},{1,3},{2,0},{3,1},{4,6},{5,7},{6,4},{7,5},{8,10},{9,11},{10,... | collective-permute-start | bytes 393224 | tf_op jit(solution)/shard_map/ppermute | solution.py:454
  69.6 1.4 %collective-permute-start.7 = (f32[2,128,128]{2,1,0:T(8,128)}, f32[2,128,128]{2,1,0:T(8,128)S(1)}, u32[]{:S(2)}, u32[]{:S(2)}) collective-permute-start(f32[2,128,128]{2,1,0:T(8,128)} %get-tuple-element.58), channel_id=1, source_target_pairs={{0,3},{1,0},{2,1},{3,2},{4,7},{5,4},{6,5},{7,6},{8,11},{9,8},{10,9... | collective-permute-start | bytes 393224 | tf_op jit(solution)/shard_map/ppermute | solution.py:454
  71.0 8.5 %input_terms.1 = bf16[512,2048]{1,0:T(8,128)(2,1)} custom-call(s32[2]{0:T(128)} %get-tuple-element.61.place_ref.pick_ref, f32[512,2048]{1,0:T(8,128)} %get-tuple-element.40.part_ref, bf16[512,96]{1,0:T(8,128)(2,1)} %get-tuple-element.32.refs_1_.suf_ref, bf16[512,128]{1,0:T(8,128)(2,1)} %b_ref.7, f32[2,128,1024]{2,1,0:T(8,128)} %get-tuple-element.54.carry_ref.own_ref, ...), custom_call_target="tpu_custom_call" | custom-call | flops 536870912 | bytes 8388608 | tf_op jit(solution)/shard_map/input_terms/pallas_call | solution.py:434
  79.5 0.7 collective-permute-done.6
  80.2 2.0 %collective-permute-done.7 = f32[2,128,128]{2,1,0:T(8,128)S(1)} collective-permute-done((f32[2,128,128]{2,1,0:T(8,128)}, f32[2,128,128]{2,1,0:T(8,128)S(1)}, u32[]{:S(2)}, u32[]{:S(2)}) %collective-permute-start.7) | collective-permute-done | bytes 131104 | tf_op jit(solution)/shard_map/ppermute | solution.py:454
  82.2 0.7 slice_bitcast_fusion
  (16 shorter events, 0.5 us)
Async XLA Ops:
  7.8 7.1 %collective-permute-start = (f32[2,136,1024]{2,1,0:T(8,128)}, f32[2,136,1024]{2,1,0:T(8,128)S(1)}, u32[]{:S(2)}, u32[]{:S(2)}) collective-permute-start(f32[2,136,1024]{2,1,0:T(8,128)} %get-tuple-element.33), channel_id=1, source_target_pairs={{0,4},{4,0},{8,12},{12,8},{16,20},{20,16},{24,28},{28,24},{1,5},{5... | collective-permute-start | bytes 3342344 | tf_op jit(solution)/shard_map/ppermute | solution.py:450
  14.8 1.0 %copy-start = (f32[2,136,1024]{2,1,0:T(8,128)}, f32[2,136,1024]{2,1,0:T(8,128)S(1)}, u32[]{:S(2)}) copy-start(f32[2,136,1024]{2,1,0:T(8,128)S(1)} %collective-permute-done.recv_ref) | copy-start | bytes 3342340
  19.1 27.9 %collective-permute-start.1 = (f32[136,1024]{1,0:T(8,128)}, f32[136,1024]{1,0:T(8,128)S(1)}, u32[]{:S(2)}, u32[]{:S(2)}) collective-permute-start(f32[136,1024]{1,0:T(8,128)} %get-tuple-element.34), channel_id=1, source_target_pairs={{0,8},{4,12},{8,16},{12,20},{16,24},{20,28},{24,0},{28,4},{1,9},{5... | collective-permute-start | bytes 1671176 | tf_op jit(solution)/shard_map/ppermute | solution.py:454
  20.3 26.8 %collective-permute-start.2 = (f32[136,1024]{1,0:T(8,128)}, f32[136,1024]{1,0:T(8,128)S(1)}, u32[]{:S(2)}, u32[]{:S(2)}) collective-permute-start(f32[136,1024]{1,0:T(8,128)} %get-tuple-element.35), channel_id=1, source_target_pairs={{0,16},{4,20},{8,24},{12,28},{16,0},{20,4},{24,8},{28,12},{1,17},{... | collective-permute-start | bytes 1671176 | tf_op jit(solution)/shard_map/ppermute | solution.py:454
  20.5 26.5 %collective-permute-start.3 = (f32[136,1024]{1,0:T(8,128)}, f32[136,1024]{1,0:T(8,128)S(1)}, u32[]{:S(2)}, u32[]{:S(2)}) collective-permute-start(f32[136,1024]{1,0:T(8,128)} %get-tuple-element.36), channel_id=1, source_target_pairs={{0,24},{4,28},{8,0},{12,4},{16,8},{20,12},{24,16},{28,20},{1,25},{... | collective-permute-start | bytes 1671176 | tf_op jit(solution)/shard_map/ppermute | solution.py:454
  47.0 0.8 copy-start.2
  47.1 1.1 %copy-start.3 = (f32[136,1024]{1,0:T(8,128)}, f32[136,1024]{1,0:T(8,128)S(1)}, u32[]{:S(2)}) copy-start(f32[136,1024]{1,0:T(8,128)S(1)} %collective-permute-done.2.refs_1_) | copy-start | bytes 1671172
  47.1 1.2 %copy-start.4 = (f32[136,1024]{1,0:T(8,128)}, f32[136,1024]{1,0:T(8,128)S(1)}, u32[]{:S(2)}) copy-start(f32[136,1024]{1,0:T(8,128)S(1)} %collective-permute-done.3.refs_2_) | copy-start | bytes 1671172
  52.3 7.3 %collective-permute-start.4 = (f32[2,128,1024]{2,1,0:T(8,128)}, f32[2,128,1024]{2,1,0:T(8,128)S(1)}, u32[]{:S(2)}, u32[]{:S(2)}) collective-permute-start(f32[2,128,1024]{2,1,0:T(8,128)} %get-tuple-element.45), channel_id=1, source_target_pairs={{0,4},{4,0},{8,12},{12,8},{16,20},{20,16},{24,28},{28,24},{1,5},{5... | collective-permute-start | bytes 3145736 | tf_op jit(solution)/shard_map/ppermute | solution.py:450
  59.6 1.0 %copy-start.1 = (f32[2,128,1024]{2,1,0:T(8,128)}, f32[2,128,1024]{2,1,0:T(8,128)S(1)}, u32[]{:S(2)}) copy-start(f32[2,128,1024]{2,1,0:T(8,128)S(1)} %collective-permute-done.4.carry_ref.other_ref) | copy-start | bytes 3145732
  67.2 15.0 %copy-start.5 = (f32[2,128,128]{2,1,0:T(8,128)S(1)}, f32[2,128,128]{2,1,0:T(8,128)}, u32[]{:S(2)}) copy-start(f32[2,128,128]{2,1,0:T(8,128)} %get-tuple-element.50) | copy-start | bytes 393220
  67.2 12.3 %collective-permute-start.5 = (f32[2,128,128]{2,1,0:T(8,128)}, f32[2,128,128]{2,1,0:T(8,128)S(1)}, u32[]{:S(2)}, u32[]{:S(2)}) collective-permute-start(f32[2,128,128]{2,1,0:T(8,128)} %get-tuple-element.56), channel_id=1, source_target_pairs={{0,1},{1,2},{2,3},{3,0},{4,5},{5,6},{6,7},{7,4},{8,9},{9,10},{10,1... | collective-permute-start | bytes 393224 | tf_op jit(solution)/shard_map/ppermute | solution.py:454
  68.5 11.7 %collective-permute-start.6 = (f32[2,128,128]{2,1,0:T(8,128)}, f32[2,128,128]{2,1,0:T(8,128)S(1)}, u32[]{:S(2)}, u32[]{:S(2)}) collective-permute-start(f32[2,128,128]{2,1,0:T(8,128)} %get-tuple-element.57), channel_id=1, source_target_pairs={{0,2},{1,3},{2,0},{3,1},{4,6},{5,7},{6,4},{7,5},{8,10},{9,11},{10,... | collective-permute-start | bytes 393224 | tf_op jit(solution)/shard_map/ppermute | solution.py:454
  69.6 12.5 %collective-permute-start.7 = (f32[2,128,128]{2,1,0:T(8,128)}, f32[2,128,128]{2,1,0:T(8,128)S(1)}, u32[]{:S(2)}, u32[]{:S(2)}) collective-permute-start(f32[2,128,128]{2,1,0:T(8,128)} %get-tuple-element.58), channel_id=1, source_target_pairs={{0,3},{1,0},{2,1},{3,2},{4,7},{5,4},{6,5},{7,6},{8,11},{9,8},{10,9... | collective-permute-start | bytes 393224 | tf_op jit(solution)/shard_map/ppermute | solution.py:454
where the time goes:
time: 84.4 us; the launch traced here: 82.9 us
  Pallas kernels  66.3 us (79%)
  starting transfers between devices  8.02 us (10%)
  local copies, waits for them, and re-layouts  3.83 us (5%)
  waiting for transfers between devices  2.66 us (3%)
  other arithmetic  1.29 us (2%)
    pallas_call x1, Pallas kernels, local_part(): pl.pallas_call(functools.partial(local_kernel, heads), grid=(count,), in_...  25.2 us
    pallas_call x2, Pallas kernels, map_terms(): pl.pallas_call(functools.partial(map_kernel, heads, count, ranks), grid_s...  13.1 us
    pallas_call x2, Pallas kernels, totals(): pl.pallas_call(functools.partial(totals_kernel, heads, count), grid_spec=...  12.3 us
    pallas_call x1, Pallas kernels, input_terms(): pl.pallas_call(functools.partial(input_kernel, heads, count), grid_spec=p...  8.5 us
    ppermute x6, starting transfers between devices, turned(): lax.ppermute(v, axis, [(i, (i + by) % length) for i in range(length)])  6.49 us
    pallas_call x1, Pallas kernels, carried(): pl.pallas_call(functools.partial(carried_kernel, chips), grid_spec=pltpu....  3.97 us
    pallas_call x1, Pallas kernels, chip_totals(): pl.pallas_call(functools.partial(chip_kernel, chips), grid_spec=pltpu.Pre...  3.26 us
    unnamed x12, local copies, waits for them, and re-layouts  3.18 us
  transfers between devices with their start and end apart: 8, of which 2 were waited for; matrix products, arithmetic and copies ran while one was open for 1% of the time, Pallas kernels for 55%

commit v1 on v0

--- a/solution.py
+++ b/solution.py
@@ -12,7 +12,9 @@
 SUB = 64
 TILE = 256
 EXTRA = 8
-PARAMS = pltpu.CompilerParams(vmem_limit_bytes=56 * 1024 * 1024)
+LANES = 128
+CORE, OTHER, CHIP, RANK = range(4)
+PARAMS = pltpu.CompilerParams(vmem_limit_bytes=24 * 1024 * 1024)
 F32 = jnp.float32
 BF16 = jnp.bfloat16
 
@@ -48,17 +50,13 @@
     return hi, mid, (rest - mid.astype(F32)).astype(BF16)
 
 
-def packed_thirds(v, heads):
-    hi, mid, lo = thirds(v)
-    group = lax.broadcasted_iota(jnp.int32, v.shape, 1) // heads
-    picked = jnp.where(group == 0, hi.astype(F32), jnp.where(group == 1, mid.astype(F32), lo.astype(F32)))
-    return picked.astype(BF16)
-
-
 def spread(heads, first, width):
-    rows = lax.broadcasted_iota(jnp.int32, (3 * heads, width), 0)
-    columns = lax.broadcasted_iota(jnp.int32, (3 * heads, width), 1)
-    return (rows % heads == first + columns // P_SIZE).astype(F32).astype(BF16)
+    rows = lax.broadcasted_iota(jnp.int32, (heads, width), 0)
+    columns = lax.broadcasted_iota(jnp.int32, (heads, width), 1)
+    offset = columns - (rows - first) * P_SIZE
+    picked = ((offset >= 0) & (offset < P_SIZE)).astype(F32)
+    rest = jnp.zeros((LANES - 3 * heads, width), F32)
+    return jnp.concatenate([picked, picked, picked, rest], axis=0).astype(BF16)
 
 
 def stacked(*parts):
@@ -69,31 +67,36 @@
     return v.astype(F32).T.astype(BF16)
 
 
-def summed_logs(table, logs3):
-    return dot(table, logs3[0], NT) + (dot(table, logs3[1], NT) + dot(table, logs3[2], NT))
-
-
 def log_parts(decays):
-    logs = jnp.log(decays)
-    return tuple(jnp.concatenate([part.astype(F32)] * 3, axis=0).astype(BF16) for part in thirds(logs))
+    return jnp.concatenate([part.astype(F32) for part in thirds(jnp.log(decays))], axis=0).astype(BF16)
+
+
+def summed_logs(logs, table):
+    heads = logs.shape[0] // 3
+    sums = dot(logs, table.astype(F32).astype(BF16))
+    return sums[:heads] + (sums[heads : 2 * heads] + sums[2 * heads :])
+
+
+def packed(v):
+    parts = [part.astype(F32) for part in thirds(v)]
+    rest = jnp.zeros((LANES - 3 * v.shape[0], v.shape[1]), F32)
+    return jnp.concatenate(parts + [rest], axis=0).T.astype(BF16)
 
 
 def device_factors(decays, pre_ref, suf_ref):
-    heads, local = decays.shape
-    logs3 = log_parts(decays)
+    local = decays.shape[1]
+    logs = log_parts(decays)
     rows = lax.broadcasted_iota(jnp.int32, (local, local), 0)
     columns = lax.broadcasted_iota(jnp.int32, (local, local), 1)
-    upto = (columns <= rows).astype(F32).astype(BF16)
-    after = (columns > rows).astype(F32).astype(BF16)
-    pre_ref[...] = packed_thirds(jnp.exp(summed_logs(upto, logs3)), heads)
-    suf_ref[...] = packed_thirds(jnp.exp(summed_logs(after, logs3)), heads)
-
-
-def totals_kernel(heads, count, pick_ref, x_ref, dy_ref, b_ref, c_ref, *refs):
-    if len(refs) == 6:
-        decays_ref, out_ref, pre_ref, suf_ref, bt_ref, ct_ref = refs
+    pre_ref[...] = packed(jnp.exp(summed_logs(logs, rows <= columns)))
+    suf_ref[...] = packed(jnp.exp(summed_logs(logs, rows > columns)))
+
+
+def totals_kernel(heads, count, half, place_ref, x_ref, dy_ref, b_ref, c_ref, *refs):
+    if len(refs) == 7:
+        decays_ref, out_ref, scaled_ref, pre_ref, suf_ref, bt_ref, ct_ref = refs
     else:
-        pre_ref, suf_ref, out_ref, bt_ref, ct_ref = refs
+        pre_ref, suf_ref, out_ref, scaled_ref, bt_ref, ct_ref = refs
         decays_ref = None
     step = pl.program_id(0)
 
@@ -105,31 +108,39 @@
             device_factors(decays_ref[...], pre_ref, suf_ref)
 
     tile = x_ref.shape[1]
-    table = spread(heads, (pick_ref[0] * count + step) * (tile // P_SIZE), tile)
+    table = spread(heads, (place_ref[half] * count + step) * (tile // P_SIZE), tile)
     before = dot(pre_ref[...], table)
     after = dot(suf_ref[...], table)
     ended = before[before.shape[0] - 1 :, :]
-    out_ref[0, :N, :] = dot12(bt_ref[...], halves(x_ref[...].astype(F32) * after))
-    out_ref[1, :N, :] = dot12(ct_ref[...], halves(dy_ref[...].astype(F32) * before))
+    for i, (source, factor, other) in enumerate(((x_ref, after, bt_ref), (dy_ref, before, ct_ref))):
+        scaled = halves(source[...].astype(F32) * factor)
+        scaled_ref[i, 0], scaled_ref[i, 1] = scaled
+        out_ref[i, :N, :] = dot12(other[...], scaled)
     out_ref[0, N:, :] = jnp.broadcast_to(ended, (EXTRA, tile))
     out_ref[1, N:, :] = jnp.broadcast_to(ended, (EXTRA, tile))
 
 
-def totals(half, x, dy, b, c, decays=None, pre=None, suf=None):
+def totals(half, place, x, dy, b, c, decays=None, pre=None, suf=None):
     local, width = x.shape
     heads = width // P_SIZE
     count = width // 2 // TILE
     whole = lambda a: pl.BlockSpec(a.shape, lambda j, pick: (0, 0))
-    column = pl.BlockSpec((local, TILE), lambda j, pick: (0, pick[0] * count + j))
-    factor = jax.ShapeDtypeStruct((local, 3 * heads), BF16)
+    column = pl.BlockSpec((local, TILE), lambda j, pick: (0, pick[half] * count + j))
+    factor = jax.ShapeDtypeStruct((local, LANES), BF16)
     rest = (pre, suf) if decays is None else (decays,)
-    out_specs = [pl.BlockSpec((2, N + EXTRA, TILE), lambda j, pick: (0, 0, j))]
-    out_shape = [jax.ShapeDtypeStruct((2, N + EXTRA, width // 2), F32)]
+    out_specs = [
+        pl.BlockSpec((2, N + EXTRA, TILE), lambda j, pick: (0, 0, j)),
+        pl.BlockSpec((2, 2, local, TILE), lambda j, pick: (0, 0, 0, j)),
+    ]
+    out_shape = [
+        jax.ShapeDtypeStruct((2, N + EXTRA, width // 2), F32),
+        jax.ShapeDtypeStruct((2, 2, local, width // 2), BF16),
+    ]
     if decays is not None:
         out_specs += [whole(factor), whole(factor)]
         out_shape += [factor, factor]
     return pl.pallas_call(
-        functools.partial(totals_kernel, heads, count),
+        functools.partial(totals_kernel, heads, count, half),
         grid_spec=pltpu.PrefetchScalarGridSpec(
             num_scalar_prefetch=1,
             grid=(count,),
@@ -141,7 +152,7 @@
         compiler_params=PARAMS,
         name="state_totals",
         cost_estimate=pl.CostEstimate(flops=8 * local * N * width // 2, bytes_accessed=4 * local * width, transcendentals=0),
-    )(half, x, dy, b, c, *rest)
+    )(place, x, dy, b, c, *rest)
 
 
 def ordered(core, mine, recv):
@@ -149,7 +160,7 @@
 
 
 def chip_kernel(chips, place_ref, mine_ref, recv_ref, *out_refs):
-    core, chip = place_ref[0], place_ref[1]
+    core, chip = place_ref[CORE], place_ref[CHIP]
     early, late = ordered(core, mine_ref[0], recv_ref[0])
     early_decay, late_decay = early[N : N + 1], late[N : N + 1]
     both = jnp.broadcast_to(early_decay * late_decay, (EXTRA, early.shape[1]))
@@ -181,7 +192,7 @@
 
 def carried_kernel(chips, place_ref, mine_ref, recv_ref, *refs):
     others, (own_ref, peer_ref) = refs[:-2], refs[-2:]
-    core, chip = place_ref[0], place_ref[1]
+    core, chip = place_ref[CORE], place_ref[CHIP]
     state = grad = jnp.zeros((N, own_ref.shape[2]), F32)
     state_weight = grad_weight = jnp.ones((1, own_ref.shape[2]), F32)
     for r, ref in enumerate(others, 1):
@@ -235,23 +246,22 @@
 
     @pl.when(step == 0)
     def _():
-        logs3 = log_parts(decays_ref[...])
+        logs = log_parts(decays_ref[...])
         rows = lax.broadcasted_iota(jnp.int32, (local, local), 0)
         columns = lax.broadcasted_iota(jnp.int32, (local, local), 1)
-        middle = (rows // SUB) * SUB + SUB // 2
-        same = rows // SUB == columns // SUB
-        later = same & (columns > middle) & (columns <= rows)
-        sooner = same & (columns > rows) & (columns <= middle)
-        signed = (later.astype(F32) - sooner.astype(F32)).astype(BF16)
-        offset = summed_logs(signed, logs3)
-        lift_ref[...] = packed_thirds(jnp.exp(offset), heads)
-        drop_ref[...] = packed_thirds(jnp.exp(-offset), heads)
-        chunk = lax.broadcasted_iota(jnp.int32, (2 * chunks, local), 0)
-        token = lax.broadcasted_iota(jnp.int32, (2 * chunks, local), 1)
-        inside = (token // SUB) == (chunk % chunks)
-        first = token % SUB <= SUB // 2
-        taken = inside & (first == (chunk < chunks))
-        rows_ref[...] = packed_thirds(jnp.exp(summed_logs(taken.astype(F32).astype(BF16), logs3)), heads)
+        start = columns & -SUB
+        middle = start + SUB // 2
+        later = (rows > middle) & (rows <= columns)
+        sooner = (rows > columns) & (rows <= middle)
+        offset = summed_logs(logs, later.astype(F32) - sooner.astype(F32))
+        lift_ref[...] = packed(jnp.exp(offset))
+        drop_ref[...] = packed(jnp.exp(-offset))
+        rows = lax.broadcasted_iota(jnp.int32, (local, LANES), 0)
+        columns = lax.broadcasted_iota(jnp.int32, (local, LANES), 1)
+        start = rows & -SUB
+        first = (rows - start <= SUB // 2) & (start == columns * SUB)
+        second = (rows - start > SUB // 2) & (start == (columns - chunks) * SUB)
+        rows_ref[...] = packed(jnp.exp(summed_logs(logs, first | second)))
         sums_ref[...] = jnp.zeros(sums_ref.shape, F32)
         map_ref[...] = jnp.zeros(map_ref.shape, F32)
         twice_ref[:, :N] = b_ref[...]
@@ -270,7 +280,7 @@
     dys_ref[0], dys_ref[1] = halves(dy_ref[...].astype(F32) * dot(lift_ref[...], table))
     drop = dot(drop_ref[...], table)
     xs_ref[0], xs_ref[1] = halves(x_ref[...].astype(F32) * drop)
-    row = dot(rows_ref[...], table)
+    row = dot(rows_ref[: 2 * chunks, :], table)
 
     state = None
     for k in range(chunks):
@@ -336,9 +346,9 @@
             jax.ShapeDtypeStruct((local, N), F32),
         ),
         scratch_shapes=[
-            pltpu.VMEM((local, 3 * heads), BF16),
-            pltpu.VMEM((local, 3 * heads), BF16),
-            pltpu.VMEM((2 * chunks, 3 * heads), BF16),
+            pltpu.VMEM((local, LANES), BF16),
+            pltpu.VMEM((local, LANES), BF16),
+            pltpu.VMEM((LANES, LANES), BF16),
             pltpu.VMEM((local, N + SUB), F32),
             pltpu.VMEM((local, 3 * SUB), BF16),
             pltpu.VMEM((local, 2 * N), BF16),
@@ -353,21 +363,19 @@
     )(x, dy, b, c, decays)
 
 
-def map_kernel(heads, count, ranks, pick_ref, x_ref, dy_ref, pre_ref, suf_ref, carry_ref, out_before_ref, map_before_ref, *refs):
+def map_kernel(count, ranks, place_ref, scaled_ref, carry_ref, out_before_ref, map_before_ref, *refs):
     messages, (out_ref, map_ref) = refs[:-2], refs[-2:]
     step = pl.program_id(0)
-    tile = dy_ref.shape[1]
 
     @pl.when(step == 0)
     def _():
         out_ref[...] = out_before_ref[...]
         map_ref[...] = map_before_ref[...]
 
-    table = spread(heads, (pick_ref[0] * count + step) * (tile // P_SIZE), tile)
-    scaled = halves(dy_ref[...].astype(F32) * dot(pre_ref[...], table))
-    out_ref[...] += dot22(scaled, halves(carry_ref[0]), NT)
-    scaled = halves(x_ref[...].astype(F32) * dot(suf_ref[...], table))
-    map_ref[...] += dot22(scaled, halves(carry_ref[1]), NT)
+    for i, sum_ref in enumerate((map_ref, out_ref)):
+        carry = halves(carry_ref[1 - i])
+        both = dot(scaled_ref[i, 0], stacked(*carry), NT)
+        sum_ref[...] += both[:, :N] + (both[:, N:] + dot(scaled_ref[i, 1], carry[0], NT))
 
     if messages:
 
@@ -375,33 +383,28 @@
         def _():
             rows = messages[0].shape[1]
             for r, message in enumerate(messages):
-                at = pl.ds(pl.multiple_of(((pick_ref[1] + r) % ranks) * rows, rows), rows)
+                at = pl.ds(pl.multiple_of(((place_ref[RANK] + r) % ranks) * rows, rows), rows)
                 message[0] = out_ref[at, :]
                 message[1] = map_ref[at, :]
 
 
-def map_terms(pick, x, dy, pre, suf, carry, out_before, map_before, ranks=0):
-    local, width = dy.shape
-    heads = width // P_SIZE
-    count = width // 2 // TILE
+def map_terms(place, scaled, carry, out_before, map_before, ranks=0):
+    local, width = scaled.shape[2:]
+    count = width // TILE
     whole = lambda a: pl.BlockSpec(a.shape, lambda j, pick: (0,) * len(a.shape))
     tokens = jax.ShapeDtypeStruct((local, N), F32)
-    column = pl.BlockSpec((local, TILE), lambda j, pick: (0, pick[0] * count + j))
     if ranks:
         out_shape = [jax.ShapeDtypeStruct((2, local // ranks, N), F32)] * ranks
         scratch = [pltpu.VMEM((local, N), F32), pltpu.VMEM((local, N), F32)]
     else:
         out_shape, scratch = [tokens, tokens], []
     return pl.pallas_call(
-        functools.partial(map_kernel, heads, count, ranks),
+        functools.partial(map_kernel, count, ranks),
         grid_spec=pltpu.PrefetchScalarGridSpec(
             num_scalar_prefetch=1,
             grid=(count,),
             in_specs=[
-                column,
-                column,
-                whole(pre),
-                whole(suf),
+                pl.BlockSpec((2, 2, local, TILE), lambda j, pick: (0, 0, 0, j)),
                 pl.BlockSpec((2, N, TILE), lambda j, pick: (0, 0, j)),
                 whole(tokens),
                 whole(tokens),
@@ -412,15 +415,15 @@
         out_shape=out_shape,
         compiler_params=PARAMS,
         name="map_terms",
-        cost_estimate=pl.CostEstimate(flops=12 * local * N * width // 2, bytes_accessed=4 * local * width, transcendentals=0),
-    )(pick, x, dy, pre, suf, carry, out_before, map_before)
+        cost_estimate=pl.CostEstimate(flops=12 * local * N * width, bytes_accessed=8 * local * width, transcendentals=0),
+    )(place, scaled, carry, out_before, map_before)
 
 
 def input_kernel(heads, count, pick_ref, part_ref, suf_ref, b_ref, own_ref, other_ref, input_ref):
     tile = part_ref.shape[1]
     step = pl.program_id(0)
     after = dot(suf_ref[...], spread(heads, step * (tile // P_SIZE), tile))
-    grad = jnp.where(step // count == pick_ref[0], own_ref[0], other_ref[0])
+    grad = jnp.where(step // count == pick_ref[CORE], own_ref[0], other_ref[0])
     input_ref[...] = (part_ref[...] + after * dot12(b_ref[...], halves(grad))).astype(BF16)
 
 
@@ -459,20 +462,19 @@
     chips = length // 2
     index, rank = lax.axis_index("seq"), lax.axis_index("head")
     core, chip = index % 2, index // 2
-    place = jnp.stack([core, chip]).astype(jnp.int32)
-    here = jnp.stack([core, rank]).astype(jnp.int32)
-    there = jnp.stack([1 - core, rank]).astype(jnp.int32)
-    sent, pre, suf = totals(there, mixer_input, output_grad, input_map, output_map, decays=decays)
+    place = jnp.stack([core, 1 - core, chip, rank]).astype(jnp.int32)
+    args = mixer_input, output_grad, input_map, output_map
+    sent, scaled_other, pre, suf = totals(OTHER, place, *args, decays=decays)
     recv = swap_cores(sent, length)
-    (mine,) = totals(here, mixer_input, output_grad, input_map, output_map, pre=pre, suf=suf)
+    mine, scaled_mine = totals(CORE, place, *args, pre=pre, suf=suf)
     messages = chip_totals(chips, place, mine, recv)
     others = [turned(message, "seq", length, 2 * r) for r, message in enumerate(messages, 1)]
-    part, out_part, map_part = local_part(mixer_input, output_grad, input_map, output_map, decays)
+    part, out_part, map_part = local_part(*args, decays)
     others, part, out_part, map_part = lax.optimization_barrier((others, part, out_part, map_part))
     own, peer = carried(chips, place, mine, recv, others)
     other = swap_cores(peer, length)
-    out_part, map_part = map_terms(here, mixer_input, output_grad, pre, suf, own, out_part, map_part)
-    shares = map_terms(there, mixer_input, output_grad, pre, suf, other, out_part, map_part, ranks)
+    out_part, map_part = map_terms(place, scaled_mine, own, out_part, map_part)
+    shares = map_terms(place, scaled_other, other, out_part, map_part, ranks)
     total = shares[0]
     own, other, shares = lax.optimization_barrier((own, other, shares))
     for r in range(1, ranks):

time: 84.4 us -> 69 us (0.82); the launches traced: 82.9 us -> 68.8 us
  Pallas kernels: 66.3 us -> 46.7 us
  waiting for transfers between devices: 2.66 us -> 6.22 us
  local copies, waits for them, and re-layouts: 3.83 us -> 6.5 us
  other arithmetic: 1.29 us -> 0.11 us
    pallas_call x4, Pallas kernels: 25.4 us -> 14.9 us  [the longest x2 8.81 us: totals(): pl.pallas_call(functools.partial(totals_kernel, heads, count, half), grid...]
    ppermute x6, waiting for transfers between devices: 2.66 us -> 6.22 us  [turned(): lax.ppermute(v, axis, [(i, (i + by) % length) for i in range(length)])]
    pallas_call x1, Pallas kernels: 8.5 us -> 5.57 us  [input_terms(): pl.pallas_call(functools.partial(input_kernel, heads, count), grid_spec=p...]
    unnamed x12 -> x16, local copies, waits for them, and re-layouts: 3.18 us -> 5.85 us
    pallas_call x1, Pallas kernels: 3.97 us -> 1.5 us  [carried(): pl.pallas_call(functools.partial(carried_kernel, chips), grid_spec=pltpu....]
    pallas_call x1, Pallas kernels: 3.26 us -> 1.14 us  [chip_totals(): pl.pallas_call(functools.partial(chip_kernel, chips), grid_spec=pltpu.Pre...]
    pallas_call x1, Pallas kernels: 25.2 us -> 23.6 us  [local_part(): pl.pallas_call(functools.partial(local_kernel, heads), grid=(count,), in_...]
    another operation x2 -> x1, other arithmetic: 1.26 us -> 0.08 us  [per_device(): place = jnp.stack([core, 1 - core, chip, rank]).astype(jnp.int32)]
  transfers between devices with their start and end apart: 8 -> 8, of which waited for: 2 -> 3; matrix products, arithmetic and copies ran while one was open for 1% -> 0% of each run, Pallas kernels for 55% -> 53%
where the time goes in v1:
time: 69 us; the launch traced here: 68.8 us
  Pallas kernels  46.7 us (68%)
  starting transfers between devices  8.41 us (12%)
  local copies, waits for them, and re-layouts  6.5 us (9%)
  waiting for transfers between devices  6.22 us (9%)
  between operations  0.77 us (1%)
    pallas_call x1, Pallas kernels, local_part(): pl.pallas_call(functools.partial(local_kernel, heads), grid=(count,), in_...  23.6 us
    pallas_call x2, Pallas kernels, totals(): pl.pallas_call(functools.partial(totals_kernel, heads, count, half), grid...  8.81 us
    ppermute x6, starting transfers between devices, turned(): lax.ppermute(v, axis, [(i, (i + by) % length) for i in range(length)])  6.6 us
    ppermute x6, waiting for transfers between devices, turned(): lax.ppermute(v, axis, [(i, (i + by) % length) for i in range(length)])  6.22 us
    pallas_call x2, Pallas kernels, map_terms(): pl.pallas_call(functools.partial(map_kernel, count, ranks), grid_spec=plt...  6.13 us
    unnamed x16, local copies, waits for them, and re-layouts  5.85 us
    pallas_call x1, Pallas kernels, input_terms(): pl.pallas_call(functools.partial(input_kernel, heads, count), grid_spec=p...  5.57 us
    ppermute x2, starting transfers between devices, swap_cores(): return lax.ppermute(v, 'seq', [(i, i ^ 1) for i in range(length)])  1.81 us
  transfers between devices with their start and end apart: 8, of which 3 were waited for; matrix products, arithmetic and copies ran while one was open for 0% of the time, Pallas kernels for 53%

profile of v1, /device:TPU:11, one launch (start us, length us, event | category | flops | bytes accessed | tf_op | source)
XLA Modules:
  0.0 68.8 jit_solution(14422401685373294641)
XLA Ops:
  0.7 1.6 %copy-done = bf16[512,2048]{1,0:T(8,128)(2,1)S(1)} copy-done((bf16[512,2048]{1,0:T(8,128)(2,1)S(1)}, bf16[512,2048]{1,0:T(8,128)(2,1)}, u32[]{:S(2)}) %copy-start) | copy-done | bytes 2097176
  2.3 1.6 %copy-done.2 = bf16[512,2048]{1,0:T(8,128)(2,1)S(1)} copy-done((bf16[512,2048]{1,0:T(8,128)(2,1)S(1)}, bf16[512,2048]{1,0:T(8,128)(2,1)}, u32[]{:S(2)}) %copy-start.2) | copy-done | bytes 2097176
  3.9 0.9 %copy-done.4 = bf16[512,128]{1,0:T(8,128)(2,1)S(1)} copy-done((bf16[512,128]{1,0:T(8,128)(2,1)S(1)}, bf16[512,128]{1,0:T(8,128)(2,1)}, u32[]{:S(2)}) %copy-start.4) | copy-done | bytes 131096
  4.8 0.9 %copy-done.5 = bf16[512,128]{1,0:T(8,128)(2,1)S(1)} copy-done((bf16[512,128]{1,0:T(8,128)(2,1)S(1)}, bf16[512,128]{1,0:T(8,128)(2,1)}, u32[]{:S(2)}) %copy-start.5) | copy-done | bytes 131096
  5.7 0.8 %copy-done.6 = f32[32,512]{1,0:T(8,128)S(1)} copy-done((f32[32,512]{1,0:T(8,128)S(1)}, f32[32,512]{1,0:T(8,128)}, u32[]{:S(2)}) %copy-start.6) | copy-done | bytes 65560
  6.6 4.5 %state_totals.2 = (f32[2,136,1024]{2,1,0:T(8,128)S(1)}, bf16[2,2,512,1024]{3,2,1,0:T(8,128)(2,1)S(1)}, bf16[512,128]{1,0:T(8,128)(2,1)S(1)}, bf16[512,128]{1,0:T(8,128)(2,1)S(1)}) custom-call(s32[4]{0:T(128)S(1)} %pad_add_fusion.place_ref.pick_ref, bf16[512,2048]{1,0:T(8,128)(2,1)S(1)} %copy-done, bf16[512,2048]{1,0:T(8,128)(2,1)S(1)} %copy-done.2, ...), custom_call_target="tpu_custom_call" | custom-call | flops 536870912 | bytes 4194304 | tf_op jit(solution)/shard_map/state_totals/pallas_call | solution.py:142
  11.1 0.7 %collective-permute-start = (f32[2,136,1024]{2,1,0:T(8,128)S(1)}, f32[2,136,1024]{2,1,0:T(8,128)S(1)}, u32[]{:S(2)}, u32[]{:S(2)}) collective-permute-start(f32[2,136,1024]{2,1,0:T(8,128)S(1)} %get-tuple-element.37), channel_id=1, source_target_pairs={{0,4},{4,0},{8,12},{12,8},{16,20},{20,16},{24,28},{28,24},{1,5},{5... | collective-permute-start | bytes 3342344 | tf_op jit(solution)/shard_map/ppermute | solution.py:453
  11.9 4.3 %state_totals.3 = (f32[2,136,1024]{2,1,0:T(8,128)S(1)}, bf16[2,2,512,1024]{3,2,1,0:T(8,128)(2,1)S(1)}) custom-call(s32[4]{0:T(128)S(1)} %pad_add_fusion.place_ref.pick_ref, bf16[512,2048]{1,0:T(8,128)(2,1)S(1)} %copy-done, bf16[512,2048]{1,0:T(8,128)(2,1)S(1)} %copy-done.2, bf16[512,128]{1,0:T(8,128)(2,1)S(1)} %copy-done.4, bf16[512,128]{1,0:T(8,128)(2,1)S(1)} %copy-done.5, ...), custom_call_target="tpu_custom_call" | custom-call | flops 536870912 | bytes 4194304 | tf_op jit(solution)/shard_map/state_totals/pallas_call | solution.py:142
  16.2 1.1 %chip_totals.1 = (f32[136,1024]{1,0:T(8,128)S(1)}, f32[136,1024]{1,0:T(8,128)S(1)}, f32[136,1024]{1,0:T(8,128)S(1)}) custom-call(s32[4]{0:T(128)S(1)} %pad_add_fusion.place_ref.pick_ref, f32[2,136,1024]{2,1,0:T(8,128)S(1)} %get-tuple-element.36.mine_ref, f32[2,136,1024]{2,1,0:T(8,128)S(1)} %collective-permute-done.recv_ref), custom_call_target="tpu_custom_call" | custom-call | flops 786432 | bytes 3145728 | tf_op jit(solution)/shard_map/chip_totals/pallas_call | solution.py:181
  17.3 1.3 %collective-permute-start.1 = (f32[136,1024]{1,0:T(8,128)S(1)}, f32[136,1024]{1,0:T(8,128)S(1)}, u32[]{:S(2)}, u32[]{:S(2)}) collective-permute-start(f32[136,1024]{1,0:T(8,128)S(1)} %get-tuple-element.38), channel_id=1, source_target_pairs={{0,8},{4,12},{8,16},{12,20},{16,24},{20,28},{24,0},{28,4},{1,9},{5... | collective-permute-start | bytes 1671176 | tf_op jit(solution)/shard_map/ppermute | solution.py:457
  18.8 1.3 %collective-permute-start.3 = (f32[136,1024]{1,0:T(8,128)S(1)}, f32[136,1024]{1,0:T(8,128)S(1)}, u32[]{:S(2)}, u32[]{:S(2)}) collective-permute-start(f32[136,1024]{1,0:T(8,128)S(1)} %get-tuple-element.40), channel_id=1, source_target_pairs={{0,24},{4,28},{8,0},{12,4},{16,8},{20,12},{24,16},{28,20},{1,25},{... | collective-permute-start | bytes 1671176 | tf_op jit(solution)/shard_map/ppermute | solution.py:457
  20.1 23.6 %local_part.1 = (f32[512,2048]{1,0:T(8,128)S(1)}, f32[512,128]{1,0:T(8,128)S(1)}, f32[512,128]{1,0:T(8,128)S(1)}) custom-call(bf16[512,2048]{1,0:T(8,128)(2,1)S(1)} %copy-done.1, bf16[512,2048]{1,0:T(8,128)(2,1)S(1)} %copy-done.3, bf16[512,128]{1,0:T(8,128)(2,1)S(1)} %copy-done.4, bf16[512,128]{1,0:T(8,128)(2,1)S(1)} %copy-done.5, f32[32,512]{1,0:T(8,128)S(1)} %copy-done.7), custom_call_target="tpu_custom_call" | custom-call | flops 5368709120 | bytes 8388608 | tf_op jit(solution)/shard_map/local_part/pallas_call | solution.py:338
  43.7 0.8 %collective-permute-done.3.refs_2_ = f32[136,1024]{1,0:T(8,128)S(1)} collective-permute-done((f32[136,1024]{1,0:T(8,128)S(1)}, f32[136,1024]{1,0:T(8,128)S(1)}, u32[]{:S(2)}, u32[]{:S(2)}) %collective-permute-start.3) | collective-permute-done | bytes 557088 | tf_op jit(solution)/shard_map/ppermute | solution.py:457
  44.5 1.5 %carried_in.1 = (f32[2,128,1024]{2,1,0:T(8,128)S(1)}, f32[2,128,1024]{2,1,0:T(8,128)S(1)}) custom-call(s32[4]{0:T(128)S(1)} %pad_add_fusion.place_ref.pick_ref, f32[2,136,1024]{2,1,0:T(8,128)S(1)} %get-tuple-element.36.mine_ref, f32[2,136,1024]{2,1,0:T(8,128)S(1)} %collective-permute-done.recv_ref, f32[136,1024]{1,0:T(8,128)S(1)} %collective-permute-done.1.refs_0_, ...), custom_call_target="tpu_custom_call" | custom-call | flops 2621440 | bytes 5767168 | tf_op jit(solution)/shard_map/carried_in/pallas_call | solution.py:224
  46.1 1.1 %collective-permute-start.4 = (f32[2,128,1024]{2,1,0:T(8,128)S(1)}, f32[2,128,1024]{2,1,0:T(8,128)S(1)}, u32[]{:S(2)}, u32[]{:S(2)}) collective-permute-start(f32[2,128,1024]{2,1,0:T(8,128)S(1)} %get-tuple-element.49), channel_id=1, source_target_pairs={{0,4},{4,0},{8,12},{12,8},{16,20},{20,16},{24,28},{28,24},{1,5},{5... | collective-permute-start | bytes 3145736 | tf_op jit(solution)/shard_map/ppermute | solution.py:453
  47.1 3.0 %map_terms.2 = (f32[512,128]{1,0:T(8,128)S(1)}, f32[512,128]{1,0:T(8,128)S(1)}) custom-call(s32[4]{0:T(128)S(1)} %pad_add_fusion.place_ref.pick_ref, bf16[2,2,512,1024]{3,2,1,0:T(8,128)(2,1)S(1)} %get-tuple-element.51.scaled_ref, f32[2,128,1024]{2,1,0:T(8,128)S(1)} %get-tuple-element.60.carry_ref.own_ref, f32[512,128]{1,0:T(8,128)S(1)} %get-tuple-element.52.out_before_ref, ...), custom_call_target="tpu_custom_call" | custom-call | flops 805306368 | bytes 4194304 | tf_op jit(solution)/shard_map/map_terms/pallas_call | solution.py:401
  50.2 3.1 %map_terms.3 = (f32[2,128,128]{2,1,0:T(8,128)S(1)}, f32[2,128,128]{2,1,0:T(8,128)S(1)}, f32[2,128,128]{2,1,0:T(8,128)S(1)}, f32[2,128,128]{2,1,0:T(8,128)S(1)}) custom-call(s32[4]{0:T(128)S(1)} %pad_add_fusion.place_ref.pick_ref, bf16[2,2,512,1024]{3,2,1,0:T(8,128)(2,1)S(1)} %get-tuple-element.50.scaled_ref, ...), custom_call_target="tpu_custom_call" | custom-call | flops 805306368 | bytes 4194304 | tf_op jit(solution)/shard_map/map_terms/pallas_call | solution.py:401
  53.3 1.3 %collective-permute-start.5 = (f32[2,128,128]{2,1,0:T(8,128)S(1)}, f32[2,128,128]{2,1,0:T(8,128)S(1)}, u32[]{:S(2)}, u32[]{:S(2)}) collective-permute-start(f32[2,128,128]{2,1,0:T(8,128)S(1)} %get-tuple-element.62), channel_id=1, source_target_pairs={{0,1},{1,2},{2,3},{3,0},{4,5},{5,6},{6,7},{7,4},{8,9},{9,10},{10,1... | collective-permute-start | bytes 393224 | tf_op jit(solution)/shard_map/ppermute | solution.py:457
  54.6 1.1 %collective-permute-start.6 = (f32[2,128,128]{2,1,0:T(8,128)S(1)}, f32[2,128,128]{2,1,0:T(8,128)S(1)}, u32[]{:S(2)}, u32[]{:S(2)}) collective-permute-start(f32[2,128,128]{2,1,0:T(8,128)S(1)} %get-tuple-element.63), channel_id=1, source_target_pairs={{0,2},{1,3},{2,0},{3,1},{4,6},{5,7},{6,4},{7,5},{8,10},{9,11},{10,... | collective-permute-start | bytes 393224 | tf_op jit(solution)/shard_map/ppermute | solution.py:457
  55.7 1.4 %collective-permute-start.7 = (f32[2,128,128]{2,1,0:T(8,128)S(1)}, f32[2,128,128]{2,1,0:T(8,128)S(1)}, u32[]{:S(2)}, u32[]{:S(2)}) collective-permute-start(f32[2,128,128]{2,1,0:T(8,128)S(1)} %get-tuple-element.64), channel_id=1, source_target_pairs={{0,3},{1,0},{2,1},{3,2},{4,7},{5,4},{6,5},{7,6},{8,11},{9,8},{10,9... | collective-permute-start | bytes 393224 | tf_op jit(solution)/shard_map/ppermute | solution.py:457
  57.1 5.6 %input_terms.1 = bf16[512,2048]{1,0:T(8,128)(2,1)} custom-call(s32[4]{0:T(128)S(1)} %pad_add_fusion.place_ref.pick_ref, f32[512,2048]{1,0:T(8,128)S(1)} %get-tuple-element.44.part_ref, bf16[512,128]{1,0:T(8,128)(2,1)S(1)} %get-tuple-element.35.refs_1_.suf_ref, bf16[512,128]{1,0:T(8,128)(2,1)S(1)} %copy-done.4, ...), custom_call_target="tpu_custom_call" | custom-call | flops 536870912 | bytes 8388608 | tf_op jit(solution)/shard_map/input_terms/pallas_call | solution.py:437
  62.7 3.3 %collective-permute-done.6 = f32[2,128,128]{2,1,0:T(8,128)S(1)} collective-permute-done((f32[2,128,128]{2,1,0:T(8,128)S(1)}, f32[2,128,128]{2,1,0:T(8,128)S(1)}, u32[]{:S(2)}, u32[]{:S(2)}) %collective-permute-start.6) | collective-permute-done | bytes 131104 | tf_op jit(solution)/shard_map/ppermute | solution.py:457
  66.0 2.1 %collective-permute-done.7 = f32[2,128,128]{2,1,0:T(8,128)S(1)} collective-permute-done((f32[2,128,128]{2,1,0:T(8,128)S(1)}, f32[2,128,128]{2,1,0:T(8,128)S(1)}, u32[]{:S(2)}, u32[]{:S(2)}) %collective-permute-start.7) | collective-permute-done | bytes 131104 | tf_op jit(solution)/shard_map/ppermute | solution.py:457
  68.1 0.7 slice_bitcast_fusion
  (19 shorter events, 0.4 us)
Async XLA Ops:
  0.7 1.6 %copy-start = (bf16[512,2048]{1,0:T(8,128)(2,1)S(1)}, bf16[512,2048]{1,0:T(8,128)(2,1)}, u32[]{:S(2)}) copy-start(bf16[512,2048]{1,0:T(8,128)(2,1)} %x_ref.5) | copy-start | bytes 6291460
  2.3 1.6 %copy-start.2 = (bf16[512,2048]{1,0:T(8,128)(2,1)S(1)}, bf16[512,2048]{1,0:T(8,128)(2,1)}, u32[]{:S(2)}) copy-start(bf16[512,2048]{1,0:T(8,128)(2,1)} %dy_ref.5) | copy-start | bytes 6291460
  3.9 0.9 %copy-start.4 = (bf16[512,128]{1,0:T(8,128)(2,1)S(1)}, bf16[512,128]{1,0:T(8,128)(2,1)}, u32[]{:S(2)}) copy-start(bf16[512,128]{1,0:T(8,128)(2,1)} %b_ref.7) | copy-start | bytes 393220
  4.8 0.9 %copy-start.5 = (bf16[512,128]{1,0:T(8,128)(2,1)S(1)}, bf16[512,128]{1,0:T(8,128)(2,1)}, u32[]{:S(2)}) copy-start(bf16[512,128]{1,0:T(8,128)(2,1)} %c_ref.5) | copy-start | bytes 393220
  5.7 0.8 %copy-start.6 = (f32[32,512]{1,0:T(8,128)S(1)}, f32[32,512]{1,0:T(8,128)}, u32[]{:S(2)}) copy-start(f32[32,512]{1,0:T(8,128)} %decays_ref.1) | copy-start | bytes 196612
  11.1 5.0 %collective-permute-start = (f32[2,136,1024]{2,1,0:T(8,128)S(1)}, f32[2,136,1024]{2,1,0:T(8,128)S(1)}, u32[]{:S(2)}, u32[]{:S(2)}) collective-permute-start(f32[2,136,1024]{2,1,0:T(8,128)S(1)} %get-tuple-element.37), channel_id=1, source_target_pairs={{0,4},{4,0},{8,12},{12,8},{16,20},{20,16},{24,28},{28,24},{1,5},{5... | collective-permute-start | bytes 3342344 | tf_op jit(solution)/shard_map/ppermute | solution.py:453
  11.9 8.2 %copy-start.3 = (bf16[512,2048]{1,0:T(8,128)(2,1)S(1)}, bf16[512,2048]{1,0:T(8,128)(2,1)}, u32[]{:S(2)}) copy-start(bf16[512,2048]{1,0:T(8,128)(2,1)} %dy_ref.5) | copy-start | bytes 6291460
  16.1 4.0 %copy-start.1 = (bf16[512,2048]{1,0:T(8,128)(2,1)S(1)}, bf16[512,2048]{1,0:T(8,128)(2,1)}, u32[]{:S(2)}) copy-start(bf16[512,2048]{1,0:T(8,128)(2,1)} %x_ref.5) | copy-start | bytes 6291460
  16.1 4.0 %copy-start.7 = (f32[32,512]{1,0:T(8,128)S(1)}, f32[32,512]{1,0:T(8,128)}, u32[]{:S(2)}) copy-start(f32[32,512]{1,0:T(8,128)} %decays_ref.1) | copy-start | bytes 196612
  17.3 26.4 %collective-permute-start.1 = (f32[136,1024]{1,0:T(8,128)S(1)}, f32[136,1024]{1,0:T(8,128)S(1)}, u32[]{:S(2)}, u32[]{:S(2)}) collective-permute-start(f32[136,1024]{1,0:T(8,128)S(1)} %get-tuple-element.38), channel_id=1, source_target_pairs={{0,8},{4,12},{8,16},{12,20},{16,24},{20,28},{24,0},{28,4},{1,9},{5... | collective-permute-start | bytes 1671176 | tf_op jit(solution)/shard_map/ppermute | solution.py:457
  18.6 25.1 %collective-permute-start.2 = (f32[136,1024]{1,0:T(8,128)S(1)}, f32[136,1024]{1,0:T(8,128)S(1)}, u32[]{:S(2)}, u32[]{:S(2)}) collective-permute-start(f32[136,1024]{1,0:T(8,128)S(1)} %get-tuple-element.39), channel_id=1, source_target_pairs={{0,16},{4,20},{8,24},{12,28},{16,0},{20,4},{24,8},{28,12},{1,17},{... | collective-permute-start | bytes 1671176 | tf_op jit(solution)/shard_map/ppermute | solution.py:457
  18.8 25.7 %collective-permute-start.3 = (f32[136,1024]{1,0:T(8,128)S(1)}, f32[136,1024]{1,0:T(8,128)S(1)}, u32[]{:S(2)}, u32[]{:S(2)}) collective-permute-start(f32[136,1024]{1,0:T(8,128)S(1)} %get-tuple-element.40), channel_id=1, source_target_pairs={{0,24},{4,28},{8,0},{12,4},{16,8},{20,12},{24,16},{28,20},{1,25},{... | collective-permute-start | bytes 1671176 | tf_op jit(solution)/shard_map/ppermute | solution.py:457
  46.1 4.1 %collective-permute-start.4 = (f32[2,128,1024]{2,1,0:T(8,128)S(1)}, f32[2,128,1024]{2,1,0:T(8,128)S(1)}, u32[]{:S(2)}, u32[]{:S(2)}) collective-permute-start(f32[2,128,1024]{2,1,0:T(8,128)S(1)} %get-tuple-element.49), channel_id=1, source_target_pairs={{0,4},{4,0},{8,12},{12,8},{16,20},{20,16},{24,28},{28,24},{1,5},{5... | collective-permute-start | bytes 3145736 | tf_op jit(solution)/shard_map/ppermute | solution.py:453
  53.3 9.4 %collective-permute-start.5 = (f32[2,128,128]{2,1,0:T(8,128)S(1)}, f32[2,128,128]{2,1,0:T(8,128)S(1)}, u32[]{:S(2)}, u32[]{:S(2)}) collective-permute-start(f32[2,128,128]{2,1,0:T(8,128)S(1)} %get-tuple-element.62), channel_id=1, source_target_pairs={{0,1},{1,2},{2,3},{3,0},{4,5},{5,6},{6,7},{7,4},{8,9},{9,10},{10,1... | collective-permute-start | bytes 393224 | tf_op jit(solution)/shard_map/ppermute | solution.py:457
  54.6 11.3 %collective-permute-start.6 = (f32[2,128,128]{2,1,0:T(8,128)S(1)}, f32[2,128,128]{2,1,0:T(8,128)S(1)}, u32[]{:S(2)}, u32[]{:S(2)}) collective-permute-start(f32[2,128,128]{2,1,0:T(8,128)S(1)} %get-tuple-element.63), channel_id=1, source_target_pairs={{0,2},{1,3},{2,0},{3,1},{4,6},{5,7},{6,4},{7,5},{8,10},{9,11},{10,... | collective-permute-start | bytes 393224 | tf_op jit(solution)/shard_map/ppermute | solution.py:457
  55.7 12.3 %collective-permute-start.7 = (f32[2,128,128]{2,1,0:T(8,128)S(1)}, f32[2,128,128]{2,1,0:T(8,128)S(1)}, u32[]{:S(2)}, u32[]{:S(2)}) collective-permute-start(f32[2,128,128]{2,1,0:T(8,128)S(1)} %get-tuple-element.64), channel_id=1, source_target_pairs={{0,3},{1,0},{2,1},{3,2},{4,7},{5,4},{6,5},{7,6},{8,11},{9,8},{10,9... | collective-permute-start | bytes 393224 | tf_op jit(solution)/shard_map/ppermute | solution.py:457

commit v2 on v1

--- a/solution.py
+++ b/solution.py
@@ -15,6 +15,7 @@
 LANES = 128
 CORE, OTHER, CHIP, RANK = range(4)
 PARAMS = pltpu.CompilerParams(vmem_limit_bytes=24 * 1024 * 1024)
+FIRST = pltpu.CompilerParams(vmem_limit_bytes=60 * 1024 * 1024)
 F32 = jnp.float32
 BF16 = jnp.bfloat16
 
@@ -149,7 +150,7 @@
             scratch_shapes=[pltpu.VMEM((N, local), BF16), pltpu.VMEM((N, local), BF16)],
         ),
         out_shape=out_shape,
-        compiler_params=PARAMS,
+        compiler_params=FIRST,
         name="state_totals",
         cost_estimate=pl.CostEstimate(flops=8 * local * N * width // 2, bytes_accessed=4 * local * width, transcendentals=0),
     )(place, x, dy, b, c, *rest)
@@ -236,95 +237,146 @@
     )(place, mine, recv, *others)
 
 
+def blocks(chunks):
+    span = 1
+    while span < chunks:
+        yield span, [at for at in range(span, chunks, 2 * span)]
+        span *= 2
+
+
+def row_bounds(chunks):
+    for span, _ in blocks(chunks):
+        for k in range(chunks):
+            middle = k * SUB + SUB // 2
+            boundary = (k // span + 1 - (k // span) % 2) * span * SUB
+            yield (boundary, middle + 1) if middle >= boundary else (middle + 1, boundary)
+
+
+def local_factors(decays, lift_ref, drop_ref, rows_ref):
+    local = decays.shape[1]
+    logs = log_parts(decays)
+    rows = lax.broadcasted_iota(jnp.int32, (local, local), 0)
+    columns = lax.broadcasted_iota(jnp.int32, (local, local), 1)
+    middle = (columns & -SUB) + SUB // 2
+    later = (rows > middle) & (rows <= columns)
+    sooner = (rows > columns) & (rows <= middle)
+    offset = summed_logs(logs, later.astype(F32) - sooner.astype(F32))
+    lift_ref[...] = packed(jnp.exp(offset))
+    drop_ref[...] = packed(jnp.exp(-offset))
+    width = rows_ref.shape[0]
+    lane = lax.broadcasted_iota(jnp.int32, (1, width), 1)
+    first = last = jnp.zeros((1, width), jnp.int32)
+    for i, (start, end) in enumerate(row_bounds(local // SUB)):
+        first, last = jnp.where(lane == i, start, first), jnp.where(lane == i, end, last)
+    rows = lax.broadcasted_iota(jnp.int32, (local, width), 0)
+    rows_ref[...] = packed(jnp.exp(summed_logs(logs, (rows >= first) & (rows < last))))
+
+
+def score_parts(b, c, ref, at, causal):
+    score = dot(b, c, NT)
+    if causal:
+        rows = lax.broadcasted_iota(jnp.int32, score.shape, 0)
+        columns = lax.broadcasted_iota(jnp.int32, score.shape, 1)
+        score = jnp.where(rows <= columns, score, 0.0)
+    hi, lo = halves(score)
+    width = score.shape[1]
+    ref[at, :width] = hi
+    ref[at, width : 2 * width] = lo
+    if ref.shape[1] > 2 * width:
+        ref[at, 2 * width :] = hi
+
+
+def scored(ref, at, dys):
+    width = dys[0].shape[0]
+    if ref.shape[1] > 2 * width:
+        return dot(ref[at, :], stacked(dys[0], dys[0], dys[1]))
+    return dot(ref[at, :], stacked(dys[0], dys[0])) + dot(ref[at, :width], dys[1])
+
+
+def add_mixed(ref, at, dys, xs):
+    width = xs[0].shape[0]
+    both = dot(dys[0], stacked(*xs), NT)
+    if width < LANES:
+        ref[at, :] += both
+        ref[at, :width] += dot(dys[1], xs[0], NT)
+    else:
+        ref[at, :] += both[:, :width] + (both[:, width:] + dot(dys[1], xs[0], NT))
+
+
+def added_up(v, width):
+    return v[:, :width] + v[:, width:] if v.shape[1] > width else v
+
+
 def local_kernel(
     heads, x_ref, dy_ref, b_ref, c_ref, decays_ref, part_ref, out_ref, map_ref,
-    lift_ref, drop_ref, rows_ref, sums_ref, scores_ref, twice_ref, bt_ref, ct_ref, dys_ref, xs_ref,
+    lift_ref, drop_ref, rows_ref, full_ref, dys_ref, xs_ref, back_ref, sums_ref, scores_ref, *level_refs,
 ):
     local, tile = x_ref.shape
     chunks = local // SUB
     step = pl.program_id(0)
+    levels = [(span, at, level_refs[2 * i], level_refs[2 * i + 1]) for i, (span, at) in enumerate(blocks(chunks))]
 
     @pl.when(step == 0)
     def _():
-        logs = log_parts(decays_ref[...])
-        rows = lax.broadcasted_iota(jnp.int32, (local, local), 0)
-        columns = lax.broadcasted_iota(jnp.int32, (local, local), 1)
-        start = columns & -SUB
-        middle = start + SUB // 2
-        later = (rows > middle) & (rows <= columns)
-        sooner = (rows > columns) & (rows <= middle)
-        offset = summed_logs(logs, later.astype(F32) - sooner.astype(F32))
-        lift_ref[...] = packed(jnp.exp(offset))
-        drop_ref[...] = packed(jnp.exp(-offset))
-        rows = lax.broadcasted_iota(jnp.int32, (local, LANES), 0)
-        columns = lax.broadcasted_iota(jnp.int32, (local, LANES), 1)
-        start = rows & -SUB
-        first = (rows - start <= SUB // 2) & (start == columns * SUB)
-        second = (rows - start > SUB // 2) & (start == (columns - chunks) * SUB)
-        rows_ref[...] = packed(jnp.exp(summed_logs(logs, first | second)))
+        local_factors(decays_ref[...], lift_ref, drop_ref, rows_ref)
         sums_ref[...] = jnp.zeros(sums_ref.shape, F32)
-        map_ref[...] = jnp.zeros(map_ref.shape, F32)
-        twice_ref[:, :N] = b_ref[...]
-        twice_ref[:, N:] = b_ref[...]
-        sooner = lax.broadcasted_iota(jnp.int32, (SUB, SUB), 0) <= lax.broadcasted_iota(jnp.int32, (SUB, SUB), 1)
         for k in range(chunks):
             at = pl.ds(k * SUB, SUB)
-            hi, lo = halves(jnp.where(sooner, dot(b_ref[at, :], c_ref[at, :], NT), 0.0))
-            scores_ref[at, :SUB] = hi
-            scores_ref[at, SUB : 2 * SUB] = lo
-            scores_ref[at, 2 * SUB :] = hi
-            bt_ref[k] = transposed(stacked(b_ref[at, :], b_ref[at, :]))
-            ct_ref[k] = transposed(stacked(c_ref[at, :], c_ref[at, :]))
+            score_parts(b_ref[at, :], c_ref[at, :], scores_ref, at, True)
+        for span, boundaries, mixed_ref, level_scores_ref in levels:
+            mixed_ref[...] = jnp.zeros(mixed_ref.shape, F32)
+            size = span * SUB
+            for i, boundary in enumerate(boundaries):
+                before, after = pl.ds((boundary - span) * SUB, size), pl.ds(boundary * SUB, size)
+                score_parts(b_ref[before, :], c_ref[after, :], level_scores_ref, pl.ds(i * size, size), False)
 
     table = spread(heads, step * (tile // P_SIZE), tile)
-    dys_ref[0], dys_ref[1] = halves(dy_ref[...].astype(F32) * dot(lift_ref[...], table))
-    drop = dot(drop_ref[...], table)
-    xs_ref[0], xs_ref[1] = halves(x_ref[...].astype(F32) * drop)
-    row = dot(rows_ref[: 2 * chunks, :], table)
-
-    state = None
+    dys_ref[...] = dy_ref[...].astype(F32) * dot(lift_ref[...], table)
+    back_ref[...] = dot(drop_ref[...], table)
+    xs_ref[...] = x_ref[...].astype(F32) * back_ref[...]
+    row = dot(rows_ref[...], table)
+
     for k in range(chunks):
         at = pl.ds(k * SUB, SUB)
-        dys, xs = (dys_ref[0, at, :], dys_ref[1, at, :]), (xs_ref[0, at, :], xs_ref[1, at, :])
-        to_middle, to_end = row[k : k + 1], row[chunks + k : chunks + k + 1]
-        if state is None:
-            against = xs
-        else:
-            scaled = halves(state * to_middle)
-            against = stacked(scaled[0], xs[0]), stacked(scaled[1], xs[1])
-        both = dot(stacked(*dys), against[0], NT)
-        summed = both[:SUB] + (both[SUB:] + dot(dys[0], against[1], NT))
-        if state is None:
-            sums_ref[at, N:] += summed
-        else:
-            sums_ref[at, :] += summed
-        if k < chunks - 1:
-            gained = to_end * dot(bt_ref[k], stacked(*xs))
-            state = gained if state is None else (to_middle * to_end) * state + gained
-    grad = None
-    for k in reversed(range(chunks)):
-        at = pl.ds(k * SUB, SUB)
-        dys, xs = (dys_ref[0, at, :], dys_ref[1, at, :]), (xs_ref[0, at, :], xs_ref[1, at, :])
-        to_middle, to_end = row[k : k + 1], row[chunks + k : chunks + k + 1]
-        summed = dot(scores_ref[at, :], stacked(dys[0], dys[0], dys[1]))
-        if grad is not None:
-            scaled = halves(grad * to_end)
-            summed = summed + dot(twice_ref[at, :], stacked(*scaled))
-            both = dot(stacked(*xs), scaled[0], NT)
-            map_ref[at, :] += both[:SUB] + (both[SUB:] + dot(xs[0], scaled[1], NT))
-        part_ref[at, :] = drop[k * SUB : (k + 1) * SUB] * summed
-        if k > 0:
-            gained = to_middle * dot(ct_ref[k], stacked(*dys))
-            grad = gained if grad is None else (to_middle * to_end) * grad + gained
+        dys, xs = halves(dys_ref[at, :]), halves(xs_ref[at, :])
+        add_mixed(sums_ref, at, dys, xs)
+        part_ref[at, :] = back_ref[at, :] * scored(scores_ref, at, dys)
+
+    for level, (span, boundaries, mixed_ref, level_scores_ref) in enumerate(levels):
+        size = span * SUB
+        for i, boundary in enumerate(boundaries):
+            at = pl.ds(i * size, size)
+            factor = lambda k: row[level * chunks + k : level * chunks + k + 1]
+            take = lambda ref, first: halves(
+                stacked(*[ref[k * SUB : (k + 1) * SUB, :] * factor(k) for k in range(first, first + span)])
+            )
+            dys, xs = take(dys_ref, boundary), take(xs_ref, boundary - span)
+            add_mixed(mixed_ref, at, dys, xs)
+            gained = scored(level_scores_ref, at, dys)
+            for q in range(span):
+                k = boundary - span + q
+                rows = pl.ds(k * SUB, SUB)
+                part_ref[rows, :] += (back_ref[rows, :] * factor(k)) * gained[q * SUB : (q + 1) * SUB]
 
     @pl.when(step == pl.num_programs(0) - 1)
     def _():
-        causal = lax.broadcasted_iota(jnp.int32, (SUB, SUB), 0) >= lax.broadcasted_iota(jnp.int32, (SUB, SUB), 1)
+        full_ref[...] = jnp.zeros(full_ref.shape, F32)
+        rows = lax.broadcasted_iota(jnp.int32, (SUB, SUB), 0)
+        columns = lax.broadcasted_iota(jnp.int32, (SUB, SUB), 1)
         for k in range(chunks):
             at = pl.ds(k * SUB, SUB)
-            mixed = jnp.where(causal, sums_ref[at, N:], 0.0)
-            out_ref[at, :] = sums_ref[at, :N] + dot21(halves(mixed), b_ref[at, :])
-            map_ref[at, :] += dot21(halves(mixed.T), c_ref[at, :])
+            full_ref[at, k * SUB : (k + 1) * SUB] = jnp.where(rows >= columns, added_up(sums_ref[at, :], SUB), 0.0)
+        for span, boundaries, mixed_ref, _ in levels:
+            size = span * SUB
+            for i, boundary in enumerate(boundaries):
+                block = added_up(mixed_ref[pl.ds(i * size, size), :], size)
+                full_ref[pl.ds(boundary * SUB, size), (boundary - span) * SUB : boundary * SUB] = block
+        map_ref[...] = jnp.zeros(map_ref.shape, F32)
+        for k in range(0, local, LANES):
+            at = pl.ds(k, LANES)
+            mixed = full_ref[at, :]
+            out_ref[at, :] = dot21(halves(mixed), b_ref[...])
+            map_ref[...] += dot21(halves(mixed.T), c_ref[at, :])
 
 
 def local_part(x, dy, b, c, decays):
@@ -335,6 +387,21 @@
     whole = lambda a: pl.BlockSpec(a.shape, lambda j: (0, 0))
     column = pl.BlockSpec((local, TILE), lambda j: (0, j))
     tokens = pl.BlockSpec((local, N), lambda j: (0, 0))
+    scratch = [
+        pltpu.VMEM((local, LANES), BF16),
+        pltpu.VMEM((local, LANES), BF16),
+        pltpu.VMEM((LANES, LANES), BF16),
+        pltpu.VMEM((local, local), F32),
+        pltpu.VMEM((local, TILE), F32),
+        pltpu.VMEM((local, TILE), F32),
+        pltpu.VMEM((local, TILE), F32),
+        pltpu.VMEM((local, 2 * SUB), F32),
+        pltpu.VMEM((local, 3 * SUB), BF16),
+    ]
+    for span, _ in blocks(chunks):
+        size = span * SUB
+        scratch.append(pltpu.VMEM((local // 2, max(size, LANES)), F32))
+        scratch.append(pltpu.VMEM((local // 2, (3 if size < LANES else 2) * size), BF16))
     return pl.pallas_call(
         functools.partial(local_kernel, heads),
         grid=(count,),
@@ -345,18 +412,7 @@
             jax.ShapeDtypeStruct((local, N), F32),
             jax.ShapeDtypeStruct((local, N), F32),
         ),
-        scratch_shapes=[
-            pltpu.VMEM((local, LANES), BF16),
-            pltpu.VMEM((local, LANES), BF16),
-            pltpu.VMEM((LANES, LANES), BF16),
-            pltpu.VMEM((local, N + SUB), F32),
-            pltpu.VMEM((local, 3 * SUB), BF16),
-            pltpu.VMEM((local, 2 * N), BF16),
-            pltpu.VMEM((chunks, N, 2 * SUB), BF16),
-            pltpu.VMEM((chunks, N, 2 * SUB), BF16),
-            pltpu.VMEM((2, local, TILE), BF16),
-            pltpu.VMEM((2, local, TILE), BF16),
-        ],
+        scratch_shapes=scratch,
         compiler_params=PARAMS,
         name="local_part",
         cost_estimate=pl.CostEstimate(flops=40 * local * N * width, bytes_accessed=8 * local * width, transcendentals=0),

time: 69 us -> 69 us (level)
  waiting for transfers between devices: 6.22 us -> 16.8 us
  Pallas kernels: 46.7 us -> 39.9 us
  local copies, waits for them, and re-layouts: 6.5 us -> 2.08 us
    pallas_call x1, Pallas kernels: 23.6 us -> 12.9 us  [local_part(): pl.pallas_call(functools.partial(local_kernel, heads), grid=(count,), in_...]
    ppermute x6, waiting for transfers between devices: 6.22 us -> 16.8 us  [turned(): lax.ppermute(v, axis, [(i, (i + by) % length) for i in range(length)])]
    unnamed x16 -> x20, local copies, waits for them, and re-layouts: 5.85 us -> 1.42 us
    pallas_call x2, Pallas kernels: 8.81 us -> 12.6 us  [totals(): pl.pallas_call(functools.partial(totals_kernel, heads, count, half), grid...]
  transfers between devices with their start and end apart: 8 -> 8, of which waited for: 3 -> 3; matrix products, arithmetic and copies ran while one was open for 0% -> 0% of each run, Pallas kernels for 53% -> 41%
where the time goes in v2:
time: 69 us; the launch traced here: 68.7 us
  Pallas kernels  39.9 us (58%)
  waiting for transfers between devices  16.8 us (24%)
  starting transfers between devices  8.42 us (12%)
  local copies, waits for them, and re-layouts  2.08 us (3%)
  between operations  0.8 us (1%)
    ppermute x6, waiting for transfers between devices, turned(): lax.ppermute(v, axis, [(i, (i + by) % length) for i in range(length)])  16.8 us
    pallas_call x1, Pallas kernels, local_part(): pl.pallas_call(functools.partial(local_kernel, heads), grid=(count,), in_...  12.9 us
    pallas_call x2, Pallas kernels, totals(): pl.pallas_call(functools.partial(totals_kernel, heads, count, half), grid...  12.6 us
    ppermute x6, starting transfers between devices, turned(): lax.ppermute(v, axis, [(i, (i + by) % length) for i in range(length)])  6.62 us
    pallas_call x2, Pallas kernels, map_terms(): pl.pallas_call(functools.partial(map_kernel, count, ranks), grid_spec=plt...  6.15 us
    pallas_call x1, Pallas kernels, input_terms(): pl.pallas_call(functools.partial(input_kernel, heads, count), grid_spec=p...  5.56 us
    ppermute x2, starting transfers between devices, swap_cores(): return lax.ppermute(v, 'seq', [(i, i ^ 1) for i in range(length)])  1.79 us
    pallas_call x1, Pallas kernels, carried(): pl.pallas_call(functools.partial(carried_kernel, chips), grid_spec=pltpu....  1.5 us
  transfers between devices with their start and end apart: 8, of which 3 were waited for; matrix products, arithmetic and copies ran while one was open for 0% of the time, Pallas kernels for 41%

profile of v2, /device:TPU:11, one launch (start us, length us, event | category | flops | bytes accessed | tf_op | source)
XLA Modules:
  0.0 68.7 jit_solution(18121889984586400140)
XLA Ops:
  0.6 0.7 pad_add_fusion.place_ref.pick_ref
  1.3 6.3 %state_totals.2 = (f32[2,136,1024]{2,1,0:T(8,128)}, bf16[2,2,512,1024]{3,2,1,0:T(8,128)(2,1)}, bf16[512,128]{1,0:T(8,128)(2,1)}, bf16[512,128]{1,0:T(8,128)(2,1)}) custom-call(s32[4]{0:T(128)} %pad_add_fusion.place_ref.pick_ref, bf16[512,2048]{1,0:T(8,128)(2,1)} %x_ref.5, bf16[512,2048]{1,0:T(8,128)(2,1)} %dy_ref.5, bf16[512,128]{1,0:T(8,128)(2,1)} %b_ref.7, ...), custom_call_target="tpu_custom_call" | custom-call | flops 536870912 | bytes 4194304 | tf_op jit(solution)/shard_map/state_totals/pallas_call | solution.py:143
  7.6 0.7 %collective-permute-start = (f32[2,136,1024]{2,1,0:T(8,128)}, f32[2,136,1024]{2,1,0:T(8,128)S(1)}, u32[]{:S(2)}, u32[]{:S(2)}) collective-permute-start(f32[2,136,1024]{2,1,0:T(8,128)} %get-tuple-element.37), channel_id=1, source_target_pairs={{0,4},{4,0},{8,12},{12,8},{16,20},{20,16},{24,28},{28,24},{1,5},{5... | collective-permute-start | bytes 3342344 | tf_op jit(solution)/shard_map/ppermute | solution.py:509
  8.3 0.0 copy-start.8
  8.3 6.3 %state_totals.3 = (f32[2,136,1024]{2,1,0:T(8,128)}, bf16[2,2,512,1024]{3,2,1,0:T(8,128)(2,1)}) custom-call(s32[4]{0:T(128)} %pad_add_fusion.place_ref.pick_ref, bf16[512,2048]{1,0:T(8,128)(2,1)} %x_ref.5, bf16[512,2048]{1,0:T(8,128)(2,1)} %dy_ref.5, bf16[512,128]{1,0:T(8,128)(2,1)} %b_ref.7, bf16[512,128]{1,0:T(8,128)(2,1)} %c_ref.5, ...), custom_call_target="tpu_custom_call" | custom-call | flops 536870912 | bytes 4194304 | tf_op jit(solution)/shard_map/state_totals/pallas_call | solution.py:143
  14.7 1.4 %copy-done.2 = f32[2,136,1024]{2,1,0:T(8,128)S(1)} copy-done((f32[2,136,1024]{2,1,0:T(8,128)S(1)}, f32[2,136,1024]{2,1,0:T(8,128)}, u32[]{:S(2)}) %copy-start.2) | copy-done | bytes 1114136
  16.0 1.1 %chip_totals.1 = (f32[136,1024]{1,0:T(8,128)S(1)}, f32[136,1024]{1,0:T(8,128)S(1)}, f32[136,1024]{1,0:T(8,128)S(1)}) custom-call(s32[4]{0:T(128)S(1)} %copy-done.9, f32[2,136,1024]{2,1,0:T(8,128)S(1)} %copy-done.2, f32[2,136,1024]{2,1,0:T(8,128)S(1)} %collective-permute-done.recv_ref), custom_call_target="tpu_custom_call" | custom-call | flops 786432 | bytes 3145728 | tf_op jit(solution)/shard_map/chip_totals/pallas_call | solution.py:182
  17.2 1.3 %collective-permute-start.1 = (f32[136,1024]{1,0:T(8,128)S(1)}, f32[136,1024]{1,0:T(8,128)S(1)}, u32[]{:S(2)}, u32[]{:S(2)}) collective-permute-start(f32[136,1024]{1,0:T(8,128)S(1)} %get-tuple-element.38), channel_id=1, source_target_pairs={{0,8},{4,12},{8,16},{12,20},{16,24},{20,28},{24,0},{28,4},{1,9},{5... | collective-permute-start | bytes 1671176 | tf_op jit(solution)/shard_map/ppermute | solution.py:513
  18.5 0.2 collective-permute-start.2
  18.7 1.3 %collective-permute-start.3 = (f32[136,1024]{1,0:T(8,128)S(1)}, f32[136,1024]{1,0:T(8,128)S(1)}, u32[]{:S(2)}, u32[]{:S(2)}) collective-permute-start(f32[136,1024]{1,0:T(8,128)S(1)} %get-tuple-element.40), channel_id=1, source_target_pairs={{0,24},{4,28},{8,0},{12,4},{16,8},{20,12},{24,16},{28,20},{1,25},{... | collective-permute-start | bytes 1671176 | tf_op jit(solution)/shard_map/ppermute | solution.py:513
  20.0 12.9 %local_part.1 = (f32[512,2048]{1,0:T(8,128)S(1)}, f32[512,128]{1,0:T(8,128)S(1)}, f32[512,128]{1,0:T(8,128)S(1)}) custom-call(bf16[512,2048]{1,0:T(8,128)(2,1)S(1)} %copy-done, bf16[512,2048]{1,0:T(8,128)(2,1)S(1)} %copy-done.1, bf16[512,128]{1,0:T(8,128)(2,1)S(1)} %copy-done.5, bf16[512,128]{1,0:T(8,128)(2,1)S(1)} %copy-done.7, f32[32,512]{1,0:T(8,128)S(1)} %copy-done.8), custom_call_target="tpu_custom_call" | custom-call | flops 5368709120 | bytes 8388608 | tf_op jit(solution)/shard_map/local_part/pallas_call | solution.py:405
  32.9 0.0 collective-permute-done.1.refs_0_
  33.0 11.4 %collective-permute-done.3.refs_2_ = f32[136,1024]{1,0:T(8,128)S(1)} collective-permute-done((f32[136,1024]{1,0:T(8,128)S(1)}, f32[136,1024]{1,0:T(8,128)S(1)}, u32[]{:S(2)}, u32[]{:S(2)}) %collective-permute-start.3) | collective-permute-done | bytes 557088 | tf_op jit(solution)/shard_map/ppermute | solution.py:513
  44.4 1.5 %carried_in.1 = (f32[2,128,1024]{2,1,0:T(8,128)S(1)}, f32[2,128,1024]{2,1,0:T(8,128)S(1)}) custom-call(s32[4]{0:T(128)S(1)} %copy-done.9, f32[2,136,1024]{2,1,0:T(8,128)S(1)} %copy-done.2, f32[2,136,1024]{2,1,0:T(8,128)S(1)} %collective-permute-done.recv_ref, f32[136,1024]{1,0:T(8,128)S(1)} %collective-permute-done.1.refs_0_, ...), custom_call_target="tpu_custom_call" | custom-call | flops 2621440 | bytes 5767168 | tf_op jit(solution)/shard_map/carried_in/pallas_call | solution.py:225
  45.9 1.1 %collective-permute-start.4 = (f32[2,128,1024]{2,1,0:T(8,128)S(1)}, f32[2,128,1024]{2,1,0:T(8,128)S(1)}, u32[]{:S(2)}, u32[]{:S(2)}) collective-permute-start(f32[2,128,1024]{2,1,0:T(8,128)S(1)} %get-tuple-element.49), channel_id=1, source_target_pairs={{0,4},{4,0},{8,12},{12,8},{16,20},{20,16},{24,28},{28,24},{1,5},{5... | collective-permute-start | bytes 3145736 | tf_op jit(solution)/shard_map/ppermute | solution.py:509
  47.0 3.1 %map_terms.2 = (f32[512,128]{1,0:T(8,128)S(1)}, f32[512,128]{1,0:T(8,128)S(1)}) custom-call(s32[4]{0:T(128)S(1)} %copy-done.9, bf16[2,2,512,1024]{3,2,1,0:T(8,128)(2,1)S(1)} %copy-done.4, f32[2,128,1024]{2,1,0:T(8,128)S(1)} %get-tuple-element.60.carry_ref.own_ref, f32[512,128]{1,0:T(8,128)S(1)} %get-tuple-element.52.out_before_ref, ...), custom_call_target="tpu_custom_call" | custom-call | flops 805306368 | bytes 4194304 | tf_op jit(solution)/shard_map/map_terms/pallas_call | solution.py:457
  50.1 3.1 %map_terms.3 = (f32[2,128,128]{2,1,0:T(8,128)S(1)}, f32[2,128,128]{2,1,0:T(8,128)S(1)}, f32[2,128,128]{2,1,0:T(8,128)S(1)}, f32[2,128,128]{2,1,0:T(8,128)S(1)}) custom-call(s32[4]{0:T(128)S(1)} %copy-done.9, bf16[2,2,512,1024]{3,2,1,0:T(8,128)(2,1)S(1)} %copy-done.3, f32[2,128,1024]{2,1,0:T(8,128)S(1)} %collective-permute-done.4.carry_ref.other_ref, ...), custom_call_target="tpu_custom_call" | custom-call | flops 805306368 | bytes 4194304 | tf_op jit(solution)/shard_map/map_terms/pallas_call | solution.py:457
  53.2 1.4 %collective-permute-start.5 = (f32[2,128,128]{2,1,0:T(8,128)S(1)}, f32[2,128,128]{2,1,0:T(8,128)S(1)}, u32[]{:S(2)}, u32[]{:S(2)}) collective-permute-start(f32[2,128,128]{2,1,0:T(8,128)S(1)} %get-tuple-element.62), channel_id=1, source_target_pairs={{0,1},{1,2},{2,3},{3,0},{4,5},{5,6},{6,7},{7,4},{8,9},{9,10},{10,1... | collective-permute-start | bytes 393224 | tf_op jit(solution)/shard_map/ppermute | solution.py:513
  54.6 1.1 %collective-permute-start.6 = (f32[2,128,128]{2,1,0:T(8,128)S(1)}, f32[2,128,128]{2,1,0:T(8,128)S(1)}, u32[]{:S(2)}, u32[]{:S(2)}) collective-permute-start(f32[2,128,128]{2,1,0:T(8,128)S(1)} %get-tuple-element.63), channel_id=1, source_target_pairs={{0,2},{1,3},{2,0},{3,1},{4,6},{5,7},{6,4},{7,5},{8,10},{9,11},{10,... | collective-permute-start | bytes 393224 | tf_op jit(solution)/shard_map/ppermute | solution.py:513
  55.7 1.4 %collective-permute-start.7 = (f32[2,128,128]{2,1,0:T(8,128)S(1)}, f32[2,128,128]{2,1,0:T(8,128)S(1)}, u32[]{:S(2)}, u32[]{:S(2)}) collective-permute-start(f32[2,128,128]{2,1,0:T(8,128)S(1)} %get-tuple-element.64), channel_id=1, source_target_pairs={{0,3},{1,0},{2,1},{3,2},{4,7},{5,4},{6,5},{7,6},{8,11},{9,8},{10,9... | collective-permute-start | bytes 393224 | tf_op jit(solution)/shard_map/ppermute | solution.py:513
  57.1 5.6 %input_terms.1 = bf16[512,2048]{1,0:T(8,128)(2,1)} custom-call(s32[4]{0:T(128)S(1)} %copy-done.9, f32[512,2048]{1,0:T(8,128)S(1)} %get-tuple-element.44.part_ref, bf16[512,128]{1,0:T(8,128)(2,1)S(1)} %copy-done.6, bf16[512,128]{1,0:T(8,128)(2,1)S(1)} %copy-done.5, f32[2,128,1024]{2,1,0:T(8,128)S(1)} %get-tuple-element.60.carry_ref.own_ref, ...), custom_call_target="tpu_custom_call" | custom-call | flops 536870912 | bytes 8388608 | tf_op jit(solution)/shard_map/input_terms/pallas_call | solution.py:493
  62.6 3.3 %collective-permute-done.6 = f32[2,128,128]{2,1,0:T(8,128)S(1)} collective-permute-done((f32[2,128,128]{2,1,0:T(8,128)S(1)}, f32[2,128,128]{2,1,0:T(8,128)S(1)}, u32[]{:S(2)}, u32[]{:S(2)}) %collective-permute-start.6) | collective-permute-done | bytes 131104 | tf_op jit(solution)/shard_map/ppermute | solution.py:513
  65.9 2.1 %collective-permute-done.7 = f32[2,128,128]{2,1,0:T(8,128)S(1)} collective-permute-done((f32[2,128,128]{2,1,0:T(8,128)S(1)}, f32[2,128,128]{2,1,0:T(8,128)S(1)}, u32[]{:S(2)}, u32[]{:S(2)}) %collective-permute-start.7) | collective-permute-done | bytes 131104 | tf_op jit(solution)/shard_map/ppermute | solution.py:513
  68.0 0.7 slice_bitcast_fusion
  (23 shorter events, 0.1 us)
Async XLA Ops:
  7.6 7.1 %collective-permute-start = (f32[2,136,1024]{2,1,0:T(8,128)}, f32[2,136,1024]{2,1,0:T(8,128)S(1)}, u32[]{:S(2)}, u32[]{:S(2)}) collective-permute-start(f32[2,136,1024]{2,1,0:T(8,128)} %get-tuple-element.37), channel_id=1, source_target_pairs={{0,4},{4,0},{8,12},{12,8},{16,20},{20,16},{24,28},{28,24},{1,5},{5... | collective-permute-start | bytes 3342344 | tf_op jit(solution)/shard_map/ppermute | solution.py:509
  8.3 6.4 %copy-start.9 = (s32[4]{0:T(128)S(1)}, s32[4]{0:T(128)}, u32[]{:S(2)}) copy-start(s32[4]{0:T(128)} %pad_add_fusion.place_ref.pick_ref) | copy-start | bytes 52
  8.3 11.7 %copy-start.1 = (bf16[512,2048]{1,0:T(8,128)(2,1)S(1)}, bf16[512,2048]{1,0:T(8,128)(2,1)}, u32[]{:S(2)}) copy-start(bf16[512,2048]{1,0:T(8,128)(2,1)} %dy_ref.5) | copy-start | bytes 6291460
  8.3 11.7 %copy-start.5 = (bf16[512,128]{1,0:T(8,128)(2,1)S(1)}, bf16[512,128]{1,0:T(8,128)(2,1)}, u32[]{:S(2)}) copy-start(bf16[512,128]{1,0:T(8,128)(2,1)} %b_ref.7) | copy-start | bytes 393220
  8.3 11.7 %copy-start.7 = (bf16[512,128]{1,0:T(8,128)(2,1)S(1)}, bf16[512,128]{1,0:T(8,128)(2,1)}, u32[]{:S(2)}) copy-start(bf16[512,128]{1,0:T(8,128)(2,1)} %c_ref.5) | copy-start | bytes 393220
  8.3 11.7 %copy-start.8 = (f32[32,512]{1,0:T(8,128)S(1)}, f32[32,512]{1,0:T(8,128)}, u32[]{:S(2)}) copy-start(f32[32,512]{1,0:T(8,128)} %decays_ref.1) | copy-start | bytes 196612
  14.6 5.4 %copy-start = (bf16[512,2048]{1,0:T(8,128)(2,1)S(1)}, bf16[512,2048]{1,0:T(8,128)(2,1)}, u32[]{:S(2)}) copy-start(bf16[512,2048]{1,0:T(8,128)(2,1)} %x_ref.5) | copy-start | bytes 6291460
  14.7 1.4 %copy-start.2 = (f32[2,136,1024]{2,1,0:T(8,128)S(1)}, f32[2,136,1024]{2,1,0:T(8,128)}, u32[]{:S(2)}) copy-start(f32[2,136,1024]{2,1,0:T(8,128)} %get-tuple-element.36.mine_ref) | copy-start | bytes 3342340
  17.2 15.8 %collective-permute-start.1 = (f32[136,1024]{1,0:T(8,128)S(1)}, f32[136,1024]{1,0:T(8,128)S(1)}, u32[]{:S(2)}, u32[]{:S(2)}) collective-permute-start(f32[136,1024]{1,0:T(8,128)S(1)} %get-tuple-element.38), channel_id=1, source_target_pairs={{0,8},{4,12},{8,16},{12,20},{16,24},{20,28},{24,0},{28,4},{1,9},{5... | collective-permute-start | bytes 1671176 | tf_op jit(solution)/shard_map/ppermute | solution.py:513
  18.5 14.5 %collective-permute-start.2 = (f32[136,1024]{1,0:T(8,128)S(1)}, f32[136,1024]{1,0:T(8,128)S(1)}, u32[]{:S(2)}, u32[]{:S(2)}) collective-permute-start(f32[136,1024]{1,0:T(8,128)S(1)} %get-tuple-element.39), channel_id=1, source_target_pairs={{0,16},{4,20},{8,24},{12,28},{16,0},{20,4},{24,8},{28,12},{1,17},{... | collective-permute-start | bytes 1671176 | tf_op jit(solution)/shard_map/ppermute | solution.py:513
  18.7 25.7 %collective-permute-start.3 = (f32[136,1024]{1,0:T(8,128)S(1)}, f32[136,1024]{1,0:T(8,128)S(1)}, u32[]{:S(2)}, u32[]{:S(2)}) collective-permute-start(f32[136,1024]{1,0:T(8,128)S(1)} %get-tuple-element.40), channel_id=1, source_target_pairs={{0,24},{4,28},{8,0},{12,4},{16,8},{20,12},{24,16},{28,20},{1,25},{... | collective-permute-start | bytes 1671176 | tf_op jit(solution)/shard_map/ppermute | solution.py:513
  20.0 27.0 %copy-start.4 = (bf16[2,2,512,1024]{3,2,1,0:T(8,128)(2,1)S(1)}, bf16[2,2,512,1024]{3,2,1,0:T(8,128)(2,1)}, u32[]{:S(2)}) copy-start(bf16[2,2,512,1024]{3,2,1,0:T(8,128)(2,1)} %get-tuple-element.51.scaled_ref) | copy-start | bytes 12582916
  45.9 4.2 %collective-permute-start.4 = (f32[2,128,1024]{2,1,0:T(8,128)S(1)}, f32[2,128,1024]{2,1,0:T(8,128)S(1)}, u32[]{:S(2)}, u32[]{:S(2)}) collective-permute-start(f32[2,128,1024]{2,1,0:T(8,128)S(1)} %get-tuple-element.49), channel_id=1, source_target_pairs={{0,4},{4,0},{8,12},{12,8},{16,20},{20,16},{24,28},{28,24},{1,5},{5... | collective-permute-start | bytes 3145736 | tf_op jit(solution)/shard_map/ppermute | solution.py:509
  47.0 3.1 %copy-start.3 = (bf16[2,2,512,1024]{3,2,1,0:T(8,128)(2,1)S(1)}, bf16[2,2,512,1024]{3,2,1,0:T(8,128)(2,1)}, u32[]{:S(2)}) copy-start(bf16[2,2,512,1024]{3,2,1,0:T(8,128)(2,1)} %get-tuple-element.50.scaled_ref) | copy-start | bytes 12582916
  50.1 7.0 %copy-start.6 = (bf16[512,128]{1,0:T(8,128)(2,1)S(1)}, bf16[512,128]{1,0:T(8,128)(2,1)}, u32[]{:S(2)}) copy-start(bf16[512,128]{1,0:T(8,128)(2,1)} %get-tuple-element.35.refs_1_.suf_ref) | copy-start | bytes 393220
  53.2 9.4 %collective-permute-start.5 = (f32[2,128,128]{2,1,0:T(8,128)S(1)}, f32[2,128,128]{2,1,0:T(8,128)S(1)}, u32[]{:S(2)}, u32[]{:S(2)}) collective-permute-start(f32[2,128,128]{2,1,0:T(8,128)S(1)} %get-tuple-element.62), channel_id=1, source_target_pairs={{0,1},{1,2},{2,3},{3,0},{4,5},{5,6},{6,7},{7,4},{8,9},{9,10},{10,1... | collective-permute-start | bytes 393224 | tf_op jit(solution)/shard_map/ppermute | solution.py:513
  54.6 11.3 %collective-permute-start.6 = (f32[2,128,128]{2,1,0:T(8,128)S(1)}, f32[2,128,128]{2,1,0:T(8,128)S(1)}, u32[]{:S(2)}, u32[]{:S(2)}) collective-permute-start(f32[2,128,128]{2,1,0:T(8,128)S(1)} %get-tuple-element.63), channel_id=1, source_target_pairs={{0,2},{1,3},{2,0},{3,1},{4,6},{5,7},{6,4},{7,5},{8,10},{9,11},{10,... | collective-permute-start | bytes 393224 | tf_op jit(solution)/shard_map/ppermute | solution.py:513
  55.7 12.3 %collective-permute-start.7 = (f32[2,128,128]{2,1,0:T(8,128)S(1)}, f32[2,128,128]{2,1,0:T(8,128)S(1)}, u32[]{:S(2)}, u32[]{:S(2)}) collective-permute-start(f32[2,128,128]{2,1,0:T(8,128)S(1)} %get-tuple-element.64), channel_id=1, source_target_pairs={{0,3},{1,0},{2,1},{3,2},{4,7},{5,4},{6,5},{7,6},{8,11},{9,8},{10,9... | collective-permute-start | bytes 393224 | tf_op jit(solution)/shard_map/ppermute | solution.py:513

commit v3 on v2

--- a/solution.py
+++ b/solution.py
@@ -94,10 +94,10 @@
 
 
 def totals_kernel(heads, count, half, place_ref, x_ref, dy_ref, b_ref, c_ref, *refs):
-    if len(refs) == 7:
-        decays_ref, out_ref, scaled_ref, pre_ref, suf_ref, bt_ref, ct_ref = refs
+    if len(refs) == 6:
+        decays_ref, out_ref, pre_ref, suf_ref, bt_ref, ct_ref = refs
     else:
-        pre_ref, suf_ref, out_ref, scaled_ref, bt_ref, ct_ref = refs
+        pre_ref, suf_ref, out_ref, bt_ref, ct_ref = refs
         decays_ref = None
     step = pl.program_id(0)
 
@@ -114,9 +114,7 @@
     after = dot(suf_ref[...], table)
     ended = before[before.shape[0] - 1 :, :]
     for i, (source, factor, other) in enumerate(((x_ref, after, bt_ref), (dy_ref, before, ct_ref))):
-        scaled = halves(source[...].astype(F32) * factor)
-        scaled_ref[i, 0], scaled_ref[i, 1] = scaled
-        out_ref[i, :N, :] = dot12(other[...], scaled)
+        out_ref[i, :N, :] = dot12(other[...], halves(source[...].astype(F32) * factor))
     out_ref[0, N:, :] = jnp.broadcast_to(ended, (EXTRA, tile))
     out_ref[1, N:, :] = jnp.broadcast_to(ended, (EXTRA, tile))
 
@@ -129,14 +127,8 @@
     column = pl.BlockSpec((local, TILE), lambda j, pick: (0, pick[half] * count + j))
     factor = jax.ShapeDtypeStruct((local, LANES), BF16)
     rest = (pre, suf) if decays is None else (decays,)
-    out_specs = [
-        pl.BlockSpec((2, N + EXTRA, TILE), lambda j, pick: (0, 0, j)),
-        pl.BlockSpec((2, 2, local, TILE), lambda j, pick: (0, 0, 0, j)),
-    ]
-    out_shape = [
-        jax.ShapeDtypeStruct((2, N + EXTRA, width // 2), F32),
-        jax.ShapeDtypeStruct((2, 2, local, width // 2), BF16),
-    ]
+    out_specs = [pl.BlockSpec((2, N + EXTRA, TILE), lambda j, pick: (0, 0, j))]
+    out_shape = [jax.ShapeDtypeStruct((2, N + EXTRA, width // 2), F32)]
     if decays is not None:
         out_specs += [whole(factor), whole(factor)]
         out_shape += [factor, factor]
@@ -189,6 +181,109 @@
         name="chip_totals",
         cost_estimate=pl.CostEstimate(flops=6 * N * width, bytes_accessed=24 * N * width, transcendentals=0),
     )(place, mine, recv)
+
+
+def sides(place_ref):
+    chip = place_ref[CHIP]
+    return chip < 2, (chip == 1) | (chip == 2)
+
+
+def first_kernel(place_ref, mine_ref, recv_ref, same_ref, cross_ref, back_ref, decay_ref):
+    left, inner = sides(place_ref)
+    core = place_ref[CORE]
+    width = mine_ref.shape[2] // 2
+    early, late = ordered(core, mine_ref[0], recv_ref[0])
+    early_decay, late_decay = early[N : N + 1], late[N : N + 1]
+    state = late_decay * early[:N] + late[:N]
+    decay = early_decay * late_decay
+    early, late = ordered(core, mine_ref[1], recv_ref[1])
+    grad = early[:N] + early_decay * late[:N]
+    out, back = jnp.where(left, state, grad), jnp.where(left, grad, state)
+    same_ref[:N, :] = out[:, :width]
+    same_ref[N : 2 * N, :] = jnp.where(inner, back[:, :width], out[:, width:])
+    rows = lax.broadcasted_iota(jnp.int32, (EXTRA, width), 0)
+    same_ref[2 * N :, :] = jnp.where(rows == 0, decay[:, :width], decay[:, width:])
+    cross_ref[...] = out[:, width:]
+    back_ref[...] = back[:, width:]
+    decay_ref[...] = jnp.broadcast_to(decay[:, width:], (EXTRA, width))
+
+
+def second_kernel(place_ref, own_ref, back_ref, same_ref, cross_ref, decay_ref, cross2_ref, same2_ref):
+    _, inner = sides(place_ref)
+    own, other = own_ref[:N, :], same_ref[:N, :]
+    own_decay, other_decay = own_ref[2 * N : 2 * N + 1, :], same_ref[2 * N : 2 * N + 1, :]
+    cross2_ref[...] = jnp.where(inner, own + own_decay * other, other + other_decay * own)
+    weight = own_ref[2 * N + 1 : 2 * N + 2, :] * decay_ref[:1, :]
+    same2_ref[...] = jnp.where(inner, back_ref[...] + weight * cross_ref[...], cross_ref[...])
+
+
+def plain_call(kernel, name, out_shape, place, *args):
+    whole = lambda a: pl.BlockSpec(a.shape, lambda j, pick: (0,) * len(a.shape))
+    return pl.pallas_call(
+        kernel,
+        grid_spec=pltpu.PrefetchScalarGridSpec(
+            num_scalar_prefetch=1,
+            grid=(1,),
+            in_specs=[whole(a) for a in args],
+            out_specs=[whole(a) for a in out_shape],
+        ),
+        out_shape=out_shape,
+        compiler_params=PARAMS,
+        name=name,
+        cost_estimate=pl.CostEstimate(
+            flops=8 * sum(a.size for a in args), bytes_accessed=4 * sum(a.size for a in args), transcendentals=0
+        ),
+    )(place, *args)
+
+
+def crossed(v, length, bit):
+    return lax.ppermute(v, "seq", [(i, i ^ bit) for i in range(length)])
+
+
+def first_phase(place, length, mine, recv):
+    half = mine.shape[2] // 2
+    shapes = [jax.ShapeDtypeStruct((rows, half), F32) for rows in (2 * N + EXTRA, N, N, EXTRA)]
+    own, cross, back, decay = plain_call(first_kernel, "first_messages", shapes, place, mine, recv)
+    return own, back, crossed(own, length, 2), crossed(cross, length, 4), crossed(decay, length, 6)
+
+
+def second_phase(place, own, back, same, cross, decay):
+    shape = jax.ShapeDtypeStruct(back.shape, F32)
+    return plain_call(second_kernel, "second_messages", [shape, shape], place, own, back, same, cross, decay)
+
+
+def carried4_kernel(
+    place_ref, mine_ref, recv_ref, same_ref, cross_ref, decay_ref, cross2_ref, same2_ref, own_ref, peer_ref
+):
+    left, inner = sides(place_ref)
+    width = cross_ref.shape[1]
+    decay_a, decay_b = same_ref[2 * N : 2 * N + 1, :], same_ref[2 * N + 1 : 2 * N + 2, :]
+    for part in range(2):
+        at = slice(part * width, (part + 1) * width)
+        out = jnp.where(inner, same_ref[part * N : (part + 1) * N, :], 0.0)
+        if part == 0:
+            back = jnp.where(inner, cross2_ref[...], same_ref[N : 2 * N, :] + decay_a * cross2_ref[...])
+        else:
+            back = same2_ref[...] + jnp.where(inner, decay_ref[:1, :], decay_b) * cross_ref[...]
+        carried_cores(
+            place_ref[CORE], jnp.where(left, out, back), jnp.where(left, back, out), mine_ref, recv_ref, own_ref, peer_ref, at
+        )
+
+
+def carried4(place, mine, recv, *others):
+    shape = jax.ShapeDtypeStruct((2, N, mine.shape[2]), F32)
+    return plain_call(carried4_kernel, "carried_in", [shape, shape], place, mine, recv, *others)
+
+
+def carried_cores(core, state, grad, mine_ref, recv_ref, own_ref, peer_ref, at):
+    early, late = ordered(core, mine_ref[0, :, at], recv_ref[0, :, at])
+    at_late = early[N : N + 1] * state + early[:N]
+    own_ref[0, :, at] = jnp.where(core == 0, state, at_late)
+    peer_ref[0, :, at] = jnp.where(core == 0, at_late, state)
+    early, late = ordered(core, mine_ref[1, :, at], recv_ref[1, :, at])
+    at_early = late[:N] + late[N : N + 1] * grad
+    own_ref[1, :, at] = jnp.where(core == 0, at_early, grad)
+    peer_ref[1, :, at] = jnp.where(core == 0, grad, at_early)
 
 
 def carried_kernel(chips, place_ref, mine_ref, recv_ref, *refs):
@@ -205,14 +300,7 @@
         ref = others[chips - r - 1]
         grad = jnp.where(later, grad + grad_weight * ref[:N, :], grad)
         grad_weight = grad_weight * ref[N : N + 1, :]
-    early, late = ordered(core, mine_ref[0], recv_ref[0])
-    at_late = early[N : N + 1] * state + early[:N]
-    own_ref[0] = jnp.where(core == 0, state, at_late)
-    peer_ref[0] = jnp.where(core == 0, at_late, state)
-    early, late = ordered(core, mine_ref[1], recv_ref[1])
-    at_early = late[:N] + late[N : N + 1] * grad
-    own_ref[1] = jnp.where(core == 0, at_early, grad)
-    peer_ref[1] = jnp.where(core == 0, grad, at_early)
+    carried_cores(core, state, grad, mine_ref, recv_ref, own_ref, peer_ref, slice(None))
 
 
 def carried(chips, place, mine, recv, others):
@@ -419,6 +507,29 @@
     )(x, dy, b, c, decays)
 
 
+def scaled_kernel(heads, x_ref, dy_ref, pre_ref, suf_ref, out_ref):
+    tile = x_ref.shape[1]
+    table = spread(heads, pl.program_id(0) * (tile // P_SIZE), tile)
+    for i, (source, factor) in enumerate(((x_ref, suf_ref), (dy_ref, pre_ref))):
+        out_ref[i, 0], out_ref[i, 1] = halves(source[...].astype(F32) * dot(factor[...], table))
+
+
+def scaled_pairs(x, dy, pre, suf):
+    local, width = x.shape
+    whole = lambda a: pl.BlockSpec(a.shape, lambda j: (0, 0))
+    column = pl.BlockSpec((local, TILE), lambda j: (0, j))
+    return pl.pallas_call(
+        functools.partial(scaled_kernel, width // P_SIZE),
+        grid=(width // TILE,),
+        in_specs=[column, column, whole(pre), whole(suf)],
+        out_specs=pl.BlockSpec((2, 2, local, TILE), lambda j: (0, 0, 0, j)),
+        out_shape=jax.ShapeDtypeStruct((2, 2, local, width), BF16),
+        compiler_params=PARAMS,
+        name="scaled_pairs",
+        cost_estimate=pl.CostEstimate(flops=4 * local * LANES * width, bytes_accessed=12 * local * width, transcendentals=0),
+    )(x, dy, pre, suf)
+
+
 def map_kernel(count, ranks, place_ref, scaled_ref, carry_ref, out_before_ref, map_before_ref, *refs):
     messages, (out_ref, map_ref) = refs[:-2], refs[-2:]
     step = pl.program_id(0)
@@ -444,9 +555,10 @@
                 message[1] = map_ref[at, :]
 
 
-def map_terms(place, scaled, carry, out_before, map_before, ranks=0):
-    local, width = scaled.shape[2:]
-    count = width // TILE
+def map_terms(half, place, scaled, carry, out_before, map_before, ranks=0):
+    local, width = scaled.shape[2], carry.shape[2]
+    tile = min(512, width)
+    count = width // tile
     whole = lambda a: pl.BlockSpec(a.shape, lambda j, pick: (0,) * len(a.shape))
     tokens = jax.ShapeDtypeStruct((local, N), F32)
     if ranks:
@@ -460,8 +572,8 @@
             num_scalar_prefetch=1,
             grid=(count,),
             in_specs=[
-                pl.BlockSpec((2, 2, local, TILE), lambda j, pick: (0, 0, 0, j)),
-                pl.BlockSpec((2, N, TILE), lambda j, pick: (0, 0, j)),
+                pl.BlockSpec((2, 2, local, tile), lambda j, pick: (0, 0, 0, pick[half] * count + j)),
+                pl.BlockSpec((2, N, tile), lambda j, pick: (0, 0, j)),
                 whole(tokens),
                 whole(tokens),
             ],
@@ -520,17 +632,28 @@
     core, chip = index % 2, index // 2
     place = jnp.stack([core, 1 - core, chip, rank]).astype(jnp.int32)
     args = mixer_input, output_grad, input_map, output_map
-    sent, scaled_other, pre, suf = totals(OTHER, place, *args, decays=decays)
+    sent, pre, suf = totals(OTHER, place, *args, decays=decays)
     recv = swap_cores(sent, length)
-    mine, scaled_mine = totals(CORE, place, *args, pre=pre, suf=suf)
-    messages = chip_totals(chips, place, mine, recv)
-    others = [turned(message, "seq", length, 2 * r) for r, message in enumerate(messages, 1)]
-    part, out_part, map_part = local_part(*args, decays)
-    others, part, out_part, map_part = lax.optimization_barrier((others, part, out_part, map_part))
-    own, peer = carried(chips, place, mine, recv, others)
+    (mine,) = totals(CORE, place, *args, pre=pre, suf=suf)
+    if chips == 4:
+        own, back, *others = first_phase(place, length, mine, recv)
+        part, out_part, map_part = local_part(*args, decays)
+        others, part, out_part, map_part = lax.optimization_barrier((others, part, out_part, map_part))
+        cross, same = second_phase(place, own, back, *others)
+        others += [crossed(cross, length, 4), crossed(same, length, 2)]
+        pre, suf, _, _ = lax.optimization_barrier((pre, suf, cross, same))
+        scaled = scaled_pairs(mixer_input, output_grad, pre, suf)
+        others, scaled = lax.optimization_barrier((others, scaled))
+        own, peer = carried4(place, mine, recv, *others)
+    else:
+        messages = chip_totals(chips, place, mine, recv)
+        others = [turned(message, "seq", length, 2 * r) for r, message in enumerate(messages, 1)]
+        part, out_part, map_part = local_part(*args, decays)
+        scaled = scaled_pairs(mixer_input, output_grad, pre, suf)
+        own, peer = carried(chips, place, mine, recv, others)
     other = swap_cores(peer, length)
-    out_part, map_part = map_terms(place, scaled_mine, own, out_part, map_part)
-    shares = map_terms(place, scaled_other, other, out_part, map_part, ranks)
+    out_part, map_part = map_terms(CORE, place, scaled, own, out_part, map_part)
+    shares = map_terms(OTHER, place, scaled, other, out_part, map_part, ranks)
     total = shares[0]
     own, other, shares = lax.optimization_barrier((own, other, shares))
     for r in range(1, ranks):

time: 69 us -> 64.1 us (0.929)
  waiting for transfers between devices: 16.8 us -> 7.26 us
  starting transfers between devices: 8.42 us -> 10.9 us
  Pallas kernels: 39.9 us -> 42.2 us
    ppermute x6 -> x3, waiting for transfers between devices: 16.8 us -> 5.35 us  [turned(): lax.ppermute(v, axis, [(i, (i + by) % length) for i in range(length)])]
    ppermute x0 -> x5, starting transfers between devices: none -> 4.27 us  [crossed(): return lax.ppermute(v, 'seq', [(i, i ^ bit) for i in range(length)])]
    pallas_call x2 -> x4, Pallas kernels: 2.64 us -> 6.84 us  [the longest x1 4.47 us: scaled_pairs(): pl.pallas_call(functools.partial(scaled_kernel, width // P_SIZE), grid=(w...]
    ppermute x6 -> x3, starting transfers between devices: 6.62 us -> 3.83 us  [turned(): lax.ppermute(v, axis, [(i, (i + by) % length) for i in range(length)])]
    ppermute x0 -> x5, waiting for transfers between devices: none -> 1.91 us  [crossed(): return lax.ppermute(v, 'seq', [(i, i ^ bit) for i in range(length)])]
    pallas_call x2, Pallas kernels: 6.15 us -> 5 us  [map_terms(): pl.pallas_call(functools.partial(map_kernel, count, ranks), grid_spec=plt...]
    ppermute x2, starting transfers between devices: 1.79 us -> 2.82 us  [swap_cores(): return lax.ppermute(v, 'seq', [(i, i ^ 1) for i in range(length)])]
    pallas_call x2, Pallas kernels: 12.6 us -> 11.8 us  [totals(): pl.pallas_call(functools.partial(totals_kernel, heads, count, half), grid...]
  transfers between devices with their start and end apart: 8 -> 10, of which waited for: 3 -> 4; matrix products, arithmetic and copies ran while one was open for 0% -> 0% of each run, Pallas kernels for 41% -> 49%
where the time goes in v3:
time: 64.1 us; the launch traced here: 63.8 us
  Pallas kernels  42.2 us (66%)
  starting transfers between devices  10.9 us (17%)
  waiting for transfers between devices  7.26 us (11%)
  local copies, waits for them, and re-layouts  2.08 us (3%)
  between operations  0.78 us (1%)
    pallas_call x1, Pallas kernels, local_part(): pl.pallas_call(functools.partial(local_kernel, heads), grid=(count,), in_...  12.9 us
    pallas_call x2, Pallas kernels, totals(): pl.pallas_call(functools.partial(totals_kernel, heads, count, half), grid...  11.8 us
    pallas_call x1, Pallas kernels, input_terms(): pl.pallas_call(functools.partial(input_kernel, heads, count), grid_spec=p...  5.58 us
    ppermute x3, waiting for transfers between devices, turned(): lax.ppermute(v, axis, [(i, (i + by) % length) for i in range(length)])  5.35 us
    pallas_call x2, Pallas kernels, map_terms(): pl.pallas_call(functools.partial(map_kernel, count, ranks), grid_spec=plt...  5 us
    pallas_call x1, Pallas kernels, scaled_pairs(): pl.pallas_call(functools.partial(scaled_kernel, width // P_SIZE), grid=(w...  4.47 us
    ppermute x5, starting transfers between devices, crossed(): return lax.ppermute(v, 'seq', [(i, i ^ bit) for i in range(length)])  4.27 us
    ppermute x3, starting transfers between devices, turned(): lax.ppermute(v, axis, [(i, (i + by) % length) for i in range(length)])  3.83 us
  transfers between devices with their start and end apart: 10, of which 4 were waited for; matrix products, arithmetic and copies ran while one was open for 0% of the time, Pallas kernels for 49%

profile of v3, /device:TPU:11, one launch (start us, length us, event | category | flops | bytes accessed | tf_op | source)
XLA Modules:
  0.0 63.8 jit_solution(6664671324286412900)
XLA Ops:
  0.6 0.6 pad_add_fusion.place_ref.pick_ref
  1.2 5.9 %state_totals.2 = (f32[2,136,1024]{2,1,0:T(8,128)}, bf16[512,128]{1,0:T(8,128)(2,1)}, bf16[512,128]{1,0:T(8,128)(2,1)}) custom-call(s32[4]{0:T(128)} %pad_add_fusion.place_ref.pick_ref, bf16[512,2048]{1,0:T(8,128)(2,1)} %x_ref.7, bf16[512,2048]{1,0:T(8,128)(2,1)} %dy_ref.7, bf16[512,128]{1,0:T(8,128)(2,1)} %b_ref.7, bf16[512,128]{1,0:T(8,128)(2,1)} %c_ref.5, ...), custom_call_target="tpu_custom_call" | custom-call | flops 536870912 | bytes 4194304 | tf_op jit(solution)/shard_map/state_totals/pallas_call | solution.py:135
  7.2 0.7 %collective-permute-start = (f32[2,136,1024]{2,1,0:T(8,128)}, f32[2,136,1024]{2,1,0:T(8,128)S(1)}, u32[]{:S(2)}, u32[]{:S(2)}) collective-permute-start(f32[2,136,1024]{2,1,0:T(8,128)} %get-tuple-element.44), channel_id=1, source_target_pairs={{0,4},{4,0},{8,12},{12,8},{16,20},{20,16},{24,28},{28,24},{1,5},{5... | collective-permute-start | bytes 3342344 | tf_op jit(solution)/shard_map/ppermute | solution.py:621
  7.8 5.9 %state_totals.3.mine_ref = f32[2,136,1024]{2,1,0:T(8,128)} custom-call(s32[4]{0:T(128)} %pad_add_fusion.place_ref.pick_ref, bf16[512,2048]{1,0:T(8,128)(2,1)} %x_ref.7, bf16[512,2048]{1,0:T(8,128)(2,1)} %dy_ref.7, bf16[512,128]{1,0:T(8,128)(2,1)} %b_ref.7, bf16[512,128]{1,0:T(8,128)(2,1)} %c_ref.5, bf16[512,128]{1,0:T(8,128)(2,1)} %get-tuple-element.59.refs_0_.pre_ref, ...), custom_call_target="tpu_custom_call" | custom-call | flops 536870912 | bytes 4194304 | tf_op jit(solution)/shard_map/state_totals/pallas_call | solution.py:135
  13.8 1.4 %copy-done.2 = f32[2,136,1024]{2,1,0:T(8,128)S(1)} copy-done((f32[2,136,1024]{2,1,0:T(8,128)S(1)}, f32[2,136,1024]{2,1,0:T(8,128)}, u32[]{:S(2)}) %copy-start.2) | copy-done | bytes 1114136
  15.2 0.8 %first_messages.1 = (f32[264,512]{1,0:T(8,128)S(1)}, f32[128,512]{1,0:T(8,128)S(1)}, f32[128,512]{1,0:T(8,128)S(1)}, f32[8,512]{1,0:T(8,128)S(1)}) custom-call(s32[4]{0:T(128)S(1)} %copy-done.9, f32[2,136,1024]{2,1,0:T(8,128)S(1)} %copy-done.2, f32[2,136,1024]{2,1,0:T(8,128)S(1)} %collective-permute-done.recv_ref), custom_call_target="tpu_custom_call" | custom-call | flops 4456448 | bytes 2228224 | tf_op jit(solution)/shard_map/first_messages/pallas_call | solution.py:222
  16.2 2.2 %collective-permute-start.3 = (f32[8,512]{1,0:T(8,128)S(1)}, f32[8,512]{1,0:T(8,128)S(1)}, u32[]{:S(2)}, u32[]{:S(2)}) collective-permute-start(f32[8,512]{1,0:T(8,128)S(1)} %get-tuple-element.47), channel_id=1, source_target_pairs={{0,24},{4,28},{8,16},{12,20},{16,8},{20,12},{24,0},{28,4},{1,25},{... | collective-permute-start | bytes 49160 | tf_op jit(solution)/shard_map/ppermute | solution.py:240
  18.7 12.9 %local_part.1 = (f32[512,2048]{1,0:T(8,128)S(1)}, f32[512,128]{1,0:T(8,128)S(1)}, f32[512,128]{1,0:T(8,128)S(1)}) custom-call(bf16[512,2048]{1,0:T(8,128)(2,1)S(1)} %copy-done, bf16[512,2048]{1,0:T(8,128)(2,1)S(1)} %copy-done.1, bf16[512,128]{1,0:T(8,128)(2,1)S(1)} %copy-done.5, bf16[512,128]{1,0:T(8,128)(2,1)S(1)} %copy-done.7, f32[32,512]{1,0:T(8,128)S(1)} %copy-done.8), custom_call_target="tpu_custom_call" | custom-call | flops 5368709120 | bytes 8388608 | tf_op jit(solution)/shard_map/local_part/pallas_call | solution.py:493
  31.7 0.6 second_messages.1
  32.3 1.3 %collective-permute-start.4 = (f32[128,512]{1,0:T(8,128)S(1)}, f32[128,512]{1,0:T(8,128)S(1)}, u32[]{:S(2)}, u32[]{:S(2)}) collective-permute-start(f32[128,512]{1,0:T(8,128)S(1)} %get-tuple-element.56), channel_id=1, source_target_pairs={{0,16},{4,20},{8,24},{12,28},{16,0},{20,4},{24,8},{28,12},{1,17},{... | collective-permute-start | bytes 786440 | tf_op jit(solution)/shard_map/ppermute | solution.py:240
  33.9 4.5 %scaled_pairs.1.scaled_ref = bf16[2,2,512,2048]{3,2,1,0:T(8,128)(2,1)S(1)} custom-call(bf16[512,2048]{1,0:T(8,128)(2,1)S(1)} %copy-done, bf16[512,2048]{1,0:T(8,128)(2,1)S(1)} %copy-done.1, bf16[512,128]{1,0:T(8,128)(2,1)S(1)} %copy-done.6, bf16[512,128]{1,0:T(8,128)(2,1)S(1)} %copy-done.4), custom_call_target="tpu_custom_call" | custom-call | flops 536870912 | bytes 12582912 | tf_op jit(solution)/shard_map/scaled_pairs/pallas_call | solution.py:521
  38.3 1.0 %collective-permute-done.4.cross2_ref = f32[128,512]{1,0:T(8,128)S(1)} collective-permute-done((f32[128,512]{1,0:T(8,128)S(1)}, f32[128,512]{1,0:T(8,128)S(1)}, u32[]{:S(2)}, u32[]{:S(2)}) %collective-permute-start.4) | collective-permute-done | bytes 262176 | tf_op jit(solution)/shard_map/ppermute | solution.py:240
  39.3 0.9 %collective-permute-done.5.same2_ref = f32[128,512]{1,0:T(8,128)S(1)} collective-permute-done((f32[128,512]{1,0:T(8,128)S(1)}, f32[128,512]{1,0:T(8,128)S(1)}, u32[]{:S(2)}, u32[]{:S(2)}) %collective-permute-start.5) | collective-permute-done | bytes 262176 | tf_op jit(solution)/shard_map/ppermute | solution.py:240
  40.2 1.0 %carried_in.1 = (f32[2,128,1024]{2,1,0:T(8,128)S(1)}, f32[2,128,1024]{2,1,0:T(8,128)S(1)}) custom-call(s32[4]{0:T(128)S(1)} %copy-done.9, f32[2,136,1024]{2,1,0:T(8,128)S(1)} %copy-done.3, f32[2,136,1024]{2,1,0:T(8,128)S(1)} %collective-permute-done.recv_ref, f32[264,512]{1,0:T(8,128)S(1)} %collective-permute-done.1.same_ref, ...), custom_call_target="tpu_custom_call" | custom-call | flops 7143424 | bytes 3571712 | tf_op jit(solution)/shard_map/carried_in/pallas_call | solution.py:222
  41.2 2.1 %collective-permute-start.6 = (f32[2,128,1024]{2,1,0:T(8,128)S(1)}, f32[2,128,1024]{2,1,0:T(8,128)S(1)}, u32[]{:S(2)}, u32[]{:S(2)}) collective-permute-start(f32[2,128,1024]{2,1,0:T(8,128)S(1)} %get-tuple-element.66), channel_id=1, source_target_pairs={{0,4},{4,0},{8,12},{12,8},{16,20},{20,16},{24,28},{28,24},{1,5},{5... | collective-permute-start | bytes 3145736 | tf_op jit(solution)/shard_map/ppermute | solution.py:621
  43.4 2.5 %map_terms.2 = (f32[512,128]{1,0:T(8,128)S(1)}, f32[512,128]{1,0:T(8,128)S(1)}) custom-call(s32[4]{0:T(128)S(1)} %copy-done.9, bf16[2,2,512,2048]{3,2,1,0:T(8,128)(2,1)S(1)} %scaled_pairs.1.scaled_ref, f32[2,128,1024]{2,1,0:T(8,128)S(1)} %get-tuple-element.76.carry_ref.own_ref, f32[512,128]{1,0:T(8,128)S(1)} %get-tuple-element.68.out_before_ref, ...), custom_call_target="tpu_custom_call" | custom-call | flops 805306368 | bytes 4194304 | tf_op jit(solution)/shard_map/map_terms/pallas_call | solution.py:569
  45.9 2.5 %map_terms.3 = (f32[2,128,128]{2,1,0:T(8,128)S(1)}, f32[2,128,128]{2,1,0:T(8,128)S(1)}, f32[2,128,128]{2,1,0:T(8,128)S(1)}, f32[2,128,128]{2,1,0:T(8,128)S(1)}) custom-call(s32[4]{0:T(128)S(1)} %copy-done.9, bf16[2,2,512,2048]{3,2,1,0:T(8,128)(2,1)S(1)} %scaled_pairs.1.scaled_ref, f32[2,128,1024]{2,1,0:T(8,128)S(1)} %collective-permute-done.6.carry_ref.other_ref, ...), custom_call_target="tpu_custom_call" | custom-call | flops 805306368 | bytes 4194304 | tf_op jit(solution)/shard_map/map_terms/pallas_call | solution.py:569
  48.4 1.4 %collective-permute-start.7 = (f32[2,128,128]{2,1,0:T(8,128)S(1)}, f32[2,128,128]{2,1,0:T(8,128)S(1)}, u32[]{:S(2)}, u32[]{:S(2)}) collective-permute-start(f32[2,128,128]{2,1,0:T(8,128)S(1)} %get-tuple-element.78), channel_id=1, source_target_pairs={{0,1},{1,2},{2,3},{3,0},{4,5},{5,6},{6,7},{7,4},{8,9},{9,10},{10,1... | collective-permute-start | bytes 393224 | tf_op jit(solution)/shard_map/ppermute | solution.py:625
  49.7 1.1 %collective-permute-start.8 = (f32[2,128,128]{2,1,0:T(8,128)S(1)}, f32[2,128,128]{2,1,0:T(8,128)S(1)}, u32[]{:S(2)}, u32[]{:S(2)}) collective-permute-start(f32[2,128,128]{2,1,0:T(8,128)S(1)} %get-tuple-element.79), channel_id=1, source_target_pairs={{0,2},{1,3},{2,0},{3,1},{4,6},{5,7},{6,4},{7,5},{8,10},{9,11},{10,... | collective-permute-start | bytes 393224 | tf_op jit(solution)/shard_map/ppermute | solution.py:625
  50.8 1.4 %collective-permute-start.9 = (f32[2,128,128]{2,1,0:T(8,128)S(1)}, f32[2,128,128]{2,1,0:T(8,128)S(1)}, u32[]{:S(2)}, u32[]{:S(2)}) collective-permute-start(f32[2,128,128]{2,1,0:T(8,128)S(1)} %get-tuple-element.80), channel_id=1, source_target_pairs={{0,3},{1,0},{2,1},{3,2},{4,7},{5,4},{6,5},{7,6},{8,11},{9,8},{10,9... | collective-permute-start | bytes 393224 | tf_op jit(solution)/shard_map/ppermute | solution.py:625
  52.2 5.6 %input_terms.1 = bf16[512,2048]{1,0:T(8,128)(2,1)} custom-call(s32[4]{0:T(128)S(1)} %copy-done.9, f32[512,2048]{1,0:T(8,128)S(1)} %get-tuple-element.51.part_ref, bf16[512,128]{1,0:T(8,128)(2,1)S(1)} %copy-done.4, bf16[512,128]{1,0:T(8,128)(2,1)S(1)} %copy-done.5, f32[2,128,1024]{2,1,0:T(8,128)S(1)} %get-tuple-element.76.carry_ref.own_ref, ...), custom_call_target="tpu_custom_call" | custom-call | flops 536870912 | bytes 8388608 | tf_op jit(solution)/shard_map/input_terms/pallas_call | solution.py:605
  57.8 3.1 %collective-permute-done.8 = f32[2,128,128]{2,1,0:T(8,128)S(1)} collective-permute-done((f32[2,128,128]{2,1,0:T(8,128)S(1)}, f32[2,128,128]{2,1,0:T(8,128)S(1)}, u32[]{:S(2)}, u32[]{:S(2)}) %collective-permute-start.8) | collective-permute-done | bytes 131104 | tf_op jit(solution)/shard_map/ppermute | solution.py:625
  60.9 2.2 %collective-permute-done.9 = f32[2,128,128]{2,1,0:T(8,128)S(1)} collective-permute-done((f32[2,128,128]{2,1,0:T(8,128)S(1)}, f32[2,128,128]{2,1,0:T(8,128)S(1)}, u32[]{:S(2)}, u32[]{:S(2)}) %collective-permute-start.9) | collective-permute-done | bytes 131104 | tf_op jit(solution)/shard_map/ppermute | solution.py:625
  63.2 0.7 %slice_bitcast_fusion = (f32[128,128]{1,0:T(8,128)}, f32[128,128]{1,0:T(8,128)}) fusion(f32[2,128,128]{2,1,0:T(8,128)S(1)} %add_add_fusion), kind=kLoop, calls=%fused_computation.1 | loop fusion | bytes 262144 | tf_op jit(solution)/shard_map/squeeze | solution.py:662
  (29 shorter events, 0.9 us)
Async XLA Ops:
  7.2 6.6 %collective-permute-start = (f32[2,136,1024]{2,1,0:T(8,128)}, f32[2,136,1024]{2,1,0:T(8,128)S(1)}, u32[]{:S(2)}, u32[]{:S(2)}) collective-permute-start(f32[2,136,1024]{2,1,0:T(8,128)} %get-tuple-element.44), channel_id=1, source_target_pairs={{0,4},{4,0},{8,12},{12,8},{16,20},{20,16},{24,28},{28,24},{1,5},{5... | collective-permute-start | bytes 3342344 | tf_op jit(solution)/shard_map/ppermute | solution.py:621
  7.8 5.9 %copy-start.9 = (s32[4]{0:T(128)S(1)}, s32[4]{0:T(128)}, u32[]{:S(2)}) copy-start(s32[4]{0:T(128)} %pad_add_fusion.place_ref.pick_ref) | copy-start | bytes 52
  7.8 10.8 %copy-start.1 = (bf16[512,2048]{1,0:T(8,128)(2,1)S(1)}, bf16[512,2048]{1,0:T(8,128)(2,1)}, u32[]{:S(2)}) copy-start(bf16[512,2048]{1,0:T(8,128)(2,1)} %dy_ref.7) | copy-start | bytes 6291460
  7.8 10.8 %copy-start.7 = (bf16[512,128]{1,0:T(8,128)(2,1)S(1)}, bf16[512,128]{1,0:T(8,128)(2,1)}, u32[]{:S(2)}) copy-start(bf16[512,128]{1,0:T(8,128)(2,1)} %c_ref.5) | copy-start | bytes 393220
  7.8 10.8 %copy-start.8 = (f32[32,512]{1,0:T(8,128)S(1)}, f32[32,512]{1,0:T(8,128)}, u32[]{:S(2)}) copy-start(f32[32,512]{1,0:T(8,128)} %decays_ref.1) | copy-start | bytes 196612
  13.7 4.9 %copy-start = (bf16[512,2048]{1,0:T(8,128)(2,1)S(1)}, bf16[512,2048]{1,0:T(8,128)(2,1)}, u32[]{:S(2)}) copy-start(bf16[512,2048]{1,0:T(8,128)(2,1)} %x_ref.7) | copy-start | bytes 6291460
  13.8 1.4 %copy-start.2 = (f32[2,136,1024]{2,1,0:T(8,128)S(1)}, f32[2,136,1024]{2,1,0:T(8,128)}, u32[]{:S(2)}) copy-start(f32[2,136,1024]{2,1,0:T(8,128)} %state_totals.3.mine_ref) | copy-start | bytes 3342340
  15.2 3.5 %copy-start.5 = (bf16[512,128]{1,0:T(8,128)(2,1)S(1)}, bf16[512,128]{1,0:T(8,128)(2,1)}, u32[]{:S(2)}) copy-start(bf16[512,128]{1,0:T(8,128)(2,1)} %b_ref.7) | copy-start | bytes 393220
  15.9 15.7 %collective-permute-start.1 = (f32[264,512]{1,0:T(8,128)S(1)}, f32[264,512]{1,0:T(8,128)S(1)}, u32[]{:S(2)}, u32[]{:S(2)}) collective-permute-start(f32[264,512]{1,0:T(8,128)S(1)} %get-tuple-element.45.own_ref), channel_id=1, source_target_pairs={{0,8},{4,12},{8,0},{12,4},{16,24},{20,28},{24,16},{28,20},{1,9},{5... | collective-permute-start | bytes 1622024 | tf_op jit(solution)/shard_map/ppermute | solution.py:240
  16.2 15.4 %collective-permute-start.3 = (f32[8,512]{1,0:T(8,128)S(1)}, f32[8,512]{1,0:T(8,128)S(1)}, u32[]{:S(2)}, u32[]{:S(2)}) collective-permute-start(f32[8,512]{1,0:T(8,128)S(1)} %get-tuple-element.47), channel_id=1, source_target_pairs={{0,24},{4,28},{8,16},{12,20},{16,8},{20,12},{24,0},{28,4},{1,25},{... | collective-permute-start | bytes 49160 | tf_op jit(solution)/shard_map/ppermute | solution.py:240
  18.4 15.4 %copy-start.4 = (bf16[512,128]{1,0:T(8,128)(2,1)S(1)}, bf16[512,128]{1,0:T(8,128)(2,1)}, u32[]{:S(2)}) copy-start(bf16[512,128]{1,0:T(8,128)(2,1)} %get-tuple-element.58.refs_1_.suf_ref) | copy-start | bytes 393220
  18.4 15.4 %copy-start.6 = (bf16[512,128]{1,0:T(8,128)(2,1)S(1)}, bf16[512,128]{1,0:T(8,128)(2,1)}, u32[]{:S(2)}) copy-start(bf16[512,128]{1,0:T(8,128)(2,1)} %get-tuple-element.59.refs_0_.pre_ref) | copy-start | bytes 393220
  18.4 13.2 %collective-permute-start.2 = (f32[128,512]{1,0:T(8,128)S(1)}, f32[128,512]{1,0:T(8,128)S(1)}, u32[]{:S(2)}, u32[]{:S(2)}) collective-permute-start(f32[128,512]{1,0:T(8,128)S(1)} %get-tuple-element.46), channel_id=1, source_target_pairs={{0,16},{4,20},{8,24},{12,28},{16,0},{20,4},{24,8},{28,12},{1,17},{... | collective-permute-start | bytes 786440 | tf_op jit(solution)/shard_map/ppermute | solution.py:240
  32.3 7.0 %collective-permute-start.4 = (f32[128,512]{1,0:T(8,128)S(1)}, f32[128,512]{1,0:T(8,128)S(1)}, u32[]{:S(2)}, u32[]{:S(2)}) collective-permute-start(f32[128,512]{1,0:T(8,128)S(1)} %get-tuple-element.56), channel_id=1, source_target_pairs={{0,16},{4,20},{8,24},{12,28},{16,0},{20,4},{24,8},{28,12},{1,17},{... | collective-permute-start | bytes 786440 | tf_op jit(solution)/shard_map/ppermute | solution.py:240
  33.6 6.6 %copy-start.3 = (f32[2,136,1024]{2,1,0:T(8,128)S(1)}, f32[2,136,1024]{2,1,0:T(8,128)}, u32[]{:S(2)}) copy-start(f32[2,136,1024]{2,1,0:T(8,128)} %state_totals.3.mine_ref) | copy-start | bytes 3342340
  33.6 6.6 %collective-permute-start.5 = (f32[128,512]{1,0:T(8,128)S(1)}, f32[128,512]{1,0:T(8,128)S(1)}, u32[]{:S(2)}, u32[]{:S(2)}) collective-permute-start(f32[128,512]{1,0:T(8,128)S(1)} %get-tuple-element.57), channel_id=1, source_target_pairs={{0,8},{4,12},{8,0},{12,4},{16,24},{20,28},{24,16},{28,20},{1,9},{5... | collective-permute-start | bytes 786440 | tf_op jit(solution)/shard_map/ppermute | solution.py:240
  41.2 4.6 %collective-permute-start.6 = (f32[2,128,1024]{2,1,0:T(8,128)S(1)}, f32[2,128,1024]{2,1,0:T(8,128)S(1)}, u32[]{:S(2)}, u32[]{:S(2)}) collective-permute-start(f32[2,128,1024]{2,1,0:T(8,128)S(1)} %get-tuple-element.66), channel_id=1, source_target_pairs={{0,4},{4,0},{8,12},{12,8},{16,20},{20,16},{24,28},{28,24},{1,5},{5... | collective-permute-start | bytes 3145736 | tf_op jit(solution)/shard_map/ppermute | solution.py:621
  48.4 9.4 %collective-permute-start.7 = (f32[2,128,128]{2,1,0:T(8,128)S(1)}, f32[2,128,128]{2,1,0:T(8,128)S(1)}, u32[]{:S(2)}, u32[]{:S(2)}) collective-permute-start(f32[2,128,128]{2,1,0:T(8,128)S(1)} %get-tuple-element.78), channel_id=1, source_target_pairs={{0,1},{1,2},{2,3},{3,0},{4,5},{5,6},{6,7},{7,4},{8,9},{9,10},{10,1... | collective-permute-start | bytes 393224 | tf_op jit(solution)/shard_map/ppermute | solution.py:625
  49.7 11.2 %collective-permute-start.8 = (f32[2,128,128]{2,1,0:T(8,128)S(1)}, f32[2,128,128]{2,1,0:T(8,128)S(1)}, u32[]{:S(2)}, u32[]{:S(2)}) collective-permute-start(f32[2,128,128]{2,1,0:T(8,128)S(1)} %get-tuple-element.79), channel_id=1, source_target_pairs={{0,2},{1,3},{2,0},{3,1},{4,6},{5,7},{6,4},{7,5},{8,10},{9,11},{10,... | collective-permute-start | bytes 393224 | tf_op jit(solution)/shard_map/ppermute | solution.py:625
  50.8 12.3 %collective-permute-start.9 = (f32[2,128,128]{2,1,0:T(8,128)S(1)}, f32[2,128,128]{2,1,0:T(8,128)S(1)}, u32[]{:S(2)}, u32[]{:S(2)}) collective-permute-start(f32[2,128,128]{2,1,0:T(8,128)S(1)} %get-tuple-element.80), channel_id=1, source_target_pairs={{0,3},{1,0},{2,1},{3,2},{4,7},{5,4},{6,5},{7,6},{8,11},{9,8},{10,9... | collective-permute-start | bytes 393224 | tf_op jit(solution)/shard_map/ppermute | solution.py:625

commit v4 on v3

v4 whole, which is shorter than its diff:
```python
import functools

import jax
import jax.numpy as jnp
from jax import lax
from jax.experimental import pallas as pl
from jax.experimental.pallas import tpu as pltpu
from jax.sharding import PartitionSpec as P

P_SIZE = 64
N = 128
SUB = 64
TILE = 256
EXTRA = 8
LANES = 128
CORE, OTHER = range(2)
PARAMS = pltpu.CompilerParams(vmem_limit_bytes=24 * 1024 * 1024)
FIRST = pltpu.CompilerParams(vmem_limit_bytes=60 * 1024 * 1024)
F32 = jnp.float32
BF16 = jnp.bfloat16

NN = (((1,), (0,)), ((), ()))
NT = (((1,), (1,)), ((), ()))


def dot(a, b, dims=NN):
    return lax.dot_general(a, b, dims, preferred_element_type=F32)


def halves(v):
    hi = v.astype(BF16)
    return hi, (v - hi.astype(F32)).astype(BF16)


def dot21(pair, b, dims=NN):
    return dot(pair[0], b, dims) + dot(pair[1], b, dims)


def dot12(a, pair, dims=NN):
    return dot(a, pair[0], dims) + dot(a, pair[1], dims)


def dot22(p, q, dims=NN):
    return dot(p[0], q[0], dims) + (dot(p[0], q[1], dims) + dot(p[1], q[0], dims))


def thirds(v):
    hi = v.astype(BF16)
    rest = v - hi.astype(F32)
    mid = rest.astype(BF16)
    return hi, mid, (rest - mid.astype(F32)).astype(BF16)


def spread(by_head, first, width):
    lanes = lax.broadcasted_iota(jnp.int32, by_head.shape, 1)
    step = LANES // P_SIZE
    shift = P_SIZE.bit_length() - 1
    taken = [
        jnp.take_along_axis(by_head, first + step * k + (lanes >> shift), axis=1) for k in range(width // LANES)
    ]
    return jnp.concatenate(taken, axis=1)


def place(half):
    core = lax.axis_index("seq") % 2
    return core if half == CORE else 1 - core


def stacked(*parts):
    return jnp.concatenate(parts, axis=0)


def transposed(v):
    return v.astype(F32).T.astype(BF16)


def log_parts(decays):
    return jnp.concatenate([part.astype(F32) for part in thirds(jnp.log(decays))], axis=0).astype(BF16)


def summed_logs(logs, table):
    heads = logs.shape[0] // 3
    sums = dot(logs, table.astype(F32).astype(BF16))
    return sums[:heads] + (sums[heads : 2 * heads] + sums[2 * heads :])


def by_token(v):
    rest = jnp.zeros((LANES - v.shape[0], v.shape[1]), F32)
    return jnp.concatenate([v, rest], axis=0).T


def device_factors(decays, pre_ref, suf_ref):
    local = decays.shape[1]
    logs = log_parts(decays)
    rows = lax.broadcasted_iota(jnp.int32, (local, local), 0)
    columns = lax.broadcasted_iota(jnp.int32, (local, local), 1)
    pre_ref[...] = by_token(jnp.exp(summed_logs(logs, rows <= columns)))
    suf_ref[...] = by_token(jnp.exp(summed_logs(logs, rows > columns)))


def totals_kernel(count, half, x_ref, dy_ref, b_ref, c_ref, *refs):
    if len(refs) == 6:
        decays_ref, out_ref, pre_ref, suf_ref, bt_ref, ct_ref = refs
    else:
        pre_ref, suf_ref, out_ref, bt_ref, ct_ref = refs
        decays_ref = None
    step = pl.program_id(0)

    @pl.when(step == 0)
    def _():
        bt_ref[...] = transposed(b_ref[...])
        ct_ref[...] = transposed(c_ref[...])
        if decays_ref is not None:
            device_factors(decays_ref[...], pre_ref, suf_ref)

    tile = x_ref.shape[1]
    first = (place(half) * count + step) * (tile // P_SIZE)
    before = spread(pre_ref[...], first, tile)
    after = spread(suf_ref[...], first, tile)
    ended = before[before.shape[0] - 1 :, :]
    for i, (source, factor, other) in enumerate(((x_ref, after, bt_ref), (dy_ref, before, ct_ref))):
        out_ref[i, :N, :] = dot12(other[...], halves(source[...].astype(F32) * factor))
    out_ref[0, N:, :] = jnp.broadcast_to(ended, (EXTRA, tile))
    out_ref[1, N:, :] = jnp.broadcast_to(ended, (EXTRA, tile))


def totals(half, x, dy, b, c, decays=None, pre=None, suf=None):
    local, width = x.shape
    count = width // 2 // TILE
    whole = lambda a: pl.BlockSpec(a.shape, lambda j: (0, 0))
    column = pl.BlockSpec((local, TILE), lambda j: (0, place(half) * count + j))
    factor = jax.ShapeDtypeStruct((local, LANES), F32)
    rest = (pre, suf) if decays is None else (decays,)
    out_specs = [pl.BlockSpec((2, N + EXTRA, TILE), lambda j: (0, 0, j))]
    out_shape = [jax.ShapeDtypeStruct((2, N + EXTRA, width // 2), F32)]
    if decays is not None:
        out_specs += [whole(factor), whole(factor)]
        out_shape += [factor, factor]
    return pl.pallas_call(
        functools.partial(totals_kernel, count, half),
        grid=(count,),
        in_specs=[column, column, whole(b), whole(c)] + [whole(a) for a in rest],
        out_specs=out_specs,
        scratch_shapes=[pltpu.VMEM((N, local), BF16), pltpu.VMEM((N, local), BF16)],
        out_shape=out_shape,
        compiler_params=FIRST,
        name="state_totals",
        cost_estimate=pl.CostEstimate(flops=8 * local * N * width // 2, bytes_accessed=4 * local * width, transcendentals=0),
    )(x, dy, b, c, *rest)


def ordered(core, mine, recv):
    return jnp.where(core == 0, mine, recv), jnp.where(core == 0, recv, mine)


def chip_kernel(chips, mine_ref, recv_ref, *out_refs):
    core, chip = place(CORE), lax.axis_index("seq") // 2
    early, late = ordered(core, mine_ref[0], recv_ref[0])
    early_decay, late_decay = early[N : N + 1], late[N : N + 1]
    both = jnp.broadcast_to(early_decay * late_decay, (EXTRA, early.shape[1]))
    state = late_decay * early[:N] + late[:N]
    early, late = ordered(core, mine_ref[1], recv_ref[1])
    grad = early[:N] + early_decay * late[:N]
    for r, out_ref in enumerate(out_refs, 1):
        out_ref[:N, :] = jnp.where(chip + r < chips, state, grad)
        out_ref[N:, :] = both


def chip_totals(chips, mine, recv):
    width = mine.shape[2]
    tile = min(512, width)
    block = pl.BlockSpec((2, N + EXTRA, tile), lambda j: (0, 0, j))
    out = pl.BlockSpec((N + EXTRA, tile), lambda j: (0, j))
    shape = jax.ShapeDtypeStruct((N + EXTRA, width), F32)
    return pl.pallas_call(
        functools.partial(chip_kernel, chips),
        grid=(width // tile,),
        in_specs=[block, block],
        out_specs=[out] * (chips - 1),
        out_shape=[shape] * (chips - 1),
        compiler_params=PARAMS,
        name="chip_totals",
        cost_estimate=pl.CostEstimate(flops=6 * N * width, bytes_accessed=24 * N * width, transcendentals=0),
    )(mine, recv)


def sides():
    chip = lax.axis_index("seq") // 2
    return chip < 2, (chip == 1) | (chip == 2)


def first_kernel(mine_ref, recv_ref, same_ref, cross_ref, back_ref, decay_ref):
    left, inner = sides()
    core = place(CORE)
    width = mine_ref.shape[2] // 2
    early, late = ordered(core, mine_ref[0], recv_ref[0])
    early_decay, late_decay = early[N : N + 1], late[N : N + 1]
    state = late_decay * early[:N] + late[:N]
    decay = early_decay * late_decay
    early, late = ordered(core, mine_ref[1], recv_ref[1])
    grad = early[:N] + early_decay * late[:N]
    out, back = jnp.where(left, state, grad), jnp.where(left, grad, state)
    same_ref[:N, :] = out[:, :width]
    same_ref[N : 2 * N, :] = jnp.where(inner, back[:, :width], out[:, width:])
    rows = lax.broadcasted_iota(jnp.int32, (EXTRA, width), 0)
    same_ref[2 * N :, :] = jnp.where(rows == 0, decay[:, :width], decay[:, width:])
    cross_ref[...] = out[:, width:]
    back_ref[...] = back[:, width:]
    decay_ref[...] = jnp.broadcast_to(decay[:, width:], (EXTRA, width))


def second_kernel(own_ref, back_ref, same_ref, cross_ref, decay_ref, cross2_ref, same2_ref):
    _, inner = sides()
    own, other = own_ref[:N, :], same_ref[:N, :]
    own_decay, other_decay = own_ref[2 * N : 2 * N + 1, :], same_ref[2 * N : 2 * N + 1, :]
    cross2_ref[...] = jnp.where(inner, own + own_decay * other, other + other_decay * own)
    weight = own_ref[2 * N + 1 : 2 * N + 2, :] * decay_ref[:1, :]
    same2_ref[...] = jnp.where(inner, back_ref[...] + weight * cross_ref[...], cross_ref[...])


def plain_call(kernel, name, out_shape, *args):
    whole = lambda a: pl.BlockSpec(a.shape, lambda j: (0,) * len(a.shape))
    size = sum(a.size for a in args)
    return pl.pallas_call(
        kernel,
        grid=(1,),
        in_specs=[whole(a) for a in args],
        out_specs=[whole(a) for a in out_shape],
        out_shape=out_shape,
        compiler_params=PARAMS,
        name=name,
        cost_estimate=pl.CostEstimate(flops=8 * size, bytes_accessed=4 * size, transcendentals=0),
    )(*args)


def crossed(v, length, bit):
    return lax.ppermute(v, "seq", [(i, i ^ bit) for i in range(length)])


def first_phase(length, mine, recv):
    half = mine.shape[2] // 2
    shapes = [jax.ShapeDtypeStruct((rows, half), F32) for rows in (2 * N + EXTRA, N, N, EXTRA)]
    own, cross, back, decay = plain_call(first_kernel, "first_messages", shapes, mine, recv)
    return own, back, crossed(own, length, 2), crossed(cross, length, 4), crossed(decay, length, 6)


def second_phase(own, back, same, cross, decay):
    shape = jax.ShapeDtypeStruct(back.shape, F32)
    return plain_call(second_kernel, "second_messages", [shape, shape], own, back, same, cross, decay)


def carried4_kernel(mine_ref, recv_ref, same_ref, cross_ref, decay_ref, cross2_ref, same2_ref, own_ref, peer_ref):
    left, inner = sides()
    width = cross_ref.shape[1]
    decay_a, decay_b = same_ref[2 * N : 2 * N + 1, :], same_ref[2 * N + 1 : 2 * N + 2, :]
    for part in range(2):
        at = slice(part * width, (part + 1) * width)
        out = jnp.where(inner, same_ref[part * N : (part + 1) * N, :], 0.0)
        if part == 0:
            back = jnp.where(inner, cross2_ref[...], same_ref[N : 2 * N, :] + decay_a * cross2_ref[...])
        else:
            back = same2_ref[...] + jnp.where(inner, decay_ref[:1, :], decay_b) * cross_ref[...]
        carried_cores(
            place(CORE), jnp.where(left, out, back), jnp.where(left, back, out), mine_ref, recv_ref, own_ref, peer_ref, at
        )


def carried4(mine, recv, *others):
    shape = jax.ShapeDtypeStruct((2, N, mine.shape[2]), F32)
    return plain_call(carried4_kernel, "carried_in", [shape, shape], mine, recv, *others)


def carried_cores(core, state, grad, mine_ref, recv_ref, own_ref, peer_ref, at):
    early, late = ordered(core, mine_ref[0, :, at], recv_ref[0, :, at])
    at_late = early[N : N + 1] * state + early[:N]
    own_ref[0, :, at] = jnp.where(core == 0, state, at_late)
    peer_ref[0, :, at] = jnp.where(core == 0, at_late, state)
    early, late = ordered(core, mine_ref[1, :, at], recv_ref[1, :, at])
    at_early = late[:N] + late[N : N + 1] * grad
    own_ref[1, :, at] = jnp.where(core == 0, at_early, grad)
    peer_ref[1, :, at] = jnp.where(core == 0, grad, at_early)


def carried_kernel(chips, mine_ref, recv_ref, *refs):
    others, (own_ref, peer_ref) = refs[:-2], refs[-2:]
    core, chip = place(CORE), lax.axis_index("seq") // 2
    state = grad = jnp.zeros((N, own_ref.shape[2]), F32)
    state_weight = grad_weight = jnp.ones((1, own_ref.shape[2]), F32)
    for r, ref in enumerate(others, 1):
        earlier = chip >= r
        state = jnp.where(earlier, state + state_weight * ref[:N, :], state)
        state_weight = state_weight * ref[N : N + 1, :]
    for r in range(1, chips):
        later = chip + r < chips
        ref = others[chips - r - 1]
        grad = jnp.where(later, grad + grad_weight * ref[:N, :], grad)
        grad_weight = grad_weight * ref[N : N + 1, :]
    carried_cores(core, state, grad, mine_ref, recv_ref, own_ref, peer_ref, slice(None))


def carried(chips, mine, recv, others):
    width = mine.shape[2]
    tile = min(512, width)
    pair = pl.BlockSpec((2, N + EXTRA, tile), lambda j: (0, 0, j))
    other = pl.BlockSpec((N + EXTRA, tile), lambda j: (0, j))
    out = pl.BlockSpec((2, N, tile), lambda j: (0, 0, j))
    shape = jax.ShapeDtypeStruct((2, N, width), F32)
    return pl.pallas_call(
        functools.partial(carried_kernel, chips),
        grid=(width // tile,),
        in_specs=[pair, pair] + [other] * len(others),
        out_specs=(out, out),
        out_shape=(shape, shape),
        compiler_params=PARAMS,
        name="carried_in",
        cost_estimate=pl.CostEstimate(flops=20 * N * width, bytes_accessed=44 * N * width, transcendentals=0),
    )(mine, recv, *others)


def blocks(chunks):
    span = 2
    while span < chunks:
        yield span, [at for at in range(span, chunks, 2 * span)]
        span *= 2


def row_bounds(chunks):
    middles = [k * SUB + SUB // 2 + 1 for k in range(chunks)]
    for span in [1] + [span for span, _ in blocks(chunks)]:
        for k, middle in enumerate(middles):
            boundary = (k // span + 1 - (k // span) % 2) * span * SUB
            yield min(boundary, middle), max(boundary, middle)
    yield from ((0, middle) for middle in middles)
    yield from ((middle, chunks * SUB) for middle in middles)


def local_factors(decays, lift_ref, drop_ref, rows_ref):
    local = decays.shape[1]
    logs = log_parts(decays)
    rows = lax.broadcasted_iota(jnp.int32, (local, local), 0)
    columns = lax.broadcasted_iota(jnp.int32, (local, local), 1)
    middle = (columns & -SUB) + SUB // 2
    later = (rows > middle) & (rows <= columns)
    sooner = (rows > columns) & (rows <= middle)
    offset = summed_logs(logs, later.astype(F32) - sooner.astype(F32))
    lift_ref[...] = by_token(jnp.exp(offset))
    drop_ref[...] = by_token(jnp.exp(-offset))
    lane = lax.broadcasted_iota(jnp.int32, (1, LANES), 1)
    first = last = jnp.zeros((1, LANES), jnp.int32)
    for i, (start, end) in enumerate(row_bounds(local // SUB)):
        first, last = jnp.where(lane == i, start, first), jnp.where(lane == i, end, last)
    rows = lax.broadcasted_iota(jnp.int32, (local, LANES), 0)
    decay = by_token(jnp.exp(summed_logs(logs, (rows >= first) & (rows < last))))
    rows_ref[...] = decay[: rows_ref.shape[0]]


def score_parts(b, c, ref, at, times, ahead=None):
    score = dot(b, c, NT)
    if ahead is not None:
        rows = lax.broadcasted_iota(jnp.int32, score.shape, 0)
        columns = lax.broadcasted_iota(jnp.int32, score.shape, 1)
        score = jnp.where(rows <= columns + ahead, score, 0.0)
    hi, lo = halves(score)
    width = score.shape[1]
    ref[at, :width] = hi
    ref[at, width : 2 * width] = lo
    if times == 3:
        ref[at, 2 * width :] = hi


def added_up(v):
    width = v.shape[1] // 2
    return v[:, :width] + v[:, width:]


def local_kernel(first_tile, continued, *refs):
    x_ref, dy_ref, b_ref, c_ref, decays_ref = refs[:5]
    refs = refs[5:]
    if continued:
        out_before_ref, map_before_ref = refs[:2]
        refs = refs[4:]
    part_ref, scaled_ref, out_ref, map_ref = refs[:4]
    lift_ref, drop_ref, rows_ref, full_ref, dys_ref, xs_ref, back_ref, sums_ref, even_ref, odd_ref = refs[4:14]
    level_refs = refs[14:]
    local, tile = x_ref.shape
    chunks = local // SUB
    step = pl.program_id(0)
    levels = [(span, at, level_refs[2 * i], level_refs[2 * i + 1]) for i, (span, at) in enumerate(blocks(chunks))]

    @pl.when(step == 0)
    def _():
        local_factors(decays_ref[...], lift_ref, drop_ref, rows_ref)
        sums_ref[...] = jnp.zeros(sums_ref.shape, F32)
        for k in range(0, chunks, 2):
            pair, even, odd = pl.ds(k * SUB, 2 * SUB), pl.ds(k * SUB, SUB), pl.ds((k + 1) * SUB, SUB)
            score_parts(b_ref[even, :], c_ref[even, :], even_ref, pl.ds(k // 2 * SUB, SUB), 3, 0)
            score_parts(b_ref[pair, :], c_ref[odd, :], odd_ref, pair, 3, SUB)
        for span, boundaries, mixed_ref, scores_ref in levels:
            mixed_ref[...] = jnp.zeros(mixed_ref.shape, F32)
            size = span * SUB
            for i, boundary in enumerate(boundaries):
                before, after = pl.ds((boundary - span) * SUB, size), pl.ds(boundary * SUB, size)
                score_parts(b_ref[before, :], c_ref[after, :], scores_ref, pl.ds(i * size, size), 2)

    first = (first_tile + step) * (tile // P_SIZE)
    dys_ref[...] = dy_ref[...].astype(F32) * spread(lift_ref[...], first, tile)
    back_ref[...] = spread(drop_ref[...], first, tile)
    xs_ref[...] = x_ref[...].astype(F32) * back_ref[...]
    row = spread(rows_ref[...], first, tile)
    factor = lambda kind, k: row[kind * chunks + k : kind * chunks + k + 1]

    for k in range(0, chunks, 2):
        even, odd, pair = pl.ds(k * SUB, SUB), pl.ds((k + 1) * SUB, SUB), pl.ds(k * SUB, 2 * SUB)
        dys, xs = halves(dys_ref[even, :]), halves(xs_ref[even, :])
        sums_ref[even, :] += dot(dys[0], stacked(*xs), NT)
        sums_ref[even, :SUB] += dot(dys[1], xs[0], NT)
        gained_even = dot(even_ref[pl.ds(k // 2 * SUB, SUB), :], stacked(dys[0], dys[0], dys[1]))
        joint = factor(0, k) * factor(0, k + 1)
        crossing = halves(xs_ref[even, :] * joint)
        dys, xs = halves(dys_ref[odd, :]), halves(xs_ref[odd, :])
        high = stacked(xs[0], crossing[0])
        both = dot(dys[0], stacked(high, xs[1], crossing[1]), NT)
        sums_ref[odd, :] += added_up(both) + dot(dys[1], high, NT)
        gained_odd = dot(odd_ref[pair, :], stacked(dys[0], dys[0], dys[1]))
        part_ref[even, :] = back_ref[even, :] * (gained_even + joint * gained_odd[:SUB])
        part_ref[odd, :] = back_ref[odd, :] * gained_odd[SUB:]

    for level, (span, boundaries, mixed_ref, scores_ref) in enumerate(levels, 1):
        size = span * SUB
        for i, boundary in enumerate(boundaries):
            at = pl.ds(i * size, size)
            take = lambda ref, start: halves(
                stacked(*[ref[k * SUB : (k + 1) * SUB, :] * factor(level, k) for k in range(start, start + span)])
            )
            dys, xs = take(dys_ref, boundary), take(xs_ref, boundary - span)
            both = dot(dys[0], stacked(*xs), NT)
            mixed_ref[at, :] += added_up(both) + dot(dys[1], xs[0], NT)
            gained = dot(scores_ref[at, :], stacked(dys[0], dys[0])) + dot(scores_ref[at, :size], dys[1])
            for q in range(span):
                k = boundary - span + q
                rows = pl.ds(k * SUB, SUB)
                part_ref[rows, :] += (back_ref[rows, :] * factor(level, k)) * gained[q * SUB : (q + 1) * SUB]

    for k in range(chunks):
        at = pl.ds(k * SUB, SUB)
        kind = len(levels) + 1
        scaled_ref[1, 0, at, :], scaled_ref[1, 1, at, :] = halves(dys_ref[at, :] * factor(kind, k))
        scaled_ref[0, 0, at, :], scaled_ref[0, 1, at, :] = halves(xs_ref[at, :] * factor(kind + 1, k))

    @pl.when(step == pl.num_programs(0) - 1)
    def _():
        full_ref[...] = jnp.zeros(full_ref.shape, F32)
        rows = lax.broadcasted_iota(jnp.int32, (SUB, SUB), 0)
        columns = lax.broadcasted_iota(jnp.int32, (SUB, SUB), 1)
        for k in range(0, chunks, 2):
            even, odd = pl.ds(k * SUB, SUB), pl.ds((k + 1) * SUB, SUB)
            full_ref[even, k * SUB : (k + 1) * SUB] = jnp.where(rows >= columns, added_up(sums_ref[even, :]), 0.0)
            full_ref[odd, (k + 1) * SUB : (k + 2) * SUB] = jnp.where(rows >= columns, sums_ref[odd, :SUB], 0.0)
            full_ref[odd, k * SUB : (k + 1) * SUB] = sums_ref[odd, SUB:]
        for span, boundaries, mixed_ref, _ in levels:
            size = span * SUB
            for i, boundary in enumerate(boundaries):
                block = mixed_ref[pl.ds(i * size, size), :]
                full_ref[pl.ds(boundary * SUB, size), (boundary - span) * SUB : boundary * SUB] = block
        map_ref[...] = map_before_ref[...] if continued else jnp.zeros(map_ref.shape, F32)
        for k in range(0, local, LANES):
            at = pl.ds(k, LANES)
            mixed = full_ref[at, :]
            gained = dot21(halves(mixed), b_ref[...])
            out_ref[at, :] = out_before_ref[at, :] + gained if continued else gained
            map_ref[...] += dot21(halves(mixed.T), c_ref[at, :])


def local_part(first_tile, count, x, dy, b, c, decays, before=None):
    local, width = x.shape
    chunks = local // SUB
    whole = lambda a: pl.BlockSpec(a.shape, lambda j: (0, 0))
    column = pl.BlockSpec((local, TILE), lambda j: (0, first_tile + j))
    tokens = pl.BlockSpec((local, N), lambda j: (0, 0))
    scratch = [
        pltpu.VMEM((local, LANES), F32),
        pltpu.VMEM((local, LANES), F32),
        pltpu.VMEM((-(-len(list(row_bounds(chunks))) // 8) * 8, LANES), F32),
        pltpu.VMEM((local, local), F32),
        pltpu.VMEM((local, TILE), F32),
        pltpu.VMEM((local, TILE), F32),
        pltpu.VMEM((local, TILE), F32),
        pltpu.VMEM((local, 2 * SUB), F32),
        pltpu.VMEM((local // 2, 3 * SUB), BF16),
        pltpu.VMEM((local, 3 * SUB), BF16),
    ]
    for span, _ in blocks(chunks):
        scratch.append(pltpu.VMEM((local // 2, span * SUB), F32))
        scratch.append(pltpu.VMEM((local // 2, 2 * span * SUB), BF16))
    in_specs = [column, column, whole(b), whole(c), whole(decays)]
    args, aliases = [x, dy, b, c, decays], {}
    if before is not None:
        part, scaled, out_part, map_part = before
        in_specs += [tokens, tokens, pl.BlockSpec(memory_space=pl.ANY), pl.BlockSpec(memory_space=pl.ANY)]
        args += [out_part, map_part, part, scaled]
        aliases = {7: 0, 8: 1}
    return pl.pallas_call(
        functools.partial(local_kernel, first_tile, before is not None),
        grid=(count,),
        in_specs=in_specs,
        out_specs=(column, pl.BlockSpec((2, 2, local, TILE), lambda j: (0, 0, 0, first_tile + j)), tokens, tokens),
        out_shape=(
            jax.ShapeDtypeStruct((local, width), F32),
            jax.ShapeDtypeStruct((2, 2, local, width), BF16),
            jax.ShapeDtypeStruct((local, N), F32),
            jax.ShapeDtypeStruct((local, N), F32),
        ),
        scratch_shapes=scratch,
        input_output_aliases=aliases,
        compiler_params=PARAMS,
        name="local_part",
        cost_estimate=pl.CostEstimate(
            flops=40 * local * N * TILE * count, bytes_accessed=8 * local * TILE * count, transcendentals=0
        ),
    )(*args)


def map_kernel(count, ranks, scaled_ref, carry_ref, out_before_ref, map_before_ref, *refs):
    messages, (out_ref, map_ref) = refs[:-2], refs[-2:]
    step = pl.program_id(0)

    @pl.when(step == 0)
    def _():
        out_ref[...] = out_before_ref[...]
        map_ref[...] = map_before_ref[...]

    for i, sum_ref in enumerate((map_ref, out_ref)):
        carry = halves(carry_ref[1 - i])
        both = dot(scaled_ref[i, 0], stacked(*carry), NT)
        sum_ref[...] += both[:, :N] + (both[:, N:] + dot(scaled_ref[i, 1], carry[0], NT))

    if messages:

        @pl.when(step == count - 1)
        def _():
            rows = messages[0].shape[1]
            for r, message in enumerate(messages):
                at = pl.ds(pl.multiple_of(((lax.axis_index("head") + r) % ranks) * rows, rows), rows)
                message[0] = out_ref[at, :]
                message[1] = map_ref[at, :]


def map_terms(half, scaled, carry, out_before, map_before, ranks=0):
    local, width = scaled.shape[2], carry.shape[2]
    tile = min(512, width)
    count = width // tile
    whole = lambda a: pl.BlockSpec(a.shape, lambda j: (0,) * len(a.shape))
    tokens = jax.ShapeDtypeStruct((local, N), F32)
    if ranks:
        out_shape = [jax.ShapeDtypeStruct((2, local // ranks, N), F32)] * ranks
        scratch = [pltpu.VMEM((local, N), F32), pltpu.VMEM((local, N), F32)]
    else:
        out_shape, scratch = [tokens, tokens], []
    return pl.pallas_call(
        functools.partial(map_kernel, count, ranks),
        grid=(count,),
        in_specs=[
            pl.BlockSpec((2, 2, local, tile), lambda j: (0, 0, 0, place(half) * count + j)),
            pl.BlockSpec((2, N, tile), lambda j: (0, 0, j)),
            whole(tokens),
            whole(tokens),
        ],
        out_specs=[whole(shape) for shape in out_shape],
        scratch_shapes=scratch,
        out_shape=out_shape,
        compiler_params=PARAMS,
        name="map_terms",
        cost_estimate=pl.CostEstimate(flops=12 * local * N * width, bytes_accessed=8 * local * width, transcendentals=0),
    )(scaled, carry, out_before, map_before)


def input_kernel(count, part_ref, suf_ref, b_ref, own_ref, other_ref, input_ref):
    tile = part_ref.shape[1]
    step = pl.program_id(0)
    after = spread(suf_ref[...], step * (tile // P_SIZE), tile)
    grad = jnp.where(step // count == place(CORE), own_ref[0], other_ref[0])
    input_ref[...] = (part_ref[...] + after * dot12(b_ref[...], halves(grad))).astype(BF16)


def input_terms(part, suf, b, own, other):
    local, width = part.shape
    count = width // 2 // TILE
    whole = lambda a: pl.BlockSpec(a.shape, lambda j: (0, 0))
    column = pl.BlockSpec((local, TILE), lambda j: (0, j))
    carry = pl.BlockSpec((1, N, TILE), lambda j: (1, 0, j % count))
    return pl.pallas_call(
        functools.partial(input_kernel, count),
        grid=(2 * count,),
        in_specs=[column, whole(suf), whole(b), carry, carry],
        out_specs=column,
        out_shape=jax.ShapeDtypeStruct((local, width), BF16),
        compiler_params=PARAMS,
        name="input_terms",
        cost_estimate=pl.CostEstimate(flops=4 * local * N * width, bytes_accessed=8 * local * width, transcendentals=0),
    )(part, suf, b, own, other)


def swap_cores(v, length):
    return lax.ppermute(v, "seq", [(i, i ^ 1) for i in range(length)])


def turned(v, axis, length, by):
    return lax.ppermute(v, axis, [(i, (i + by) % length) for i in range(length)])


def per_device(mixer_input, output_grad, input_map, output_map, decays):
    length, ranks = lax.axis_size("seq"), lax.axis_size("head")
    chips = length // 2
    args = mixer_input, output_grad, input_map, output_map
    sent, pre, suf = totals(OTHER, *args, decays=decays)
    recv = swap_cores(sent, length)
    (mine,) = totals(CORE, *args, pre=pre, suf=suf)
    tiles = mixer_input.shape[1] // TILE
    if chips == 4:
        ahead = tiles * 3 // 4
        own, back, *others = first_phase(length, mine, recv)
        result = local_part(0, ahead, *args, decays)
        others, result = lax.optimization_barrier((others, result))
        cross, same = second_phase(own, back, *others)
        others += [crossed(cross, length, 4), crossed(same, length, 2)]
        result, _, _ = lax.optimization_barrier((result, cross, same))
        result = local_part(ahead, tiles - ahead, *args, decays, result)
        others, result = lax.optimization_barrier((others, result))
        own, peer = carried4(mine, recv, *others)
    else:
        messages = chip_totals(chips, mine, recv)
        others = [turned(message, "seq", length, 2 * r) for r, message in enumerate(messages, 1)]
        result = local_part(0, tiles, *args, decays)
        own, peer = carried(chips, mine, recv, others)
    part, scaled, out_part, map_part = result
    other = swap_cores(peer, length)
    out_part, map_part = map_terms(CORE, scaled, own, out_part, map_part)
    shares = map_terms(OTHER, scaled, other, out_part, map_part, ranks)
    total = shares[0]
    own, other, shares = lax.optimization_barrier((own, other, shares))
    for r in range(1, ranks):
        total = total + turned(shares[r], "head", ranks, r)
    input_grad = input_terms(part, suf, input_map, own, other)
    return input_grad, total[1], total[0]


def solution(mesh):
    in_specs = (
        P("seq", "head"),
        P("seq", "head"),
        P("seq", None),
        P("seq", None),
        P("head", "seq"),
    )
    out_specs = (P("seq", "head"), P(("seq", "head"), None), P(("seq", "head"), None))
    return jax.shard_map(
        per_device, mesh=mesh, in_specs=in_specs, out_specs=out_specs, check_vma=False
    )
```

time: 64.1 us -> 59.9 us (0.934)
  Pallas kernels: 42.2 us -> 37.9 us
  waiting for transfers between devices: 7.26 us -> 8.55 us
    pallas_call x10, Pallas kernels: 42.2 us -> 37.9 us  [the longest x2 16.5 us: local_part(): pl.pallas_call(functools.partial(local_kernel, first_tile, before is not...]
    ppermute x3, waiting for transfers between devices: 5.35 us -> 6.17 us  [turned(): lax.ppermute(v, axis, [(i, (i + by) % length) for i in range(length)])]
    unnamed x20 -> x16, local copies, waits for them, and re-layouts: 1.42 us -> 1.41 us
  transfers between devices with their start and end apart: 10 -> 10, of which waited for: 4 -> 6; matrix products, arithmetic and copies ran while one was open for 0% -> 0% of each run, Pallas kernels for 49% -> 49%
where the time goes in v4:
time: 59.9 us; the launch traced here: 59.7 us
  Pallas kernels  37.9 us (63%)
  starting transfers between devices  10.4 us (17%)
  waiting for transfers between devices  8.55 us (14%)
  local copies, waits for them, and re-layouts  2.07 us (3%)
  between operations  0.72 us (1%)
    pallas_call x2, Pallas kernels, local_part(): pl.pallas_call(functools.partial(local_kernel, first_tile, before is not...  16.5 us
    pallas_call x2, Pallas kernels, totals(): pl.pallas_call(functools.partial(totals_kernel, count, half), grid=(count...  12 us
    ppermute x3, waiting for transfers between devices, turned(): lax.ppermute(v, axis, [(i, (i + by) % length) for i in range(length)])  6.17 us
    pallas_call x1, Pallas kernels, input_terms(): pl.pallas_call(functools.partial(input_kernel, count), grid=(2 * count,),...  4.74 us
    pallas_call x2, Pallas kernels, map_terms(): pl.pallas_call(functools.partial(map_kernel, count, ranks), grid=(count,)...  4 us
    ppermute x3, starting transfers between devices, turned(): lax.ppermute(v, axis, [(i, (i + by) % length) for i in range(length)])  3.82 us
    ppermute x5, starting transfers between devices, crossed(): return lax.ppermute(v, 'seq', [(i, i ^ bit) for i in range(length)])  3.73 us
    ppermute x2, starting transfers between devices, swap_cores(): return lax.ppermute(v, 'seq', [(i, i ^ 1) for i in range(length)])  2.82 us
  transfers between devices with their start and end apart: 10, of which 6 were waited for; matrix products, arithmetic and copies ran while one was open for 0% of the time, Pallas kernels for 49%

profile of v4, /device:TPU:11, one launch (start us, length us, event | category | flops | bytes accessed | tf_op | source)
XLA Modules:
  0.0 59.7 jit_solution(12217451470937527982)
XLA Ops:
  0.6 6.0 %state_totals.2 = (f32[2,136,1024]{2,1,0:T(8,128)}, f32[512,128]{1,0:T(8,128)}, f32[512,128]{1,0:T(8,128)}) custom-call(bf16[512,2048]{1,0:T(8,128)(2,1)} %refs_0_.5, bf16[512,2048]{1,0:T(8,128)(2,1)} %refs_1_.3, bf16[512,128]{1,0:T(8,128)(2,1)} %b_ref.5, bf16[512,128]{1,0:T(8,128)(2,1)} %refs_3_.3, f32[32,512]{1,0:T(8,128)} %refs_4_.3), custom_call_target="tpu_custom_call" | custom-call | flops 536870912 | bytes 4194304 | tf_op jit(solution)/shard_map/state_totals/pallas_call | solution.py:139
  6.6 0.7 %collective-permute-start = (f32[2,136,1024]{2,1,0:T(8,128)}, f32[2,136,1024]{2,1,0:T(8,128)S(1)}, u32[]{:S(2)}, u32[]{:S(2)}) collective-permute-start(f32[2,136,1024]{2,1,0:T(8,128)} %get-tuple-element.55), channel_id=1, source_target_pairs={{0,4},{4,0},{8,12},{12,8},{16,20},{20,16},{24,28},{28,24},{1,5},{5... | collective-permute-start | bytes 3342344 | tf_op jit(solution)/shard_map/ppermute | solution.py:604
  7.3 6.0 %state_totals.3.mine_ref = f32[2,136,1024]{2,1,0:T(8,128)} custom-call(bf16[512,2048]{1,0:T(8,128)(2,1)} %refs_0_.5, bf16[512,2048]{1,0:T(8,128)(2,1)} %refs_1_.3, bf16[512,128]{1,0:T(8,128)(2,1)} %b_ref.5, bf16[512,128]{1,0:T(8,128)(2,1)} %refs_3_.3, f32[512,128]{1,0:T(8,128)} %get-tuple-element.53.refs_0_, f32[512,128]{1,0:T(8,128)} %get-tuple-element.54.refs_1_.suf_ref), custom_call_target="tpu_custom_call" | custom-call | flops 536870912 | bytes 4194304 | tf_op jit(solution)/shard_map/state_totals/pallas_call | solution.py:139
  13.3 1.4 %copy-done.2 = f32[2,136,1024]{2,1,0:T(8,128)S(1)} copy-done((f32[2,136,1024]{2,1,0:T(8,128)S(1)}, f32[2,136,1024]{2,1,0:T(8,128)}, u32[]{:S(2)}) %copy-start.2) | copy-done | bytes 1114136
  14.9 0.3 collective-permute-start.1
  15.3 2.2 %collective-permute-start.3 = (f32[8,512]{1,0:T(8,128)S(1)}, f32[8,512]{1,0:T(8,128)S(1)}, u32[]{:S(2)}, u32[]{:S(2)}) collective-permute-start(f32[8,512]{1,0:T(8,128)S(1)} %get-tuple-element.58), channel_id=1, source_target_pairs={{0,24},{4,28},{8,16},{12,20},{16,8},{20,12},{24,0},{28,4},{1,25},{... | collective-permute-start | bytes 49160 | tf_op jit(solution)/shard_map/ppermute | solution.py:237
  17.7 11.6 %local_part.2 = (f32[512,2048]{1,0:T(8,128)S(1)}, bf16[2,2,512,2048]{3,2,1,0:T(8,128)(2,1)S(1)}, f32[512,128]{1,0:T(8,128)S(1)}, f32[512,128]{1,0:T(8,128)S(1)}) custom-call(bf16[512,2048]{1,0:T(8,128)(2,1)S(1)} %copy-done, bf16[512,2048]{1,0:T(8,128)(2,1)S(1)} %copy-done.1, bf16[512,128]{1,0:T(8,128)(2,1)S(1)} %copy-done.4, bf16[512,128]{1,0:T(8,128)(2,1)S(1)} %copy-done.5, ...), custom_call_target="tpu_custom_call" | custom-call | flops 4026531840 | bytes 6291456 | tf_op jit(solution)/shard_map/local_part/pallas_call | solution.py:502
  29.3 0.6 collective-permute-done.3.decay_ref
  30.0 0.8 %collective-permute-start.4 = (f32[128,512]{1,0:T(8,128)S(1)}, f32[128,512]{1,0:T(8,128)S(1)}, u32[]{:S(2)}, u32[]{:S(2)}) collective-permute-start(f32[128,512]{1,0:T(8,128)S(1)} %get-tuple-element.67), channel_id=1, source_target_pairs={{0,16},{4,20},{8,24},{12,28},{16,0},{20,4},{24,8},{28,12},{1,17},{... | collective-permute-start | bytes 786440 | tf_op jit(solution)/shard_map/ppermute | solution.py:237
  31.0 4.9 %local_part.3 = (f32[512,2048]{1,0:T(8,128)S(1)}, bf16[2,2,512,2048]{3,2,1,0:T(8,128)(2,1)S(1)}, f32[512,128]{1,0:T(8,128)S(1)}, f32[512,128]{1,0:T(8,128)S(1)}) custom-call(bf16[512,2048]{1,0:T(8,128)(2,1)S(1)} %copy-done, bf16[512,2048]{1,0:T(8,128)(2,1)S(1)} %copy-done.1, ...), custom_call_target="tpu_custom_call", output_to_operand_aliasing={{0}: (7, {}), {1}: (8, {})} | custom-call | flops 1342177280 | bytes 2097152 | tf_op jit(solution)/shard_map/local_part/pallas_call | solution.py:502
  35.9 0.8 %collective-permute-done.4.cross2_ref = f32[128,512]{1,0:T(8,128)S(1)} collective-permute-done((f32[128,512]{1,0:T(8,128)S(1)}, f32[128,512]{1,0:T(8,128)S(1)}, u32[]{:S(2)}, u32[]{:S(2)}) %collective-permute-start.4) | collective-permute-done | bytes 262176 | tf_op jit(solution)/shard_map/ppermute | solution.py:237
  36.7 0.7 %collective-permute-done.5.same2_ref = f32[128,512]{1,0:T(8,128)S(1)} collective-permute-done((f32[128,512]{1,0:T(8,128)S(1)}, f32[128,512]{1,0:T(8,128)S(1)}, u32[]{:S(2)}, u32[]{:S(2)}) %collective-permute-start.5) | collective-permute-done | bytes 262176 | tf_op jit(solution)/shard_map/ppermute | solution.py:237
  37.4 0.4 carried_in.1
  37.8 2.1 %collective-permute-start.6 = (f32[2,128,1024]{2,1,0:T(8,128)S(1)}, f32[2,128,1024]{2,1,0:T(8,128)S(1)}, u32[]{:S(2)}, u32[]{:S(2)}) collective-permute-start(f32[2,128,1024]{2,1,0:T(8,128)S(1)} %get-tuple-element.88), channel_id=1, source_target_pairs={{0,4},{4,0},{8,12},{12,8},{16,20},{20,16},{24,28},{28,24},{1,5},{5... | collective-permute-start | bytes 3145736 | tf_op jit(solution)/shard_map/ppermute | solution.py:604
  39.9 2.0 %map_terms.2 = (f32[512,128]{1,0:T(8,128)S(1)}, f32[512,128]{1,0:T(8,128)S(1)}) custom-call(bf16[2,2,512,2048]{3,2,1,0:T(8,128)(2,1)S(1)} %get-tuple-element.89.scaled_ref, f32[2,128,1024]{2,1,0:T(8,128)S(1)} %get-tuple-element.98.carry_ref.own_ref, f32[512,128]{1,0:T(8,128)S(1)} %get-tuple-element.90.out_before_ref, ...), custom_call_target="tpu_custom_call" | custom-call | flops 805306368 | bytes 4194304 | tf_op jit(solution)/shard_map/map_terms/pallas_call | solution.py:559
  41.9 0.3 collective-permute-done.6.carry_ref.other_ref
  42.2 2.0 %map_terms.3 = (f32[2,128,128]{2,1,0:T(8,128)S(1)}, f32[2,128,128]{2,1,0:T(8,128)S(1)}, f32[2,128,128]{2,1,0:T(8,128)S(1)}, f32[2,128,128]{2,1,0:T(8,128)S(1)}) custom-call(bf16[2,2,512,2048]{3,2,1,0:T(8,128)(2,1)S(1)} %get-tuple-element.89.scaled_ref, f32[2,128,1024]{2,1,0:T(8,128)S(1)} %collective-permute-done.6.carry_ref.other_ref, ...), custom_call_target="tpu_custom_call" | custom-call | flops 805306368 | bytes 4194304 | tf_op jit(solution)/shard_map/map_terms/pallas_call | solution.py:559
  44.2 1.4 %collective-permute-start.7 = (f32[2,128,128]{2,1,0:T(8,128)S(1)}, f32[2,128,128]{2,1,0:T(8,128)S(1)}, u32[]{:S(2)}, u32[]{:S(2)}) collective-permute-start(f32[2,128,128]{2,1,0:T(8,128)S(1)} %get-tuple-element.100), channel_id=1, source_target_pairs={{0,1},{1,2},{2,3},{3,0},{4,5},{5,6},{6,7},{7,4},{8,9},{9,10},{10,1... | collective-permute-start | bytes 393224 | tf_op jit(solution)/shard_map/ppermute | solution.py:608
  45.6 1.1 %collective-permute-start.8 = (f32[2,128,128]{2,1,0:T(8,128)S(1)}, f32[2,128,128]{2,1,0:T(8,128)S(1)}, u32[]{:S(2)}, u32[]{:S(2)}) collective-permute-start(f32[2,128,128]{2,1,0:T(8,128)S(1)} %get-tuple-element.101), channel_id=1, source_target_pairs={{0,2},{1,3},{2,0},{3,1},{4,6},{5,7},{6,4},{7,5},{8,10},{9,11},{10,... | collective-permute-start | bytes 393224 | tf_op jit(solution)/shard_map/ppermute | solution.py:608
  46.7 1.4 %collective-permute-start.9 = (f32[2,128,128]{2,1,0:T(8,128)S(1)}, f32[2,128,128]{2,1,0:T(8,128)S(1)}, u32[]{:S(2)}, u32[]{:S(2)}) collective-permute-start(f32[2,128,128]{2,1,0:T(8,128)S(1)} %get-tuple-element.102), channel_id=1, source_target_pairs={{0,3},{1,0},{2,1},{3,2},{4,7},{5,4},{6,5},{7,6},{8,11},{9,8},{10,9... | collective-permute-start | bytes 393224 | tf_op jit(solution)/shard_map/ppermute | solution.py:608
  48.1 4.7 %input_terms.1 = bf16[512,2048]{1,0:T(8,128)(2,1)} custom-call(f32[512,2048]{1,0:T(8,128)S(1)} %get-tuple-element.81.part_ref, f32[512,128]{1,0:T(8,128)S(1)} %copy-done.6, bf16[512,128]{1,0:T(8,128)(2,1)S(1)} %copy-done.4, f32[2,128,1024]{2,1,0:T(8,128)S(1)} %get-tuple-element.98.carry_ref.own_ref, ...), custom_call_target="tpu_custom_call" | custom-call | flops 536870912 | bytes 8388608 | tf_op jit(solution)/shard_map/input_terms/pallas_call | solution.py:591
  52.8 3.7 %collective-permute-done.8 = f32[2,128,128]{2,1,0:T(8,128)S(1)} collective-permute-done((f32[2,128,128]{2,1,0:T(8,128)S(1)}, f32[2,128,128]{2,1,0:T(8,128)S(1)}, u32[]{:S(2)}, u32[]{:S(2)}) %collective-permute-start.8) | collective-permute-done | bytes 131104 | tf_op jit(solution)/shard_map/ppermute | solution.py:608
  56.5 2.4 %collective-permute-done.9 = f32[2,128,128]{2,1,0:T(8,128)S(1)} collective-permute-done((f32[2,128,128]{2,1,0:T(8,128)S(1)}, f32[2,128,128]{2,1,0:T(8,128)S(1)}, u32[]{:S(2)}, u32[]{:S(2)}) %collective-permute-start.9) | collective-permute-done | bytes 131104 | tf_op jit(solution)/shard_map/ppermute | solution.py:608
  59.0 0.7 %slice_bitcast_fusion = (f32[128,128]{1,0:T(8,128)}, f32[128,128]{1,0:T(8,128)}) fusion(f32[2,128,128]{2,1,0:T(8,128)S(1)} %add_add_fusion), kind=kLoop, calls=%fused_computation.1 | loop fusion | bytes 262144 | tf_op jit(solution)/shard_map/squeeze | solution.py:644
  (24 shorter events, 0.8 us)
Async XLA Ops:
  6.6 6.7 %collective-permute-start = (f32[2,136,1024]{2,1,0:T(8,128)}, f32[2,136,1024]{2,1,0:T(8,128)S(1)}, u32[]{:S(2)}, u32[]{:S(2)}) collective-permute-start(f32[2,136,1024]{2,1,0:T(8,128)} %get-tuple-element.55), channel_id=1, source_target_pairs={{0,4},{4,0},{8,12},{12,8},{16,20},{20,16},{24,28},{28,24},{1,5},{5... | collective-permute-start | bytes 3342344 | tf_op jit(solution)/shard_map/ppermute | solution.py:604
  7.3 10.4 %copy-start.1 = (bf16[512,2048]{1,0:T(8,128)(2,1)S(1)}, bf16[512,2048]{1,0:T(8,128)(2,1)}, u32[]{:S(2)}) copy-start(bf16[512,2048]{1,0:T(8,128)(2,1)} %refs_1_.3) | copy-start | bytes 6291460
  7.3 10.4 %copy-start.5 = (bf16[512,128]{1,0:T(8,128)(2,1)S(1)}, bf16[512,128]{1,0:T(8,128)(2,1)}, u32[]{:S(2)}) copy-start(bf16[512,128]{1,0:T(8,128)(2,1)} %refs_3_.3) | copy-start | bytes 393220
  7.3 10.4 %copy-start.7 = (f32[32,512]{1,0:T(8,128)S(1)}, f32[32,512]{1,0:T(8,128)}, u32[]{:S(2)}) copy-start(f32[32,512]{1,0:T(8,128)} %refs_4_.3) | copy-start | bytes 196612
  13.3 4.4 %copy-start = (bf16[512,2048]{1,0:T(8,128)(2,1)S(1)}, bf16[512,2048]{1,0:T(8,128)(2,1)}, u32[]{:S(2)}) copy-start(bf16[512,2048]{1,0:T(8,128)(2,1)} %refs_0_.5) | copy-start | bytes 6291460
  13.3 1.4 %copy-start.2 = (f32[2,136,1024]{2,1,0:T(8,128)S(1)}, f32[2,136,1024]{2,1,0:T(8,128)}, u32[]{:S(2)}) copy-start(f32[2,136,1024]{2,1,0:T(8,128)} %state_totals.3.mine_ref) | copy-start | bytes 3342340
  14.7 3.0 %copy-start.4 = (bf16[512,128]{1,0:T(8,128)(2,1)S(1)}, bf16[512,128]{1,0:T(8,128)(2,1)}, u32[]{:S(2)}) copy-start(bf16[512,128]{1,0:T(8,128)(2,1)} %b_ref.5) | copy-start | bytes 393220
  14.9 15.0 %collective-permute-start.1 = (f32[264,512]{1,0:T(8,128)S(1)}, f32[264,512]{1,0:T(8,128)S(1)}, u32[]{:S(2)}, u32[]{:S(2)}) collective-permute-start(f32[264,512]{1,0:T(8,128)S(1)} %get-tuple-element.56.own_ref), channel_id=1, source_target_pairs={{0,8},{4,12},{8,0},{12,4},{16,24},{20,28},{24,16},{28,20},{1,9},{5... | collective-permute-start | bytes 1622024 | tf_op jit(solution)/shard_map/ppermute | solution.py:237
  15.3 14.6 %collective-permute-start.3 = (f32[8,512]{1,0:T(8,128)S(1)}, f32[8,512]{1,0:T(8,128)S(1)}, u32[]{:S(2)}, u32[]{:S(2)}) collective-permute-start(f32[8,512]{1,0:T(8,128)S(1)} %get-tuple-element.58), channel_id=1, source_target_pairs={{0,24},{4,28},{8,16},{12,20},{16,8},{20,12},{24,0},{28,4},{1,25},{... | collective-permute-start | bytes 49160 | tf_op jit(solution)/shard_map/ppermute | solution.py:237
  17.4 12.5 %collective-permute-start.2 = (f32[128,512]{1,0:T(8,128)S(1)}, f32[128,512]{1,0:T(8,128)S(1)}, u32[]{:S(2)}, u32[]{:S(2)}) collective-permute-start(f32[128,512]{1,0:T(8,128)S(1)} %get-tuple-element.57), channel_id=1, source_target_pairs={{0,16},{4,20},{8,24},{12,28},{16,0},{20,4},{24,8},{28,12},{1,17},{... | collective-permute-start | bytes 786440 | tf_op jit(solution)/shard_map/ppermute | solution.py:237
  30.0 6.8 %collective-permute-start.4 = (f32[128,512]{1,0:T(8,128)S(1)}, f32[128,512]{1,0:T(8,128)S(1)}, u32[]{:S(2)}, u32[]{:S(2)}) collective-permute-start(f32[128,512]{1,0:T(8,128)S(1)} %get-tuple-element.67), channel_id=1, source_target_pairs={{0,16},{4,20},{8,24},{12,28},{16,0},{20,4},{24,8},{28,12},{1,17},{... | collective-permute-start | bytes 786440 | tf_op jit(solution)/shard_map/ppermute | solution.py:237
  30.8 6.6 %copy-start.3 = (f32[2,136,1024]{2,1,0:T(8,128)S(1)}, f32[2,136,1024]{2,1,0:T(8,128)}, u32[]{:S(2)}) copy-start(f32[2,136,1024]{2,1,0:T(8,128)} %state_totals.3.mine_ref) | copy-start | bytes 3342340
  30.8 6.6 %collective-permute-start.5 = (f32[128,512]{1,0:T(8,128)S(1)}, f32[128,512]{1,0:T(8,128)S(1)}, u32[]{:S(2)}, u32[]{:S(2)}) collective-permute-start(f32[128,512]{1,0:T(8,128)S(1)} %get-tuple-element.68), channel_id=1, source_target_pairs={{0,8},{4,12},{8,0},{12,4},{16,24},{20,28},{24,16},{28,20},{1,9},{5... | collective-permute-start | bytes 786440 | tf_op jit(solution)/shard_map/ppermute | solution.py:237
  37.8 4.4 %collective-permute-start.6 = (f32[2,128,1024]{2,1,0:T(8,128)S(1)}, f32[2,128,1024]{2,1,0:T(8,128)S(1)}, u32[]{:S(2)}, u32[]{:S(2)}) collective-permute-start(f32[2,128,1024]{2,1,0:T(8,128)S(1)} %get-tuple-element.88), channel_id=1, source_target_pairs={{0,4},{4,0},{8,12},{12,8},{16,20},{20,16},{24,28},{28,24},{1,5},{5... | collective-permute-start | bytes 3145736 | tf_op jit(solution)/shard_map/ppermute | solution.py:604
  42.2 5.9 %copy-start.6 = (f32[512,128]{1,0:T(8,128)S(1)}, f32[512,128]{1,0:T(8,128)}, u32[]{:S(2)}) copy-start(f32[512,128]{1,0:T(8,128)} %get-tuple-element.54.refs_1_.suf_ref) | copy-start | bytes 786436
  44.2 8.6 %collective-permute-start.7 = (f32[2,128,128]{2,1,0:T(8,128)S(1)}, f32[2,128,128]{2,1,0:T(8,128)S(1)}, u32[]{:S(2)}, u32[]{:S(2)}) collective-permute-start(f32[2,128,128]{2,1,0:T(8,128)S(1)} %get-tuple-element.100), channel_id=1, source_target_pairs={{0,1},{1,2},{2,3},{3,0},{4,5},{5,6},{6,7},{7,4},{8,9},{9,10},{10,1... | collective-permute-start | bytes 393224 | tf_op jit(solution)/shard_map/ppermute | solution.py:608
  45.6 10.9 %collective-permute-start.8 = (f32[2,128,128]{2,1,0:T(8,128)S(1)}, f32[2,128,128]{2,1,0:T(8,128)S(1)}, u32[]{:S(2)}, u32[]{:S(2)}) collective-permute-start(f32[2,128,128]{2,1,0:T(8,128)S(1)} %get-tuple-element.101), channel_id=1, source_target_pairs={{0,2},{1,3},{2,0},{3,1},{4,6},{5,7},{6,4},{7,5},{8,10},{9,11},{10,... | collective-permute-start | bytes 393224 | tf_op jit(solution)/shard_map/ppermute | solution.py:608
  46.7 12.3 %collective-permute-start.9 = (f32[2,128,128]{2,1,0:T(8,128)S(1)}, f32[2,128,128]{2,1,0:T(8,128)S(1)}, u32[]{:S(2)}, u32[]{:S(2)}) collective-permute-start(f32[2,128,128]{2,1,0:T(8,128)S(1)} %get-tuple-element.102), channel_id=1, source_target_pairs={{0,3},{1,0},{2,1},{3,2},{4,7},{5,4},{6,5},{7,6},{8,11},{9,8},{10,9... | collective-permute-start | bytes 393224 | tf_op jit(solution)/shard_map/ppermute | solution.py:608

commit v5 on v4

--- a/solution.py
+++ b/solution.py
@@ -15,7 +15,7 @@
 LANES = 128
 CORE, OTHER = range(2)
 PARAMS = pltpu.CompilerParams(vmem_limit_bytes=24 * 1024 * 1024)
-FIRST = pltpu.CompilerParams(vmem_limit_bytes=60 * 1024 * 1024)
+FIRST = pltpu.CompilerParams(vmem_limit_bytes=56 * 1024 * 1024)
 F32 = jnp.float32
 BF16 = jnp.bfloat16
 
@@ -98,55 +98,53 @@
     suf_ref[...] = by_token(jnp.exp(summed_logs(logs, rows > columns)))
 
 
-def totals_kernel(count, half, x_ref, dy_ref, b_ref, c_ref, *refs):
-    if len(refs) == 6:
-        decays_ref, out_ref, pre_ref, suf_ref, bt_ref, ct_ref = refs
-    else:
-        pre_ref, suf_ref, out_ref, bt_ref, ct_ref = refs
-        decays_ref = None
+def totals_kernel(half, x_ref, dy_ref, b_ref, c_ref, decays_ref, out_ref, pre_ref, suf_ref):
+    rows, width = x_ref.shape
     step = pl.program_id(0)
 
     @pl.when(step == 0)
     def _():
-        bt_ref[...] = transposed(b_ref[...])
-        ct_ref[...] = transposed(c_ref[...])
-        if decays_ref is not None:
-            device_factors(decays_ref[...], pre_ref, suf_ref)
-
-    tile = x_ref.shape[1]
-    first = (place(half) * count + step) * (tile // P_SIZE)
-    before = spread(pre_ref[...], first, tile)
-    after = spread(suf_ref[...], first, tile)
-    ended = before[before.shape[0] - 1 :, :]
-    for i, (source, factor, other) in enumerate(((x_ref, after, bt_ref), (dy_ref, before, ct_ref))):
-        out_ref[i, :N, :] = dot12(other[...], halves(source[...].astype(F32) * factor))
-    out_ref[0, N:, :] = jnp.broadcast_to(ended, (EXTRA, tile))
-    out_ref[1, N:, :] = jnp.broadcast_to(ended, (EXTRA, tile))
-
-
-def totals(half, x, dy, b, c, decays=None, pre=None, suf=None):
+        device_factors(decays_ref[...], pre_ref, suf_ref)
+
+    first = place(half) * (width // P_SIZE)
+    at = pl.ds(pl.multiple_of(step * rows, rows), rows)
+    for i, (source, factor, other) in enumerate(((x_ref, suf_ref, b_ref), (dy_ref, pre_ref, c_ref))):
+        scaled = halves(source[...].astype(F32) * spread(factor[at, :], first, width))
+        turned_map = transposed(other[at, :])
+        gained = dot(jnp.concatenate([turned_map, turned_map], axis=1), stacked(*scaled))
+
+        @pl.when(step == 0)
+        def _():
+            out_ref[i, :N, :] = gained
+
+        @pl.when(step > 0)
+        def _():
+            out_ref[i, :N, :] += gained
+
+    @pl.when(step == pl.num_programs(0) - 1)
+    def _():
+        last = pre_ref[pre_ref.shape[0] - EXTRA :, :]
+        ended = jnp.broadcast_to(spread(last, first, width)[EXTRA - 1 :], (EXTRA, width))
+        out_ref[0, N:, :] = ended
+        out_ref[1, N:, :] = ended
+
+
+def totals(half, x, dy, b, c, decays, params):
     local, width = x.shape
-    count = width // 2 // TILE
+    width //= 2
     whole = lambda a: pl.BlockSpec(a.shape, lambda j: (0, 0))
-    column = pl.BlockSpec((local, TILE), lambda j: (0, place(half) * count + j))
+    rows = pl.BlockSpec((LANES, width), lambda j: (j, place(half)))
     factor = jax.ShapeDtypeStruct((local, LANES), F32)
-    rest = (pre, suf) if decays is None else (decays,)
-    out_specs = [pl.BlockSpec((2, N + EXTRA, TILE), lambda j: (0, 0, j))]
-    out_shape = [jax.ShapeDtypeStruct((2, N + EXTRA, width // 2), F32)]
-    if decays is not None:
-        out_specs += [whole(factor), whole(factor)]
-        out_shape += [factor, factor]
     return pl.pallas_call(
-        functools.partial(totals_kernel, count, half),
-        grid=(count,),
-        in_specs=[column, column, whole(b), whole(c)] + [whole(a) for a in rest],
-        out_specs=out_specs,
-        scratch_shapes=[pltpu.VMEM((N, local), BF16), pltpu.VMEM((N, local), BF16)],
-        out_shape=out_shape,
-        compiler_params=FIRST,
+        functools.partial(totals_kernel, half),
+        grid=(local // LANES,),
+        in_specs=[rows, rows, whole(b), whole(c), whole(decays)],
+        out_specs=[pl.BlockSpec((2, N + EXTRA, width), lambda j: (0, 0, 0)), whole(factor), whole(factor)],
+        out_shape=[jax.ShapeDtypeStruct((2, N + EXTRA, width), F32), factor, factor],
+        compiler_params=params,
         name="state_totals",
-        cost_estimate=pl.CostEstimate(flops=8 * local * N * width // 2, bytes_accessed=4 * local * width, transcendentals=0),
-    )(x, dy, b, c, *rest)
+        cost_estimate=pl.CostEstimate(flops=8 * local * N * width, bytes_accessed=4 * local * width, transcendentals=0),
+    )(x, dy, b, c, decays)
 
 
 def ordered(core, mine, recv):
@@ -612,9 +610,9 @@
     length, ranks = lax.axis_size("seq"), lax.axis_size("head")
     chips = length // 2
     args = mixer_input, output_grad, input_map, output_map
-    sent, pre, suf = totals(OTHER, *args, decays=decays)
+    sent, _, _ = totals(OTHER, *args, decays, FIRST)
     recv = swap_cores(sent, length)
-    (mine,) = totals(CORE, *args, pre=pre, suf=suf)
+    mine, _, suf = totals(CORE, *args, decays, PARAMS)
     tiles = mixer_input.shape[1] // TILE
     if chips == 4:
         ahead = tiles * 3 // 4

time: 59.9 us -> 61.3 us (1.023)
  Pallas kernels: 37.9 us -> 40.7 us
  local copies, waits for them, and re-layouts: 2.07 us -> 0.68 us
    pallas_call x2, Pallas kernels: 12 us -> 14.8 us  [totals(): pl.pallas_call(functools.partial(totals_kernel, half), grid=(local // LAN...]
    unnamed x16 -> x10, local copies, waits for them, and re-layouts: 1.41 us -> 0.02 us
where the time goes in v5:
time: 61.3 us; the launch traced here: 61.1 us
  Pallas kernels  40.7 us (66%)
  starting transfers between devices  10.3 us (17%)
  waiting for transfers between devices  8.65 us (14%)
  between operations  0.75 us (1%)
  local copies, waits for them, and re-layouts  0.68 us (1%)
    pallas_call x2, Pallas kernels, local_part(): pl.pallas_call(functools.partial(local_kernel, first_tile, before is not...  16.5 us
    pallas_call x2, Pallas kernels, totals(): pl.pallas_call(functools.partial(totals_kernel, half), grid=(local // LAN...  14.8 us
    ppermute x3, waiting for transfers between devices, turned(): lax.ppermute(v, axis, [(i, (i + by) % length) for i in range(length)])  6.18 us
    pallas_call x1, Pallas kernels, input_terms(): pl.pallas_call(functools.partial(input_kernel, count), grid=(2 * count,),...  4.74 us
    pallas_call x2, Pallas kernels, map_terms(): pl.pallas_call(functools.partial(map_kernel, count, ranks), grid=(count,)...  3.98 us
    ppermute x3, starting transfers between devices, turned(): lax.ppermute(v, axis, [(i, (i + by) % length) for i in range(length)])  3.82 us
    ppermute x5, starting transfers between devices, crossed(): return lax.ppermute(v, 'seq', [(i, i ^ bit) for i in range(length)])  3.68 us
    ppermute x2, starting transfers between devices, swap_cores(): return lax.ppermute(v, 'seq', [(i, i ^ 1) for i in range(length)])  2.8 us
  transfers between devices with their start and end apart: 10, of which 6 were waited for; matrix products, arithmetic and copies ran while one was open for 0% of the time, Pallas kernels for 49%

profile of v5, /device:TPU:11, one launch (start us, length us, event | category | flops | bytes accessed | tf_op | source)
XLA Modules:
  0.0 61.1 jit_solution(9760621032899189561)
XLA Ops:
  0.7 8.2 %state_totals.3 = (f32[2,136,1024]{2,1,0:T(8,128)}, f32[512,128]{1,0:T(8,128)}, f32[512,128]{1,0:T(8,128)}) custom-call(bf16[512,2048]{1,0:T(8,128)(2,1)} %refs_0_.3, bf16[512,2048]{1,0:T(8,128)(2,1)} %refs_1_.3, bf16[512,128]{1,0:T(8,128)(2,1)} %b_ref.5, bf16[512,128]{1,0:T(8,128)(2,1)} %refs_3_.3, f32[32,512]{1,0:T(8,128)} %refs_4_.3), custom_call_target="tpu_custom_call" | custom-call | flops 536870912 | bytes 2097152 | tf_op jit(solution)/shard_map/state_totals/pallas_call | solution.py:138
  8.9 0.7 %collective-permute-start = (f32[2,136,1024]{2,1,0:T(8,128)}, f32[2,136,1024]{2,1,0:T(8,128)S(1)}, u32[]{:S(2)}, u32[]{:S(2)}) collective-permute-start(f32[2,136,1024]{2,1,0:T(8,128)} %get-tuple-element.54), channel_id=1, source_target_pairs={{0,4},{4,0},{8,12},{12,8},{16,20},{20,16},{24,28},{28,24},{1,5},{5... | collective-permute-start | bytes 3342344 | tf_op jit(solution)/shard_map/ppermute | solution.py:602
  9.6 6.6 %state_totals.2 = (f32[2,136,1024]{2,1,0:T(8,128)S(1)}, f32[512,128]{1,0:T(8,128)}, f32[512,128]{1,0:T(8,128)S(1)}) custom-call(bf16[512,2048]{1,0:T(8,128)(2,1)S(1)} %copy-done, bf16[512,2048]{1,0:T(8,128)(2,1)S(1)} %copy-done.1, bf16[512,128]{1,0:T(8,128)(2,1)S(1)} %copy-done.2, bf16[512,128]{1,0:T(8,128)(2,1)S(1)} %copy-done.3, f32[32,512]{1,0:T(8,128)S(1)} %copy-done.4), custom_call_target="tpu_custom_call" | custom-call | flops 536870912 | bytes 2097152 | tf_op jit(solution)/shard_map/state_totals/pallas_call | solution.py:138
  16.4 0.3 collective-permute-start.1
  16.7 2.2 %collective-permute-start.3 = (f32[8,512]{1,0:T(8,128)S(1)}, f32[8,512]{1,0:T(8,128)S(1)}, u32[]{:S(2)}, u32[]{:S(2)}) collective-permute-start(f32[8,512]{1,0:T(8,128)S(1)} %get-tuple-element.57), channel_id=1, source_target_pairs={{0,24},{4,28},{8,16},{12,20},{16,8},{20,12},{24,0},{28,4},{1,25},{... | collective-permute-start | bytes 49160 | tf_op jit(solution)/shard_map/ppermute | solution.py:235
  19.1 11.6 %local_part.2 = (f32[512,2048]{1,0:T(8,128)S(1)}, bf16[2,2,512,2048]{3,2,1,0:T(8,128)(2,1)S(1)}, f32[512,128]{1,0:T(8,128)S(1)}, f32[512,128]{1,0:T(8,128)S(1)}) custom-call(bf16[512,2048]{1,0:T(8,128)(2,1)S(1)} %copy-done, bf16[512,2048]{1,0:T(8,128)(2,1)S(1)} %copy-done.1, bf16[512,128]{1,0:T(8,128)(2,1)S(1)} %copy-done.2, bf16[512,128]{1,0:T(8,128)(2,1)S(1)} %copy-done.3, ...), custom_call_target="tpu_custom_call" | custom-call | flops 4026531840 | bytes 6291456 | tf_op jit(solution)/shard_map/local_part/pallas_call | solution.py:500
  30.8 0.6 %collective-permute-done.3.decay_ref = f32[8,512]{1,0:T(8,128)S(1)} collective-permute-done((f32[8,512]{1,0:T(8,128)S(1)}, f32[8,512]{1,0:T(8,128)S(1)}, u32[]{:S(2)}, u32[]{:S(2)}) %collective-permute-start.3) | collective-permute-done | bytes 16416 | tf_op jit(solution)/shard_map/ppermute | solution.py:235
  31.5 0.7 %collective-permute-start.4 = (f32[128,512]{1,0:T(8,128)S(1)}, f32[128,512]{1,0:T(8,128)S(1)}, u32[]{:S(2)}, u32[]{:S(2)}) collective-permute-start(f32[128,512]{1,0:T(8,128)S(1)} %get-tuple-element.66), channel_id=1, source_target_pairs={{0,16},{4,20},{8,24},{12,28},{16,0},{20,4},{24,8},{28,12},{1,17},{... | collective-permute-start | bytes 786440 | tf_op jit(solution)/shard_map/ppermute | solution.py:235
  32.2 0.2 collective-permute-start.5
  32.4 4.9 %local_part.3 = (f32[512,2048]{1,0:T(8,128)S(1)}, bf16[2,2,512,2048]{3,2,1,0:T(8,128)(2,1)S(1)}, f32[512,128]{1,0:T(8,128)S(1)}, f32[512,128]{1,0:T(8,128)S(1)}) custom-call(bf16[512,2048]{1,0:T(8,128)(2,1)S(1)} %copy-done, bf16[512,2048]{1,0:T(8,128)(2,1)S(1)} %copy-done.1, ...), custom_call_target="tpu_custom_call", output_to_operand_aliasing={{0}: (7, {}), {1}: (8, {})} | custom-call | flops 1342177280 | bytes 2097152 | tf_op jit(solution)/shard_map/local_part/pallas_call | solution.py:500
  37.3 0.9 %collective-permute-done.4.cross2_ref = f32[128,512]{1,0:T(8,128)S(1)} collective-permute-done((f32[128,512]{1,0:T(8,128)S(1)}, f32[128,512]{1,0:T(8,128)S(1)}, u32[]{:S(2)}, u32[]{:S(2)}) %collective-permute-start.4) | collective-permute-done | bytes 262176 | tf_op jit(solution)/shard_map/ppermute | solution.py:235
  38.2 0.6 %collective-permute-done.5.same2_ref = f32[128,512]{1,0:T(8,128)S(1)} collective-permute-done((f32[128,512]{1,0:T(8,128)S(1)}, f32[128,512]{1,0:T(8,128)S(1)}, u32[]{:S(2)}, u32[]{:S(2)}) %collective-permute-start.5) | collective-permute-done | bytes 262176 | tf_op jit(solution)/shard_map/ppermute | solution.py:235
  38.9 0.4 carried_in.1
  39.2 2.1 %collective-permute-start.6 = (f32[2,128,1024]{2,1,0:T(8,128)S(1)}, f32[2,128,1024]{2,1,0:T(8,128)S(1)}, u32[]{:S(2)}, u32[]{:S(2)}) collective-permute-start(f32[2,128,1024]{2,1,0:T(8,128)S(1)} %get-tuple-element.88), channel_id=1, source_target_pairs={{0,4},{4,0},{8,12},{12,8},{16,20},{20,16},{24,28},{28,24},{1,5},{5... | collective-permute-start | bytes 3145736 | tf_op jit(solution)/shard_map/ppermute | solution.py:602
  41.3 2.0 %map_terms.2 = (f32[512,128]{1,0:T(8,128)S(1)}, f32[512,128]{1,0:T(8,128)S(1)}) custom-call(bf16[2,2,512,2048]{3,2,1,0:T(8,128)(2,1)S(1)} %get-tuple-element.89.scaled_ref, f32[2,128,1024]{2,1,0:T(8,128)S(1)} %get-tuple-element.98.carry_ref.own_ref, f32[512,128]{1,0:T(8,128)S(1)} %get-tuple-element.90.out_before_ref, ...), custom_call_target="tpu_custom_call" | custom-call | flops 805306368 | bytes 4194304 | tf_op jit(solution)/shard_map/map_terms/pallas_call | solution.py:557
  43.3 0.3 collective-permute-done.6.carry_ref.other_ref
  43.6 2.0 %map_terms.3 = (f32[2,128,128]{2,1,0:T(8,128)S(1)}, f32[2,128,128]{2,1,0:T(8,128)S(1)}, f32[2,128,128]{2,1,0:T(8,128)S(1)}, f32[2,128,128]{2,1,0:T(8,128)S(1)}) custom-call(bf16[2,2,512,2048]{3,2,1,0:T(8,128)(2,1)S(1)} %get-tuple-element.89.scaled_ref, f32[2,128,1024]{2,1,0:T(8,128)S(1)} %collective-permute-done.6.carry_ref.other_ref, ...), custom_call_target="tpu_custom_call" | custom-call | flops 805306368 | bytes 4194304 | tf_op jit(solution)/shard_map/map_terms/pallas_call | solution.py:557
  45.7 1.3 %collective-permute-start.7 = (f32[2,128,128]{2,1,0:T(8,128)S(1)}, f32[2,128,128]{2,1,0:T(8,128)S(1)}, u32[]{:S(2)}, u32[]{:S(2)}) collective-permute-start(f32[2,128,128]{2,1,0:T(8,128)S(1)} %get-tuple-element.100), channel_id=1, source_target_pairs={{0,1},{1,2},{2,3},{3,0},{4,5},{5,6},{6,7},{7,4},{8,9},{9,10},{10,1... | collective-permute-start | bytes 393224 | tf_op jit(solution)/shard_map/ppermute | solution.py:606
  47.0 1.1 %collective-permute-start.8 = (f32[2,128,128]{2,1,0:T(8,128)S(1)}, f32[2,128,128]{2,1,0:T(8,128)S(1)}, u32[]{:S(2)}, u32[]{:S(2)}) collective-permute-start(f32[2,128,128]{2,1,0:T(8,128)S(1)} %get-tuple-element.101), channel_id=1, source_target_pairs={{0,2},{1,3},{2,0},{3,1},{4,6},{5,7},{6,4},{7,5},{8,10},{9,11},{10,... | collective-permute-start | bytes 393224 | tf_op jit(solution)/shard_map/ppermute | solution.py:606
  48.1 1.4 %collective-permute-start.9 = (f32[2,128,128]{2,1,0:T(8,128)S(1)}, f32[2,128,128]{2,1,0:T(8,128)S(1)}, u32[]{:S(2)}, u32[]{:S(2)}) collective-permute-start(f32[2,128,128]{2,1,0:T(8,128)S(1)} %get-tuple-element.102), channel_id=1, source_target_pairs={{0,3},{1,0},{2,1},{3,2},{4,7},{5,4},{6,5},{7,6},{8,11},{9,8},{10,9... | collective-permute-start | bytes 393224 | tf_op jit(solution)/shard_map/ppermute | solution.py:606
  49.5 4.7 %input_terms.1 = bf16[512,2048]{1,0:T(8,128)(2,1)} custom-call(f32[512,2048]{1,0:T(8,128)S(1)} %get-tuple-element.80.part_ref, f32[512,128]{1,0:T(8,128)S(1)} %get-tuple-element.81.suf_ref, bf16[512,128]{1,0:T(8,128)(2,1)S(1)} %copy-done.2, f32[2,128,1024]{2,1,0:T(8,128)S(1)} %get-tuple-element.98.carry_ref.own_ref, ...), custom_call_target="tpu_custom_call" | custom-call | flops 536870912 | bytes 8388608 | tf_op jit(solution)/shard_map/input_terms/pallas_call | solution.py:589
  54.2 3.7 %collective-permute-done.8 = f32[2,128,128]{2,1,0:T(8,128)S(1)} collective-permute-done((f32[2,128,128]{2,1,0:T(8,128)S(1)}, f32[2,128,128]{2,1,0:T(8,128)S(1)}, u32[]{:S(2)}, u32[]{:S(2)}) %collective-permute-start.8) | collective-permute-done | bytes 131104 | tf_op jit(solution)/shard_map/ppermute | solution.py:606
  57.9 2.5 %collective-permute-done.9 = f32[2,128,128]{2,1,0:T(8,128)S(1)} collective-permute-done((f32[2,128,128]{2,1,0:T(8,128)S(1)}, f32[2,128,128]{2,1,0:T(8,128)S(1)}, u32[]{:S(2)}, u32[]{:S(2)}) %collective-permute-start.9) | collective-permute-done | bytes 131104 | tf_op jit(solution)/shard_map/ppermute | solution.py:606
  60.4 0.7 %slice_bitcast_fusion = (f32[128,128]{1,0:T(8,128)}, f32[128,128]{1,0:T(8,128)}) fusion(f32[2,128,128]{2,1,0:T(8,128)S(1)} %add_add_fusion), kind=kLoop, calls=%fused_computation.1 | loop fusion | bytes 262144 | tf_op jit(solution)/shard_map/squeeze | solution.py:642
  (18 shorter events, 0.6 us)
Async XLA Ops:
  0.6 8.9 %copy-start.2 = (bf16[512,128]{1,0:T(8,128)(2,1)S(1)}, bf16[512,128]{1,0:T(8,128)(2,1)}, u32[]{:S(2)}) copy-start(bf16[512,128]{1,0:T(8,128)(2,1)} %b_ref.5) | copy-start | bytes 393220
  0.6 8.9 %copy-start.4 = (f32[32,512]{1,0:T(8,128)S(1)}, f32[32,512]{1,0:T(8,128)}, u32[]{:S(2)}) copy-start(f32[32,512]{1,0:T(8,128)} %refs_4_.3) | copy-start | bytes 196612
  0.7 8.9 %copy-start.3 = (bf16[512,128]{1,0:T(8,128)(2,1)S(1)}, bf16[512,128]{1,0:T(8,128)(2,1)}, u32[]{:S(2)}) copy-start(bf16[512,128]{1,0:T(8,128)(2,1)} %refs_3_.3) | copy-start | bytes 393220
  0.7 8.9 %copy-start.1 = (bf16[512,2048]{1,0:T(8,128)(2,1)S(1)}, bf16[512,2048]{1,0:T(8,128)(2,1)}, u32[]{:S(2)}) copy-start(bf16[512,2048]{1,0:T(8,128)(2,1)} %refs_1_.3) | copy-start | bytes 6291460
  0.7 8.9 %copy-start = (bf16[512,2048]{1,0:T(8,128)(2,1)S(1)}, bf16[512,2048]{1,0:T(8,128)(2,1)}, u32[]{:S(2)}) copy-start(bf16[512,2048]{1,0:T(8,128)(2,1)} %refs_0_.3) | copy-start | bytes 6291460
  8.9 7.3 %collective-permute-start = (f32[2,136,1024]{2,1,0:T(8,128)}, f32[2,136,1024]{2,1,0:T(8,128)S(1)}, u32[]{:S(2)}, u32[]{:S(2)}) collective-permute-start(f32[2,136,1024]{2,1,0:T(8,128)} %get-tuple-element.54), channel_id=1, source_target_pairs={{0,4},{4,0},{8,12},{12,8},{16,20},{20,16},{24,28},{28,24},{1,5},{5... | collective-permute-start | bytes 3342344 | tf_op jit(solution)/shard_map/ppermute | solution.py:602
  16.4 15.0 %collective-permute-start.1 = (f32[264,512]{1,0:T(8,128)S(1)}, f32[264,512]{1,0:T(8,128)S(1)}, u32[]{:S(2)}, u32[]{:S(2)}) collective-permute-start(f32[264,512]{1,0:T(8,128)S(1)} %get-tuple-element.55.own_ref), channel_id=1, source_target_pairs={{0,8},{4,12},{8,0},{12,4},{16,24},{20,28},{24,16},{28,20},{1,9},{5... | collective-permute-start | bytes 1622024 | tf_op jit(solution)/shard_map/ppermute | solution.py:235
  16.7 14.7 %collective-permute-start.3 = (f32[8,512]{1,0:T(8,128)S(1)}, f32[8,512]{1,0:T(8,128)S(1)}, u32[]{:S(2)}, u32[]{:S(2)}) collective-permute-start(f32[8,512]{1,0:T(8,128)S(1)} %get-tuple-element.57), channel_id=1, source_target_pairs={{0,24},{4,28},{8,16},{12,20},{16,8},{20,12},{24,0},{28,4},{1,25},{... | collective-permute-start | bytes 49160 | tf_op jit(solution)/shard_map/ppermute | solution.py:235
  18.9 12.5 %collective-permute-start.2 = (f32[128,512]{1,0:T(8,128)S(1)}, f32[128,512]{1,0:T(8,128)S(1)}, u32[]{:S(2)}, u32[]{:S(2)}) collective-permute-start(f32[128,512]{1,0:T(8,128)S(1)} %get-tuple-element.56), channel_id=1, source_target_pairs={{0,16},{4,20},{8,24},{12,28},{16,0},{20,4},{24,8},{28,12},{1,17},{... | collective-permute-start | bytes 786440 | tf_op jit(solution)/shard_map/ppermute | solution.py:235
  31.5 6.8 %collective-permute-start.4 = (f32[128,512]{1,0:T(8,128)S(1)}, f32[128,512]{1,0:T(8,128)S(1)}, u32[]{:S(2)}, u32[]{:S(2)}) collective-permute-start(f32[128,512]{1,0:T(8,128)S(1)} %get-tuple-element.66), channel_id=1, source_target_pairs={{0,16},{4,20},{8,24},{12,28},{16,0},{20,4},{24,8},{28,12},{1,17},{... | collective-permute-start | bytes 786440 | tf_op jit(solution)/shard_map/ppermute | solution.py:235
  32.2 6.7 %collective-permute-start.5 = (f32[128,512]{1,0:T(8,128)S(1)}, f32[128,512]{1,0:T(8,128)S(1)}, u32[]{:S(2)}, u32[]{:S(2)}) collective-permute-start(f32[128,512]{1,0:T(8,128)S(1)} %get-tuple-element.67), channel_id=1, source_target_pairs={{0,8},{4,12},{8,0},{12,4},{16,24},{20,28},{24,16},{28,20},{1,9},{5... | collective-permute-start | bytes 786440 | tf_op jit(solution)/shard_map/ppermute | solution.py:235
  39.2 4.4 %collective-permute-start.6 = (f32[2,128,1024]{2,1,0:T(8,128)S(1)}, f32[2,128,1024]{2,1,0:T(8,128)S(1)}, u32[]{:S(2)}, u32[]{:S(2)}) collective-permute-start(f32[2,128,1024]{2,1,0:T(8,128)S(1)} %get-tuple-element.88), channel_id=1, source_target_pairs={{0,4},{4,0},{8,12},{12,8},{16,20},{20,16},{24,28},{28,24},{1,5},{5... | collective-permute-start | bytes 3145736 | tf_op jit(solution)/shard_map/ppermute | solution.py:602
  45.7 8.6 %collective-permute-start.7 = (f32[2,128,128]{2,1,0:T(8,128)S(1)}, f32[2,128,128]{2,1,0:T(8,128)S(1)}, u32[]{:S(2)}, u32[]{:S(2)}) collective-permute-start(f32[2,128,128]{2,1,0:T(8,128)S(1)} %get-tuple-element.100), channel_id=1, source_target_pairs={{0,1},{1,2},{2,3},{3,0},{4,5},{5,6},{6,7},{7,4},{8,9},{9,10},{10,1... | collective-permute-start | bytes 393224 | tf_op jit(solution)/shard_map/ppermute | solution.py:606
  47.0 10.9 %collective-permute-start.8 = (f32[2,128,128]{2,1,0:T(8,128)S(1)}, f32[2,128,128]{2,1,0:T(8,128)S(1)}, u32[]{:S(2)}, u32[]{:S(2)}) collective-permute-start(f32[2,128,128]{2,1,0:T(8,128)S(1)} %get-tuple-element.101), channel_id=1, source_target_pairs={{0,2},{1,3},{2,0},{3,1},{4,6},{5,7},{6,4},{7,5},{8,10},{9,11},{10,... | collective-permute-start | bytes 393224 | tf_op jit(solution)/shard_map/ppermute | solution.py:606
  48.1 12.3 %collective-permute-start.9 = (f32[2,128,128]{2,1,0:T(8,128)S(1)}, f32[2,128,128]{2,1,0:T(8,128)S(1)}, u32[]{:S(2)}, u32[]{:S(2)}) collective-permute-start(f32[2,128,128]{2,1,0:T(8,128)S(1)} %get-tuple-element.102), channel_id=1, source_target_pairs={{0,3},{1,0},{2,1},{3,2},{4,7},{5,4},{6,5},{7,6},{8,11},{9,8},{10,9... | collective-permute-start | bytes 393224 | tf_op jit(solution)/shard_map/ppermute | solution.py:606

commit v6 on v4

--- a/solution.py
+++ b/solution.py
@@ -12,10 +12,11 @@
 SUB = 64
 TILE = 256
 EXTRA = 8
+PARTS = 4
 LANES = 128
 CORE, OTHER = range(2)
 PARAMS = pltpu.CompilerParams(vmem_limit_bytes=24 * 1024 * 1024)
-FIRST = pltpu.CompilerParams(vmem_limit_bytes=60 * 1024 * 1024)
+FIRST = pltpu.CompilerParams(vmem_limit_bytes=56 * 1024 * 1024)
 F32 = jnp.float32
 BF16 = jnp.bfloat16
 
@@ -89,64 +90,84 @@
     return jnp.concatenate([v, rest], axis=0).T
 
 
-def device_factors(decays, pre_ref, suf_ref):
+def packed(v):
+    parts = [part.astype(F32) for part in thirds(v)]
+    rest = jnp.zeros((LANES - 3 * v.shape[0], v.shape[1]), F32)
+    return jnp.concatenate(parts + [rest], axis=0).T.astype(BF16)
+
+
+def spread_table(heads, first, width):
+    rows = lax.broadcasted_iota(jnp.int32, (heads, width), 0)
+    columns = lax.broadcasted_iota(jnp.int32, (heads, width), 1)
+    offset = columns - (rows - first) * P_SIZE
+    picked = ((offset >= 0) & (offset < P_SIZE)).astype(F32)
+    rest = jnp.zeros((LANES - 3 * heads, width), F32)
+    return jnp.concatenate([picked, picked, picked, rest], axis=0).astype(BF16)
+
+
+def device_factors(decays, ref):
     local = decays.shape[1]
     logs = log_parts(decays)
     rows = lax.broadcasted_iota(jnp.int32, (local, local), 0)
     columns = lax.broadcasted_iota(jnp.int32, (local, local), 1)
-    pre_ref[...] = by_token(jnp.exp(summed_logs(logs, rows <= columns)))
-    suf_ref[...] = by_token(jnp.exp(summed_logs(logs, rows > columns)))
-
-
-def totals_kernel(count, half, x_ref, dy_ref, b_ref, c_ref, *refs):
-    if len(refs) == 6:
-        decays_ref, out_ref, pre_ref, suf_ref, bt_ref, ct_ref = refs
+    ref[:, :LANES] = packed(jnp.exp(summed_logs(logs, rows <= columns)))
+    ref[:, LANES:] = packed(jnp.exp(summed_logs(logs, rows > columns)))
+
+
+def totals_kernel(heads, count, half, made, *refs):
+    x_refs, dy_refs, (b_ref, c_ref) = refs[:PARTS], refs[PARTS : 2 * PARTS], refs[2 * PARTS : 2 * PARTS + 2]
+    refs = refs[2 * PARTS + 2 :]
+    if made:
+        factor_ref, out_ref, bt_ref, ct_ref = refs
     else:
-        pre_ref, suf_ref, out_ref, bt_ref, ct_ref = refs
-        decays_ref = None
+        decays_ref, out_ref, factor_ref, bt_ref, ct_ref = refs
     step = pl.program_id(0)
 
     @pl.when(step == 0)
     def _():
         bt_ref[...] = transposed(b_ref[...])
         ct_ref[...] = transposed(c_ref[...])
-        if decays_ref is not None:
-            device_factors(decays_ref[...], pre_ref, suf_ref)
-
-    tile = x_ref.shape[1]
-    first = (place(half) * count + step) * (tile // P_SIZE)
-    before = spread(pre_ref[...], first, tile)
-    after = spread(suf_ref[...], first, tile)
+        if not made:
+            device_factors(decays_ref[...], factor_ref)
+
+    tile = x_refs[0].shape[1]
+    table = spread_table(heads, (place(half) * count + step) * (tile // P_SIZE), tile)
+    before = dot(factor_ref[:, :LANES], table)
+    after = dot(factor_ref[:, LANES:], table)
     ended = before[before.shape[0] - 1 :, :]
-    for i, (source, factor, other) in enumerate(((x_ref, after, bt_ref), (dy_ref, before, ct_ref))):
-        out_ref[i, :N, :] = dot12(other[...], halves(source[...].astype(F32) * factor))
-    out_ref[0, N:, :] = jnp.broadcast_to(ended, (EXTRA, tile))
-    out_ref[1, N:, :] = jnp.broadcast_to(ended, (EXTRA, tile))
-
-
-def totals(half, x, dy, b, c, decays=None, pre=None, suf=None):
+    for i, (sources, factor, other) in enumerate(((x_refs, after, bt_ref), (dy_refs, before, ct_ref))):
+        source = stacked(*[ref[...].astype(F32) for ref in sources])
+        out_ref[i, :N, :] = dot12(other[...], halves(source * factor))
+        out_ref[i, N:, :] = jnp.broadcast_to(ended, (EXTRA, tile))
+
+
+def totals(half, x, dy, b, c, decays=None, factors=None):
     local, width = x.shape
     count = width // 2 // TILE
     whole = lambda a: pl.BlockSpec(a.shape, lambda j: (0, 0))
-    column = pl.BlockSpec((local, TILE), lambda j: (0, place(half) * count + j))
-    factor = jax.ShapeDtypeStruct((local, LANES), F32)
-    rest = (pre, suf) if decays is None else (decays,)
+    columns = [
+        pl.BlockSpec((local // PARTS, TILE), functools.partial(lambda part, j: (part, place(half) * count + j), part))
+        for part in range(PARTS)
+    ]
+    factor = jax.ShapeDtypeStruct((local, 2 * LANES), BF16)
+    made = factors is not None
+    last = factors if made else decays
     out_specs = [pl.BlockSpec((2, N + EXTRA, TILE), lambda j: (0, 0, j))]
     out_shape = [jax.ShapeDtypeStruct((2, N + EXTRA, width // 2), F32)]
-    if decays is not None:
-        out_specs += [whole(factor), whole(factor)]
-        out_shape += [factor, factor]
+    if not made:
+        out_specs.append(whole(factor))
+        out_shape.append(factor)
     return pl.pallas_call(
-        functools.partial(totals_kernel, count, half),
+        functools.partial(totals_kernel, width // P_SIZE, count, half, made),
         grid=(count,),
-        in_specs=[column, column, whole(b), whole(c)] + [whole(a) for a in rest],
+        in_specs=columns + columns + [whole(b), whole(c), whole(last)],
         out_specs=out_specs,
         scratch_shapes=[pltpu.VMEM((N, local), BF16), pltpu.VMEM((N, local), BF16)],
         out_shape=out_shape,
-        compiler_params=FIRST,
+        compiler_params=PARAMS if made else FIRST,
         name="state_totals",
         cost_estimate=pl.CostEstimate(flops=8 * local * N * width // 2, bytes_accessed=4 * local * width, transcendentals=0),
-    )(x, dy, b, c, *rest)
+    )(*[x] * PARTS, *[dy] * PARTS, b, c, last)
 
 
 def ordered(core, mine, recv):
@@ -574,30 +595,30 @@
     )(scaled, carry, out_before, map_before)
 
 
-def input_kernel(count, part_ref, suf_ref, b_ref, own_ref, other_ref, input_ref):
+def input_kernel(heads, count, part_ref, suf_ref, b_ref, own_ref, other_ref, input_ref):
     tile = part_ref.shape[1]
     step = pl.program_id(0)
-    after = spread(suf_ref[...], step * (tile // P_SIZE), tile)
+    after = dot(suf_ref[...], spread_table(heads, step * (tile // P_SIZE), tile))
     grad = jnp.where(step // count == place(CORE), own_ref[0], other_ref[0])
     input_ref[...] = (part_ref[...] + after * dot12(b_ref[...], halves(grad))).astype(BF16)
 
 
-def input_terms(part, suf, b, own, other):
+def input_terms(part, factors, b, own, other):
     local, width = part.shape
     count = width // 2 // TILE
     whole = lambda a: pl.BlockSpec(a.shape, lambda j: (0, 0))
     column = pl.BlockSpec((local, TILE), lambda j: (0, j))
     carry = pl.BlockSpec((1, N, TILE), lambda j: (1, 0, j % count))
     return pl.pallas_call(
-        functools.partial(input_kernel, count),
+        functools.partial(input_kernel, width // P_SIZE, count),
         grid=(2 * count,),
-        in_specs=[column, whole(suf), whole(b), carry, carry],
+        in_specs=[column, pl.BlockSpec((local, LANES), lambda j: (0, 1)), whole(b), carry, carry],
         out_specs=column,
         out_shape=jax.ShapeDtypeStruct((local, width), BF16),
         compiler_params=PARAMS,
         name="input_terms",
         cost_estimate=pl.CostEstimate(flops=4 * local * N * width, bytes_accessed=8 * local * width, transcendentals=0),
-    )(part, suf, b, own, other)
+    )(part, factors, b, own, other)
 
 
 def swap_cores(v, length):
@@ -612,9 +633,9 @@
     length, ranks = lax.axis_size("seq"), lax.axis_size("head")
     chips = length // 2
     args = mixer_input, output_grad, input_map, output_map
-    sent, pre, suf = totals(OTHER, *args, decays=decays)
+    sent, factors = totals(OTHER, *args, decays=decays)
     recv = swap_cores(sent, length)
-    (mine,) = totals(CORE, *args, pre=pre, suf=suf)
+    (mine,) = totals(CORE, *args, factors=factors)
     tiles = mixer_input.shape[1] // TILE
     if chips == 4:
         ahead = tiles * 3 // 4
@@ -640,7 +661,7 @@
     own, other, shares = lax.optimization_barrier((own, other, shares))
     for r in range(1, ranks):
         total = total + turned(shares[r], "head", ranks, r)
-    input_grad = input_terms(part, suf, input_map, own, other)
+    input_grad = input_terms(part, factors, input_map, own, other)
     return input_grad, total[1], total[0]
 
 

time: 59.9 us -> 57 us (0.952)
  Pallas kernels: 37.9 us -> 35.6 us
    pallas_call x3, Pallas kernels: 16.7 us -> 14.4 us  [the longest x2 9.4 us: totals(): pl.pallas_call(functools.partial(totals_kernel, width // P_SIZE, count, h...]
    unnamed x16 -> x14, local copies, waits for them, and re-layouts: 1.41 us -> 0.97 us
  transfers between devices with their start and end apart: 10 -> 10, of which waited for: 6 -> 6; matrix products, arithmetic and copies ran while one was open for 0% -> 0% of each run, Pallas kernels for 49% -> 48%
where the time goes in v6:
time: 57 us; the launch traced here: 56.7 us
  Pallas kernels  35.6 us (62%)
  starting transfers between devices  10.3 us (18%)
  waiting for transfers between devices  8.35 us (15%)
  local copies, waits for them, and re-layouts  1.63 us (3%)
  between operations  0.77 us (1%)
    pallas_call x2, Pallas kernels, local_part(): pl.pallas_call(functools.partial(local_kernel, first_tile, before is not...  16.5 us
    pallas_call x2, Pallas kernels, totals(): pl.pallas_call(functools.partial(totals_kernel, width // P_SIZE, count, h...  9.4 us
    ppermute x3, waiting for transfers between devices, turned(): lax.ppermute(v, axis, [(i, (i + by) % length) for i in range(length)])  5.87 us
    pallas_call x1, Pallas kernels, input_terms(): pl.pallas_call(functools.partial(input_kernel, width // P_SIZE, count), g...  5.04 us
    pallas_call x2, Pallas kernels, map_terms(): pl.pallas_call(functools.partial(map_kernel, count, ranks), grid=(count,)...  3.97 us
    ppermute x3, starting transfers between devices, turned(): lax.ppermute(v, axis, [(i, (i + by) % length) for i in range(length)])  3.82 us
    ppermute x5, starting transfers between devices, crossed(): return lax.ppermute(v, 'seq', [(i, i ^ bit) for i in range(length)])  3.69 us
    ppermute x2, starting transfers between devices, swap_cores(): return lax.ppermute(v, 'seq', [(i, i ^ 1) for i in range(length)])  2.81 us
  transfers between devices with their start and end apart: 10, of which 6 were waited for; matrix products, arithmetic and copies ran while one was open for 0% of the time, Pallas kernels for 48%

profile of v6, /device:TPU:11, one launch (start us, length us, event | category | flops | bytes accessed | tf_op | source)
XLA Modules:
  0.0 56.7 jit_solution(3883168303577752)
XLA Ops:
  0.7 5.8 %state_totals.2 = (f32[2,136,1024]{2,1,0:T(8,128)}, bf16[512,256]{1,0:T(8,128)(2,1)}) custom-call(bf16[512,2048]{1,0:T(8,128)(2,1)} %refs_0_.7, bf16[512,2048]{1,0:T(8,128)(2,1)} %refs_0_.7, bf16[512,2048]{1,0:T(8,128)(2,1)} %refs_0_.7, bf16[512,2048]{1,0:T(8,128)(2,1)} %refs_0_.7, bf16[512,2048]{1,0:T(8,128)(2,1)} %refs_1_.7, bf16[512,2048]{1,0:T(8,128)(2,1)} %refs_1_.7, ...), custom_call_target="tpu_custom_call" | custom-call | flops 536870912 | bytes 4194304 | tf_op jit(solution)/shard_map/state_totals/pallas_call | solution.py:160
  6.4 0.7 %collective-permute-start = (f32[2,136,1024]{2,1,0:T(8,128)}, f32[2,136,1024]{2,1,0:T(8,128)S(1)}, u32[]{:S(2)}, u32[]{:S(2)}) collective-permute-start(f32[2,136,1024]{2,1,0:T(8,128)} %get-tuple-element.53), channel_id=1, source_target_pairs={{0,4},{4,0},{8,12},{12,8},{16,20},{20,16},{24,28},{28,24},{1,5},{5... | collective-permute-start | bytes 3342344 | tf_op jit(solution)/shard_map/ppermute | solution.py:625
  7.1 0.9 %copy-done.4 = bf16[512,256]{1,0:T(8,128)(2,1)S(1)} copy-done((bf16[512,256]{1,0:T(8,128)(2,1)S(1)}, bf16[512,256]{1,0:T(8,128)(2,1)}, u32[]{:S(2)}) %copy-start.4) | copy-done | bytes 262168
  8.1 3.6 %state_totals.3.mine_ref = f32[2,136,1024]{2,1,0:T(8,128)S(1)} custom-call(bf16[512,2048]{1,0:T(8,128)(2,1)S(1)} %copy-done, bf16[512,2048]{1,0:T(8,128)(2,1)S(1)} %copy-done, bf16[512,2048]{1,0:T(8,128)(2,1)S(1)} %copy-done, bf16[512,2048]{1,0:T(8,128)(2,1)S(1)} %copy-done, bf16[512,2048]{1,0:T(8,128)(2,1)S(1)} %copy-done.1, ...), custom_call_target="tpu_custom_call" | custom-call | flops 536870912 | bytes 4194304 | tf_op jit(solution)/shard_map/state_totals/pallas_call | solution.py:160
  12.0 0.3 collective-permute-start.1
  12.3 2.2 %collective-permute-start.3 = (f32[8,512]{1,0:T(8,128)S(1)}, f32[8,512]{1,0:T(8,128)S(1)}, u32[]{:S(2)}, u32[]{:S(2)}) collective-permute-start(f32[8,512]{1,0:T(8,128)S(1)} %get-tuple-element.56), channel_id=1, source_target_pairs={{0,24},{4,28},{8,16},{12,20},{16,8},{20,12},{24,0},{28,4},{1,25},{... | collective-permute-start | bytes 49160 | tf_op jit(solution)/shard_map/ppermute | solution.py:258
  14.7 11.6 %local_part.2 = (f32[512,2048]{1,0:T(8,128)S(1)}, bf16[2,2,512,2048]{3,2,1,0:T(8,128)(2,1)S(1)}, f32[512,128]{1,0:T(8,128)S(1)}, f32[512,128]{1,0:T(8,128)S(1)}) custom-call(bf16[512,2048]{1,0:T(8,128)(2,1)S(1)} %copy-done, bf16[512,2048]{1,0:T(8,128)(2,1)S(1)} %copy-done.1, bf16[512,128]{1,0:T(8,128)(2,1)S(1)} %copy-done.2, bf16[512,128]{1,0:T(8,128)(2,1)S(1)} %copy-done.3, ...), custom_call_target="tpu_custom_call" | custom-call | flops 4026531840 | bytes 6291456 | tf_op jit(solution)/shard_map/local_part/pallas_call | solution.py:523
  26.3 0.6 %collective-permute-done.3.decay_ref = f32[8,512]{1,0:T(8,128)S(1)} collective-permute-done((f32[8,512]{1,0:T(8,128)S(1)}, f32[8,512]{1,0:T(8,128)S(1)}, u32[]{:S(2)}, u32[]{:S(2)}) %collective-permute-start.3) | collective-permute-done | bytes 16416 | tf_op jit(solution)/shard_map/ppermute | solution.py:258
  27.1 0.7 %collective-permute-start.4 = (f32[128,512]{1,0:T(8,128)S(1)}, f32[128,512]{1,0:T(8,128)S(1)}, u32[]{:S(2)}, u32[]{:S(2)}) collective-permute-start(f32[128,512]{1,0:T(8,128)S(1)} %get-tuple-element.65), channel_id=1, source_target_pairs={{0,16},{4,20},{8,24},{12,28},{16,0},{20,4},{24,8},{28,12},{1,17},{... | collective-permute-start | bytes 786440 | tf_op jit(solution)/shard_map/ppermute | solution.py:258
  28.0 4.9 %local_part.3 = (f32[512,2048]{1,0:T(8,128)S(1)}, bf16[2,2,512,2048]{3,2,1,0:T(8,128)(2,1)S(1)}, f32[512,128]{1,0:T(8,128)S(1)}, f32[512,128]{1,0:T(8,128)S(1)}) custom-call(bf16[512,2048]{1,0:T(8,128)(2,1)S(1)} %copy-done, bf16[512,2048]{1,0:T(8,128)(2,1)S(1)} %copy-done.1, ...), custom_call_target="tpu_custom_call", output_to_operand_aliasing={{0}: (7, {}), {1}: (8, {})} | custom-call | flops 1342177280 | bytes 2097152 | tf_op jit(solution)/shard_map/local_part/pallas_call | solution.py:523
  32.9 0.9 %collective-permute-done.4.cross2_ref = f32[128,512]{1,0:T(8,128)S(1)} collective-permute-done((f32[128,512]{1,0:T(8,128)S(1)}, f32[128,512]{1,0:T(8,128)S(1)}, u32[]{:S(2)}, u32[]{:S(2)}) %collective-permute-start.4) | collective-permute-done | bytes 262176 | tf_op jit(solution)/shard_map/ppermute | solution.py:258
  33.8 0.6 %collective-permute-done.5.same2_ref = f32[128,512]{1,0:T(8,128)S(1)} collective-permute-done((f32[128,512]{1,0:T(8,128)S(1)}, f32[128,512]{1,0:T(8,128)S(1)}, u32[]{:S(2)}, u32[]{:S(2)}) %collective-permute-start.5) | collective-permute-done | bytes 262176 | tf_op jit(solution)/shard_map/ppermute | solution.py:258
  34.4 0.4 carried_in.1
  34.8 2.1 %collective-permute-start.6 = (f32[2,128,1024]{2,1,0:T(8,128)S(1)}, f32[2,128,1024]{2,1,0:T(8,128)S(1)}, u32[]{:S(2)}, u32[]{:S(2)}) collective-permute-start(f32[2,128,1024]{2,1,0:T(8,128)S(1)} %get-tuple-element.86), channel_id=1, source_target_pairs={{0,4},{4,0},{8,12},{12,8},{16,20},{20,16},{24,28},{28,24},{1,5},{5... | collective-permute-start | bytes 3145736 | tf_op jit(solution)/shard_map/ppermute | solution.py:625
  36.9 2.0 %map_terms.2 = (f32[512,128]{1,0:T(8,128)S(1)}, f32[512,128]{1,0:T(8,128)S(1)}) custom-call(bf16[2,2,512,2048]{3,2,1,0:T(8,128)(2,1)S(1)} %get-tuple-element.87.scaled_ref, f32[2,128,1024]{2,1,0:T(8,128)S(1)} %get-tuple-element.96.carry_ref.own_ref, f32[512,128]{1,0:T(8,128)S(1)} %get-tuple-element.88.out_before_ref, ...), custom_call_target="tpu_custom_call" | custom-call | flops 805306368 | bytes 4194304 | tf_op jit(solution)/shard_map/map_terms/pallas_call | solution.py:580
  38.9 0.3 collective-permute-done.6.carry_ref.other_ref
  39.2 2.0 %map_terms.3 = (f32[2,128,128]{2,1,0:T(8,128)S(1)}, f32[2,128,128]{2,1,0:T(8,128)S(1)}, f32[2,128,128]{2,1,0:T(8,128)S(1)}, f32[2,128,128]{2,1,0:T(8,128)S(1)}) custom-call(bf16[2,2,512,2048]{3,2,1,0:T(8,128)(2,1)S(1)} %get-tuple-element.87.scaled_ref, f32[2,128,1024]{2,1,0:T(8,128)S(1)} %collective-permute-done.6.carry_ref.other_ref, ...), custom_call_target="tpu_custom_call" | custom-call | flops 805306368 | bytes 4194304 | tf_op jit(solution)/shard_map/map_terms/pallas_call | solution.py:580
  41.2 1.3 %collective-permute-start.7 = (f32[2,128,128]{2,1,0:T(8,128)S(1)}, f32[2,128,128]{2,1,0:T(8,128)S(1)}, u32[]{:S(2)}, u32[]{:S(2)}) collective-permute-start(f32[2,128,128]{2,1,0:T(8,128)S(1)} %get-tuple-element.98), channel_id=1, source_target_pairs={{0,1},{1,2},{2,3},{3,0},{4,5},{5,6},{6,7},{7,4},{8,9},{9,10},{10,1... | collective-permute-start | bytes 393224 | tf_op jit(solution)/shard_map/ppermute | solution.py:629
  42.6 1.1 %collective-permute-start.8 = (f32[2,128,128]{2,1,0:T(8,128)S(1)}, f32[2,128,128]{2,1,0:T(8,128)S(1)}, u32[]{:S(2)}, u32[]{:S(2)}) collective-permute-start(f32[2,128,128]{2,1,0:T(8,128)S(1)} %get-tuple-element.99), channel_id=1, source_target_pairs={{0,2},{1,3},{2,0},{3,1},{4,6},{5,7},{6,4},{7,5},{8,10},{9,11},{10,... | collective-permute-start | bytes 393224 | tf_op jit(solution)/shard_map/ppermute | solution.py:629
  43.7 1.4 %collective-permute-start.9 = (f32[2,128,128]{2,1,0:T(8,128)S(1)}, f32[2,128,128]{2,1,0:T(8,128)S(1)}, u32[]{:S(2)}, u32[]{:S(2)}) collective-permute-start(f32[2,128,128]{2,1,0:T(8,128)S(1)} %get-tuple-element.100), channel_id=1, source_target_pairs={{0,3},{1,0},{2,1},{3,2},{4,7},{5,4},{6,5},{7,6},{8,11},{9,8},{10,9... | collective-permute-start | bytes 393224 | tf_op jit(solution)/shard_map/ppermute | solution.py:629
  45.1 5.0 %input_terms.1 = bf16[512,2048]{1,0:T(8,128)(2,1)} custom-call(f32[512,2048]{1,0:T(8,128)S(1)} %get-tuple-element.79.part_ref, bf16[512,256]{1,0:T(8,128)(2,1)S(1)} %copy-done.5, bf16[512,128]{1,0:T(8,128)(2,1)S(1)} %copy-done.2, f32[2,128,1024]{2,1,0:T(8,128)S(1)} %get-tuple-element.96.carry_ref.own_ref, ...), custom_call_target="tpu_custom_call" | custom-call | flops 536870912 | bytes 8388608 | tf_op jit(solution)/shard_map/input_terms/pallas_call | solution.py:612
  50.1 3.4 %collective-permute-done.8 = f32[2,128,128]{2,1,0:T(8,128)S(1)} collective-permute-done((f32[2,128,128]{2,1,0:T(8,128)S(1)}, f32[2,128,128]{2,1,0:T(8,128)S(1)}, u32[]{:S(2)}, u32[]{:S(2)}) %collective-permute-start.8) | collective-permute-done | bytes 131104 | tf_op jit(solution)/shard_map/ppermute | solution.py:629
  53.5 2.5 %collective-permute-done.9 = f32[2,128,128]{2,1,0:T(8,128)S(1)} collective-permute-done((f32[2,128,128]{2,1,0:T(8,128)S(1)}, f32[2,128,128]{2,1,0:T(8,128)S(1)}, u32[]{:S(2)}, u32[]{:S(2)}) %collective-permute-start.9) | collective-permute-done | bytes 131104 | tf_op jit(solution)/shard_map/ppermute | solution.py:629
  56.0 0.7 %slice_bitcast_fusion = (f32[128,128]{1,0:T(8,128)}, f32[128,128]{1,0:T(8,128)}) fusion(f32[2,128,128]{2,1,0:T(8,128)S(1)} %add_add_fusion), kind=kLoop, calls=%fused_computation.1 | loop fusion | bytes 262144 | tf_op jit(solution)/shard_map/squeeze | solution.py:665
  (22 shorter events, 0.8 us)
Async XLA Ops:
  0.6 6.5 %copy-start.2 = (bf16[512,128]{1,0:T(8,128)(2,1)S(1)}, bf16[512,128]{1,0:T(8,128)(2,1)}, u32[]{:S(2)}) copy-start(bf16[512,128]{1,0:T(8,128)(2,1)} %b_ref.1) | copy-start | bytes 393220
  0.6 6.5 %copy-start.3 = (bf16[512,128]{1,0:T(8,128)(2,1)S(1)}, bf16[512,128]{1,0:T(8,128)(2,1)}, u32[]{:S(2)}) copy-start(bf16[512,128]{1,0:T(8,128)(2,1)} %refs_3_.7) | copy-start | bytes 393220
  0.7 6.5 %copy-start.1 = (bf16[512,2048]{1,0:T(8,128)(2,1)S(1)}, bf16[512,2048]{1,0:T(8,128)(2,1)}, u32[]{:S(2)}) copy-start(bf16[512,2048]{1,0:T(8,128)(2,1)} %refs_1_.7) | copy-start | bytes 6291460
  0.7 6.4 %copy-start = (bf16[512,2048]{1,0:T(8,128)(2,1)S(1)}, bf16[512,2048]{1,0:T(8,128)(2,1)}, u32[]{:S(2)}) copy-start(bf16[512,2048]{1,0:T(8,128)(2,1)} %refs_0_.7) | copy-start | bytes 6291460
  6.4 5.3 %collective-permute-start = (f32[2,136,1024]{2,1,0:T(8,128)}, f32[2,136,1024]{2,1,0:T(8,128)S(1)}, u32[]{:S(2)}, u32[]{:S(2)}) collective-permute-start(f32[2,136,1024]{2,1,0:T(8,128)} %get-tuple-element.53), channel_id=1, source_target_pairs={{0,4},{4,0},{8,12},{12,8},{16,20},{20,16},{24,28},{28,24},{1,5},{5... | collective-permute-start | bytes 3342344 | tf_op jit(solution)/shard_map/ppermute | solution.py:625
  7.1 1.0 %copy-start.4 = (bf16[512,256]{1,0:T(8,128)(2,1)S(1)}, bf16[512,256]{1,0:T(8,128)(2,1)}, u32[]{:S(2)}) copy-start(bf16[512,256]{1,0:T(8,128)(2,1)} %get-tuple-element.52.refs_10_.suf_ref) | copy-start | bytes 786436
  11.7 3.0 %copy-start.6 = (f32[32,512]{1,0:T(8,128)S(1)}, f32[32,512]{1,0:T(8,128)}, u32[]{:S(2)}) copy-start(f32[32,512]{1,0:T(8,128)} %refs_4_.7) | copy-start | bytes 196612
  12.0 15.0 %collective-permute-start.1 = (f32[264,512]{1,0:T(8,128)S(1)}, f32[264,512]{1,0:T(8,128)S(1)}, u32[]{:S(2)}, u32[]{:S(2)}) collective-permute-start(f32[264,512]{1,0:T(8,128)S(1)} %get-tuple-element.54.own_ref), channel_id=1, source_target_pairs={{0,8},{4,12},{8,0},{12,4},{16,24},{20,28},{24,16},{28,20},{1,9},{5... | collective-permute-start | bytes 1622024 | tf_op jit(solution)/shard_map/ppermute | solution.py:258
  12.3 14.6 %collective-permute-start.3 = (f32[8,512]{1,0:T(8,128)S(1)}, f32[8,512]{1,0:T(8,128)S(1)}, u32[]{:S(2)}, u32[]{:S(2)}) collective-permute-start(f32[8,512]{1,0:T(8,128)S(1)} %get-tuple-element.56), channel_id=1, source_target_pairs={{0,24},{4,28},{8,16},{12,20},{16,8},{20,12},{24,0},{28,4},{1,25},{... | collective-permute-start | bytes 49160 | tf_op jit(solution)/shard_map/ppermute | solution.py:258
  14.5 12.5 %collective-permute-start.2 = (f32[128,512]{1,0:T(8,128)S(1)}, f32[128,512]{1,0:T(8,128)S(1)}, u32[]{:S(2)}, u32[]{:S(2)}) collective-permute-start(f32[128,512]{1,0:T(8,128)S(1)} %get-tuple-element.55), channel_id=1, source_target_pairs={{0,16},{4,20},{8,24},{12,28},{16,0},{20,4},{24,8},{28,12},{1,17},{... | collective-permute-start | bytes 786440 | tf_op jit(solution)/shard_map/ppermute | solution.py:258
  27.1 6.8 %collective-permute-start.4 = (f32[128,512]{1,0:T(8,128)S(1)}, f32[128,512]{1,0:T(8,128)S(1)}, u32[]{:S(2)}, u32[]{:S(2)}) collective-permute-start(f32[128,512]{1,0:T(8,128)S(1)} %get-tuple-element.65), channel_id=1, source_target_pairs={{0,16},{4,20},{8,24},{12,28},{16,0},{20,4},{24,8},{28,12},{1,17},{... | collective-permute-start | bytes 786440 | tf_op jit(solution)/shard_map/ppermute | solution.py:258
  27.8 6.7 %collective-permute-start.5 = (f32[128,512]{1,0:T(8,128)S(1)}, f32[128,512]{1,0:T(8,128)S(1)}, u32[]{:S(2)}, u32[]{:S(2)}) collective-permute-start(f32[128,512]{1,0:T(8,128)S(1)} %get-tuple-element.66), channel_id=1, source_target_pairs={{0,8},{4,12},{8,0},{12,4},{16,24},{20,28},{24,16},{28,20},{1,9},{5... | collective-permute-start | bytes 786440 | tf_op jit(solution)/shard_map/ppermute | solution.py:258
  34.8 4.4 %collective-permute-start.6 = (f32[2,128,1024]{2,1,0:T(8,128)S(1)}, f32[2,128,1024]{2,1,0:T(8,128)S(1)}, u32[]{:S(2)}, u32[]{:S(2)}) collective-permute-start(f32[2,128,1024]{2,1,0:T(8,128)S(1)} %get-tuple-element.86), channel_id=1, source_target_pairs={{0,4},{4,0},{8,12},{12,8},{16,20},{20,16},{24,28},{28,24},{1,5},{5... | collective-permute-start | bytes 3145736 | tf_op jit(solution)/shard_map/ppermute | solution.py:625
  39.2 5.8 %copy-start.5 = (bf16[512,256]{1,0:T(8,128)(2,1)S(1)}, bf16[512,256]{1,0:T(8,128)(2,1)}, u32[]{:S(2)}) copy-start(bf16[512,256]{1,0:T(8,128)(2,1)} %get-tuple-element.52.refs_10_.suf_ref) | copy-start | bytes 786436
  41.2 8.9 %collective-permute-start.7 = (f32[2,128,128]{2,1,0:T(8,128)S(1)}, f32[2,128,128]{2,1,0:T(8,128)S(1)}, u32[]{:S(2)}, u32[]{:S(2)}) collective-permute-start(f32[2,128,128]{2,1,0:T(8,128)S(1)} %get-tuple-element.98), channel_id=1, source_target_pairs={{0,1},{1,2},{2,3},{3,0},{4,5},{5,6},{6,7},{7,4},{8,9},{9,10},{10,1... | collective-permute-start | bytes 393224 | tf_op jit(solution)/shard_map/ppermute | solution.py:629
  42.6 10.9 %collective-permute-start.8 = (f32[2,128,128]{2,1,0:T(8,128)S(1)}, f32[2,128,128]{2,1,0:T(8,128)S(1)}, u32[]{:S(2)}, u32[]{:S(2)}) collective-permute-start(f32[2,128,128]{2,1,0:T(8,128)S(1)} %get-tuple-element.99), channel_id=1, source_target_pairs={{0,2},{1,3},{2,0},{3,1},{4,6},{5,7},{6,4},{7,5},{8,10},{9,11},{10,... | collective-permute-start | bytes 393224 | tf_op jit(solution)/shard_map/ppermute | solution.py:629
  43.7 12.3 %collective-permute-start.9 = (f32[2,128,128]{2,1,0:T(8,128)S(1)}, f32[2,128,128]{2,1,0:T(8,128)S(1)}, u32[]{:S(2)}, u32[]{:S(2)}) collective-permute-start(f32[2,128,128]{2,1,0:T(8,128)S(1)} %get-tuple-element.100), channel_id=1, source_target_pairs={{0,3},{1,0},{2,1},{3,2},{4,7},{5,4},{6,5},{7,6},{8,11},{9,8},{10,9... | collective-permute-start | bytes 393224 | tf_op jit(solution)/shard_map/ppermute | solution.py:629

commit v7 on v6

--- a/solution.py
+++ b/solution.py
@@ -11,12 +11,13 @@
 N = 128
 SUB = 64
 TILE = 256
+WIDE = 512
 EXTRA = 8
 PARTS = 4
 LANES = 128
 CORE, OTHER = range(2)
 PARAMS = pltpu.CompilerParams(vmem_limit_bytes=24 * 1024 * 1024)
-FIRST = pltpu.CompilerParams(vmem_limit_bytes=56 * 1024 * 1024)
+FIRST = pltpu.CompilerParams(vmem_limit_bytes=52 * 1024 * 1024)
 F32 = jnp.float32
 BF16 = jnp.bfloat16
 
@@ -496,16 +497,16 @@
     local, width = x.shape
     chunks = local // SUB
     whole = lambda a: pl.BlockSpec(a.shape, lambda j: (0, 0))
-    column = pl.BlockSpec((local, TILE), lambda j: (0, first_tile + j))
+    column = pl.BlockSpec((local, WIDE), lambda j: (0, first_tile + j))
     tokens = pl.BlockSpec((local, N), lambda j: (0, 0))
     scratch = [
         pltpu.VMEM((local, LANES), F32),
         pltpu.VMEM((local, LANES), F32),
         pltpu.VMEM((-(-len(list(row_bounds(chunks))) // 8) * 8, LANES), F32),
         pltpu.VMEM((local, local), F32),
-        pltpu.VMEM((local, TILE), F32),
-        pltpu.VMEM((local, TILE), F32),
-        pltpu.VMEM((local, TILE), F32),
+        pltpu.VMEM((local, WIDE), F32),
+        pltpu.VMEM((local, WIDE), F32),
+        pltpu.VMEM((local, WIDE), F32),
         pltpu.VMEM((local, 2 * SUB), F32),
         pltpu.VMEM((local // 2, 3 * SUB), BF16),
         pltpu.VMEM((local, 3 * SUB), BF16),
@@ -524,7 +525,7 @@
         functools.partial(local_kernel, first_tile, before is not None),
         grid=(count,),
         in_specs=in_specs,
-        out_specs=(column, pl.BlockSpec((2, 2, local, TILE), lambda j: (0, 0, 0, first_tile + j)), tokens, tokens),
+        out_specs=(column, pl.BlockSpec((2, 2, local, WIDE), lambda j: (0, 0, 0, first_tile + j)), tokens, tokens),
         out_shape=(
             jax.ShapeDtypeStruct((local, width), F32),
             jax.ShapeDtypeStruct((2, 2, local, width), BF16),
@@ -536,7 +537,7 @@
         compiler_params=PARAMS,
         name="local_part",
         cost_estimate=pl.CostEstimate(
-            flops=40 * local * N * TILE * count, bytes_accessed=8 * local * TILE * count, transcendentals=0
+            flops=40 * local * N * WIDE * count, bytes_accessed=8 * local * WIDE * count, transcendentals=0
         ),
     )(*args)
 
@@ -568,7 +569,7 @@
 
 def map_terms(half, scaled, carry, out_before, map_before, ranks=0):
     local, width = scaled.shape[2], carry.shape[2]
-    tile = min(512, width)
+    tile = min(WIDE, width)
     count = width // tile
     whole = lambda a: pl.BlockSpec(a.shape, lambda j: (0,) * len(a.shape))
     tokens = jax.ShapeDtypeStruct((local, N), F32)
@@ -605,10 +606,10 @@
 
 def input_terms(part, factors, b, own, other):
     local, width = part.shape
-    count = width // 2 // TILE
+    count = width // 2 // WIDE
     whole = lambda a: pl.BlockSpec(a.shape, lambda j: (0, 0))
-    column = pl.BlockSpec((local, TILE), lambda j: (0, j))
-    carry = pl.BlockSpec((1, N, TILE), lambda j: (1, 0, j % count))
+    column = pl.BlockSpec((local, WIDE), lambda j: (0, j))
+    carry = pl.BlockSpec((1, N, WIDE), lambda j: (1, 0, j % count))
     return pl.pallas_call(
         functools.partial(input_kernel, width // P_SIZE, count),
         grid=(2 * count,),
@@ -621,6 +622,12 @@
     )(part, factors, b, own, other)
 
 
+def sums_kernel(*refs):
+    shares, (map_ref, out_ref) = refs[:-2], refs[-2:]
+    for i, ref in enumerate((out_ref, map_ref)):
+        ref[...] = functools.reduce(lambda a, b: a + b, [share[i] for share in shares])
+
+
 def swap_cores(v, length):
     return lax.ppermute(v, "seq", [(i, i ^ 1) for i in range(length)])
 
@@ -636,7 +643,7 @@
     sent, factors = totals(OTHER, *args, decays=decays)
     recv = swap_cores(sent, length)
     (mine,) = totals(CORE, *args, factors=factors)
-    tiles = mixer_input.shape[1] // TILE
+    tiles = mixer_input.shape[1] // WIDE
     if chips == 4:
         ahead = tiles * 3 // 4
         own, back, *others = first_phase(length, mine, recv)
@@ -657,12 +664,12 @@
     other = swap_cores(peer, length)
     out_part, map_part = map_terms(CORE, scaled, own, out_part, map_part)
     shares = map_terms(OTHER, scaled, other, out_part, map_part, ranks)
-    total = shares[0]
     own, other, shares = lax.optimization_barrier((own, other, shares))
-    for r in range(1, ranks):
-        total = total + turned(shares[r], "head", ranks, r)
+    sums = [shares[0]] + [turned(shares[r], "head", ranks, r) for r in range(1, ranks)]
     input_grad = input_terms(part, factors, input_map, own, other)
-    return input_grad, total[1], total[0]
+    shape = jax.ShapeDtypeStruct(shares[0].shape[1:], F32)
+    input_map_grad, output_map_grad = plain_call(sums_kernel, "head_sums", [shape, shape], *sums)
+    return input_grad, input_map_grad, output_map_grad
 
 
 def solution(mesh):

time: 57 us -> 57.6 us (1.011)
  Pallas kernels: 35.6 us -> 31.9 us
  waiting for transfers between devices: 8.35 us -> 11.3 us
  local copies, waits for them, and re-layouts: 1.63 us -> 3.07 us
    unnamed x14 -> x16, local copies, waits for them, and re-layouts: 0.97 us -> 3.07 us
    pallas_call x2, Pallas kernels: 16.5 us -> 14.6 us  [local_part(): pl.pallas_call(functools.partial(local_kernel, first_tile, before is not...]
    ppermute x5, waiting for transfers between devices: 2.15 us -> 3.75 us  [crossed(): return lax.ppermute(v, 'seq', [(i, i ^ bit) for i in range(length)])]
    ppermute x3, waiting for transfers between devices: 5.87 us -> 7.24 us  [turned(): lax.ppermute(v, axis, [(i, (i + by) % length) for i in range(length)])]
    pallas_call x1, Pallas kernels: 5.04 us -> 3.68 us  [input_terms(): pl.pallas_call(functools.partial(input_kernel, width // P_SIZE, count), g...]
    pallas_call x2, Pallas kernels: 9.4 us -> 8.34 us  [totals(): pl.pallas_call(functools.partial(totals_kernel, width // P_SIZE, count, h...]
    pallas_call x3 -> x4, Pallas kernels: 0.67 us -> 1.35 us  [plain_call(): pl.pallas_call(kernel, grid=(1,), in_specs=[whole(a) for a in args], out_...]
    squeeze x1 -> x0, local copies, waits for them, and re-layouts: 0.66 us -> none  [per_device(): return (input_grad, total[1], total[0])]
  transfers between devices with their start and end apart: 10 -> 10, of which waited for: 6 -> 5; matrix products, arithmetic and copies ran while one was open for 0% -> 0% of each run, Pallas kernels for 48% -> 42%
where the time goes in v7:
time: 57.6 us; the launch traced here: 57.3 us
  Pallas kernels  31.9 us (55%)
  waiting for transfers between devices  11.3 us (20%)
  starting transfers between devices  10.2 us (18%)
  local copies, waits for them, and re-layouts  3.07 us (5%)
  between operations  0.77 us (1%)
    pallas_call x2, Pallas kernels, local_part(): pl.pallas_call(functools.partial(local_kernel, first_tile, before is not...  14.6 us
    pallas_call x2, Pallas kernels, totals(): pl.pallas_call(functools.partial(totals_kernel, width // P_SIZE, count, h...  8.34 us
    ppermute x3, waiting for transfers between devices, turned(): lax.ppermute(v, axis, [(i, (i + by) % length) for i in range(length)])  7.24 us
    pallas_call x2, Pallas kernels, map_terms(): pl.pallas_call(functools.partial(map_kernel, count, ranks), grid=(count,)...  3.97 us
    ppermute x3, starting transfers between devices, turned(): lax.ppermute(v, axis, [(i, (i + by) % length) for i in range(length)])  3.81 us
    ppermute x5, waiting for transfers between devices, crossed(): return lax.ppermute(v, 'seq', [(i, i ^ bit) for i in range(length)])  3.75 us
    pallas_call x1, Pallas kernels, input_terms(): pl.pallas_call(functools.partial(input_kernel, width // P_SIZE, count), g...  3.68 us
    ppermute x5, starting transfers between devices, crossed(): return lax.ppermute(v, 'seq', [(i, i ^ bit) for i in range(length)])  3.26 us
  transfers between devices with their start and end apart: 10, of which 5 were waited for; matrix products, arithmetic and copies ran while one was open for 0% of the time, Pallas kernels for 42%

profile of v7, /device:TPU:11, one launch (start us, length us, event | category | flops | bytes accessed | tf_op | source)
XLA Modules:
  0.0 57.3 jit_solution(9028154603365591415)
XLA Ops:
  0.7 1.0 %copy-done.2 = bf16[512,128]{1,0:T(8,128)(2,1)S(1)} copy-done((bf16[512,128]{1,0:T(8,128)(2,1)S(1)}, bf16[512,128]{1,0:T(8,128)(2,1)}, u32[]{:S(2)}) %copy-start.2) | copy-done | bytes 131096
  1.7 1.1 %copy-done.4 = bf16[512,128]{1,0:T(8,128)(2,1)S(1)} copy-done((bf16[512,128]{1,0:T(8,128)(2,1)S(1)}, bf16[512,128]{1,0:T(8,128)(2,1)}, u32[]{:S(2)}) %copy-start.4) | copy-done | bytes 131096
  2.9 0.8 %copy-done.6 = f32[32,512]{1,0:T(8,128)S(1)} copy-done((f32[32,512]{1,0:T(8,128)S(1)}, f32[32,512]{1,0:T(8,128)}, u32[]{:S(2)}) %copy-start.6) | copy-done | bytes 65560
  3.7 4.7 %state_totals.2 = (f32[2,136,1024]{2,1,0:T(8,128)S(1)}, bf16[512,256]{1,0:T(8,128)(2,1)S(1)}) custom-call(bf16[512,2048]{1,0:T(8,128)(2,1)} %refs_0_.7, bf16[512,2048]{1,0:T(8,128)(2,1)} %refs_0_.7, bf16[512,2048]{1,0:T(8,128)(2,1)} %refs_0_.7, bf16[512,2048]{1,0:T(8,128)(2,1)} %refs_0_.7, bf16[512,2048]{1,0:T(8,128)(2,1)} %refs_1_.7, ...), custom_call_target="tpu_custom_call" | custom-call | flops 536870912 | bytes 4194304 | tf_op jit(solution)/shard_map/state_totals/pallas_call | solution.py:161
  8.4 0.7 %collective-permute-start = (f32[2,136,1024]{2,1,0:T(8,128)S(1)}, f32[2,136,1024]{2,1,0:T(8,128)S(1)}, u32[]{:S(2)}, u32[]{:S(2)}) collective-permute-start(f32[2,136,1024]{2,1,0:T(8,128)S(1)} %get-tuple-element.56), channel_id=1, source_target_pairs={{0,4},{4,0},{8,12},{12,8},{16,20},{20,16},{24,28},{28,24},{1,5},{5... | collective-permute-start | bytes 3342344 | tf_op jit(solution)/shard_map/ppermute | solution.py:632
  9.1 3.7 %state_totals.3.mine_ref = f32[2,136,1024]{2,1,0:T(8,128)S(1)} custom-call(bf16[512,2048]{1,0:T(8,128)(2,1)S(1)} %copy-done, bf16[512,2048]{1,0:T(8,128)(2,1)S(1)} %copy-done, bf16[512,2048]{1,0:T(8,128)(2,1)S(1)} %copy-done, bf16[512,2048]{1,0:T(8,128)(2,1)S(1)} %copy-done, bf16[512,2048]{1,0:T(8,128)(2,1)S(1)} %copy-done.1, ...), custom_call_target="tpu_custom_call" | custom-call | flops 536870912 | bytes 4194304 | tf_op jit(solution)/shard_map/state_totals/pallas_call | solution.py:161
  13.1 0.3 collective-permute-start.1
  13.4 2.2 %collective-permute-start.3 = (f32[8,512]{1,0:T(8,128)S(1)}, f32[8,512]{1,0:T(8,128)S(1)}, u32[]{:S(2)}, u32[]{:S(2)}) collective-permute-start(f32[8,512]{1,0:T(8,128)S(1)} %get-tuple-element.59), channel_id=1, source_target_pairs={{0,24},{4,28},{8,16},{12,20},{16,8},{20,12},{24,0},{28,4},{1,25},{... | collective-permute-start | bytes 49160 | tf_op jit(solution)/shard_map/ppermute | solution.py:259
  15.8 10.3 %local_part.2 = (f32[512,2048]{1,0:T(8,128)S(1)}, bf16[2,2,512,2048]{3,2,1,0:T(8,128)(2,1)S(1)}, f32[512,128]{1,0:T(8,128)S(1)}, f32[512,128]{1,0:T(8,128)S(1)}) custom-call(bf16[512,2048]{1,0:T(8,128)(2,1)S(1)} %copy-done, bf16[512,2048]{1,0:T(8,128)(2,1)S(1)} %copy-done.1, bf16[512,128]{1,0:T(8,128)(2,1)S(1)} %copy-done.3, bf16[512,128]{1,0:T(8,128)(2,1)S(1)} %copy-done.5, ...), custom_call_target="tpu_custom_call" | custom-call | flops 4026531840 | bytes 6291456 | tf_op jit(solution)/shard_map/local_part/pallas_call | solution.py:524
  26.2 1.8 %collective-permute-done.3.decay_ref = f32[8,512]{1,0:T(8,128)S(1)} collective-permute-done((f32[8,512]{1,0:T(8,128)S(1)}, f32[8,512]{1,0:T(8,128)S(1)}, u32[]{:S(2)}, u32[]{:S(2)}) %collective-permute-start.3) | collective-permute-done | bytes 16416 | tf_op jit(solution)/shard_map/ppermute | solution.py:259
  28.6 4.2 %local_part.3 = (f32[512,2048]{1,0:T(8,128)S(1)}, bf16[2,2,512,2048]{3,2,1,0:T(8,128)(2,1)S(1)}, f32[512,128]{1,0:T(8,128)S(1)}, f32[512,128]{1,0:T(8,128)S(1)}) custom-call(bf16[512,2048]{1,0:T(8,128)(2,1)S(1)} %copy-done, bf16[512,2048]{1,0:T(8,128)(2,1)S(1)} %copy-done.1, ...), custom_call_target="tpu_custom_call", output_to_operand_aliasing={{0}: (7, {}), {1}: (8, {})} | custom-call | flops 1342177280 | bytes 2097152 | tf_op jit(solution)/shard_map/local_part/pallas_call | solution.py:524
  32.9 1.9 %collective-permute-done.4.cross2_ref = f32[128,512]{1,0:T(8,128)S(1)} collective-permute-done((f32[128,512]{1,0:T(8,128)S(1)}, f32[128,512]{1,0:T(8,128)S(1)}, u32[]{:S(2)}, u32[]{:S(2)}) %collective-permute-start.4) | collective-permute-done | bytes 262176 | tf_op jit(solution)/shard_map/ppermute | solution.py:259
  34.8 0.4 carried_in.1
  35.2 2.4 %collective-permute-start.6 = (f32[2,128,1024]{2,1,0:T(8,128)S(1)}, f32[2,128,1024]{2,1,0:T(8,128)S(1)}, u32[]{:S(2)}, u32[]{:S(2)}) collective-permute-start(f32[2,128,1024]{2,1,0:T(8,128)S(1)} %get-tuple-element.89), channel_id=1, source_target_pairs={{0,4},{4,0},{8,12},{12,8},{16,20},{20,16},{24,28},{28,24},{1,5},{5... | collective-permute-start | bytes 3145736 | tf_op jit(solution)/shard_map/ppermute | solution.py:632
  37.5 2.0 %map_terms.2 = (f32[512,128]{1,0:T(8,128)S(1)}, f32[512,128]{1,0:T(8,128)S(1)}) custom-call(bf16[2,2,512,2048]{3,2,1,0:T(8,128)(2,1)S(1)} %get-tuple-element.90.scaled_ref, f32[2,128,1024]{2,1,0:T(8,128)S(1)} %get-tuple-element.99.carry_ref.own_ref, f32[512,128]{1,0:T(8,128)S(1)} %get-tuple-element.91.out_before_ref, ...), custom_call_target="tpu_custom_call" | custom-call | flops 805306368 | bytes 4194304 | tf_op jit(solution)/shard_map/map_terms/pallas_call | solution.py:581
  39.5 0.3 collective-permute-done.6.carry_ref.other_ref
  39.8 2.0 %map_terms.3 = (f32[2,128,128]{2,1,0:T(8,128)S(1)}, f32[2,128,128]{2,1,0:T(8,128)S(1)}, f32[2,128,128]{2,1,0:T(8,128)S(1)}, f32[2,128,128]{2,1,0:T(8,128)S(1)}) custom-call(bf16[2,2,512,2048]{3,2,1,0:T(8,128)(2,1)S(1)} %get-tuple-element.90.scaled_ref, f32[2,128,1024]{2,1,0:T(8,128)S(1)} %collective-permute-done.6.carry_ref.other_ref, ...), custom_call_target="tpu_custom_call" | custom-call | flops 805306368 | bytes 4194304 | tf_op jit(solution)/shard_map/map_terms/pallas_call | solution.py:581
  41.8 1.4 %collective-permute-start.7 = (f32[2,128,128]{2,1,0:T(8,128)S(1)}, f32[2,128,128]{2,1,0:T(8,128)S(1)}, u32[]{:S(2)}, u32[]{:S(2)}) collective-permute-start(f32[2,128,128]{2,1,0:T(8,128)S(1)} %get-tuple-element.102), channel_id=1, source_target_pairs={{0,1},{1,2},{2,3},{3,0},{4,5},{5,6},{6,7},{7,4},{8,9},{9,10},{10,1... | collective-permute-start | bytes 393224 | tf_op jit(solution)/shard_map/ppermute | solution.py:636
  43.2 1.1 %collective-permute-start.8 = (f32[2,128,128]{2,1,0:T(8,128)S(1)}, f32[2,128,128]{2,1,0:T(8,128)S(1)}, u32[]{:S(2)}, u32[]{:S(2)}) collective-permute-start(f32[2,128,128]{2,1,0:T(8,128)S(1)} %get-tuple-element.103), channel_id=1, source_target_pairs={{0,2},{1,3},{2,0},{3,1},{4,6},{5,7},{6,4},{7,5},{8,10},{9,11},{10,... | collective-permute-start | bytes 393224 | tf_op jit(solution)/shard_map/ppermute | solution.py:636
  44.3 1.4 %collective-permute-start.9 = (f32[2,128,128]{2,1,0:T(8,128)S(1)}, f32[2,128,128]{2,1,0:T(8,128)S(1)}, u32[]{:S(2)}, u32[]{:S(2)}) collective-permute-start(f32[2,128,128]{2,1,0:T(8,128)S(1)} %get-tuple-element.104), channel_id=1, source_target_pairs={{0,3},{1,0},{2,1},{3,2},{4,7},{5,4},{6,5},{7,6},{8,11},{9,8},{10,9... | collective-permute-start | bytes 393224 | tf_op jit(solution)/shard_map/ppermute | solution.py:636
  45.7 3.7 %input_terms.1 = bf16[512,2048]{1,0:T(8,128)(2,1)} custom-call(f32[512,2048]{1,0:T(8,128)S(1)} %get-tuple-element.82.part_ref, bf16[512,256]{1,0:T(8,128)(2,1)S(1)} %get-tuple-element.55.refs_10_.suf_ref, bf16[512,128]{1,0:T(8,128)(2,1)S(1)} %copy-done.3, f32[2,128,1024]{2,1,0:T(8,128)S(1)} %get-tuple-element.99.carry_ref.own_ref, ...), custom_call_target="tpu_custom_call" | custom-call | flops 536870912 | bytes 8388608 | tf_op jit(solution)/shard_map/input_terms/pallas_call | solution.py:613
  49.3 4.8 %collective-permute-done.8.refs_2_ = f32[2,128,128]{2,1,0:T(8,128)S(1)} collective-permute-done((f32[2,128,128]{2,1,0:T(8,128)S(1)}, f32[2,128,128]{2,1,0:T(8,128)S(1)}, u32[]{:S(2)}, u32[]{:S(2)}) %collective-permute-start.8) | collective-permute-done | bytes 131104 | tf_op jit(solution)/shard_map/ppermute | solution.py:636
  54.1 2.4 %collective-permute-done.9.refs_3_ = f32[2,128,128]{2,1,0:T(8,128)S(1)} collective-permute-done((f32[2,128,128]{2,1,0:T(8,128)S(1)}, f32[2,128,128]{2,1,0:T(8,128)S(1)}, u32[]{:S(2)}, u32[]{:S(2)}) %collective-permute-start.9) | collective-permute-done | bytes 131104 | tf_op jit(solution)/shard_map/ppermute | solution.py:636
  56.6 0.7 %head_sums.1 = (f32[128,128]{1,0:T(8,128)}, f32[128,128]{1,0:T(8,128)}) custom-call(f32[2,128,128]{2,1,0:T(8,128)S(1)} %get-tuple-element.101.refs_0_, f32[2,128,128]{2,1,0:T(8,128)S(1)} %collective-permute-done.7.refs_1_, f32[2,128,128]{2,1,0:T(8,128)S(1)} %collective-permute-done.8.refs_2_, f32[2,128,128]{2,1,0:T(8,128)S(1)} %collective-permute-done.9.refs_3_), custom_call_target="tpu_custom_call" | custom-call | flops 1048576 | bytes 524288 | tf_op jit(solution)/shard_map/head_sums/pallas_call | solution.py:246
  (23 shorter events, 1.1 us)
Async XLA Ops:
  0.6 8.5 %copy-start.1 = (bf16[512,2048]{1,0:T(8,128)(2,1)S(1)}, bf16[512,2048]{1,0:T(8,128)(2,1)}, u32[]{:S(2)}) copy-start(bf16[512,2048]{1,0:T(8,128)(2,1)} %refs_1_.7) | copy-start | bytes 6291460
  0.6 8.5 %copy-start = (bf16[512,2048]{1,0:T(8,128)(2,1)S(1)}, bf16[512,2048]{1,0:T(8,128)(2,1)}, u32[]{:S(2)}) copy-start(bf16[512,2048]{1,0:T(8,128)(2,1)} %refs_0_.7) | copy-start | bytes 6291460
  0.6 1.1 %copy-start.2 = (bf16[512,128]{1,0:T(8,128)(2,1)S(1)}, bf16[512,128]{1,0:T(8,128)(2,1)}, u32[]{:S(2)}) copy-start(bf16[512,128]{1,0:T(8,128)(2,1)} %b_ref.1) | copy-start | bytes 393220
  1.7 1.2 %copy-start.4 = (bf16[512,128]{1,0:T(8,128)(2,1)S(1)}, bf16[512,128]{1,0:T(8,128)(2,1)}, u32[]{:S(2)}) copy-start(bf16[512,128]{1,0:T(8,128)(2,1)} %refs_3_.7) | copy-start | bytes 393220
  2.9 0.8 %copy-start.6 = (f32[32,512]{1,0:T(8,128)S(1)}, f32[32,512]{1,0:T(8,128)}, u32[]{:S(2)}) copy-start(f32[32,512]{1,0:T(8,128)} %refs_4_.7) | copy-start | bytes 196612
  8.4 4.5 %collective-permute-start = (f32[2,136,1024]{2,1,0:T(8,128)S(1)}, f32[2,136,1024]{2,1,0:T(8,128)S(1)}, u32[]{:S(2)}, u32[]{:S(2)}) collective-permute-start(f32[2,136,1024]{2,1,0:T(8,128)S(1)} %get-tuple-element.56), channel_id=1, source_target_pairs={{0,4},{4,0},{8,12},{12,8},{16,20},{20,16},{24,28},{28,24},{1,5},{5... | collective-permute-start | bytes 3342344 | tf_op jit(solution)/shard_map/ppermute | solution.py:632
  12.8 3.0 %copy-start.3 = (bf16[512,128]{1,0:T(8,128)(2,1)S(1)}, bf16[512,128]{1,0:T(8,128)(2,1)}, u32[]{:S(2)}) copy-start(bf16[512,128]{1,0:T(8,128)(2,1)} %b_ref.1) | copy-start | bytes 393220
  12.8 3.0 %copy-start.5 = (bf16[512,128]{1,0:T(8,128)(2,1)S(1)}, bf16[512,128]{1,0:T(8,128)(2,1)}, u32[]{:S(2)}) copy-start(bf16[512,128]{1,0:T(8,128)(2,1)} %refs_3_.7) | copy-start | bytes 393220
  12.8 3.0 %copy-start.7 = (f32[32,512]{1,0:T(8,128)S(1)}, f32[32,512]{1,0:T(8,128)}, u32[]{:S(2)}) copy-start(f32[32,512]{1,0:T(8,128)} %refs_4_.7) | copy-start | bytes 196612
  13.1 14.9 %collective-permute-start.1 = (f32[264,512]{1,0:T(8,128)S(1)}, f32[264,512]{1,0:T(8,128)S(1)}, u32[]{:S(2)}, u32[]{:S(2)}) collective-permute-start(f32[264,512]{1,0:T(8,128)S(1)} %get-tuple-element.57.own_ref), channel_id=1, source_target_pairs={{0,8},{4,12},{8,0},{12,4},{16,24},{20,28},{24,16},{28,20},{1,9},{5... | collective-permute-start | bytes 1622024 | tf_op jit(solution)/shard_map/ppermute | solution.py:259
  13.4 14.6 %collective-permute-start.3 = (f32[8,512]{1,0:T(8,128)S(1)}, f32[8,512]{1,0:T(8,128)S(1)}, u32[]{:S(2)}, u32[]{:S(2)}) collective-permute-start(f32[8,512]{1,0:T(8,128)S(1)} %get-tuple-element.59), channel_id=1, source_target_pairs={{0,24},{4,28},{8,16},{12,20},{16,8},{20,12},{24,0},{28,4},{1,25},{... | collective-permute-start | bytes 49160 | tf_op jit(solution)/shard_map/ppermute | solution.py:259
  15.6 12.4 %collective-permute-start.2 = (f32[128,512]{1,0:T(8,128)S(1)}, f32[128,512]{1,0:T(8,128)S(1)}, u32[]{:S(2)}, u32[]{:S(2)}) collective-permute-start(f32[128,512]{1,0:T(8,128)S(1)} %get-tuple-element.58), channel_id=1, source_target_pairs={{0,16},{4,20},{8,24},{12,28},{16,0},{20,4},{24,8},{28,12},{1,17},{... | collective-permute-start | bytes 786440 | tf_op jit(solution)/shard_map/ppermute | solution.py:259
  28.1 6.7 %collective-permute-start.4 = (f32[128,512]{1,0:T(8,128)S(1)}, f32[128,512]{1,0:T(8,128)S(1)}, u32[]{:S(2)}, u32[]{:S(2)}) collective-permute-start(f32[128,512]{1,0:T(8,128)S(1)} %get-tuple-element.68), channel_id=1, source_target_pairs={{0,16},{4,20},{8,24},{12,28},{16,0},{20,4},{24,8},{28,12},{1,17},{... | collective-permute-start | bytes 786440 | tf_op jit(solution)/shard_map/ppermute | solution.py:259
  28.4 6.4 %collective-permute-start.5 = (f32[128,512]{1,0:T(8,128)S(1)}, f32[128,512]{1,0:T(8,128)S(1)}, u32[]{:S(2)}, u32[]{:S(2)}) collective-permute-start(f32[128,512]{1,0:T(8,128)S(1)} %get-tuple-element.69), channel_id=1, source_target_pairs={{0,8},{4,12},{8,0},{12,4},{16,24},{20,28},{24,16},{28,20},{1,9},{5... | collective-permute-start | bytes 786440 | tf_op jit(solution)/shard_map/ppermute | solution.py:259
  35.2 4.7 %collective-permute-start.6 = (f32[2,128,1024]{2,1,0:T(8,128)S(1)}, f32[2,128,1024]{2,1,0:T(8,128)S(1)}, u32[]{:S(2)}, u32[]{:S(2)}) collective-permute-start(f32[2,128,1024]{2,1,0:T(8,128)S(1)} %get-tuple-element.89), channel_id=1, source_target_pairs={{0,4},{4,0},{8,12},{12,8},{16,20},{20,16},{24,28},{28,24},{1,5},{5... | collective-permute-start | bytes 3145736 | tf_op jit(solution)/shard_map/ppermute | solution.py:632
  41.8 7.5 %collective-permute-start.7 = (f32[2,128,128]{2,1,0:T(8,128)S(1)}, f32[2,128,128]{2,1,0:T(8,128)S(1)}, u32[]{:S(2)}, u32[]{:S(2)}) collective-permute-start(f32[2,128,128]{2,1,0:T(8,128)S(1)} %get-tuple-element.102), channel_id=1, source_target_pairs={{0,1},{1,2},{2,3},{3,0},{4,5},{5,6},{6,7},{7,4},{8,9},{9,10},{10,1... | collective-permute-start | bytes 393224 | tf_op jit(solution)/shard_map/ppermute | solution.py:636
  43.2 10.9 %collective-permute-start.8 = (f32[2,128,128]{2,1,0:T(8,128)S(1)}, f32[2,128,128]{2,1,0:T(8,128)S(1)}, u32[]{:S(2)}, u32[]{:S(2)}) collective-permute-start(f32[2,128,128]{2,1,0:T(8,128)S(1)} %get-tuple-element.103), channel_id=1, source_target_pairs={{0,2},{1,3},{2,0},{3,1},{4,6},{5,7},{6,4},{7,5},{8,10},{9,11},{10,... | collective-permute-start | bytes 393224 | tf_op jit(solution)/shard_map/ppermute | solution.py:636
  44.3 12.3 %collective-permute-start.9 = (f32[2,128,128]{2,1,0:T(8,128)S(1)}, f32[2,128,128]{2,1,0:T(8,128)S(1)}, u32[]{:S(2)}, u32[]{:S(2)}) collective-permute-start(f32[2,128,128]{2,1,0:T(8,128)S(1)} %get-tuple-element.104), channel_id=1, source_target_pairs={{0,3},{1,0},{2,1},{3,2},{4,7},{5,4},{6,5},{7,6},{8,11},{9,8},{10,9... | collective-permute-start | bytes 393224 | tf_op jit(solution)/shard_map/ppermute | solution.py:636

commit v8 on v7

--- a/solution.py
+++ b/solution.py
@@ -17,7 +17,7 @@
 LANES = 128
 CORE, OTHER = range(2)
 PARAMS = pltpu.CompilerParams(vmem_limit_bytes=24 * 1024 * 1024)
-FIRST = pltpu.CompilerParams(vmem_limit_bytes=52 * 1024 * 1024)
+FIRST = pltpu.CompilerParams(vmem_limit_bytes=56 * 1024 * 1024)
 F32 = jnp.float32
 BF16 = jnp.bfloat16
 
@@ -211,7 +211,7 @@
     return chip < 2, (chip == 1) | (chip == 2)
 
 
-def first_kernel(mine_ref, recv_ref, same_ref, cross_ref, back_ref, decay_ref):
+def first_kernel(mine_ref, recv_ref, same_ref, later_ref, cross_ref, back_ref, decay_ref):
     left, inner = sides()
     core = place(CORE)
     width = mine_ref.shape[2] // 2
@@ -223,9 +223,9 @@
     grad = early[:N] + early_decay * late[:N]
     out, back = jnp.where(left, state, grad), jnp.where(left, grad, state)
     same_ref[:N, :] = out[:, :width]
-    same_ref[N : 2 * N, :] = jnp.where(inner, back[:, :width], out[:, width:])
+    later_ref[...] = jnp.where(inner, back[:, :width], out[:, width:])
     rows = lax.broadcasted_iota(jnp.int32, (EXTRA, width), 0)
-    same_ref[2 * N :, :] = jnp.where(rows == 0, decay[:, :width], decay[:, width:])
+    same_ref[N:, :] = jnp.where(rows == 0, decay[:, :width], decay[:, width:])
     cross_ref[...] = out[:, width:]
     back_ref[...] = back[:, width:]
     decay_ref[...] = jnp.broadcast_to(decay[:, width:], (EXTRA, width))
@@ -234,9 +234,9 @@
 def second_kernel(own_ref, back_ref, same_ref, cross_ref, decay_ref, cross2_ref, same2_ref):
     _, inner = sides()
     own, other = own_ref[:N, :], same_ref[:N, :]
-    own_decay, other_decay = own_ref[2 * N : 2 * N + 1, :], same_ref[2 * N : 2 * N + 1, :]
+    own_decay, other_decay = own_ref[N : N + 1, :], same_ref[N : N + 1, :]
     cross2_ref[...] = jnp.where(inner, own + own_decay * other, other + other_decay * own)
-    weight = own_ref[2 * N + 1 : 2 * N + 2, :] * decay_ref[:1, :]
+    weight = own_ref[N + 1 : N + 2, :] * decay_ref[:1, :]
     same2_ref[...] = jnp.where(inner, back_ref[...] + weight * cross_ref[...], cross_ref[...])
 
 
@@ -261,9 +261,10 @@
 
 def first_phase(length, mine, recv):
     half = mine.shape[2] // 2
-    shapes = [jax.ShapeDtypeStruct((rows, half), F32) for rows in (2 * N + EXTRA, N, N, EXTRA)]
-    own, cross, back, decay = plain_call(first_kernel, "first_messages", shapes, mine, recv)
-    return own, back, crossed(own, length, 2), crossed(cross, length, 4), crossed(decay, length, 6)
+    shapes = [jax.ShapeDtypeStruct((rows, half), F32) for rows in (N + EXTRA, N, N, N, EXTRA)]
+    own, later, cross, back, decay = plain_call(first_kernel, "first_messages", shapes, mine, recv)
+    same, cross, decay = crossed(own, length, 2), crossed(cross, length, 4), crossed(decay, length, 6)
+    return own, back, same, cross, decay, crossed(later, length, 2)
 
 
 def second_phase(own, back, same, cross, decay):
@@ -271,15 +272,17 @@
     return plain_call(second_kernel, "second_messages", [shape, shape], own, back, same, cross, decay)
 
 
-def carried4_kernel(mine_ref, recv_ref, same_ref, cross_ref, decay_ref, cross2_ref, same2_ref, own_ref, peer_ref):
+def carried4_kernel(
+    mine_ref, recv_ref, same_ref, cross_ref, decay_ref, later_ref, cross2_ref, same2_ref, own_ref, peer_ref
+):
     left, inner = sides()
     width = cross_ref.shape[1]
-    decay_a, decay_b = same_ref[2 * N : 2 * N + 1, :], same_ref[2 * N + 1 : 2 * N + 2, :]
+    decay_a, decay_b = same_ref[N : N + 1, :], same_ref[N + 1 : N + 2, :]
     for part in range(2):
         at = slice(part * width, (part + 1) * width)
-        out = jnp.where(inner, same_ref[part * N : (part + 1) * N, :], 0.0)
+        out = jnp.where(inner, later_ref[...] if part else same_ref[:N, :], 0.0)
         if part == 0:
-            back = jnp.where(inner, cross2_ref[...], same_ref[N : 2 * N, :] + decay_a * cross2_ref[...])
+            back = jnp.where(inner, cross2_ref[...], later_ref[...] + decay_a * cross2_ref[...])
         else:
             back = same2_ref[...] + jnp.where(inner, decay_ref[:1, :], decay_b) * cross_ref[...]
         carried_cores(
@@ -645,15 +648,15 @@
     (mine,) = totals(CORE, *args, factors=factors)
     tiles = mixer_input.shape[1] // WIDE
     if chips == 4:
-        ahead = tiles * 3 // 4
-        own, back, *others = first_phase(length, mine, recv)
+        ahead = tiles // 2
+        own, back, *others, later = first_phase(length, mine, recv)
         result = local_part(0, ahead, *args, decays)
         others, result = lax.optimization_barrier((others, result))
         cross, same = second_phase(own, back, *others)
-        others += [crossed(cross, length, 4), crossed(same, length, 2)]
-        result, _, _ = lax.optimization_barrier((result, cross, same))
+        crossing = [crossed(cross, length, 4), crossed(same, length, 2)]
+        result, later, _, _ = lax.optimization_barrier((result, later, cross, same))
         result = local_part(ahead, tiles - ahead, *args, decays, result)
-        others, result = lax.optimization_barrier((others, result))
+        others, result = lax.optimization_barrier((others + [later] + crossing, result))
         own, peer = carried4(mine, recv, *others)
     else:
         messages = chip_totals(chips, mine, recv)

time: 57.6 us -> 55.4 us (0.962)
  waiting for transfers between devices: 11.3 us -> 8.8 us
  local copies, waits for them, and re-layouts: 3.07 us -> 0.97 us
  Pallas kernels: 31.9 us -> 33.2 us
  starting transfers between devices: 10.2 us -> 11 us
    ppermute x5 -> x6, waiting for transfers between devices: 3.75 us -> 1.25 us  [crossed(): return lax.ppermute(v, 'seq', [(i, i ^ bit) for i in range(length)])]
    ppermute x5 -> x6, starting transfers between devices: 3.26 us -> 5.51 us  [crossed(): return lax.ppermute(v, 'seq', [(i, i ^ bit) for i in range(length)])]
    unnamed x16 -> x14, local copies, waits for them, and re-layouts: 3.07 us -> 0.97 us
    ppermute x2, starting transfers between devices: 3.13 us -> 1.68 us  [swap_cores(): return lax.ppermute(v, 'seq', [(i, i ^ 1) for i in range(length)])]
    pallas_call x2, Pallas kernels: 8.34 us -> 9.4 us  [totals(): pl.pallas_call(functools.partial(totals_kernel, width // P_SIZE, count, h...]
  transfers between devices with their start and end apart: 10 -> 11, of which waited for: 5 -> 4; matrix products, arithmetic and copies ran while one was open for 0% -> 0% of each run, Pallas kernels for 42% -> 44%
where the time goes in v8:
time: 55.4 us; the launch traced here: 54.8 us
  Pallas kernels  33.2 us (60%)
  starting transfers between devices  11 us (20%)
  waiting for transfers between devices  8.8 us (16%)
  local copies, waits for them, and re-layouts  0.97 us (2%)
  between operations  0.8 us (1%)
    pallas_call x2, Pallas kernels, local_part(): pl.pallas_call(functools.partial(local_kernel, first_tile, before is not...  14.8 us
    pallas_call x2, Pallas kernels, totals(): pl.pallas_call(functools.partial(totals_kernel, width // P_SIZE, count, h...  9.4 us
    ppermute x3, waiting for transfers between devices, turned(): lax.ppermute(v, axis, [(i, (i + by) % length) for i in range(length)])  7.23 us
    ppermute x6, starting transfers between devices, crossed(): return lax.ppermute(v, 'seq', [(i, i ^ bit) for i in range(length)])  5.51 us
    pallas_call x2, Pallas kernels, map_terms(): pl.pallas_call(functools.partial(map_kernel, count, ranks), grid=(count,)...  3.97 us
    ppermute x3, starting transfers between devices, turned(): lax.ppermute(v, axis, [(i, (i + by) % length) for i in range(length)])  3.85 us
    pallas_call x1, Pallas kernels, input_terms(): pl.pallas_call(functools.partial(input_kernel, width // P_SIZE, count), g...  3.68 us
    ppermute x2, starting transfers between devices, swap_cores(): return lax.ppermute(v, 'seq', [(i, i ^ 1) for i in range(length)])  1.68 us
  transfers between devices with their start and end apart: 11, of which 4 were waited for; matrix products, arithmetic and copies ran while one was open for 0% of the time, Pallas kernels for 44%

profile of v8, /device:TPU:11, one launch (start us, length us, event | category | flops | bytes accessed | tf_op | source)
XLA Modules:
  0.0 54.8 jit_solution(15527164472206300520)
XLA Ops:
  0.7 5.8 %state_totals.2 = (f32[2,136,1024]{2,1,0:T(8,128)}, bf16[512,256]{1,0:T(8,128)(2,1)}) custom-call(bf16[512,2048]{1,0:T(8,128)(2,1)} %refs_0_.7, bf16[512,2048]{1,0:T(8,128)(2,1)} %refs_0_.7, bf16[512,2048]{1,0:T(8,128)(2,1)} %refs_0_.7, bf16[512,2048]{1,0:T(8,128)(2,1)} %refs_0_.7, bf16[512,2048]{1,0:T(8,128)(2,1)} %refs_1_.7, bf16[512,2048]{1,0:T(8,128)(2,1)} %refs_1_.7, ...), custom_call_target="tpu_custom_call" | custom-call | flops 536870912 | bytes 4194304 | tf_op jit(solution)/shard_map/state_totals/pallas_call | solution.py:161
  6.4 0.7 %collective-permute-start = (f32[2,136,1024]{2,1,0:T(8,128)}, f32[2,136,1024]{2,1,0:T(8,128)S(1)}, u32[]{:S(2)}, u32[]{:S(2)}) collective-permute-start(f32[2,136,1024]{2,1,0:T(8,128)} %get-tuple-element.59), channel_id=1, source_target_pairs={{0,4},{4,0},{8,12},{12,8},{16,20},{20,16},{24,28},{28,24},{1,5},{5... | collective-permute-start | bytes 3342344 | tf_op jit(solution)/shard_map/ppermute | solution.py:635
  7.1 0.9 %copy-done.4 = bf16[512,256]{1,0:T(8,128)(2,1)S(1)} copy-done((bf16[512,256]{1,0:T(8,128)(2,1)S(1)}, bf16[512,256]{1,0:T(8,128)(2,1)}, u32[]{:S(2)}) %copy-start.4) | copy-done | bytes 262168
  8.1 3.6 %state_totals.3.mine_ref = f32[2,136,1024]{2,1,0:T(8,128)S(1)} custom-call(bf16[512,2048]{1,0:T(8,128)(2,1)S(1)} %copy-done, bf16[512,2048]{1,0:T(8,128)(2,1)S(1)} %copy-done, bf16[512,2048]{1,0:T(8,128)(2,1)S(1)} %copy-done, bf16[512,2048]{1,0:T(8,128)(2,1)S(1)} %copy-done, bf16[512,2048]{1,0:T(8,128)(2,1)S(1)} %copy-done.1, ...), custom_call_target="tpu_custom_call" | custom-call | flops 536870912 | bytes 4194304 | tf_op jit(solution)/shard_map/state_totals/pallas_call | solution.py:161
  12.0 0.3 collective-permute-start.1
  12.3 1.2 %collective-permute-start.2 = (f32[128,512]{1,0:T(8,128)S(1)}, f32[128,512]{1,0:T(8,128)S(1)}, u32[]{:S(2)}, u32[]{:S(2)}) collective-permute-start(f32[128,512]{1,0:T(8,128)S(1)} %get-tuple-element.61), channel_id=1, source_target_pairs={{0,16},{4,20},{8,24},{12,28},{16,0},{20,4},{24,8},{28,12},{1,17},{... | collective-permute-start | bytes 786440 | tf_op jit(solution)/shard_map/ppermute | solution.py:259
  13.6 1.1 %collective-permute-start.3 = (f32[8,512]{1,0:T(8,128)S(1)}, f32[8,512]{1,0:T(8,128)S(1)}, u32[]{:S(2)}, u32[]{:S(2)}) collective-permute-start(f32[8,512]{1,0:T(8,128)S(1)} %get-tuple-element.62), channel_id=1, source_target_pairs={{0,24},{4,28},{8,16},{12,20},{16,8},{20,12},{24,0},{28,4},{1,25},{... | collective-permute-start | bytes 49160 | tf_op jit(solution)/shard_map/ppermute | solution.py:259
  15.0 7.4 %local_part.2 = (f32[512,2048]{1,0:T(8,128)S(1)}, bf16[2,2,512,2048]{3,2,1,0:T(8,128)(2,1)S(1)}, f32[512,128]{1,0:T(8,128)S(1)}, f32[512,128]{1,0:T(8,128)S(1)}) custom-call(bf16[512,2048]{1,0:T(8,128)(2,1)S(1)} %copy-done, bf16[512,2048]{1,0:T(8,128)(2,1)S(1)} %copy-done.1, bf16[512,128]{1,0:T(8,128)(2,1)S(1)} %copy-done.2, bf16[512,128]{1,0:T(8,128)(2,1)S(1)} %copy-done.3, ...), custom_call_target="tpu_custom_call" | custom-call | flops 2684354560 | bytes 4194304 | tf_op jit(solution)/shard_map/local_part/pallas_call | solution.py:527
  22.5 1.3 %collective-permute-start.5 = (f32[128,512]{1,0:T(8,128)S(1)}, f32[128,512]{1,0:T(8,128)S(1)}, u32[]{:S(2)}, u32[]{:S(2)}) collective-permute-start(f32[128,512]{1,0:T(8,128)S(1)} %get-tuple-element.76), channel_id=1, source_target_pairs={{0,16},{4,20},{8,24},{12,28},{16,0},{20,4},{24,8},{28,12},{1,17},{... | collective-permute-start | bytes 786440 | tf_op jit(solution)/shard_map/ppermute | solution.py:259
  23.8 1.2 %collective-permute-start.6 = (f32[128,512]{1,0:T(8,128)S(1)}, f32[128,512]{1,0:T(8,128)S(1)}, u32[]{:S(2)}, u32[]{:S(2)}) collective-permute-start(f32[128,512]{1,0:T(8,128)S(1)} %get-tuple-element.77), channel_id=1, source_target_pairs={{0,8},{4,12},{8,0},{12,4},{16,24},{20,28},{24,16},{28,20},{1,9},{5... | collective-permute-start | bytes 786440 | tf_op jit(solution)/shard_map/ppermute | solution.py:259
  25.0 1.2 %collective-permute-done.4.later_ref = f32[128,512]{1,0:T(8,128)S(1)} collective-permute-done((f32[128,512]{1,0:T(8,128)S(1)}, f32[128,512]{1,0:T(8,128)S(1)}, u32[]{:S(2)}, u32[]{:S(2)}) %collective-permute-start.4) | collective-permute-done | bytes 262176 | tf_op jit(solution)/shard_map/ppermute | solution.py:259
  26.3 7.4 %local_part.3 = (f32[512,2048]{1,0:T(8,128)S(1)}, bf16[2,2,512,2048]{3,2,1,0:T(8,128)(2,1)S(1)}, f32[512,128]{1,0:T(8,128)S(1)}, f32[512,128]{1,0:T(8,128)S(1)}) custom-call(bf16[512,2048]{1,0:T(8,128)(2,1)S(1)} %copy-done, bf16[512,2048]{1,0:T(8,128)(2,1)S(1)} %copy-done.1, ...), custom_call_target="tpu_custom_call", output_to_operand_aliasing={{0}: (7, {}), {1}: (8, {})} | custom-call | flops 2684354560 | bytes 4194304 | tf_op jit(solution)/shard_map/local_part/pallas_call | solution.py:527
  33.7 0.4 carried_in.1
  34.1 1.0 %collective-permute-start.7 = (f32[2,128,1024]{2,1,0:T(8,128)S(1)}, f32[2,128,1024]{2,1,0:T(8,128)S(1)}, u32[]{:S(2)}, u32[]{:S(2)}) collective-permute-start(f32[2,128,1024]{2,1,0:T(8,128)S(1)} %get-tuple-element.95), channel_id=1, source_target_pairs={{0,4},{4,0},{8,12},{12,8},{16,20},{20,16},{24,28},{28,24},{1,5},{5... | collective-permute-start | bytes 3145736 | tf_op jit(solution)/shard_map/ppermute | solution.py:635
  35.1 2.0 %map_terms.2 = (f32[512,128]{1,0:T(8,128)S(1)}, f32[512,128]{1,0:T(8,128)S(1)}) custom-call(bf16[2,2,512,2048]{3,2,1,0:T(8,128)(2,1)S(1)} %get-tuple-element.96.scaled_ref, f32[2,128,1024]{2,1,0:T(8,128)S(1)} %get-tuple-element.105.carry_ref.own_ref, f32[512,128]{1,0:T(8,128)S(1)} %get-tuple-element.97.out_before_ref, ...), custom_call_target="tpu_custom_call" | custom-call | flops 805306368 | bytes 4194304 | tf_op jit(solution)/shard_map/map_terms/pallas_call | solution.py:584
  37.0 0.3 collective-permute-done.7.carry_ref.other_ref
  37.3 2.0 %map_terms.3 = (f32[2,128,128]{2,1,0:T(8,128)S(1)}, f32[2,128,128]{2,1,0:T(8,128)S(1)}, f32[2,128,128]{2,1,0:T(8,128)S(1)}, f32[2,128,128]{2,1,0:T(8,128)S(1)}) custom-call(bf16[2,2,512,2048]{3,2,1,0:T(8,128)(2,1)S(1)} %get-tuple-element.96.scaled_ref, f32[2,128,1024]{2,1,0:T(8,128)S(1)} %collective-permute-done.7.carry_ref.other_ref, ...), custom_call_target="tpu_custom_call" | custom-call | flops 805306368 | bytes 4194304 | tf_op jit(solution)/shard_map/map_terms/pallas_call | solution.py:584
  39.4 1.4 %collective-permute-start.8 = (f32[2,128,128]{2,1,0:T(8,128)S(1)}, f32[2,128,128]{2,1,0:T(8,128)S(1)}, u32[]{:S(2)}, u32[]{:S(2)}) collective-permute-start(f32[2,128,128]{2,1,0:T(8,128)S(1)} %get-tuple-element.108), channel_id=1, source_target_pairs={{0,1},{1,2},{2,3},{3,0},{4,5},{5,6},{6,7},{7,4},{8,9},{9,10},{10,1... | collective-permute-start | bytes 393224 | tf_op jit(solution)/shard_map/ppermute | solution.py:639
  40.8 1.1 %collective-permute-start.9 = (f32[2,128,128]{2,1,0:T(8,128)S(1)}, f32[2,128,128]{2,1,0:T(8,128)S(1)}, u32[]{:S(2)}, u32[]{:S(2)}) collective-permute-start(f32[2,128,128]{2,1,0:T(8,128)S(1)} %get-tuple-element.109), channel_id=1, source_target_pairs={{0,2},{1,3},{2,0},{3,1},{4,6},{5,7},{6,4},{7,5},{8,10},{9,11},{10,... | collective-permute-start | bytes 393224 | tf_op jit(solution)/shard_map/ppermute | solution.py:639
  41.8 1.4 %collective-permute-start.10 = (f32[2,128,128]{2,1,0:T(8,128)S(1)}, f32[2,128,128]{2,1,0:T(8,128)S(1)}, u32[]{:S(2)}, u32[]{:S(2)}) collective-permute-start(f32[2,128,128]{2,1,0:T(8,128)S(1)} %get-tuple-element.110), channel_id=1, source_target_pairs={{0,3},{1,0},{2,1},{3,2},{4,7},{5,4},{6,5},{7,6},{8,11},{9,8},{10,9... | collective-permute-start | bytes 393224 | tf_op jit(solution)/shard_map/ppermute | solution.py:639
  43.2 3.7 %input_terms.1 = bf16[512,2048]{1,0:T(8,128)(2,1)} custom-call(f32[512,2048]{1,0:T(8,128)S(1)} %get-tuple-element.87.part_ref, bf16[512,256]{1,0:T(8,128)(2,1)S(1)} %copy-done.5, bf16[512,128]{1,0:T(8,128)(2,1)S(1)} %copy-done.2, f32[2,128,1024]{2,1,0:T(8,128)S(1)} %get-tuple-element.105.carry_ref.own_ref, ...), custom_call_target="tpu_custom_call" | custom-call | flops 536870912 | bytes 8388608 | tf_op jit(solution)/shard_map/input_terms/pallas_call | solution.py:616
  46.9 4.8 %collective-permute-done.9.refs_2_ = f32[2,128,128]{2,1,0:T(8,128)S(1)} collective-permute-done((f32[2,128,128]{2,1,0:T(8,128)S(1)}, f32[2,128,128]{2,1,0:T(8,128)S(1)}, u32[]{:S(2)}, u32[]{:S(2)}) %collective-permute-start.9) | collective-permute-done | bytes 131104 | tf_op jit(solution)/shard_map/ppermute | solution.py:639
  51.7 2.4 %collective-permute-done.10.refs_3_ = f32[2,128,128]{2,1,0:T(8,128)S(1)} collective-permute-done((f32[2,128,128]{2,1,0:T(8,128)S(1)}, f32[2,128,128]{2,1,0:T(8,128)S(1)}, u32[]{:S(2)}, u32[]{:S(2)}) %collective-permute-start.10) | collective-permute-done | bytes 131104 | tf_op jit(solution)/shard_map/ppermute | solution.py:639
  54.1 0.7 %head_sums.1 = (f32[128,128]{1,0:T(8,128)}, f32[128,128]{1,0:T(8,128)}) custom-call(f32[2,128,128]{2,1,0:T(8,128)S(1)} %get-tuple-element.107.refs_0_, f32[2,128,128]{2,1,0:T(8,128)S(1)} %collective-permute-done.8.refs_1_, f32[2,128,128]{2,1,0:T(8,128)S(1)} %collective-permute-done.9.refs_2_, f32[2,128,128]{2,1,0:T(8,128)S(1)} %collective-permute-done.10.refs_3_), custom_call_target="tpu_custom_call" | custom-call | flops 1048576 | bytes 524288 | tf_op jit(solution)/shard_map/head_sums/pallas_call | solution.py:246
  (23 shorter events, 0.6 us)
Async XLA Ops:
  0.6 6.5 %copy-start.2 = (bf16[512,128]{1,0:T(8,128)(2,1)S(1)}, bf16[512,128]{1,0:T(8,128)(2,1)}, u32[]{:S(2)}) copy-start(bf16[512,128]{1,0:T(8,128)(2,1)} %b_ref.1) | copy-start | bytes 393220
  0.6 6.5 %copy-start.3 = (bf16[512,128]{1,0:T(8,128)(2,1)S(1)}, bf16[512,128]{1,0:T(8,128)(2,1)}, u32[]{:S(2)}) copy-start(bf16[512,128]{1,0:T(8,128)(2,1)} %refs_3_.7) | copy-start | bytes 393220
  0.7 6.5 %copy-start.1 = (bf16[512,2048]{1,0:T(8,128)(2,1)S(1)}, bf16[512,2048]{1,0:T(8,128)(2,1)}, u32[]{:S(2)}) copy-start(bf16[512,2048]{1,0:T(8,128)(2,1)} %refs_1_.7) | copy-start | bytes 6291460
  0.7 6.4 %copy-start = (bf16[512,2048]{1,0:T(8,128)(2,1)S(1)}, bf16[512,2048]{1,0:T(8,128)(2,1)}, u32[]{:S(2)}) copy-start(bf16[512,2048]{1,0:T(8,128)(2,1)} %refs_0_.7) | copy-start | bytes 6291460
  6.4 5.3 %collective-permute-start = (f32[2,136,1024]{2,1,0:T(8,128)}, f32[2,136,1024]{2,1,0:T(8,128)S(1)}, u32[]{:S(2)}, u32[]{:S(2)}) collective-permute-start(f32[2,136,1024]{2,1,0:T(8,128)} %get-tuple-element.59), channel_id=1, source_target_pairs={{0,4},{4,0},{8,12},{12,8},{16,20},{20,16},{24,28},{28,24},{1,5},{5... | collective-permute-start | bytes 3342344 | tf_op jit(solution)/shard_map/ppermute | solution.py:635
  7.1 1.0 %copy-start.4 = (bf16[512,256]{1,0:T(8,128)(2,1)S(1)}, bf16[512,256]{1,0:T(8,128)(2,1)}, u32[]{:S(2)}) copy-start(bf16[512,256]{1,0:T(8,128)(2,1)} %get-tuple-element.58.refs_10_.suf_ref) | copy-start | bytes 786436
  11.7 3.3 %copy-start.6 = (f32[32,512]{1,0:T(8,128)S(1)}, f32[32,512]{1,0:T(8,128)}, u32[]{:S(2)}) copy-start(f32[32,512]{1,0:T(8,128)} %refs_4_.7) | copy-start | bytes 196612
  12.0 10.4 %collective-permute-start.1 = (f32[136,512]{1,0:T(8,128)S(1)}, f32[136,512]{1,0:T(8,128)S(1)}, u32[]{:S(2)}, u32[]{:S(2)}) collective-permute-start(f32[136,512]{1,0:T(8,128)S(1)} %get-tuple-element.60.own_ref), channel_id=1, source_target_pairs={{0,8},{4,12},{8,0},{12,4},{16,24},{20,28},{24,16},{28,20},{1,9},{5... | collective-permute-start | bytes 835592 | tf_op jit(solution)/shard_map/ppermute | solution.py:259
  12.3 10.1 %collective-permute-start.2 = (f32[128,512]{1,0:T(8,128)S(1)}, f32[128,512]{1,0:T(8,128)S(1)}, u32[]{:S(2)}, u32[]{:S(2)}) collective-permute-start(f32[128,512]{1,0:T(8,128)S(1)} %get-tuple-element.61), channel_id=1, source_target_pairs={{0,16},{4,20},{8,24},{12,28},{16,0},{20,4},{24,8},{28,12},{1,17},{... | collective-permute-start | bytes 786440 | tf_op jit(solution)/shard_map/ppermute | solution.py:259
  13.6 8.8 %collective-permute-start.3 = (f32[8,512]{1,0:T(8,128)S(1)}, f32[8,512]{1,0:T(8,128)S(1)}, u32[]{:S(2)}, u32[]{:S(2)}) collective-permute-start(f32[8,512]{1,0:T(8,128)S(1)} %get-tuple-element.62), channel_id=1, source_target_pairs={{0,24},{4,28},{8,16},{12,20},{16,8},{20,12},{24,0},{28,4},{1,25},{... | collective-permute-start | bytes 49160 | tf_op jit(solution)/shard_map/ppermute | solution.py:259
  14.7 11.6 %collective-permute-start.4 = (f32[128,512]{1,0:T(8,128)S(1)}, f32[128,512]{1,0:T(8,128)S(1)}, u32[]{:S(2)}, u32[]{:S(2)}) collective-permute-start(f32[128,512]{1,0:T(8,128)S(1)} %get-tuple-element.74), channel_id=1, source_target_pairs={{0,8},{4,12},{8,0},{12,4},{16,24},{20,28},{24,16},{28,20},{1,9},{5... | collective-permute-start | bytes 786440 | tf_op jit(solution)/shard_map/ppermute | solution.py:259
  22.5 11.2 %collective-permute-start.5 = (f32[128,512]{1,0:T(8,128)S(1)}, f32[128,512]{1,0:T(8,128)S(1)}, u32[]{:S(2)}, u32[]{:S(2)}) collective-permute-start(f32[128,512]{1,0:T(8,128)S(1)} %get-tuple-element.76), channel_id=1, source_target_pairs={{0,16},{4,20},{8,24},{12,28},{16,0},{20,4},{24,8},{28,12},{1,17},{... | collective-permute-start | bytes 786440 | tf_op jit(solution)/shard_map/ppermute | solution.py:259
  23.8 9.9 %collective-permute-start.6 = (f32[128,512]{1,0:T(8,128)S(1)}, f32[128,512]{1,0:T(8,128)S(1)}, u32[]{:S(2)}, u32[]{:S(2)}) collective-permute-start(f32[128,512]{1,0:T(8,128)S(1)} %get-tuple-element.77), channel_id=1, source_target_pairs={{0,8},{4,12},{8,0},{12,4},{16,24},{20,28},{24,16},{28,20},{1,9},{5... | collective-permute-start | bytes 786440 | tf_op jit(solution)/shard_map/ppermute | solution.py:259
  34.1 3.3 %collective-permute-start.7 = (f32[2,128,1024]{2,1,0:T(8,128)S(1)}, f32[2,128,1024]{2,1,0:T(8,128)S(1)}, u32[]{:S(2)}, u32[]{:S(2)}) collective-permute-start(f32[2,128,1024]{2,1,0:T(8,128)S(1)} %get-tuple-element.95), channel_id=1, source_target_pairs={{0,4},{4,0},{8,12},{12,8},{16,20},{20,16},{24,28},{28,24},{1,5},{5... | collective-permute-start | bytes 3145736 | tf_op jit(solution)/shard_map/ppermute | solution.py:635
  37.3 5.9 %copy-start.5 = (bf16[512,256]{1,0:T(8,128)(2,1)S(1)}, bf16[512,256]{1,0:T(8,128)(2,1)}, u32[]{:S(2)}) copy-start(bf16[512,256]{1,0:T(8,128)(2,1)} %get-tuple-element.58.refs_10_.suf_ref) | copy-start | bytes 786436
  39.4 7.5 %collective-permute-start.8 = (f32[2,128,128]{2,1,0:T(8,128)S(1)}, f32[2,128,128]{2,1,0:T(8,128)S(1)}, u32[]{:S(2)}, u32[]{:S(2)}) collective-permute-start(f32[2,128,128]{2,1,0:T(8,128)S(1)} %get-tuple-element.108), channel_id=1, source_target_pairs={{0,1},{1,2},{2,3},{3,0},{4,5},{5,6},{6,7},{7,4},{8,9},{9,10},{10,1... | collective-permute-start | bytes 393224 | tf_op jit(solution)/shard_map/ppermute | solution.py:639
  40.8 10.9 %collective-permute-start.9 = (f32[2,128,128]{2,1,0:T(8,128)S(1)}, f32[2,128,128]{2,1,0:T(8,128)S(1)}, u32[]{:S(2)}, u32[]{:S(2)}) collective-permute-start(f32[2,128,128]{2,1,0:T(8,128)S(1)} %get-tuple-element.109), channel_id=1, source_target_pairs={{0,2},{1,3},{2,0},{3,1},{4,6},{5,7},{6,4},{7,5},{8,10},{9,11},{10,... | collective-permute-start | bytes 393224 | tf_op jit(solution)/shard_map/ppermute | solution.py:639
  41.8 12.3 %collective-permute-start.10 = (f32[2,128,128]{2,1,0:T(8,128)S(1)}, f32[2,128,128]{2,1,0:T(8,128)S(1)}, u32[]{:S(2)}, u32[]{:S(2)}) collective-permute-start(f32[2,128,128]{2,1,0:T(8,128)S(1)} %get-tuple-element.110), channel_id=1, source_target_pairs={{0,3},{1,0},{2,1},{3,2},{4,7},{5,4},{6,5},{7,6},{8,11},{9,8},{10,9... | collective-permute-start | bytes 393224 | tf_op jit(solution)/shard_map/ppermute | solution.py:639

commit v9 on v8

--- a/solution.py
+++ b/solution.py
@@ -13,7 +13,6 @@
 TILE = 256
 WIDE = 512
 EXTRA = 8
-PARTS = 4
 LANES = 128
 CORE, OTHER = range(2)
 PARAMS = pltpu.CompilerParams(vmem_limit_bytes=24 * 1024 * 1024)
@@ -115,60 +114,99 @@
     ref[:, LANES:] = packed(jnp.exp(summed_logs(logs, rows > columns)))
 
 
-def totals_kernel(heads, count, half, made, *refs):
-    x_refs, dy_refs, (b_ref, c_ref) = refs[:PARTS], refs[PARTS : 2 * PARTS], refs[2 * PARTS : 2 * PARTS + 2]
-    refs = refs[2 * PARTS + 2 :]
-    if made:
-        factor_ref, out_ref, bt_ref, ct_ref = refs
-    else:
-        decays_ref, out_ref, factor_ref, bt_ref, ct_ref = refs
+def tile_totals(heads, first, x, dy, bt_ref, ct_ref, factor_ref, out_ref):
+    tile = x.shape[1]
+    table = spread_table(heads, first, tile)
+    before = dot(factor_ref[:, :LANES], table)
+    after = dot(factor_ref[:, LANES:], table)
+    ended = jnp.broadcast_to(before[before.shape[0] - 1 :, :], (EXTRA, tile))
+    for i, (source, factor, other) in enumerate(((x, after, bt_ref), (dy, before, ct_ref))):
+        out_ref[i, :N, :] = dot12(other[...], halves(source.astype(F32) * factor))
+        out_ref[i, N:, :] = ended
+
+
+def other_kernel(
+    heads, x_ref, dy_ref, b_ref, c_ref, decays_ref, out_ref, factor_ref, x_buf, dy_buf, out_buf, bt_ref, ct_ref, arrived, sent
+):
+    count, _, tile = x_buf.shape
+    base = place(OTHER) * count
+    loads = []
+    for k in range(count):
+        columns = pl.ds(pl.multiple_of((base + k) * tile, tile), tile)
+        for i, (source, buf) in enumerate(((x_ref, x_buf), (dy_ref, dy_buf))):
+            loads.append(pltpu.make_async_copy(source.at[:, columns], buf.at[k], arrived.at[i, k]))
+            loads[-1].start()
+    bt_ref[...] = transposed(b_ref[...])
+    ct_ref[...] = transposed(c_ref[...])
+    device_factors(decays_ref[...], factor_ref)
+    stores = []
+    for k in range(count):
+        loads[2 * k].wait()
+        loads[2 * k + 1].wait()
+        first = (base + k) * (tile // P_SIZE)
+        tile_totals(heads, first, x_buf[k], dy_buf[k], bt_ref, ct_ref, factor_ref, out_buf.at[k])
+        stores.append(pltpu.make_async_copy(out_buf.at[k], out_ref.at[:, :, pl.ds(k * tile, tile)], sent.at[k]))
+        stores[-1].start()
+    for store in stores:
+        store.wait()
+
+
+def other_totals(x, dy, b, c, decays):
+    local, width = x.shape
+    count = width // 2 // TILE
+    anywhere = pl.BlockSpec(memory_space=pl.ANY)
+    whole = lambda a: pl.BlockSpec(a.shape, lambda j: (0, 0))
+    factor = jax.ShapeDtypeStruct((local, 2 * LANES), BF16)
+    return pl.pallas_call(
+        functools.partial(other_kernel, width // P_SIZE),
+        grid=(1,),
+        in_specs=[anywhere, anywhere, whole(b), whole(c), whole(decays)],
+        out_specs=[anywhere, whole(factor)],
+        out_shape=[jax.ShapeDtypeStruct((2, N + EXTRA, width // 2), F32), factor],
+        scratch_shapes=[
+            pltpu.VMEM((count, local, TILE), BF16),
+            pltpu.VMEM((count, local, TILE), BF16),
+            pltpu.VMEM((count, 2, N + EXTRA, TILE), F32),
+            pltpu.VMEM((N, local), BF16),
+            pltpu.VMEM((N, local), BF16),
+            pltpu.SemaphoreType.DMA((2, count)),
+            pltpu.SemaphoreType.DMA((count,)),
+        ],
+        compiler_params=FIRST,
+        name="other_totals",
+        cost_estimate=pl.CostEstimate(flops=8 * local * N * width // 2, bytes_accessed=4 * local * width, transcendentals=0),
+    )(x, dy, b, c, decays)
+
+
+def own_kernel(heads, count, x_ref, dy_ref, b_ref, c_ref, factor_ref, out_ref, bt_ref, ct_ref):
     step = pl.program_id(0)
 
     @pl.when(step == 0)
     def _():
         bt_ref[...] = transposed(b_ref[...])
         ct_ref[...] = transposed(c_ref[...])
-        if not made:
-            device_factors(decays_ref[...], factor_ref)
-
-    tile = x_refs[0].shape[1]
-    table = spread_table(heads, (place(half) * count + step) * (tile // P_SIZE), tile)
-    before = dot(factor_ref[:, :LANES], table)
-    after = dot(factor_ref[:, LANES:], table)
-    ended = before[before.shape[0] - 1 :, :]
-    for i, (sources, factor, other) in enumerate(((x_refs, after, bt_ref), (dy_refs, before, ct_ref))):
-        source = stacked(*[ref[...].astype(F32) for ref in sources])
-        out_ref[i, :N, :] = dot12(other[...], halves(source * factor))
-        out_ref[i, N:, :] = jnp.broadcast_to(ended, (EXTRA, tile))
-
-
-def totals(half, x, dy, b, c, decays=None, factors=None):
+
+    first = (place(CORE) * count + step) * (x_ref.shape[1] // P_SIZE)
+    tile_totals(heads, first, x_ref[...], dy_ref[...], bt_ref, ct_ref, factor_ref, out_ref)
+
+
+def own_totals(x, dy, b, c, factors):
     local, width = x.shape
-    count = width // 2 // TILE
+    tile = min(WIDE, width // 2)
+    count = width // 2 // tile
     whole = lambda a: pl.BlockSpec(a.shape, lambda j: (0, 0))
-    columns = [
-        pl.BlockSpec((local // PARTS, TILE), functools.partial(lambda part, j: (part, place(half) * count + j), part))
-        for part in range(PARTS)
-    ]
-    factor = jax.ShapeDtypeStruct((local, 2 * LANES), BF16)
-    made = factors is not None
-    last = factors if made else decays
-    out_specs = [pl.BlockSpec((2, N + EXTRA, TILE), lambda j: (0, 0, j))]
-    out_shape = [jax.ShapeDtypeStruct((2, N + EXTRA, width // 2), F32)]
-    if not made:
-        out_specs.append(whole(factor))
-        out_shape.append(factor)
+    column = pl.BlockSpec((local, tile), lambda j: (0, place(CORE) * count + j))
     return pl.pallas_call(
-        functools.partial(totals_kernel, width // P_SIZE, count, half, made),
+        functools.partial(own_kernel, width // P_SIZE, count),
         grid=(count,),
-        in_specs=columns + columns + [whole(b), whole(c), whole(last)],
-        out_specs=out_specs,
+        in_specs=[column, column, whole(b), whole(c), whole(factors)],
+        out_specs=pl.BlockSpec((2, N + EXTRA, tile), lambda j: (0, 0, j)),
         scratch_shapes=[pltpu.VMEM((N, local), BF16), pltpu.VMEM((N, local), BF16)],
-        out_shape=out_shape,
-        compiler_params=PARAMS if made else FIRST,
-        name="state_totals",
+        out_shape=jax.ShapeDtypeStruct((2, N + EXTRA, width // 2), F32),
+        compiler_params=PARAMS,
+        name="own_totals",
         cost_estimate=pl.CostEstimate(flops=8 * local * N * width // 2, bytes_accessed=4 * local * width, transcendentals=0),
-    )(*[x] * PARTS, *[dy] * PARTS, b, c, last)
+    )(x, dy, b, c, factors)
 
 
 def ordered(core, mine, recv):
@@ -643,9 +681,9 @@
     length, ranks = lax.axis_size("seq"), lax.axis_size("head")
     chips = length // 2
     args = mixer_input, output_grad, input_map, output_map
-    sent, factors = totals(OTHER, *args, decays=decays)
+    sent, factors = other_totals(*args, decays)
     recv = swap_cores(sent, length)
-    (mine,) = totals(CORE, *args, factors=factors)
+    mine = own_totals(*args, factors)
     tiles = mixer_input.shape[1] // WIDE
     if chips == 4:
         ahead = tiles // 2

time: 55.4 us -> 54.6 us (0.986)
  Pallas kernels: 33.2 us -> 32.5 us
    pallas_call x2, Pallas kernels: 9.4 us -> 8.62 us  [the longest x1 6.33 us: other_totals(): pl.pallas_call(functools.partial(other_kernel, width // P_SIZE), grid=(1,...]
  transfers between devices with their start and end apart: 11 -> 11, of which waited for: 4 -> 4; matrix products, arithmetic and copies ran while one was open for 0% -> 0% of each run, Pallas kernels for 44% -> 42%
where the time goes in v9:
time: 54.6 us; the launch traced here: 54.1 us
  Pallas kernels  32.5 us (60%)
  starting transfers between devices  11 us (20%)
  waiting for transfers between devices  8.82 us (16%)
  local copies, waits for them, and re-layouts  0.97 us (2%)
  between operations  0.81 us (1%)
    pallas_call x2, Pallas kernels, local_part(): pl.pallas_call(functools.partial(local_kernel, first_tile, before is not...  14.8 us
    ppermute x3, waiting for transfers between devices, turned(): lax.ppermute(v, axis, [(i, (i + by) % length) for i in range(length)])  7.23 us
    pallas_call x1, Pallas kernels, other_totals(): pl.pallas_call(functools.partial(other_kernel, width // P_SIZE), grid=(1,...  6.33 us
    ppermute x6, starting transfers between devices, crossed(): return lax.ppermute(v, 'seq', [(i, i ^ bit) for i in range(length)])  5.47 us
    pallas_call x2, Pallas kernels, map_terms(): pl.pallas_call(functools.partial(map_kernel, count, ranks), grid=(count,)...  4 us
    ppermute x3, starting transfers between devices, turned(): lax.ppermute(v, axis, [(i, (i + by) % length) for i in range(length)])  3.78 us
    pallas_call x1, Pallas kernels, input_terms(): pl.pallas_call(functools.partial(input_kernel, width // P_SIZE, count), g...  3.68 us
    pallas_call x1, Pallas kernels, own_totals(): pl.pallas_call(functools.partial(own_kernel, width // P_SIZE, count), gri...  2.29 us
  transfers between devices with their start and end apart: 11, of which 4 were waited for; matrix products, arithmetic and copies ran while one was open for 0% of the time, Pallas kernels for 42%

profile of v9, /device:TPU:11, one launch (start us, length us, event | category | flops | bytes accessed | tf_op | source)
XLA Modules:
  0.0 54.1 jit_solution(7193694829866024595)
XLA Ops:
  0.7 6.3 %other_totals.1 = (f32[2,136,1024]{2,1,0:T(8,128)}, bf16[512,256]{1,0:T(8,128)(2,1)}) custom-call(bf16[512,2048]{1,0:T(8,128)(2,1)} %refs_0_.3, bf16[512,2048]{1,0:T(8,128)(2,1)} %refs_1_.3, bf16[512,128]{1,0:T(8,128)(2,1)} %b_ref.5, bf16[512,128]{1,0:T(8,128)(2,1)} %refs_3_.3, f32[32,512]{1,0:T(8,128)} %refs_4_.3), custom_call_target="tpu_custom_call" | custom-call | flops 536870912 | bytes 4194304 | tf_op jit(solution)/shard_map/other_totals/pallas_call | solution.py:160
  7.0 0.7 %collective-permute-start = (f32[2,136,1024]{2,1,0:T(8,128)}, f32[2,136,1024]{2,1,0:T(8,128)S(1)}, u32[]{:S(2)}, u32[]{:S(2)}) collective-permute-start(f32[2,136,1024]{2,1,0:T(8,128)} %get-tuple-element.59), channel_id=1, source_target_pairs={{0,4},{4,0},{8,12},{12,8},{16,20},{20,16},{24,28},{28,24},{1,5},{5... | collective-permute-start | bytes 3342344 | tf_op jit(solution)/shard_map/ppermute | solution.py:673
  7.8 0.9 %copy-done.4 = bf16[512,256]{1,0:T(8,128)(2,1)S(1)} copy-done((bf16[512,256]{1,0:T(8,128)(2,1)S(1)}, bf16[512,256]{1,0:T(8,128)(2,1)}, u32[]{:S(2)}) %copy-start.4) | copy-done | bytes 262168
  8.7 2.3 %own_totals.1.mine_ref = f32[2,136,1024]{2,1,0:T(8,128)S(1)} custom-call(bf16[512,2048]{1,0:T(8,128)(2,1)S(1)} %copy-done, bf16[512,2048]{1,0:T(8,128)(2,1)S(1)} %copy-done.1, bf16[512,128]{1,0:T(8,128)(2,1)S(1)} %copy-done.2, bf16[512,128]{1,0:T(8,128)(2,1)S(1)} %copy-done.3, bf16[512,256]{1,0:T(8,128)(2,1)S(1)} %copy-done.4), custom_call_target="tpu_custom_call" | custom-call | flops 536870912 | bytes 4194304 | tf_op jit(solution)/shard_map/own_totals/pallas_call | solution.py:199
  11.3 0.3 collective-permute-start.1
  11.6 1.3 %collective-permute-start.2 = (f32[128,512]{1,0:T(8,128)S(1)}, f32[128,512]{1,0:T(8,128)S(1)}, u32[]{:S(2)}, u32[]{:S(2)}) collective-permute-start(f32[128,512]{1,0:T(8,128)S(1)} %get-tuple-element.61), channel_id=1, source_target_pairs={{0,16},{4,20},{8,24},{12,28},{16,0},{20,4},{24,8},{28,12},{1,17},{... | collective-permute-start | bytes 786440 | tf_op jit(solution)/shard_map/ppermute | solution.py:297
  12.8 1.2 %collective-permute-start.3 = (f32[8,512]{1,0:T(8,128)S(1)}, f32[8,512]{1,0:T(8,128)S(1)}, u32[]{:S(2)}, u32[]{:S(2)}) collective-permute-start(f32[8,512]{1,0:T(8,128)S(1)} %get-tuple-element.62), channel_id=1, source_target_pairs={{0,24},{4,28},{8,16},{12,20},{16,8},{20,12},{24,0},{28,4},{1,25},{... | collective-permute-start | bytes 49160 | tf_op jit(solution)/shard_map/ppermute | solution.py:297
  14.2 7.4 %local_part.2 = (f32[512,2048]{1,0:T(8,128)S(1)}, bf16[2,2,512,2048]{3,2,1,0:T(8,128)(2,1)S(1)}, f32[512,128]{1,0:T(8,128)S(1)}, f32[512,128]{1,0:T(8,128)S(1)}) custom-call(bf16[512,2048]{1,0:T(8,128)(2,1)S(1)} %copy-done, bf16[512,2048]{1,0:T(8,128)(2,1)S(1)} %copy-done.1, bf16[512,128]{1,0:T(8,128)(2,1)S(1)} %copy-done.2, bf16[512,128]{1,0:T(8,128)(2,1)S(1)} %copy-done.3, ...), custom_call_target="tpu_custom_call" | custom-call | flops 2684354560 | bytes 4194304 | tf_op jit(solution)/shard_map/local_part/pallas_call | solution.py:565
  21.8 1.3 %collective-permute-start.5 = (f32[128,512]{1,0:T(8,128)S(1)}, f32[128,512]{1,0:T(8,128)S(1)}, u32[]{:S(2)}, u32[]{:S(2)}) collective-permute-start(f32[128,512]{1,0:T(8,128)S(1)} %get-tuple-element.76), channel_id=1, source_target_pairs={{0,16},{4,20},{8,24},{12,28},{16,0},{20,4},{24,8},{28,12},{1,17},{... | collective-permute-start | bytes 786440 | tf_op jit(solution)/shard_map/ppermute | solution.py:297
  23.1 1.2 %collective-permute-start.6 = (f32[128,512]{1,0:T(8,128)S(1)}, f32[128,512]{1,0:T(8,128)S(1)}, u32[]{:S(2)}, u32[]{:S(2)}) collective-permute-start(f32[128,512]{1,0:T(8,128)S(1)} %get-tuple-element.77), channel_id=1, source_target_pairs={{0,8},{4,12},{8,0},{12,4},{16,24},{20,28},{24,16},{28,20},{1,9},{5... | collective-permute-start | bytes 786440 | tf_op jit(solution)/shard_map/ppermute | solution.py:297
  24.3 1.3 %collective-permute-done.4.later_ref = f32[128,512]{1,0:T(8,128)S(1)} collective-permute-done((f32[128,512]{1,0:T(8,128)S(1)}, f32[128,512]{1,0:T(8,128)S(1)}, u32[]{:S(2)}, u32[]{:S(2)}) %collective-permute-start.4) | collective-permute-done | bytes 262176 | tf_op jit(solution)/shard_map/ppermute | solution.py:297
  25.6 7.4 %local_part.3 = (f32[512,2048]{1,0:T(8,128)S(1)}, bf16[2,2,512,2048]{3,2,1,0:T(8,128)(2,1)S(1)}, f32[512,128]{1,0:T(8,128)S(1)}, f32[512,128]{1,0:T(8,128)S(1)}) custom-call(bf16[512,2048]{1,0:T(8,128)(2,1)S(1)} %copy-done, bf16[512,2048]{1,0:T(8,128)(2,1)S(1)} %copy-done.1, ...), custom_call_target="tpu_custom_call", output_to_operand_aliasing={{0}: (7, {}), {1}: (8, {})} | custom-call | flops 2684354560 | bytes 4194304 | tf_op jit(solution)/shard_map/local_part/pallas_call | solution.py:565
  33.0 0.4 carried_in.1
  33.3 1.0 %collective-permute-start.7 = (f32[2,128,1024]{2,1,0:T(8,128)S(1)}, f32[2,128,1024]{2,1,0:T(8,128)S(1)}, u32[]{:S(2)}, u32[]{:S(2)}) collective-permute-start(f32[2,128,1024]{2,1,0:T(8,128)S(1)} %get-tuple-element.95), channel_id=1, source_target_pairs={{0,4},{4,0},{8,12},{12,8},{16,20},{20,16},{24,28},{28,24},{1,5},{5... | collective-permute-start | bytes 3145736 | tf_op jit(solution)/shard_map/ppermute | solution.py:673
  34.4 2.0 %map_terms.2 = (f32[512,128]{1,0:T(8,128)S(1)}, f32[512,128]{1,0:T(8,128)S(1)}) custom-call(bf16[2,2,512,2048]{3,2,1,0:T(8,128)(2,1)S(1)} %get-tuple-element.96.scaled_ref, f32[2,128,1024]{2,1,0:T(8,128)S(1)} %get-tuple-element.105.carry_ref.own_ref, f32[512,128]{1,0:T(8,128)S(1)} %get-tuple-element.97.out_before_ref, ...), custom_call_target="tpu_custom_call" | custom-call | flops 805306368 | bytes 4194304 | tf_op jit(solution)/shard_map/map_terms/pallas_call | solution.py:622
  36.3 0.3 collective-permute-done.7.carry_ref.other_ref
  36.7 2.0 %map_terms.3 = (f32[2,128,128]{2,1,0:T(8,128)S(1)}, f32[2,128,128]{2,1,0:T(8,128)S(1)}, f32[2,128,128]{2,1,0:T(8,128)S(1)}, f32[2,128,128]{2,1,0:T(8,128)S(1)}) custom-call(bf16[2,2,512,2048]{3,2,1,0:T(8,128)(2,1)S(1)} %get-tuple-element.96.scaled_ref, f32[2,128,1024]{2,1,0:T(8,128)S(1)} %collective-permute-done.7.carry_ref.other_ref, ...), custom_call_target="tpu_custom_call" | custom-call | flops 805306368 | bytes 4194304 | tf_op jit(solution)/shard_map/map_terms/pallas_call | solution.py:622
  38.7 1.4 %collective-permute-start.8 = (f32[2,128,128]{2,1,0:T(8,128)S(1)}, f32[2,128,128]{2,1,0:T(8,128)S(1)}, u32[]{:S(2)}, u32[]{:S(2)}) collective-permute-start(f32[2,128,128]{2,1,0:T(8,128)S(1)} %get-tuple-element.108), channel_id=1, source_target_pairs={{0,1},{1,2},{2,3},{3,0},{4,5},{5,6},{6,7},{7,4},{8,9},{9,10},{10,1... | collective-permute-start | bytes 393224 | tf_op jit(solution)/shard_map/ppermute | solution.py:677
  40.1 1.0 %collective-permute-start.9 = (f32[2,128,128]{2,1,0:T(8,128)S(1)}, f32[2,128,128]{2,1,0:T(8,128)S(1)}, u32[]{:S(2)}, u32[]{:S(2)}) collective-permute-start(f32[2,128,128]{2,1,0:T(8,128)S(1)} %get-tuple-element.109), channel_id=1, source_target_pairs={{0,2},{1,3},{2,0},{3,1},{4,6},{5,7},{6,4},{7,5},{8,10},{9,11},{10,... | collective-permute-start | bytes 393224 | tf_op jit(solution)/shard_map/ppermute | solution.py:677
  41.1 1.4 %collective-permute-start.10 = (f32[2,128,128]{2,1,0:T(8,128)S(1)}, f32[2,128,128]{2,1,0:T(8,128)S(1)}, u32[]{:S(2)}, u32[]{:S(2)}) collective-permute-start(f32[2,128,128]{2,1,0:T(8,128)S(1)} %get-tuple-element.110), channel_id=1, source_target_pairs={{0,3},{1,0},{2,1},{3,2},{4,7},{5,4},{6,5},{7,6},{8,11},{9,8},{10,9... | collective-permute-start | bytes 393224 | tf_op jit(solution)/shard_map/ppermute | solution.py:677
  42.5 3.7 %input_terms.1 = bf16[512,2048]{1,0:T(8,128)(2,1)} custom-call(f32[512,2048]{1,0:T(8,128)S(1)} %get-tuple-element.87.part_ref, bf16[512,256]{1,0:T(8,128)(2,1)S(1)} %copy-done.5, bf16[512,128]{1,0:T(8,128)(2,1)S(1)} %copy-done.2, f32[2,128,1024]{2,1,0:T(8,128)S(1)} %get-tuple-element.105.carry_ref.own_ref, ...), custom_call_target="tpu_custom_call" | custom-call | flops 536870912 | bytes 8388608 | tf_op jit(solution)/shard_map/input_terms/pallas_call | solution.py:654
  46.2 4.8 %collective-permute-done.9.refs_2_ = f32[2,128,128]{2,1,0:T(8,128)S(1)} collective-permute-done((f32[2,128,128]{2,1,0:T(8,128)S(1)}, f32[2,128,128]{2,1,0:T(8,128)S(1)}, u32[]{:S(2)}, u32[]{:S(2)}) %collective-permute-start.9) | collective-permute-done | bytes 131104 | tf_op jit(solution)/shard_map/ppermute | solution.py:677
  51.0 2.4 %collective-permute-done.10.refs_3_ = f32[2,128,128]{2,1,0:T(8,128)S(1)} collective-permute-done((f32[2,128,128]{2,1,0:T(8,128)S(1)}, f32[2,128,128]{2,1,0:T(8,128)S(1)}, u32[]{:S(2)}, u32[]{:S(2)}) %collective-permute-start.10) | collective-permute-done | bytes 131104 | tf_op jit(solution)/shard_map/ppermute | solution.py:677
  53.4 0.7 %head_sums.1 = (f32[128,128]{1,0:T(8,128)}, f32[128,128]{1,0:T(8,128)}) custom-call(f32[2,128,128]{2,1,0:T(8,128)S(1)} %get-tuple-element.107.refs_0_, f32[2,128,128]{2,1,0:T(8,128)S(1)} %collective-permute-done.8.refs_1_, f32[2,128,128]{2,1,0:T(8,128)S(1)} %collective-permute-done.9.refs_2_, f32[2,128,128]{2,1,0:T(8,128)S(1)} %collective-permute-done.10.refs_3_), custom_call_target="tpu_custom_call" | custom-call | flops 1048576 | bytes 524288 | tf_op jit(solution)/shard_map/head_sums/pallas_call | solution.py:284
  (23 shorter events, 0.6 us)
Async XLA Ops:
  0.6 7.1 %copy-start.2 = (bf16[512,128]{1,0:T(8,128)(2,1)S(1)}, bf16[512,128]{1,0:T(8,128)(2,1)}, u32[]{:S(2)}) copy-start(bf16[512,128]{1,0:T(8,128)(2,1)} %b_ref.5) | copy-start | bytes 393220
  0.6 7.1 %copy-start.3 = (bf16[512,128]{1,0:T(8,128)(2,1)S(1)}, bf16[512,128]{1,0:T(8,128)(2,1)}, u32[]{:S(2)}) copy-start(bf16[512,128]{1,0:T(8,128)(2,1)} %refs_3_.3) | copy-start | bytes 393220
  0.7 7.1 %copy-start.1 = (bf16[512,2048]{1,0:T(8,128)(2,1)S(1)}, bf16[512,2048]{1,0:T(8,128)(2,1)}, u32[]{:S(2)}) copy-start(bf16[512,2048]{1,0:T(8,128)(2,1)} %refs_1_.3) | copy-start | bytes 6291460
  0.7 7.1 %copy-start = (bf16[512,2048]{1,0:T(8,128)(2,1)S(1)}, bf16[512,2048]{1,0:T(8,128)(2,1)}, u32[]{:S(2)}) copy-start(bf16[512,2048]{1,0:T(8,128)(2,1)} %refs_0_.3) | copy-start | bytes 6291460
  7.0 4.0 %collective-permute-start = (f32[2,136,1024]{2,1,0:T(8,128)}, f32[2,136,1024]{2,1,0:T(8,128)S(1)}, u32[]{:S(2)}, u32[]{:S(2)}) collective-permute-start(f32[2,136,1024]{2,1,0:T(8,128)} %get-tuple-element.59), channel_id=1, source_target_pairs={{0,4},{4,0},{8,12},{12,8},{16,20},{20,16},{24,28},{28,24},{1,5},{5... | collective-permute-start | bytes 3342344 | tf_op jit(solution)/shard_map/ppermute | solution.py:673
  7.8 1.0 %copy-start.4 = (bf16[512,256]{1,0:T(8,128)(2,1)S(1)}, bf16[512,256]{1,0:T(8,128)(2,1)}, u32[]{:S(2)}) copy-start(bf16[512,256]{1,0:T(8,128)(2,1)} %get-tuple-element.58.factor_ref.suf_ref) | copy-start | bytes 786436
  11.0 3.2 %copy-start.6 = (f32[32,512]{1,0:T(8,128)S(1)}, f32[32,512]{1,0:T(8,128)}, u32[]{:S(2)}) copy-start(f32[32,512]{1,0:T(8,128)} %refs_4_.3) | copy-start | bytes 196612
  11.3 10.4 %collective-permute-start.1 = (f32[136,512]{1,0:T(8,128)S(1)}, f32[136,512]{1,0:T(8,128)S(1)}, u32[]{:S(2)}, u32[]{:S(2)}) collective-permute-start(f32[136,512]{1,0:T(8,128)S(1)} %get-tuple-element.60.own_ref), channel_id=1, source_target_pairs={{0,8},{4,12},{8,0},{12,4},{16,24},{20,28},{24,16},{28,20},{1,9},{5... | collective-permute-start | bytes 835592 | tf_op jit(solution)/shard_map/ppermute | solution.py:297
  11.6 10.1 %collective-permute-start.2 = (f32[128,512]{1,0:T(8,128)S(1)}, f32[128,512]{1,0:T(8,128)S(1)}, u32[]{:S(2)}, u32[]{:S(2)}) collective-permute-start(f32[128,512]{1,0:T(8,128)S(1)} %get-tuple-element.61), channel_id=1, source_target_pairs={{0,16},{4,20},{8,24},{12,28},{16,0},{20,4},{24,8},{28,12},{1,17},{... | collective-permute-start | bytes 786440 | tf_op jit(solution)/shard_map/ppermute | solution.py:297
  12.8 8.8 %collective-permute-start.3 = (f32[8,512]{1,0:T(8,128)S(1)}, f32[8,512]{1,0:T(8,128)S(1)}, u32[]{:S(2)}, u32[]{:S(2)}) collective-permute-start(f32[8,512]{1,0:T(8,128)S(1)} %get-tuple-element.62), channel_id=1, source_target_pairs={{0,24},{4,28},{8,16},{12,20},{16,8},{20,12},{24,0},{28,4},{1,25},{... | collective-permute-start | bytes 49160 | tf_op jit(solution)/shard_map/ppermute | solution.py:297
  14.0 11.6 %collective-permute-start.4 = (f32[128,512]{1,0:T(8,128)S(1)}, f32[128,512]{1,0:T(8,128)S(1)}, u32[]{:S(2)}, u32[]{:S(2)}) collective-permute-start(f32[128,512]{1,0:T(8,128)S(1)} %get-tuple-element.74), channel_id=1, source_target_pairs={{0,8},{4,12},{8,0},{12,4},{16,24},{20,28},{24,16},{28,20},{1,9},{5... | collective-permute-start | bytes 786440 | tf_op jit(solution)/shard_map/ppermute | solution.py:297
  21.8 11.2 %collective-permute-start.5 = (f32[128,512]{1,0:T(8,128)S(1)}, f32[128,512]{1,0:T(8,128)S(1)}, u32[]{:S(2)}, u32[]{:S(2)}) collective-permute-start(f32[128,512]{1,0:T(8,128)S(1)} %get-tuple-element.76), channel_id=1, source_target_pairs={{0,16},{4,20},{8,24},{12,28},{16,0},{20,4},{24,8},{28,12},{1,17},{... | collective-permute-start | bytes 786440 | tf_op jit(solution)/shard_map/ppermute | solution.py:297
  23.1 9.9 %collective-permute-start.6 = (f32[128,512]{1,0:T(8,128)S(1)}, f32[128,512]{1,0:T(8,128)S(1)}, u32[]{:S(2)}, u32[]{:S(2)}) collective-permute-start(f32[128,512]{1,0:T(8,128)S(1)} %get-tuple-element.77), channel_id=1, source_target_pairs={{0,8},{4,12},{8,0},{12,4},{16,24},{20,28},{24,16},{28,20},{1,9},{5... | collective-permute-start | bytes 786440 | tf_op jit(solution)/shard_map/ppermute | solution.py:297
  33.3 3.3 %collective-permute-start.7 = (f32[2,128,1024]{2,1,0:T(8,128)S(1)}, f32[2,128,1024]{2,1,0:T(8,128)S(1)}, u32[]{:S(2)}, u32[]{:S(2)}) collective-permute-start(f32[2,128,1024]{2,1,0:T(8,128)S(1)} %get-tuple-element.95), channel_id=1, source_target_pairs={{0,4},{4,0},{8,12},{12,8},{16,20},{20,16},{24,28},{28,24},{1,5},{5... | collective-permute-start | bytes 3145736 | tf_op jit(solution)/shard_map/ppermute | solution.py:673
  36.6 5.8 %copy-start.5 = (bf16[512,256]{1,0:T(8,128)(2,1)S(1)}, bf16[512,256]{1,0:T(8,128)(2,1)}, u32[]{:S(2)}) copy-start(bf16[512,256]{1,0:T(8,128)(2,1)} %get-tuple-element.58.factor_ref.suf_ref) | copy-start | bytes 786436
  38.7 7.5 %collective-permute-start.8 = (f32[2,128,128]{2,1,0:T(8,128)S(1)}, f32[2,128,128]{2,1,0:T(8,128)S(1)}, u32[]{:S(2)}, u32[]{:S(2)}) collective-permute-start(f32[2,128,128]{2,1,0:T(8,128)S(1)} %get-tuple-element.108), channel_id=1, source_target_pairs={{0,1},{1,2},{2,3},{3,0},{4,5},{5,6},{6,7},{7,4},{8,9},{9,10},{10,1... | collective-permute-start | bytes 393224 | tf_op jit(solution)/shard_map/ppermute | solution.py:677
  40.1 10.9 %collective-permute-start.9 = (f32[2,128,128]{2,1,0:T(8,128)S(1)}, f32[2,128,128]{2,1,0:T(8,128)S(1)}, u32[]{:S(2)}, u32[]{:S(2)}) collective-permute-start(f32[2,128,128]{2,1,0:T(8,128)S(1)} %get-tuple-element.109), channel_id=1, source_target_pairs={{0,2},{1,3},{2,0},{3,1},{4,6},{5,7},{6,4},{7,5},{8,10},{9,11},{10,... | collective-permute-start | bytes 393224 | tf_op jit(solution)/shard_map/ppermute | solution.py:677
  41.1 12.3 %collective-permute-start.10 = (f32[2,128,128]{2,1,0:T(8,128)S(1)}, f32[2,128,128]{2,1,0:T(8,128)S(1)}, u32[]{:S(2)}, u32[]{:S(2)}) collective-permute-start(f32[2,128,128]{2,1,0:T(8,128)S(1)} %get-tuple-element.110), channel_id=1, source_target_pairs={{0,3},{1,0},{2,1},{3,2},{4,7},{5,4},{6,5},{7,6},{8,11},{9,8},{10,9... | collective-permute-start | bytes 393224 | tf_op jit(solution)/shard_map/ppermute | solution.py:677

commit v10 on v9

--- a/solution.py
+++ b/solution.py
@@ -85,6 +85,11 @@
     return sums[:heads] + (sums[heads : 2 * heads] + sums[2 * heads :])
 
 
+def block_sums(logs, table):
+    blocks_of = [logs[:, k : k + LANES] for k in range(0, logs.shape[1], LANES)]
+    return [summed_logs(block, table) for block in blocks_of]
+
+
 def by_token(v):
     rest = jnp.zeros((LANES - v.shape[0], v.shape[1]), F32)
     return jnp.concatenate([v, rest], axis=0).T
@@ -106,12 +111,20 @@
 
 
 def device_factors(decays, ref):
-    local = decays.shape[1]
     logs = log_parts(decays)
-    rows = lax.broadcasted_iota(jnp.int32, (local, local), 0)
-    columns = lax.broadcasted_iota(jnp.int32, (local, local), 1)
-    ref[:, :LANES] = packed(jnp.exp(summed_logs(logs, rows <= columns)))
-    ref[:, LANES:] = packed(jnp.exp(summed_logs(logs, rows > columns)))
+    rows = lax.broadcasted_iota(jnp.int32, (LANES, LANES), 0)
+    columns = lax.broadcasted_iota(jnp.int32, (LANES, LANES), 1)
+    before, after = block_sums(logs, rows <= columns), block_sums(logs, rows > columns)
+    totals_of = [block[:, LANES - 1 :] for block in before]
+    ahead = behind = jnp.zeros(totals_of[0].shape, F32)
+    for k, total in enumerate(totals_of):
+        before[k] = before[k] + ahead
+        ahead = ahead + total
+    for k in reversed(range(len(totals_of))):
+        after[k] = after[k] + behind
+        behind = behind + totals_of[k]
+    ref[:, :LANES] = packed(jnp.exp(jnp.concatenate(before, axis=1)))
+    ref[:, LANES:] = packed(jnp.exp(jnp.concatenate(after, axis=1)))
 
 
 def tile_totals(heads, first, x, dy, bt_ref, ct_ref, factor_ref, out_ref):
@@ -400,12 +413,12 @@
 def local_factors(decays, lift_ref, drop_ref, rows_ref):
     local = decays.shape[1]
     logs = log_parts(decays)
-    rows = lax.broadcasted_iota(jnp.int32, (local, local), 0)
-    columns = lax.broadcasted_iota(jnp.int32, (local, local), 1)
+    rows = lax.broadcasted_iota(jnp.int32, (LANES, LANES), 0)
+    columns = lax.broadcasted_iota(jnp.int32, (LANES, LANES), 1)
     middle = (columns & -SUB) + SUB // 2
     later = (rows > middle) & (rows <= columns)
     sooner = (rows > columns) & (rows <= middle)
-    offset = summed_logs(logs, later.astype(F32) - sooner.astype(F32))
+    offset = jnp.concatenate(block_sums(logs, later.astype(F32) - sooner.astype(F32)), axis=1)
     lift_ref[...] = by_token(jnp.exp(offset))
     drop_ref[...] = by_token(jnp.exp(-offset))
     lane = lax.broadcasted_iota(jnp.int32, (1, LANES), 1)
@@ -478,14 +491,14 @@
         sums_ref[even, :] += dot(dys[0], stacked(*xs), NT)
         sums_ref[even, :SUB] += dot(dys[1], xs[0], NT)
         gained_even = dot(even_ref[pl.ds(k // 2 * SUB, SUB), :], stacked(dys[0], dys[0], dys[1]))
-        joint = factor(0, k) * factor(0, k + 1)
-        crossing = halves(xs_ref[even, :] * joint)
+        crossing = halves((xs_ref[even, :] * factor(0, k)) * factor(0, k + 1))
         dys, xs = halves(dys_ref[odd, :]), halves(xs_ref[odd, :])
         high = stacked(xs[0], crossing[0])
         both = dot(dys[0], stacked(high, xs[1], crossing[1]), NT)
         sums_ref[odd, :] += added_up(both) + dot(dys[1], high, NT)
         gained_odd = dot(odd_ref[pair, :], stacked(dys[0], dys[0], dys[1]))
-        part_ref[even, :] = back_ref[even, :] * (gained_even + joint * gained_odd[:SUB])
+        ahead = (back_ref[even, :] * factor(0, k)) * (factor(0, k + 1) * gained_odd[:SUB])
+        part_ref[even, :] = back_ref[even, :] * gained_even + ahead
         part_ref[odd, :] = back_ref[odd, :] * gained_odd[SUB:]
 
     for level, (span, boundaries, mixed_ref, scores_ref) in enumerate(levels, 1):

time: 54.6 us -> 54.6 us (level)
  no operation moved by 1% of the time
where the time goes in v10:
time: 54.6 us; the launch traced here: 54.1 us
  Pallas kernels  32.5 us (60%)
  starting transfers between devices  11 us (20%)
  waiting for transfers between devices  8.79 us (16%)
  local copies, waits for them, and re-layouts  0.97 us (2%)
  between operations  0.81 us (1%)
    pallas_call x2, Pallas kernels, local_part(): pl.pallas_call(functools.partial(local_kernel, first_tile, before is not...  14.8 us
    ppermute x3, waiting for transfers between devices, turned(): lax.ppermute(v, axis, [(i, (i + by) % length) for i in range(length)])  7.22 us
    pallas_call x1, Pallas kernels, other_totals(): pl.pallas_call(functools.partial(other_kernel, width // P_SIZE), grid=(1,...  6.33 us
    ppermute x6, starting transfers between devices, crossed(): return lax.ppermute(v, 'seq', [(i, i ^ bit) for i in range(length)])  5.48 us
    pallas_call x2, Pallas kernels, map_terms(): pl.pallas_call(functools.partial(map_kernel, count, ranks), grid=(count,)...  3.99 us
    ppermute x3, starting transfers between devices, turned(): lax.ppermute(v, axis, [(i, (i + by) % length) for i in range(length)])  3.85 us
    pallas_call x1, Pallas kernels, input_terms(): pl.pallas_call(functools.partial(input_kernel, width // P_SIZE, count), g...  3.69 us
    pallas_call x1, Pallas kernels, own_totals(): pl.pallas_call(functools.partial(own_kernel, width // P_SIZE, count), gri...  2.29 us
  transfers between devices with their start and end apart: 11, of which 4 were waited for; matrix products, arithmetic and copies ran while one was open for 0% of the time, Pallas kernels for 42%

profile of v10, /device:TPU:11, one launch (start us, length us, event | category | flops | bytes accessed | tf_op | source)
XLA Modules:
  0.0 54.1 jit_solution(13650113858786606512)
XLA Ops:
  0.7 6.3 %other_totals.1 = (f32[2,136,1024]{2,1,0:T(8,128)}, bf16[512,256]{1,0:T(8,128)(2,1)}) custom-call(bf16[512,2048]{1,0:T(8,128)(2,1)} %refs_0_.3, bf16[512,2048]{1,0:T(8,128)(2,1)} %refs_1_.3, bf16[512,128]{1,0:T(8,128)(2,1)} %b_ref.5, bf16[512,128]{1,0:T(8,128)(2,1)} %refs_3_.3, f32[32,512]{1,0:T(8,128)} %refs_4_.3), custom_call_target="tpu_custom_call" | custom-call | flops 536870912 | bytes 4194304 | tf_op jit(solution)/shard_map/other_totals/pallas_call | solution.py:173
  7.0 0.7 %collective-permute-start = (f32[2,136,1024]{2,1,0:T(8,128)}, f32[2,136,1024]{2,1,0:T(8,128)S(1)}, u32[]{:S(2)}, u32[]{:S(2)}) collective-permute-start(f32[2,136,1024]{2,1,0:T(8,128)} %get-tuple-element.59), channel_id=1, source_target_pairs={{0,4},{4,0},{8,12},{12,8},{16,20},{20,16},{24,28},{28,24},{1,5},{5... | collective-permute-start | bytes 3342344 | tf_op jit(solution)/shard_map/ppermute | solution.py:686
  7.8 0.9 %copy-done.4 = bf16[512,256]{1,0:T(8,128)(2,1)S(1)} copy-done((bf16[512,256]{1,0:T(8,128)(2,1)S(1)}, bf16[512,256]{1,0:T(8,128)(2,1)}, u32[]{:S(2)}) %copy-start.4) | copy-done | bytes 262168
  8.7 2.3 %own_totals.1.mine_ref = f32[2,136,1024]{2,1,0:T(8,128)S(1)} custom-call(bf16[512,2048]{1,0:T(8,128)(2,1)S(1)} %copy-done, bf16[512,2048]{1,0:T(8,128)(2,1)S(1)} %copy-done.1, bf16[512,128]{1,0:T(8,128)(2,1)S(1)} %copy-done.2, bf16[512,128]{1,0:T(8,128)(2,1)S(1)} %copy-done.3, bf16[512,256]{1,0:T(8,128)(2,1)S(1)} %copy-done.4), custom_call_target="tpu_custom_call" | custom-call | flops 536870912 | bytes 4194304 | tf_op jit(solution)/shard_map/own_totals/pallas_call | solution.py:212
  11.3 0.3 collective-permute-start.1
  11.6 1.2 %collective-permute-start.2 = (f32[128,512]{1,0:T(8,128)S(1)}, f32[128,512]{1,0:T(8,128)S(1)}, u32[]{:S(2)}, u32[]{:S(2)}) collective-permute-start(f32[128,512]{1,0:T(8,128)S(1)} %get-tuple-element.61), channel_id=1, source_target_pairs={{0,16},{4,20},{8,24},{12,28},{16,0},{20,4},{24,8},{28,12},{1,17},{... | collective-permute-start | bytes 786440 | tf_op jit(solution)/shard_map/ppermute | solution.py:310
  12.8 1.1 %collective-permute-start.3 = (f32[8,512]{1,0:T(8,128)S(1)}, f32[8,512]{1,0:T(8,128)S(1)}, u32[]{:S(2)}, u32[]{:S(2)}) collective-permute-start(f32[8,512]{1,0:T(8,128)S(1)} %get-tuple-element.62), channel_id=1, source_target_pairs={{0,24},{4,28},{8,16},{12,20},{16,8},{20,12},{24,0},{28,4},{1,25},{... | collective-permute-start | bytes 49160 | tf_op jit(solution)/shard_map/ppermute | solution.py:310
  14.2 7.4 %local_part.2 = (f32[512,2048]{1,0:T(8,128)S(1)}, bf16[2,2,512,2048]{3,2,1,0:T(8,128)(2,1)S(1)}, f32[512,128]{1,0:T(8,128)S(1)}, f32[512,128]{1,0:T(8,128)S(1)}) custom-call(bf16[512,2048]{1,0:T(8,128)(2,1)S(1)} %copy-done, bf16[512,2048]{1,0:T(8,128)(2,1)S(1)} %copy-done.1, bf16[512,128]{1,0:T(8,128)(2,1)S(1)} %copy-done.2, bf16[512,128]{1,0:T(8,128)(2,1)S(1)} %copy-done.3, ...), custom_call_target="tpu_custom_call" | custom-call | flops 2684354560 | bytes 4194304 | tf_op jit(solution)/shard_map/local_part/pallas_call | solution.py:578
  21.8 1.3 %collective-permute-start.5 = (f32[128,512]{1,0:T(8,128)S(1)}, f32[128,512]{1,0:T(8,128)S(1)}, u32[]{:S(2)}, u32[]{:S(2)}) collective-permute-start(f32[128,512]{1,0:T(8,128)S(1)} %get-tuple-element.76), channel_id=1, source_target_pairs={{0,16},{4,20},{8,24},{12,28},{16,0},{20,4},{24,8},{28,12},{1,17},{... | collective-permute-start | bytes 786440 | tf_op jit(solution)/shard_map/ppermute | solution.py:310
  23.1 1.2 %collective-permute-start.6 = (f32[128,512]{1,0:T(8,128)S(1)}, f32[128,512]{1,0:T(8,128)S(1)}, u32[]{:S(2)}, u32[]{:S(2)}) collective-permute-start(f32[128,512]{1,0:T(8,128)S(1)} %get-tuple-element.77), channel_id=1, source_target_pairs={{0,8},{4,12},{8,0},{12,4},{16,24},{20,28},{24,16},{28,20},{1,9},{5... | collective-permute-start | bytes 786440 | tf_op jit(solution)/shard_map/ppermute | solution.py:310
  24.3 1.2 %collective-permute-done.4.later_ref = f32[128,512]{1,0:T(8,128)S(1)} collective-permute-done((f32[128,512]{1,0:T(8,128)S(1)}, f32[128,512]{1,0:T(8,128)S(1)}, u32[]{:S(2)}, u32[]{:S(2)}) %collective-permute-start.4) | collective-permute-done | bytes 262176 | tf_op jit(solution)/shard_map/ppermute | solution.py:310
  25.5 7.4 %local_part.3 = (f32[512,2048]{1,0:T(8,128)S(1)}, bf16[2,2,512,2048]{3,2,1,0:T(8,128)(2,1)S(1)}, f32[512,128]{1,0:T(8,128)S(1)}, f32[512,128]{1,0:T(8,128)S(1)}) custom-call(bf16[512,2048]{1,0:T(8,128)(2,1)S(1)} %copy-done, bf16[512,2048]{1,0:T(8,128)(2,1)S(1)} %copy-done.1, ...), custom_call_target="tpu_custom_call", output_to_operand_aliasing={{0}: (7, {}), {1}: (8, {})} | custom-call | flops 2684354560 | bytes 4194304 | tf_op jit(solution)/shard_map/local_part/pallas_call | solution.py:578
  33.0 0.4 carried_in.1
  33.4 1.0 %collective-permute-start.7 = (f32[2,128,1024]{2,1,0:T(8,128)S(1)}, f32[2,128,1024]{2,1,0:T(8,128)S(1)}, u32[]{:S(2)}, u32[]{:S(2)}) collective-permute-start(f32[2,128,1024]{2,1,0:T(8,128)S(1)} %get-tuple-element.95), channel_id=1, source_target_pairs={{0,4},{4,0},{8,12},{12,8},{16,20},{20,16},{24,28},{28,24},{1,5},{5... | collective-permute-start | bytes 3145736 | tf_op jit(solution)/shard_map/ppermute | solution.py:686
  34.3 2.0 %map_terms.2 = (f32[512,128]{1,0:T(8,128)S(1)}, f32[512,128]{1,0:T(8,128)S(1)}) custom-call(bf16[2,2,512,2048]{3,2,1,0:T(8,128)(2,1)S(1)} %get-tuple-element.96.scaled_ref, f32[2,128,1024]{2,1,0:T(8,128)S(1)} %get-tuple-element.105.carry_ref.own_ref, f32[512,128]{1,0:T(8,128)S(1)} %get-tuple-element.97.out_before_ref, ...), custom_call_target="tpu_custom_call" | custom-call | flops 805306368 | bytes 4194304 | tf_op jit(solution)/shard_map/map_terms/pallas_call | solution.py:635
  36.3 0.3 collective-permute-done.7.carry_ref.other_ref
  36.6 2.0 %map_terms.3 = (f32[2,128,128]{2,1,0:T(8,128)S(1)}, f32[2,128,128]{2,1,0:T(8,128)S(1)}, f32[2,128,128]{2,1,0:T(8,128)S(1)}, f32[2,128,128]{2,1,0:T(8,128)S(1)}) custom-call(bf16[2,2,512,2048]{3,2,1,0:T(8,128)(2,1)S(1)} %get-tuple-element.96.scaled_ref, f32[2,128,1024]{2,1,0:T(8,128)S(1)} %collective-permute-done.7.carry_ref.other_ref, ...), custom_call_target="tpu_custom_call" | custom-call | flops 805306368 | bytes 4194304 | tf_op jit(solution)/shard_map/map_terms/pallas_call | solution.py:635
  38.7 1.4 %collective-permute-start.8 = (f32[2,128,128]{2,1,0:T(8,128)S(1)}, f32[2,128,128]{2,1,0:T(8,128)S(1)}, u32[]{:S(2)}, u32[]{:S(2)}) collective-permute-start(f32[2,128,128]{2,1,0:T(8,128)S(1)} %get-tuple-element.108), channel_id=1, source_target_pairs={{0,1},{1,2},{2,3},{3,0},{4,5},{5,6},{6,7},{7,4},{8,9},{9,10},{10,1... | collective-permute-start | bytes 393224 | tf_op jit(solution)/shard_map/ppermute | solution.py:690
  40.0 1.1 %collective-permute-start.9 = (f32[2,128,128]{2,1,0:T(8,128)S(1)}, f32[2,128,128]{2,1,0:T(8,128)S(1)}, u32[]{:S(2)}, u32[]{:S(2)}) collective-permute-start(f32[2,128,128]{2,1,0:T(8,128)S(1)} %get-tuple-element.109), channel_id=1, source_target_pairs={{0,2},{1,3},{2,0},{3,1},{4,6},{5,7},{6,4},{7,5},{8,10},{9,11},{10,... | collective-permute-start | bytes 393224 | tf_op jit(solution)/shard_map/ppermute | solution.py:690
  41.1 1.4 %collective-permute-start.10 = (f32[2,128,128]{2,1,0:T(8,128)S(1)}, f32[2,128,128]{2,1,0:T(8,128)S(1)}, u32[]{:S(2)}, u32[]{:S(2)}) collective-permute-start(f32[2,128,128]{2,1,0:T(8,128)S(1)} %get-tuple-element.110), channel_id=1, source_target_pairs={{0,3},{1,0},{2,1},{3,2},{4,7},{5,4},{6,5},{7,6},{8,11},{9,8},{10,9... | collective-permute-start | bytes 393224 | tf_op jit(solution)/shard_map/ppermute | solution.py:690
  42.5 3.7 %input_terms.1 = bf16[512,2048]{1,0:T(8,128)(2,1)} custom-call(f32[512,2048]{1,0:T(8,128)S(1)} %get-tuple-element.87.part_ref, bf16[512,256]{1,0:T(8,128)(2,1)S(1)} %copy-done.5, bf16[512,128]{1,0:T(8,128)(2,1)S(1)} %copy-done.2, f32[2,128,1024]{2,1,0:T(8,128)S(1)} %get-tuple-element.105.carry_ref.own_ref, ...), custom_call_target="tpu_custom_call" | custom-call | flops 536870912 | bytes 8388608 | tf_op jit(solution)/shard_map/input_terms/pallas_call | solution.py:667
  46.2 4.7 %collective-permute-done.9.refs_2_ = f32[2,128,128]{2,1,0:T(8,128)S(1)} collective-permute-done((f32[2,128,128]{2,1,0:T(8,128)S(1)}, f32[2,128,128]{2,1,0:T(8,128)S(1)}, u32[]{:S(2)}, u32[]{:S(2)}) %collective-permute-start.9) | collective-permute-done | bytes 131104 | tf_op jit(solution)/shard_map/ppermute | solution.py:690
  51.0 2.5 %collective-permute-done.10.refs_3_ = f32[2,128,128]{2,1,0:T(8,128)S(1)} collective-permute-done((f32[2,128,128]{2,1,0:T(8,128)S(1)}, f32[2,128,128]{2,1,0:T(8,128)S(1)}, u32[]{:S(2)}, u32[]{:S(2)}) %collective-permute-start.10) | collective-permute-done | bytes 131104 | tf_op jit(solution)/shard_map/ppermute | solution.py:690
  53.4 0.7 %head_sums.1 = (f32[128,128]{1,0:T(8,128)}, f32[128,128]{1,0:T(8,128)}) custom-call(f32[2,128,128]{2,1,0:T(8,128)S(1)} %get-tuple-element.107.refs_0_, f32[2,128,128]{2,1,0:T(8,128)S(1)} %collective-permute-done.8.refs_1_, f32[2,128,128]{2,1,0:T(8,128)S(1)} %collective-permute-done.9.refs_2_, f32[2,128,128]{2,1,0:T(8,128)S(1)} %collective-permute-done.10.refs_3_), custom_call_target="tpu_custom_call" | custom-call | flops 1048576 | bytes 524288 | tf_op jit(solution)/shard_map/head_sums/pallas_call | solution.py:297
  (23 shorter events, 0.6 us)
Async XLA Ops:
  0.6 7.1 %copy-start.2 = (bf16[512,128]{1,0:T(8,128)(2,1)S(1)}, bf16[512,128]{1,0:T(8,128)(2,1)}, u32[]{:S(2)}) copy-start(bf16[512,128]{1,0:T(8,128)(2,1)} %b_ref.5) | copy-start | bytes 393220
  0.6 7.1 %copy-start.3 = (bf16[512,128]{1,0:T(8,128)(2,1)S(1)}, bf16[512,128]{1,0:T(8,128)(2,1)}, u32[]{:S(2)}) copy-start(bf16[512,128]{1,0:T(8,128)(2,1)} %refs_3_.3) | copy-start | bytes 393220
  0.7 7.1 %copy-start.1 = (bf16[512,2048]{1,0:T(8,128)(2,1)S(1)}, bf16[512,2048]{1,0:T(8,128)(2,1)}, u32[]{:S(2)}) copy-start(bf16[512,2048]{1,0:T(8,128)(2,1)} %refs_1_.3) | copy-start | bytes 6291460
  0.7 7.1 %copy-start = (bf16[512,2048]{1,0:T(8,128)(2,1)S(1)}, bf16[512,2048]{1,0:T(8,128)(2,1)}, u32[]{:S(2)}) copy-start(bf16[512,2048]{1,0:T(8,128)(2,1)} %refs_0_.3) | copy-start | bytes 6291460
  7.0 4.0 %collective-permute-start = (f32[2,136,1024]{2,1,0:T(8,128)}, f32[2,136,1024]{2,1,0:T(8,128)S(1)}, u32[]{:S(2)}, u32[]{:S(2)}) collective-permute-start(f32[2,136,1024]{2,1,0:T(8,128)} %get-tuple-element.59), channel_id=1, source_target_pairs={{0,4},{4,0},{8,12},{12,8},{16,20},{20,16},{24,28},{28,24},{1,5},{5... | collective-permute-start | bytes 3342344 | tf_op jit(solution)/shard_map/ppermute | solution.py:686
  7.7 1.0 %copy-start.4 = (bf16[512,256]{1,0:T(8,128)(2,1)S(1)}, bf16[512,256]{1,0:T(8,128)(2,1)}, u32[]{:S(2)}) copy-start(bf16[512,256]{1,0:T(8,128)(2,1)} %get-tuple-element.58.factor_ref.suf_ref) | copy-start | bytes 786436
  11.0 3.3 %copy-start.6 = (f32[32,512]{1,0:T(8,128)S(1)}, f32[32,512]{1,0:T(8,128)}, u32[]{:S(2)}) copy-start(f32[32,512]{1,0:T(8,128)} %refs_4_.3) | copy-start | bytes 196612
  11.3 10.4 %collective-permute-start.1 = (f32[136,512]{1,0:T(8,128)S(1)}, f32[136,512]{1,0:T(8,128)S(1)}, u32[]{:S(2)}, u32[]{:S(2)}) collective-permute-start(f32[136,512]{1,0:T(8,128)S(1)} %get-tuple-element.60.own_ref), channel_id=1, source_target_pairs={{0,8},{4,12},{8,0},{12,4},{16,24},{20,28},{24,16},{28,20},{1,9},{5... | collective-permute-start | bytes 835592 | tf_op jit(solution)/shard_map/ppermute | solution.py:310
  11.6 10.1 %collective-permute-start.2 = (f32[128,512]{1,0:T(8,128)S(1)}, f32[128,512]{1,0:T(8,128)S(1)}, u32[]{:S(2)}, u32[]{:S(2)}) collective-permute-start(f32[128,512]{1,0:T(8,128)S(1)} %get-tuple-element.61), channel_id=1, source_target_pairs={{0,16},{4,20},{8,24},{12,28},{16,0},{20,4},{24,8},{28,12},{1,17},{... | collective-permute-start | bytes 786440 | tf_op jit(solution)/shard_map/ppermute | solution.py:310
  12.8 8.8 %collective-permute-start.3 = (f32[8,512]{1,0:T(8,128)S(1)}, f32[8,512]{1,0:T(8,128)S(1)}, u32[]{:S(2)}, u32[]{:S(2)}) collective-permute-start(f32[8,512]{1,0:T(8,128)S(1)} %get-tuple-element.62), channel_id=1, source_target_pairs={{0,24},{4,28},{8,16},{12,20},{16,8},{20,12},{24,0},{28,4},{1,25},{... | collective-permute-start | bytes 49160 | tf_op jit(solution)/shard_map/ppermute | solution.py:310
  14.0 11.6 %collective-permute-start.4 = (f32[128,512]{1,0:T(8,128)S(1)}, f32[128,512]{1,0:T(8,128)S(1)}, u32[]{:S(2)}, u32[]{:S(2)}) collective-permute-start(f32[128,512]{1,0:T(8,128)S(1)} %get-tuple-element.74), channel_id=1, source_target_pairs={{0,8},{4,12},{8,0},{12,4},{16,24},{20,28},{24,16},{28,20},{1,9},{5... | collective-permute-start | bytes 786440 | tf_op jit(solution)/shard_map/ppermute | solution.py:310
  21.8 11.2 %collective-permute-start.5 = (f32[128,512]{1,0:T(8,128)S(1)}, f32[128,512]{1,0:T(8,128)S(1)}, u32[]{:S(2)}, u32[]{:S(2)}) collective-permute-start(f32[128,512]{1,0:T(8,128)S(1)} %get-tuple-element.76), channel_id=1, source_target_pairs={{0,16},{4,20},{8,24},{12,28},{16,0},{20,4},{24,8},{28,12},{1,17},{... | collective-permute-start | bytes 786440 | tf_op jit(solution)/shard_map/ppermute | solution.py:310
  23.1 9.9 %collective-permute-start.6 = (f32[128,512]{1,0:T(8,128)S(1)}, f32[128,512]{1,0:T(8,128)S(1)}, u32[]{:S(2)}, u32[]{:S(2)}) collective-permute-start(f32[128,512]{1,0:T(8,128)S(1)} %get-tuple-element.77), channel_id=1, source_target_pairs={{0,8},{4,12},{8,0},{12,4},{16,24},{20,28},{24,16},{28,20},{1,9},{5... | collective-permute-start | bytes 786440 | tf_op jit(solution)/shard_map/ppermute | solution.py:310
  33.4 3.3 %collective-permute-start.7 = (f32[2,128,1024]{2,1,0:T(8,128)S(1)}, f32[2,128,1024]{2,1,0:T(8,128)S(1)}, u32[]{:S(2)}, u32[]{:S(2)}) collective-permute-start(f32[2,128,1024]{2,1,0:T(8,128)S(1)} %get-tuple-element.95), channel_id=1, source_target_pairs={{0,4},{4,0},{8,12},{12,8},{16,20},{20,16},{24,28},{28,24},{1,5},{5... | collective-permute-start | bytes 3145736 | tf_op jit(solution)/shard_map/ppermute | solution.py:686
  36.6 5.9 %copy-start.5 = (bf16[512,256]{1,0:T(8,128)(2,1)S(1)}, bf16[512,256]{1,0:T(8,128)(2,1)}, u32[]{:S(2)}) copy-start(bf16[512,256]{1,0:T(8,128)(2,1)} %get-tuple-element.58.factor_ref.suf_ref) | copy-start | bytes 786436
  38.7 7.6 %collective-permute-start.8 = (f32[2,128,128]{2,1,0:T(8,128)S(1)}, f32[2,128,128]{2,1,0:T(8,128)S(1)}, u32[]{:S(2)}, u32[]{:S(2)}) collective-permute-start(f32[2,128,128]{2,1,0:T(8,128)S(1)} %get-tuple-element.108), channel_id=1, source_target_pairs={{0,1},{1,2},{2,3},{3,0},{4,5},{5,6},{6,7},{7,4},{8,9},{9,10},{10,1... | collective-permute-start | bytes 393224 | tf_op jit(solution)/shard_map/ppermute | solution.py:690
  40.0 10.9 %collective-permute-start.9 = (f32[2,128,128]{2,1,0:T(8,128)S(1)}, f32[2,128,128]{2,1,0:T(8,128)S(1)}, u32[]{:S(2)}, u32[]{:S(2)}) collective-permute-start(f32[2,128,128]{2,1,0:T(8,128)S(1)} %get-tuple-element.109), channel_id=1, source_target_pairs={{0,2},{1,3},{2,0},{3,1},{4,6},{5,7},{6,4},{7,5},{8,10},{9,11},{10,... | collective-permute-start | bytes 393224 | tf_op jit(solution)/shard_map/ppermute | solution.py:690
  41.1 12.3 %collective-permute-start.10 = (f32[2,128,128]{2,1,0:T(8,128)S(1)}, f32[2,128,128]{2,1,0:T(8,128)S(1)}, u32[]{:S(2)}, u32[]{:S(2)}) collective-permute-start(f32[2,128,128]{2,1,0:T(8,128)S(1)} %get-tuple-element.110), channel_id=1, source_target_pairs={{0,3},{1,0},{2,1},{3,2},{4,7},{5,4},{6,5},{7,6},{8,11},{9,8},{10,9... | collective-permute-start | bytes 393224 | tf_op jit(solution)/shard_map/ppermute | solution.py:690

commit v11 on v10

--- a/solution.py
+++ b/solution.py
@@ -16,7 +16,7 @@
 LANES = 128
 CORE, OTHER = range(2)
 PARAMS = pltpu.CompilerParams(vmem_limit_bytes=24 * 1024 * 1024)
-FIRST = pltpu.CompilerParams(vmem_limit_bytes=56 * 1024 * 1024)
+FIRST = pltpu.CompilerParams(vmem_limit_bytes=60 * 1024 * 1024)
 F32 = jnp.float32
 BF16 = jnp.bfloat16
 
@@ -138,88 +138,74 @@
         out_ref[i, N:, :] = ended
 
 
-def other_kernel(
-    heads, x_ref, dy_ref, b_ref, c_ref, decays_ref, out_ref, factor_ref, x_buf, dy_buf, out_buf, bt_ref, ct_ref, arrived, sent
+def totals_kernel(
+    heads, x_ref, dy_ref, b_ref, c_ref, decays_ref, other_ref, own_ref, factor_ref,
+    x_buf, dy_buf, out_buf, b_buf, c_buf, decays_buf, bt_ref, ct_ref, arrived, small, sent,
 ):
-    count, _, tile = x_buf.shape
-    base = place(OTHER) * count
+    tiles, _, tile = x_buf.shape
+    count = tiles // 2
+    smalls = [
+        pltpu.make_async_copy(source, buf, small.at[i])
+        for i, (source, buf) in enumerate(((decays_ref, decays_buf), (b_ref, b_buf), (c_ref, c_buf)))
+    ]
+    for load in smalls:
+        load.start()
+    first_tile = [place(half) * count + k for half in (OTHER, CORE) for k in range(count)]
     loads = []
-    for k in range(count):
-        columns = pl.ds(pl.multiple_of((base + k) * tile, tile), tile)
+    for k in range(tiles):
+        columns = pl.ds(pl.multiple_of(first_tile[k] * tile, tile), tile)
         for i, (source, buf) in enumerate(((x_ref, x_buf), (dy_ref, dy_buf))):
             loads.append(pltpu.make_async_copy(source.at[:, columns], buf.at[k], arrived.at[i, k]))
             loads[-1].start()
-    bt_ref[...] = transposed(b_ref[...])
-    ct_ref[...] = transposed(c_ref[...])
-    device_factors(decays_ref[...], factor_ref)
+    smalls[0].wait()
+    device_factors(decays_buf[...], factor_ref)
+    smalls[1].wait()
+    smalls[2].wait()
+    bt_ref[...] = transposed(b_buf[...])
+    ct_ref[...] = transposed(c_buf[...])
     stores = []
-    for k in range(count):
+    for k in range(tiles):
         loads[2 * k].wait()
         loads[2 * k + 1].wait()
-        first = (base + k) * (tile // P_SIZE)
+        first = first_tile[k] * (tile // P_SIZE)
         tile_totals(heads, first, x_buf[k], dy_buf[k], bt_ref, ct_ref, factor_ref, out_buf.at[k])
-        stores.append(pltpu.make_async_copy(out_buf.at[k], out_ref.at[:, :, pl.ds(k * tile, tile)], sent.at[k]))
+        target = own_ref if k >= count else other_ref
+        columns = pl.ds(k % count * tile, tile)
+        stores.append(pltpu.make_async_copy(out_buf.at[k], target.at[:, :, columns], sent.at[k]))
         stores[-1].start()
     for store in stores:
         store.wait()
 
 
-def other_totals(x, dy, b, c, decays):
+def totals(x, dy, b, c, decays):
     local, width = x.shape
-    count = width // 2 // TILE
+    tiles = width // TILE
     anywhere = pl.BlockSpec(memory_space=pl.ANY)
-    whole = lambda a: pl.BlockSpec(a.shape, lambda j: (0, 0))
     factor = jax.ShapeDtypeStruct((local, 2 * LANES), BF16)
+    half = jax.ShapeDtypeStruct((2, N + EXTRA, width // 2), F32)
     return pl.pallas_call(
-        functools.partial(other_kernel, width // P_SIZE),
+        functools.partial(totals_kernel, width // P_SIZE),
         grid=(1,),
-        in_specs=[anywhere, anywhere, whole(b), whole(c), whole(decays)],
-        out_specs=[anywhere, whole(factor)],
-        out_shape=[jax.ShapeDtypeStruct((2, N + EXTRA, width // 2), F32), factor],
+        in_specs=[anywhere] * 5,
+        out_specs=[anywhere, anywhere, pl.BlockSpec(factor.shape, lambda j: (0, 0))],
+        out_shape=[half, half, factor],
         scratch_shapes=[
-            pltpu.VMEM((count, local, TILE), BF16),
-            pltpu.VMEM((count, local, TILE), BF16),
-            pltpu.VMEM((count, 2, N + EXTRA, TILE), F32),
+            pltpu.VMEM((tiles, local, TILE), BF16),
+            pltpu.VMEM((tiles, local, TILE), BF16),
+            pltpu.VMEM((tiles, 2, N + EXTRA, TILE), F32),
+            pltpu.VMEM(b.shape, BF16),
+            pltpu.VMEM(c.shape, BF16),
+            pltpu.VMEM(decays.shape, F32),
             pltpu.VMEM((N, local), BF16),
             pltpu.VMEM((N, local), BF16),
-            pltpu.SemaphoreType.DMA((2, count)),
-            pltpu.SemaphoreType.DMA((count,)),
+            pltpu.SemaphoreType.DMA((2, tiles)),
+            pltpu.SemaphoreType.DMA((3,)),
+            pltpu.SemaphoreType.DMA((tiles,)),
         ],
         compiler_params=FIRST,
-        name="other_totals",
-        cost_estimate=pl.CostEstimate(flops=8 * local * N * width // 2, bytes_accessed=4 * local * width, transcendentals=0),
+        name="state_totals",
+        cost_estimate=pl.CostEstimate(flops=8 * local * N * width, bytes_accessed=4 * local * width, transcendentals=0),
     )(x, dy, b, c, decays)
-
-
-def own_kernel(heads, count, x_ref, dy_ref, b_ref, c_ref, factor_ref, out_ref, bt_ref, ct_ref):
-    step = pl.program_id(0)
-
-    @pl.when(step == 0)
-    def _():
-        bt_ref[...] = transposed(b_ref[...])
-        ct_ref[...] = transposed(c_ref[...])
-
-    first = (place(CORE) * count + step) * (x_ref.shape[1] // P_SIZE)
-    tile_totals(heads, first, x_ref[...], dy_ref[...], bt_ref, ct_ref, factor_ref, out_ref)
-
-
-def own_totals(x, dy, b, c, factors):
-    local, width = x.shape
-    tile = min(WIDE, width // 2)
-    count = width // 2 // tile
-    whole = lambda a: pl.BlockSpec(a.shape, lambda j: (0, 0))
-    column = pl.BlockSpec((local, tile), lambda j: (0, place(CORE) * count + j))
-    return pl.pallas_call(
-        functools.partial(own_kernel, width // P_SIZE, count),
-        grid=(count,),
-        in_specs=[column, column, whole(b), whole(c), whole(factors)],
-        out_specs=pl.BlockSpec((2, N + EXTRA, tile), lambda j: (0, 0, j)),
-        scratch_shapes=[pltpu.VMEM((N, local), BF16), pltpu.VMEM((N, local), BF16)],
-        out_shape=jax.ShapeDtypeStruct((2, N + EXTRA, width // 2), F32),
-        compiler_params=PARAMS,
-        name="own_totals",
-        cost_estimate=pl.CostEstimate(flops=8 * local * N * width // 2, bytes_accessed=4 * local * width, transcendentals=0),
-    )(x, dy, b, c, factors)
 
 
 def ordered(core, mine, recv):
@@ -308,6 +294,25 @@
 
 def crossed(v, length, bit):
     return lax.ppermute(v, "seq", [(i, i ^ bit) for i in range(length)])
+
+
+def copy_kernel(from_ref, to_ref):
+    to_ref[...] = from_ref[...]
+
+
+def nearer(v):
+    tile = min(WIDE, v.shape[2])
+    block = pl.BlockSpec((2, N + EXTRA, tile), lambda j: (0, 0, j))
+    return pl.pallas_call(
+        copy_kernel,
+        grid=(v.shape[2] // tile,),
+        in_specs=[block],
+        out_specs=block,
+        out_shape=jax.ShapeDtypeStruct(v.shape, F32),
+        compiler_params=PARAMS,
+        name="nearer",
+        cost_estimate=pl.CostEstimate(flops=v.size, bytes_accessed=8 * v.size, transcendentals=0),
+    )(v)
 
 
 def first_phase(length, mine, recv):
@@ -694,9 +699,9 @@
     length, ranks = lax.axis_size("seq"), lax.axis_size("head")
     chips = length // 2
     args = mixer_input, output_grad, input_map, output_map
-    sent, factors = other_totals(*args, decays)
+    sent, mine, factors = totals(*args, decays)
     recv = swap_cores(sent, length)
-    mine = own_totals(*args, factors)
+    mine = nearer(mine)
     tiles = mixer_input.shape[1] // WIDE
     if chips == 4:
         ahead = tiles // 2

time: 54.6 us -> 56.8 us (1.040)
  Pallas kernels: 32.5 us -> 33.2 us
    ppermute x2, waiting for transfers between devices: 0.31 us -> 1.16 us  [swap_cores(): return lax.ppermute(v, 'seq', [(i, i ^ 1) for i in range(length)])]
    pallas_call x2, Pallas kernels: 8.63 us -> 9.33 us  [the longest x1 8.86 us: totals(): pl.pallas_call(functools.partial(totals_kernel, width // P_SIZE), grid=(1...]
  transfers between devices with their start and end apart: 11 -> 11, of which waited for: 4 -> 5; matrix products, arithmetic and copies ran while one was open for 0% -> 0% of each run, Pallas kernels for 42% -> 38%
where the time goes in v11:
time: 56.8 us; the launch traced here: 55.9 us
  Pallas kernels  33.2 us (58%)
  starting transfers between devices  11.4 us (20%)
  waiting for transfers between devices  9.24 us (16%)
  local copies, waits for them, and re-layouts  1.27 us (2%)
  between operations  0.77 us (1%)
    pallas_call x2, Pallas kernels, local_part(): pl.pallas_call(functools.partial(local_kernel, first_tile, before is not...  14.8 us
    pallas_call x1, Pallas kernels, totals(): pl.pallas_call(functools.partial(totals_kernel, width // P_SIZE), grid=(1...  8.86 us
    ppermute x3, waiting for transfers between devices, turned(): lax.ppermute(v, axis, [(i, (i + by) % length) for i in range(length)])  7.22 us
    ppermute x6, starting transfers between devices, crossed(): return lax.ppermute(v, 'seq', [(i, i ^ bit) for i in range(length)])  5.47 us
    pallas_call x2, Pallas kernels, map_terms(): pl.pallas_call(functools.partial(map_kernel, count, ranks), grid=(count,)...  3.99 us
    ppermute x3, starting transfers between devices, turned(): lax.ppermute(v, axis, [(i, (i + by) % length) for i in range(length)])  3.79 us
    pallas_call x1, Pallas kernels, input_terms(): pl.pallas_call(functools.partial(input_kernel, width // P_SIZE, count), g...  3.69 us
    ppermute x2, starting transfers between devices, swap_cores(): return lax.ppermute(v, 'seq', [(i, i ^ 1) for i in range(length)])  2.16 us
  transfers between devices with their start and end apart: 11, of which 5 were waited for; matrix products, arithmetic and copies ran while one was open for 0% of the time, Pallas kernels for 38%

profile of v11, /device:TPU:11, one launch (start us, length us, event | category | flops | bytes accessed | tf_op | source)
XLA Modules:
  0.0 55.9 jit_solution(14835452837803199065)
XLA Ops:
  0.6 8.9 %state_totals.1 = (f32[2,136,1024]{2,1,0:T(8,128)}, f32[2,136,1024]{2,1,0:T(8,128)}, bf16[512,256]{1,0:T(8,128)(2,1)}) custom-call(bf16[512,2048]{1,0:T(8,128)(2,1)} %refs_0_.3, bf16[512,2048]{1,0:T(8,128)(2,1)} %refs_1_.3, bf16[512,128]{1,0:T(8,128)(2,1)} %b_ref.3, bf16[512,128]{1,0:T(8,128)(2,1)} %refs_3_.3, f32[32,512]{1,0:T(8,128)} %refs_4_.3), custom_call_target="tpu_custom_call" | custom-call | flops 1073741824 | bytes 4194304 | tf_op jit(solution)/shard_map/state_totals/pallas_call | solution.py:186
  9.5 0.8 %collective-permute-start = (f32[2,136,1024]{2,1,0:T(8,128)}, f32[2,136,1024]{2,1,0:T(8,128)S(1)}, u32[]{:S(2)}, u32[]{:S(2)}) collective-permute-start(f32[2,136,1024]{2,1,0:T(8,128)} %get-tuple-element.60), channel_id=1, source_target_pairs={{0,4},{4,0},{8,12},{12,8},{16,20},{20,16},{24,28},{28,24},{1,5},{5... | collective-permute-start | bytes 3342344 | tf_op jit(solution)/shard_map/ppermute | solution.py:691
  10.3 1.2 %copy-done.3 = f32[2,136,1024]{2,1,0:T(8,128)S(1)} copy-done((f32[2,136,1024]{2,1,0:T(8,128)S(1)}, f32[2,136,1024]{2,1,0:T(8,128)}, u32[]{:S(2)}) %copy-start.3) | copy-done | bytes 1114136
  11.6 0.5 nearer.1.mine_ref
  12.0 0.9 %collective-permute-done.recv_ref = f32[2,136,1024]{2,1,0:T(8,128)S(1)} collective-permute-done((f32[2,136,1024]{2,1,0:T(8,128)}, f32[2,136,1024]{2,1,0:T(8,128)S(1)}, u32[]{:S(2)}, u32[]{:S(2)}) %collective-permute-start) | collective-permute-done | bytes 1114144 | tf_op jit(solution)/shard_map/ppermute | solution.py:691
  13.4 1.2 %collective-permute-start.2 = (f32[128,512]{1,0:T(8,128)S(1)}, f32[128,512]{1,0:T(8,128)S(1)}, u32[]{:S(2)}, u32[]{:S(2)}) collective-permute-start(f32[128,512]{1,0:T(8,128)S(1)} %get-tuple-element.62), channel_id=1, source_target_pairs={{0,16},{4,20},{8,24},{12,28},{16,0},{20,4},{24,8},{28,12},{1,17},{... | collective-permute-start | bytes 786440 | tf_op jit(solution)/shard_map/ppermute | solution.py:296
  14.7 1.2 %collective-permute-start.3 = (f32[8,512]{1,0:T(8,128)S(1)}, f32[8,512]{1,0:T(8,128)S(1)}, u32[]{:S(2)}, u32[]{:S(2)}) collective-permute-start(f32[8,512]{1,0:T(8,128)S(1)} %get-tuple-element.63), channel_id=1, source_target_pairs={{0,24},{4,28},{8,16},{12,20},{16,8},{20,12},{24,0},{28,4},{1,25},{... | collective-permute-start | bytes 49160 | tf_op jit(solution)/shard_map/ppermute | solution.py:296
  16.1 7.4 %local_part.2 = (f32[512,2048]{1,0:T(8,128)S(1)}, bf16[2,2,512,2048]{3,2,1,0:T(8,128)(2,1)S(1)}, f32[512,128]{1,0:T(8,128)S(1)}, f32[512,128]{1,0:T(8,128)S(1)}) custom-call(bf16[512,2048]{1,0:T(8,128)(2,1)S(1)} %copy-done, bf16[512,2048]{1,0:T(8,128)(2,1)S(1)} %copy-done.1, bf16[512,128]{1,0:T(8,128)(2,1)S(1)} %copy-done.2, bf16[512,128]{1,0:T(8,128)(2,1)S(1)} %copy-done.4, ...), custom_call_target="tpu_custom_call" | custom-call | flops 2684354560 | bytes 4194304 | tf_op jit(solution)/shard_map/local_part/pallas_call | solution.py:583
  23.7 1.3 %collective-permute-start.5 = (f32[128,512]{1,0:T(8,128)S(1)}, f32[128,512]{1,0:T(8,128)S(1)}, u32[]{:S(2)}, u32[]{:S(2)}) collective-permute-start(f32[128,512]{1,0:T(8,128)S(1)} %get-tuple-element.77), channel_id=1, source_target_pairs={{0,16},{4,20},{8,24},{12,28},{16,0},{20,4},{24,8},{28,12},{1,17},{... | collective-permute-start | bytes 786440 | tf_op jit(solution)/shard_map/ppermute | solution.py:296
  25.0 1.2 %collective-permute-start.6 = (f32[128,512]{1,0:T(8,128)S(1)}, f32[128,512]{1,0:T(8,128)S(1)}, u32[]{:S(2)}, u32[]{:S(2)}) collective-permute-start(f32[128,512]{1,0:T(8,128)S(1)} %get-tuple-element.78), channel_id=1, source_target_pairs={{0,8},{4,12},{8,0},{12,4},{16,24},{20,28},{24,16},{28,20},{1,9},{5... | collective-permute-start | bytes 786440 | tf_op jit(solution)/shard_map/ppermute | solution.py:296
  26.2 0.8 %collective-permute-done.4.later_ref = f32[128,512]{1,0:T(8,128)S(1)} collective-permute-done((f32[128,512]{1,0:T(8,128)S(1)}, f32[128,512]{1,0:T(8,128)S(1)}, u32[]{:S(2)}, u32[]{:S(2)}) %collective-permute-start.4) | collective-permute-done | bytes 262176 | tf_op jit(solution)/shard_map/ppermute | solution.py:296
  27.0 7.4 %local_part.3 = (f32[512,2048]{1,0:T(8,128)S(1)}, bf16[2,2,512,2048]{3,2,1,0:T(8,128)(2,1)S(1)}, f32[512,128]{1,0:T(8,128)S(1)}, f32[512,128]{1,0:T(8,128)S(1)}) custom-call(bf16[512,2048]{1,0:T(8,128)(2,1)S(1)} %copy-done, bf16[512,2048]{1,0:T(8,128)(2,1)S(1)} %copy-done.1, ...), custom_call_target="tpu_custom_call", output_to_operand_aliasing={{0}: (7, {}), {1}: (8, {})} | custom-call | flops 2684354560 | bytes 4194304 | tf_op jit(solution)/shard_map/local_part/pallas_call | solution.py:583
  34.5 0.4 carried_in.1
  34.8 1.4 %collective-permute-start.7 = (f32[2,128,1024]{2,1,0:T(8,128)S(1)}, f32[2,128,1024]{2,1,0:T(8,128)S(1)}, u32[]{:S(2)}, u32[]{:S(2)}) collective-permute-start(f32[2,128,1024]{2,1,0:T(8,128)S(1)} %get-tuple-element.97), channel_id=1, source_target_pairs={{0,4},{4,0},{8,12},{12,8},{16,20},{20,16},{24,28},{28,24},{1,5},{5... | collective-permute-start | bytes 3145736 | tf_op jit(solution)/shard_map/ppermute | solution.py:691
  36.2 2.0 %map_terms.2 = (f32[512,128]{1,0:T(8,128)S(1)}, f32[512,128]{1,0:T(8,128)S(1)}) custom-call(bf16[2,2,512,2048]{3,2,1,0:T(8,128)(2,1)S(1)} %get-tuple-element.98.scaled_ref, f32[2,128,1024]{2,1,0:T(8,128)S(1)} %get-tuple-element.107.carry_ref.own_ref, f32[512,128]{1,0:T(8,128)S(1)} %get-tuple-element.99.out_before_ref, ...), custom_call_target="tpu_custom_call" | custom-call | flops 805306368 | bytes 4194304 | tf_op jit(solution)/shard_map/map_terms/pallas_call | solution.py:640
  38.2 0.3 collective-permute-done.7.carry_ref.other_ref
  38.5 2.0 %map_terms.3 = (f32[2,128,128]{2,1,0:T(8,128)S(1)}, f32[2,128,128]{2,1,0:T(8,128)S(1)}, f32[2,128,128]{2,1,0:T(8,128)S(1)}, f32[2,128,128]{2,1,0:T(8,128)S(1)}) custom-call(bf16[2,2,512,2048]{3,2,1,0:T(8,128)(2,1)S(1)} %get-tuple-element.98.scaled_ref, f32[2,128,1024]{2,1,0:T(8,128)S(1)} %collective-permute-done.7.carry_ref.other_ref, ...), custom_call_target="tpu_custom_call" | custom-call | flops 805306368 | bytes 4194304 | tf_op jit(solution)/shard_map/map_terms/pallas_call | solution.py:640
  40.5 1.3 %collective-permute-start.8 = (f32[2,128,128]{2,1,0:T(8,128)S(1)}, f32[2,128,128]{2,1,0:T(8,128)S(1)}, u32[]{:S(2)}, u32[]{:S(2)}) collective-permute-start(f32[2,128,128]{2,1,0:T(8,128)S(1)} %get-tuple-element.110), channel_id=1, source_target_pairs={{0,1},{1,2},{2,3},{3,0},{4,5},{5,6},{6,7},{7,4},{8,9},{9,10},{10,1... | collective-permute-start | bytes 393224 | tf_op jit(solution)/shard_map/ppermute | solution.py:695
  41.8 1.1 %collective-permute-start.9 = (f32[2,128,128]{2,1,0:T(8,128)S(1)}, f32[2,128,128]{2,1,0:T(8,128)S(1)}, u32[]{:S(2)}, u32[]{:S(2)}) collective-permute-start(f32[2,128,128]{2,1,0:T(8,128)S(1)} %get-tuple-element.111), channel_id=1, source_target_pairs={{0,2},{1,3},{2,0},{3,1},{4,6},{5,7},{6,4},{7,5},{8,10},{9,11},{10,... | collective-permute-start | bytes 393224 | tf_op jit(solution)/shard_map/ppermute | solution.py:695
  42.9 1.4 %collective-permute-start.10 = (f32[2,128,128]{2,1,0:T(8,128)S(1)}, f32[2,128,128]{2,1,0:T(8,128)S(1)}, u32[]{:S(2)}, u32[]{:S(2)}) collective-permute-start(f32[2,128,128]{2,1,0:T(8,128)S(1)} %get-tuple-element.112), channel_id=1, source_target_pairs={{0,3},{1,0},{2,1},{3,2},{4,7},{5,4},{6,5},{7,6},{8,11},{9,8},{10,9... | collective-permute-start | bytes 393224 | tf_op jit(solution)/shard_map/ppermute | solution.py:695
  44.3 3.7 %input_terms.1 = bf16[512,2048]{1,0:T(8,128)(2,1)} custom-call(f32[512,2048]{1,0:T(8,128)S(1)} %get-tuple-element.88.part_ref, bf16[512,256]{1,0:T(8,128)(2,1)S(1)} %copy-done.6, bf16[512,128]{1,0:T(8,128)(2,1)S(1)} %copy-done.2, f32[2,128,1024]{2,1,0:T(8,128)S(1)} %get-tuple-element.107.carry_ref.own_ref, ...), custom_call_target="tpu_custom_call" | custom-call | flops 536870912 | bytes 8388608 | tf_op jit(solution)/shard_map/input_terms/pallas_call | solution.py:672
  48.0 4.8 %collective-permute-done.9.refs_2_ = f32[2,128,128]{2,1,0:T(8,128)S(1)} collective-permute-done((f32[2,128,128]{2,1,0:T(8,128)S(1)}, f32[2,128,128]{2,1,0:T(8,128)S(1)}, u32[]{:S(2)}, u32[]{:S(2)}) %collective-permute-start.9) | collective-permute-done | bytes 131104 | tf_op jit(solution)/shard_map/ppermute | solution.py:695
  52.8 2.5 %collective-permute-done.10.refs_3_ = f32[2,128,128]{2,1,0:T(8,128)S(1)} collective-permute-done((f32[2,128,128]{2,1,0:T(8,128)S(1)}, f32[2,128,128]{2,1,0:T(8,128)S(1)}, u32[]{:S(2)}, u32[]{:S(2)}) %collective-permute-start.10) | collective-permute-done | bytes 131104 | tf_op jit(solution)/shard_map/ppermute | solution.py:695
  55.2 0.7 %head_sums.1 = (f32[128,128]{1,0:T(8,128)}, f32[128,128]{1,0:T(8,128)}) custom-call(f32[2,128,128]{2,1,0:T(8,128)S(1)} %get-tuple-element.109.refs_0_, f32[2,128,128]{2,1,0:T(8,128)S(1)} %collective-permute-done.8.refs_1_, f32[2,128,128]{2,1,0:T(8,128)S(1)} %collective-permute-done.9.refs_2_, f32[2,128,128]{2,1,0:T(8,128)S(1)} %collective-permute-done.10.refs_3_), custom_call_target="tpu_custom_call" | custom-call | flops 1048576 | bytes 524288 | tf_op jit(solution)/shard_map/head_sums/pallas_call | solution.py:283
  (23 shorter events, 0.9 us)
Async XLA Ops:
  0.6 15.4 %copy-start.5 = (f32[32,512]{1,0:T(8,128)S(1)}, f32[32,512]{1,0:T(8,128)}, u32[]{:S(2)}) copy-start(f32[32,512]{1,0:T(8,128)} %refs_4_.3) | copy-start | bytes 196612
  9.5 3.4 %collective-permute-start = (f32[2,136,1024]{2,1,0:T(8,128)}, f32[2,136,1024]{2,1,0:T(8,128)S(1)}, u32[]{:S(2)}, u32[]{:S(2)}) collective-permute-start(f32[2,136,1024]{2,1,0:T(8,128)} %get-tuple-element.60), channel_id=1, source_target_pairs={{0,4},{4,0},{8,12},{12,8},{16,20},{20,16},{24,28},{28,24},{1,5},{5... | collective-permute-start | bytes 3342344 | tf_op jit(solution)/shard_map/ppermute | solution.py:691
  10.3 1.2 %copy-start.3 = (f32[2,136,1024]{2,1,0:T(8,128)S(1)}, f32[2,136,1024]{2,1,0:T(8,128)}, u32[]{:S(2)}) copy-start(f32[2,136,1024]{2,1,0:T(8,128)} %get-tuple-element.59.from_ref) | copy-start | bytes 3342340
  11.6 4.5 %copy-start = (bf16[512,2048]{1,0:T(8,128)(2,1)S(1)}, bf16[512,2048]{1,0:T(8,128)(2,1)}, u32[]{:S(2)}) copy-start(bf16[512,2048]{1,0:T(8,128)(2,1)} %refs_0_.3) | copy-start | bytes 6291460
  11.6 4.5 %copy-start.1 = (bf16[512,2048]{1,0:T(8,128)(2,1)S(1)}, bf16[512,2048]{1,0:T(8,128)(2,1)}, u32[]{:S(2)}) copy-start(bf16[512,2048]{1,0:T(8,128)(2,1)} %refs_1_.3) | copy-start | bytes 6291460
  11.6 4.5 %copy-start.2 = (bf16[512,128]{1,0:T(8,128)(2,1)S(1)}, bf16[512,128]{1,0:T(8,128)(2,1)}, u32[]{:S(2)}) copy-start(bf16[512,128]{1,0:T(8,128)(2,1)} %b_ref.3) | copy-start | bytes 393220
  11.6 4.5 %copy-start.4 = (bf16[512,128]{1,0:T(8,128)(2,1)S(1)}, bf16[512,128]{1,0:T(8,128)(2,1)}, u32[]{:S(2)}) copy-start(bf16[512,128]{1,0:T(8,128)(2,1)} %refs_3_.3) | copy-start | bytes 393220
  13.1 10.4 %collective-permute-start.1 = (f32[136,512]{1,0:T(8,128)S(1)}, f32[136,512]{1,0:T(8,128)S(1)}, u32[]{:S(2)}, u32[]{:S(2)}) collective-permute-start(f32[136,512]{1,0:T(8,128)S(1)} %get-tuple-element.61.own_ref), channel_id=1, source_target_pairs={{0,8},{4,12},{8,0},{12,4},{16,24},{20,28},{24,16},{28,20},{1,9},{5... | collective-permute-start | bytes 835592 | tf_op jit(solution)/shard_map/ppermute | solution.py:296
  13.4 10.1 %collective-permute-start.2 = (f32[128,512]{1,0:T(8,128)S(1)}, f32[128,512]{1,0:T(8,128)S(1)}, u32[]{:S(2)}, u32[]{:S(2)}) collective-permute-start(f32[128,512]{1,0:T(8,128)S(1)} %get-tuple-element.62), channel_id=1, source_target_pairs={{0,16},{4,20},{8,24},{12,28},{16,0},{20,4},{24,8},{28,12},{1,17},{... | collective-permute-start | bytes 786440 | tf_op jit(solution)/shard_map/ppermute | solution.py:296
  14.7 8.9 %collective-permute-start.3 = (f32[8,512]{1,0:T(8,128)S(1)}, f32[8,512]{1,0:T(8,128)S(1)}, u32[]{:S(2)}, u32[]{:S(2)}) collective-permute-start(f32[8,512]{1,0:T(8,128)S(1)} %get-tuple-element.63), channel_id=1, source_target_pairs={{0,24},{4,28},{8,16},{12,20},{16,8},{20,12},{24,0},{28,4},{1,25},{... | collective-permute-start | bytes 49160 | tf_op jit(solution)/shard_map/ppermute | solution.py:296
  15.8 11.2 %collective-permute-start.4 = (f32[128,512]{1,0:T(8,128)S(1)}, f32[128,512]{1,0:T(8,128)S(1)}, u32[]{:S(2)}, u32[]{:S(2)}) collective-permute-start(f32[128,512]{1,0:T(8,128)S(1)} %get-tuple-element.75), channel_id=1, source_target_pairs={{0,8},{4,12},{8,0},{12,4},{16,24},{20,28},{24,16},{28,20},{1,9},{5... | collective-permute-start | bytes 786440 | tf_op jit(solution)/shard_map/ppermute | solution.py:296
  23.7 10.8 %collective-permute-start.5 = (f32[128,512]{1,0:T(8,128)S(1)}, f32[128,512]{1,0:T(8,128)S(1)}, u32[]{:S(2)}, u32[]{:S(2)}) collective-permute-start(f32[128,512]{1,0:T(8,128)S(1)} %get-tuple-element.77), channel_id=1, source_target_pairs={{0,16},{4,20},{8,24},{12,28},{16,0},{20,4},{24,8},{28,12},{1,17},{... | collective-permute-start | bytes 786440 | tf_op jit(solution)/shard_map/ppermute | solution.py:296
  25.0 9.5 %collective-permute-start.6 = (f32[128,512]{1,0:T(8,128)S(1)}, f32[128,512]{1,0:T(8,128)S(1)}, u32[]{:S(2)}, u32[]{:S(2)}) collective-permute-start(f32[128,512]{1,0:T(8,128)S(1)} %get-tuple-element.78), channel_id=1, source_target_pairs={{0,8},{4,12},{8,0},{12,4},{16,24},{20,28},{24,16},{28,20},{1,9},{5... | collective-permute-start | bytes 786440 | tf_op jit(solution)/shard_map/ppermute | solution.py:296
  34.8 3.6 %collective-permute-start.7 = (f32[2,128,1024]{2,1,0:T(8,128)S(1)}, f32[2,128,1024]{2,1,0:T(8,128)S(1)}, u32[]{:S(2)}, u32[]{:S(2)}) collective-permute-start(f32[2,128,1024]{2,1,0:T(8,128)S(1)} %get-tuple-element.97), channel_id=1, source_target_pairs={{0,4},{4,0},{8,12},{12,8},{16,20},{20,16},{24,28},{28,24},{1,5},{5... | collective-permute-start | bytes 3145736 | tf_op jit(solution)/shard_map/ppermute | solution.py:691
  38.5 5.8 %copy-start.6 = (bf16[512,256]{1,0:T(8,128)(2,1)S(1)}, bf16[512,256]{1,0:T(8,128)(2,1)}, u32[]{:S(2)}) copy-start(bf16[512,256]{1,0:T(8,128)(2,1)} %get-tuple-element.89.suf_ref) | copy-start | bytes 786436
  40.5 7.5 %collective-permute-start.8 = (f32[2,128,128]{2,1,0:T(8,128)S(1)}, f32[2,128,128]{2,1,0:T(8,128)S(1)}, u32[]{:S(2)}, u32[]{:S(2)}) collective-permute-start(f32[2,128,128]{2,1,0:T(8,128)S(1)} %get-tuple-element.110), channel_id=1, source_target_pairs={{0,1},{1,2},{2,3},{3,0},{4,5},{5,6},{6,7},{7,4},{8,9},{9,10},{10,1... | collective-permute-start | bytes 393224 | tf_op jit(solution)/shard_map/ppermute | solution.py:695
  41.8 10.9 %collective-permute-start.9 = (f32[2,128,128]{2,1,0:T(8,128)S(1)}, f32[2,128,128]{2,1,0:T(8,128)S(1)}, u32[]{:S(2)}, u32[]{:S(2)}) collective-permute-start(f32[2,128,128]{2,1,0:T(8,128)S(1)} %get-tuple-element.111), channel_id=1, source_target_pairs={{0,2},{1,3},{2,0},{3,1},{4,6},{5,7},{6,4},{7,5},{8,10},{9,11},{10,... | collective-permute-start | bytes 393224 | tf_op jit(solution)/shard_map/ppermute | solution.py:695
  42.9 12.3 %collective-permute-start.10 = (f32[2,128,128]{2,1,0:T(8,128)S(1)}, f32[2,128,128]{2,1,0:T(8,128)S(1)}, u32[]{:S(2)}, u32[]{:S(2)}) collective-permute-start(f32[2,128,128]{2,1,0:T(8,128)S(1)} %get-tuple-element.112), channel_id=1, source_target_pairs={{0,3},{1,0},{2,1},{3,2},{4,7},{5,4},{6,5},{7,6},{8,11},{9,8},{10,9... | collective-permute-start | bytes 393224 | tf_op jit(solution)/shard_map/ppermute | solution.py:695

commit v12 on v10

--- a/solution.py
+++ b/solution.py
@@ -13,6 +13,7 @@
 TILE = 256
 WIDE = 512
 EXTRA = 8
+PARTS = 4
 LANES = 128
 CORE, OTHER = range(2)
 PARAMS = pltpu.CompilerParams(vmem_limit_bytes=24 * 1024 * 1024)
@@ -139,25 +140,37 @@
 
 
 def other_kernel(
-    heads, x_ref, dy_ref, b_ref, c_ref, decays_ref, out_ref, factor_ref, x_buf, dy_buf, out_buf, bt_ref, ct_ref, arrived, sent
+    heads, x_ref, dy_ref, b_ref, c_ref, decays_ref, out_ref, factor_ref,
+    x_buf, dy_buf, out_buf, b_buf, c_buf, decays_buf, bt_ref, ct_ref, arrived, small, sent,
 ):
-    count, _, tile = x_buf.shape
-    base = place(OTHER) * count
+    local, width = x_buf.shape
+    count, _, _, tile = out_buf.shape
+    smalls = [
+        pltpu.make_async_copy(source, buf, small.at[i])
+        for i, (source, buf) in enumerate(((decays_ref, decays_buf), (b_ref, b_buf), (c_ref, c_buf)))
+    ]
+    for load in smalls:
+        load.start()
+    columns = pl.ds(pl.multiple_of(place(OTHER) * width, width), width)
     loads = []
-    for k in range(count):
-        columns = pl.ds(pl.multiple_of((base + k) * tile, tile), tile)
-        for i, (source, buf) in enumerate(((x_ref, x_buf), (dy_ref, dy_buf))):
-            loads.append(pltpu.make_async_copy(source.at[:, columns], buf.at[k], arrived.at[i, k]))
+    for i, (source, buf) in enumerate(((x_ref, x_buf), (dy_ref, dy_buf))):
+        for k in range(PARTS):
+            rows = pl.ds(k * (local // PARTS), local // PARTS)
+            loads.append(pltpu.make_async_copy(source.at[rows, columns], buf.at[rows, :], arrived.at[i, k]))
             loads[-1].start()
-    bt_ref[...] = transposed(b_ref[...])
-    ct_ref[...] = transposed(c_ref[...])
-    device_factors(decays_ref[...], factor_ref)
+    smalls[0].wait()
+    device_factors(decays_buf[...], factor_ref)
+    smalls[1].wait()
+    smalls[2].wait()
+    bt_ref[...] = transposed(b_buf[...])
+    ct_ref[...] = transposed(c_buf[...])
+    for load in loads:
+        load.wait()
     stores = []
     for k in range(count):
-        loads[2 * k].wait()
-        loads[2 * k + 1].wait()
-        first = (base + k) * (tile // P_SIZE)
-        tile_totals(heads, first, x_buf[k], dy_buf[k], bt_ref, ct_ref, factor_ref, out_buf.at[k])
+        first = (place(OTHER) * count + k) * (tile // P_SIZE)
+        x, dy = x_buf[:, k * tile : (k + 1) * tile], dy_buf[:, k * tile : (k + 1) * tile]
+        tile_totals(heads, first, x, dy, bt_ref, ct_ref, factor_ref, out_buf.at[k])
         stores.append(pltpu.make_async_copy(out_buf.at[k], out_ref.at[:, :, pl.ds(k * tile, tile)], sent.at[k]))
         stores[-1].start()
     for store in stores:
@@ -166,23 +179,27 @@
 
 def other_totals(x, dy, b, c, decays):
     local, width = x.shape
-    count = width // 2 // TILE
+    tile = min(WIDE, width // 2)
+    count = width // 2 // tile
     anywhere = pl.BlockSpec(memory_space=pl.ANY)
-    whole = lambda a: pl.BlockSpec(a.shape, lambda j: (0, 0))
     factor = jax.ShapeDtypeStruct((local, 2 * LANES), BF16)
     return pl.pallas_call(
         functools.partial(other_kernel, width // P_SIZE),
         grid=(1,),
-        in_specs=[anywhere, anywhere, whole(b), whole(c), whole(decays)],
-        out_specs=[anywhere, whole(factor)],
+        in_specs=[anywhere] * 5,
+        out_specs=[anywhere, pl.BlockSpec(factor.shape, lambda j: (0, 0))],
         out_shape=[jax.ShapeDtypeStruct((2, N + EXTRA, width // 2), F32), factor],
         scratch_shapes=[
-            pltpu.VMEM((count, local, TILE), BF16),
-            pltpu.VMEM((count, local, TILE), BF16),
-            pltpu.VMEM((count, 2, N + EXTRA, TILE), F32),
+            pltpu.VMEM((local, width // 2), BF16),
+            pltpu.VMEM((local, width // 2), BF16),
+            pltpu.VMEM((count, 2, N + EXTRA, tile), F32),
+            pltpu.VMEM(b.shape, BF16),
+            pltpu.VMEM(c.shape, BF16),
+            pltpu.VMEM(decays.shape, F32),
             pltpu.VMEM((N, local), BF16),
             pltpu.VMEM((N, local), BF16),
-            pltpu.SemaphoreType.DMA((2, count)),
+            pltpu.SemaphoreType.DMA((2, PARTS)),
+            pltpu.SemaphoreType.DMA((3,)),
             pltpu.SemaphoreType.DMA((count,)),
         ],
         compiler_params=FIRST,

time: 54.6 us -> 53.4 us (0.978)
  Pallas kernels: 32.5 us -> 31.2 us
    pallas_call x1, Pallas kernels: 6.33 us -> 5.1 us  [other_totals(): pl.pallas_call(functools.partial(other_kernel, width // P_SIZE), grid=(1,...]
  transfers between devices with their start and end apart: 11 -> 11, of which waited for: 4 -> 4; matrix products, arithmetic and copies ran while one was open for 0% -> 0% of each run, Pallas kernels for 42% -> 43%
where the time goes in v12:
time: 53.4 us; the launch traced here: 52.8 us
  Pallas kernels  31.2 us (58%)
  starting transfers between devices  11 us (21%)
  waiting for transfers between devices  8.8 us (16%)
  local copies, waits for them, and re-layouts  0.97 us (2%)
  between operations  0.81 us (2%)
    pallas_call x2, Pallas kernels, local_part(): pl.pallas_call(functools.partial(local_kernel, first_tile, before is not...  14.8 us
    ppermute x3, waiting for transfers between devices, turned(): lax.ppermute(v, axis, [(i, (i + by) % length) for i in range(length)])  7.22 us
    ppermute x6, starting transfers between devices, crossed(): return lax.ppermute(v, 'seq', [(i, i ^ bit) for i in range(length)])  5.49 us
    pallas_call x1, Pallas kernels, other_totals(): pl.pallas_call(functools.partial(other_kernel, width // P_SIZE), grid=(1,...  5.1 us
    pallas_call x2, Pallas kernels, map_terms(): pl.pallas_call(functools.partial(map_kernel, count, ranks), grid=(count,)...  3.97 us
    ppermute x3, starting transfers between devices, turned(): lax.ppermute(v, axis, [(i, (i + by) % length) for i in range(length)])  3.8 us
    pallas_call x1, Pallas kernels, input_terms(): pl.pallas_call(functools.partial(input_kernel, width // P_SIZE, count), g...  3.69 us
    pallas_call x1, Pallas kernels, own_totals(): pl.pallas_call(functools.partial(own_kernel, width // P_SIZE, count), gri...  2.29 us
  transfers between devices with their start and end apart: 11, of which 4 were waited for; matrix products, arithmetic and copies ran while one was open for 0% of the time, Pallas kernels for 43%

profile of v12, /device:TPU:11, one launch (start us, length us, event | category | flops | bytes accessed | tf_op | source)
XLA Modules:
  0.0 52.8 jit_solution(6888980926697531043)
XLA Ops:
  0.7 5.1 %other_totals.1 = (f32[2,136,1024]{2,1,0:T(8,128)}, bf16[512,256]{1,0:T(8,128)(2,1)}) custom-call(bf16[512,2048]{1,0:T(8,128)(2,1)} %refs_0_.3, bf16[512,2048]{1,0:T(8,128)(2,1)} %refs_1_.3, bf16[512,128]{1,0:T(8,128)(2,1)} %b_ref.5, bf16[512,128]{1,0:T(8,128)(2,1)} %refs_3_.3, f32[32,512]{1,0:T(8,128)} %refs_4_.3), custom_call_target="tpu_custom_call" | custom-call | flops 536870912 | bytes 4194304 | tf_op jit(solution)/shard_map/other_totals/pallas_call | solution.py:186
  5.8 0.7 %collective-permute-start = (f32[2,136,1024]{2,1,0:T(8,128)}, f32[2,136,1024]{2,1,0:T(8,128)S(1)}, u32[]{:S(2)}, u32[]{:S(2)}) collective-permute-start(f32[2,136,1024]{2,1,0:T(8,128)} %get-tuple-element.59), channel_id=1, source_target_pairs={{0,4},{4,0},{8,12},{12,8},{16,20},{20,16},{24,28},{28,24},{1,5},{5... | collective-permute-start | bytes 3342344 | tf_op jit(solution)/shard_map/ppermute | solution.py:703
  6.5 0.9 %copy-done.4 = bf16[512,256]{1,0:T(8,128)(2,1)S(1)} copy-done((bf16[512,256]{1,0:T(8,128)(2,1)S(1)}, bf16[512,256]{1,0:T(8,128)(2,1)}, u32[]{:S(2)}) %copy-start.4) | copy-done | bytes 262168
  7.5 2.3 %own_totals.1.mine_ref = f32[2,136,1024]{2,1,0:T(8,128)S(1)} custom-call(bf16[512,2048]{1,0:T(8,128)(2,1)S(1)} %copy-done, bf16[512,2048]{1,0:T(8,128)(2,1)S(1)} %copy-done.1, bf16[512,128]{1,0:T(8,128)(2,1)S(1)} %copy-done.2, bf16[512,128]{1,0:T(8,128)(2,1)S(1)} %copy-done.3, bf16[512,256]{1,0:T(8,128)(2,1)S(1)} %copy-done.4), custom_call_target="tpu_custom_call" | custom-call | flops 536870912 | bytes 4194304 | tf_op jit(solution)/shard_map/own_totals/pallas_call | solution.py:229
  10.0 0.3 collective-permute-start.1
  10.4 1.3 %collective-permute-start.2 = (f32[128,512]{1,0:T(8,128)S(1)}, f32[128,512]{1,0:T(8,128)S(1)}, u32[]{:S(2)}, u32[]{:S(2)}) collective-permute-start(f32[128,512]{1,0:T(8,128)S(1)} %get-tuple-element.61), channel_id=1, source_target_pairs={{0,16},{4,20},{8,24},{12,28},{16,0},{20,4},{24,8},{28,12},{1,17},{... | collective-permute-start | bytes 786440 | tf_op jit(solution)/shard_map/ppermute | solution.py:327
  11.6 1.2 %collective-permute-start.3 = (f32[8,512]{1,0:T(8,128)S(1)}, f32[8,512]{1,0:T(8,128)S(1)}, u32[]{:S(2)}, u32[]{:S(2)}) collective-permute-start(f32[8,512]{1,0:T(8,128)S(1)} %get-tuple-element.62), channel_id=1, source_target_pairs={{0,24},{4,28},{8,16},{12,20},{16,8},{20,12},{24,0},{28,4},{1,25},{... | collective-permute-start | bytes 49160 | tf_op jit(solution)/shard_map/ppermute | solution.py:327
  13.0 7.4 %local_part.2 = (f32[512,2048]{1,0:T(8,128)S(1)}, bf16[2,2,512,2048]{3,2,1,0:T(8,128)(2,1)S(1)}, f32[512,128]{1,0:T(8,128)S(1)}, f32[512,128]{1,0:T(8,128)S(1)}) custom-call(bf16[512,2048]{1,0:T(8,128)(2,1)S(1)} %copy-done, bf16[512,2048]{1,0:T(8,128)(2,1)S(1)} %copy-done.1, bf16[512,128]{1,0:T(8,128)(2,1)S(1)} %copy-done.2, bf16[512,128]{1,0:T(8,128)(2,1)S(1)} %copy-done.3, ...), custom_call_target="tpu_custom_call" | custom-call | flops 2684354560 | bytes 4194304 | tf_op jit(solution)/shard_map/local_part/pallas_call | solution.py:595
  20.6 1.3 %collective-permute-start.5 = (f32[128,512]{1,0:T(8,128)S(1)}, f32[128,512]{1,0:T(8,128)S(1)}, u32[]{:S(2)}, u32[]{:S(2)}) collective-permute-start(f32[128,512]{1,0:T(8,128)S(1)} %get-tuple-element.76), channel_id=1, source_target_pairs={{0,16},{4,20},{8,24},{12,28},{16,0},{20,4},{24,8},{28,12},{1,17},{... | collective-permute-start | bytes 786440 | tf_op jit(solution)/shard_map/ppermute | solution.py:327
  21.9 1.2 %collective-permute-start.6 = (f32[128,512]{1,0:T(8,128)S(1)}, f32[128,512]{1,0:T(8,128)S(1)}, u32[]{:S(2)}, u32[]{:S(2)}) collective-permute-start(f32[128,512]{1,0:T(8,128)S(1)} %get-tuple-element.77), channel_id=1, source_target_pairs={{0,8},{4,12},{8,0},{12,4},{16,24},{20,28},{24,16},{28,20},{1,9},{5... | collective-permute-start | bytes 786440 | tf_op jit(solution)/shard_map/ppermute | solution.py:327
  23.1 1.2 %collective-permute-done.4.later_ref = f32[128,512]{1,0:T(8,128)S(1)} collective-permute-done((f32[128,512]{1,0:T(8,128)S(1)}, f32[128,512]{1,0:T(8,128)S(1)}, u32[]{:S(2)}, u32[]{:S(2)}) %collective-permute-start.4) | collective-permute-done | bytes 262176 | tf_op jit(solution)/shard_map/ppermute | solution.py:327
  24.3 7.4 %local_part.3 = (f32[512,2048]{1,0:T(8,128)S(1)}, bf16[2,2,512,2048]{3,2,1,0:T(8,128)(2,1)S(1)}, f32[512,128]{1,0:T(8,128)S(1)}, f32[512,128]{1,0:T(8,128)S(1)}) custom-call(bf16[512,2048]{1,0:T(8,128)(2,1)S(1)} %copy-done, bf16[512,2048]{1,0:T(8,128)(2,1)S(1)} %copy-done.1, ...), custom_call_target="tpu_custom_call", output_to_operand_aliasing={{0}: (7, {}), {1}: (8, {})} | custom-call | flops 2684354560 | bytes 4194304 | tf_op jit(solution)/shard_map/local_part/pallas_call | solution.py:595
  31.8 0.4 carried_in.1
  32.1 1.0 %collective-permute-start.7 = (f32[2,128,1024]{2,1,0:T(8,128)S(1)}, f32[2,128,1024]{2,1,0:T(8,128)S(1)}, u32[]{:S(2)}, u32[]{:S(2)}) collective-permute-start(f32[2,128,1024]{2,1,0:T(8,128)S(1)} %get-tuple-element.95), channel_id=1, source_target_pairs={{0,4},{4,0},{8,12},{12,8},{16,20},{20,16},{24,28},{28,24},{1,5},{5... | collective-permute-start | bytes 3145736 | tf_op jit(solution)/shard_map/ppermute | solution.py:703
  33.1 2.0 %map_terms.2 = (f32[512,128]{1,0:T(8,128)S(1)}, f32[512,128]{1,0:T(8,128)S(1)}) custom-call(bf16[2,2,512,2048]{3,2,1,0:T(8,128)(2,1)S(1)} %get-tuple-element.96.scaled_ref, f32[2,128,1024]{2,1,0:T(8,128)S(1)} %get-tuple-element.105.carry_ref.own_ref, f32[512,128]{1,0:T(8,128)S(1)} %get-tuple-element.97.out_before_ref, ...), custom_call_target="tpu_custom_call" | custom-call | flops 805306368 | bytes 4194304 | tf_op jit(solution)/shard_map/map_terms/pallas_call | solution.py:652
  35.1 0.3 collective-permute-done.7.carry_ref.other_ref
  35.4 2.0 %map_terms.3 = (f32[2,128,128]{2,1,0:T(8,128)S(1)}, f32[2,128,128]{2,1,0:T(8,128)S(1)}, f32[2,128,128]{2,1,0:T(8,128)S(1)}, f32[2,128,128]{2,1,0:T(8,128)S(1)}) custom-call(bf16[2,2,512,2048]{3,2,1,0:T(8,128)(2,1)S(1)} %get-tuple-element.96.scaled_ref, f32[2,128,1024]{2,1,0:T(8,128)S(1)} %collective-permute-done.7.carry_ref.other_ref, ...), custom_call_target="tpu_custom_call" | custom-call | flops 805306368 | bytes 4194304 | tf_op jit(solution)/shard_map/map_terms/pallas_call | solution.py:652
  37.5 1.4 %collective-permute-start.8 = (f32[2,128,128]{2,1,0:T(8,128)S(1)}, f32[2,128,128]{2,1,0:T(8,128)S(1)}, u32[]{:S(2)}, u32[]{:S(2)}) collective-permute-start(f32[2,128,128]{2,1,0:T(8,128)S(1)} %get-tuple-element.108), channel_id=1, source_target_pairs={{0,1},{1,2},{2,3},{3,0},{4,5},{5,6},{6,7},{7,4},{8,9},{9,10},{10,1... | collective-permute-start | bytes 393224 | tf_op jit(solution)/shard_map/ppermute | solution.py:707
  38.8 1.0 %collective-permute-start.9 = (f32[2,128,128]{2,1,0:T(8,128)S(1)}, f32[2,128,128]{2,1,0:T(8,128)S(1)}, u32[]{:S(2)}, u32[]{:S(2)}) collective-permute-start(f32[2,128,128]{2,1,0:T(8,128)S(1)} %get-tuple-element.109), channel_id=1, source_target_pairs={{0,2},{1,3},{2,0},{3,1},{4,6},{5,7},{6,4},{7,5},{8,10},{9,11},{10,... | collective-permute-start | bytes 393224 | tf_op jit(solution)/shard_map/ppermute | solution.py:707
  39.9 1.4 %collective-permute-start.10 = (f32[2,128,128]{2,1,0:T(8,128)S(1)}, f32[2,128,128]{2,1,0:T(8,128)S(1)}, u32[]{:S(2)}, u32[]{:S(2)}) collective-permute-start(f32[2,128,128]{2,1,0:T(8,128)S(1)} %get-tuple-element.110), channel_id=1, source_target_pairs={{0,3},{1,0},{2,1},{3,2},{4,7},{5,4},{6,5},{7,6},{8,11},{9,8},{10,9... | collective-permute-start | bytes 393224 | tf_op jit(solution)/shard_map/ppermute | solution.py:707
  41.3 3.7 %input_terms.1 = bf16[512,2048]{1,0:T(8,128)(2,1)} custom-call(f32[512,2048]{1,0:T(8,128)S(1)} %get-tuple-element.87.part_ref, bf16[512,256]{1,0:T(8,128)(2,1)S(1)} %copy-done.5, bf16[512,128]{1,0:T(8,128)(2,1)S(1)} %copy-done.2, f32[2,128,1024]{2,1,0:T(8,128)S(1)} %get-tuple-element.105.carry_ref.own_ref, ...), custom_call_target="tpu_custom_call" | custom-call | flops 536870912 | bytes 8388608 | tf_op jit(solution)/shard_map/input_terms/pallas_call | solution.py:684
  44.9 4.8 %collective-permute-done.9.refs_2_ = f32[2,128,128]{2,1,0:T(8,128)S(1)} collective-permute-done((f32[2,128,128]{2,1,0:T(8,128)S(1)}, f32[2,128,128]{2,1,0:T(8,128)S(1)}, u32[]{:S(2)}, u32[]{:S(2)}) %collective-permute-start.9) | collective-permute-done | bytes 131104 | tf_op jit(solution)/shard_map/ppermute | solution.py:707
  49.8 2.4 %collective-permute-done.10.refs_3_ = f32[2,128,128]{2,1,0:T(8,128)S(1)} collective-permute-done((f32[2,128,128]{2,1,0:T(8,128)S(1)}, f32[2,128,128]{2,1,0:T(8,128)S(1)}, u32[]{:S(2)}, u32[]{:S(2)}) %collective-permute-start.10) | collective-permute-done | bytes 131104 | tf_op jit(solution)/shard_map/ppermute | solution.py:707
  52.2 0.7 %head_sums.1 = (f32[128,128]{1,0:T(8,128)}, f32[128,128]{1,0:T(8,128)}) custom-call(f32[2,128,128]{2,1,0:T(8,128)S(1)} %get-tuple-element.107.refs_0_, f32[2,128,128]{2,1,0:T(8,128)S(1)} %collective-permute-done.8.refs_1_, f32[2,128,128]{2,1,0:T(8,128)S(1)} %collective-permute-done.9.refs_2_, f32[2,128,128]{2,1,0:T(8,128)S(1)} %collective-permute-done.10.refs_3_), custom_call_target="tpu_custom_call" | custom-call | flops 1048576 | bytes 524288 | tf_op jit(solution)/shard_map/head_sums/pallas_call | solution.py:314
  (23 shorter events, 0.6 us)
Async XLA Ops:
  0.6 5.9 %copy-start.2 = (bf16[512,128]{1,0:T(8,128)(2,1)S(1)}, bf16[512,128]{1,0:T(8,128)(2,1)}, u32[]{:S(2)}) copy-start(bf16[512,128]{1,0:T(8,128)(2,1)} %b_ref.5) | copy-start | bytes 393220
  0.6 5.9 %copy-start.3 = (bf16[512,128]{1,0:T(8,128)(2,1)S(1)}, bf16[512,128]{1,0:T(8,128)(2,1)}, u32[]{:S(2)}) copy-start(bf16[512,128]{1,0:T(8,128)(2,1)} %refs_3_.3) | copy-start | bytes 393220
  0.7 5.9 %copy-start.1 = (bf16[512,2048]{1,0:T(8,128)(2,1)S(1)}, bf16[512,2048]{1,0:T(8,128)(2,1)}, u32[]{:S(2)}) copy-start(bf16[512,2048]{1,0:T(8,128)(2,1)} %refs_1_.3) | copy-start | bytes 6291460
  0.7 5.9 %copy-start = (bf16[512,2048]{1,0:T(8,128)(2,1)S(1)}, bf16[512,2048]{1,0:T(8,128)(2,1)}, u32[]{:S(2)}) copy-start(bf16[512,2048]{1,0:T(8,128)(2,1)} %refs_0_.3) | copy-start | bytes 6291460
  5.8 4.0 %collective-permute-start = (f32[2,136,1024]{2,1,0:T(8,128)}, f32[2,136,1024]{2,1,0:T(8,128)S(1)}, u32[]{:S(2)}, u32[]{:S(2)}) collective-permute-start(f32[2,136,1024]{2,1,0:T(8,128)} %get-tuple-element.59), channel_id=1, source_target_pairs={{0,4},{4,0},{8,12},{12,8},{16,20},{20,16},{24,28},{28,24},{1,5},{5... | collective-permute-start | bytes 3342344 | tf_op jit(solution)/shard_map/ppermute | solution.py:703
  6.5 1.0 %copy-start.4 = (bf16[512,256]{1,0:T(8,128)(2,1)S(1)}, bf16[512,256]{1,0:T(8,128)(2,1)}, u32[]{:S(2)}) copy-start(bf16[512,256]{1,0:T(8,128)(2,1)} %get-tuple-element.58.factor_ref.suf_ref) | copy-start | bytes 786436
  9.8 3.2 %copy-start.6 = (f32[32,512]{1,0:T(8,128)S(1)}, f32[32,512]{1,0:T(8,128)}, u32[]{:S(2)}) copy-start(f32[32,512]{1,0:T(8,128)} %refs_4_.3) | copy-start | bytes 196612
  10.0 10.4 %collective-permute-start.1 = (f32[136,512]{1,0:T(8,128)S(1)}, f32[136,512]{1,0:T(8,128)S(1)}, u32[]{:S(2)}, u32[]{:S(2)}) collective-permute-start(f32[136,512]{1,0:T(8,128)S(1)} %get-tuple-element.60.own_ref), channel_id=1, source_target_pairs={{0,8},{4,12},{8,0},{12,4},{16,24},{20,28},{24,16},{28,20},{1,9},{5... | collective-permute-start | bytes 835592 | tf_op jit(solution)/shard_map/ppermute | solution.py:327
  10.4 10.1 %collective-permute-start.2 = (f32[128,512]{1,0:T(8,128)S(1)}, f32[128,512]{1,0:T(8,128)S(1)}, u32[]{:S(2)}, u32[]{:S(2)}) collective-permute-start(f32[128,512]{1,0:T(8,128)S(1)} %get-tuple-element.61), channel_id=1, source_target_pairs={{0,16},{4,20},{8,24},{12,28},{16,0},{20,4},{24,8},{28,12},{1,17},{... | collective-permute-start | bytes 786440 | tf_op jit(solution)/shard_map/ppermute | solution.py:327
  11.6 8.8 %collective-permute-start.3 = (f32[8,512]{1,0:T(8,128)S(1)}, f32[8,512]{1,0:T(8,128)S(1)}, u32[]{:S(2)}, u32[]{:S(2)}) collective-permute-start(f32[8,512]{1,0:T(8,128)S(1)} %get-tuple-element.62), channel_id=1, source_target_pairs={{0,24},{4,28},{8,16},{12,20},{16,8},{20,12},{24,0},{28,4},{1,25},{... | collective-permute-start | bytes 49160 | tf_op jit(solution)/shard_map/ppermute | solution.py:327
  12.8 11.6 %collective-permute-start.4 = (f32[128,512]{1,0:T(8,128)S(1)}, f32[128,512]{1,0:T(8,128)S(1)}, u32[]{:S(2)}, u32[]{:S(2)}) collective-permute-start(f32[128,512]{1,0:T(8,128)S(1)} %get-tuple-element.74), channel_id=1, source_target_pairs={{0,8},{4,12},{8,0},{12,4},{16,24},{20,28},{24,16},{28,20},{1,9},{5... | collective-permute-start | bytes 786440 | tf_op jit(solution)/shard_map/ppermute | solution.py:327
  20.6 11.2 %collective-permute-start.5 = (f32[128,512]{1,0:T(8,128)S(1)}, f32[128,512]{1,0:T(8,128)S(1)}, u32[]{:S(2)}, u32[]{:S(2)}) collective-permute-start(f32[128,512]{1,0:T(8,128)S(1)} %get-tuple-element.76), channel_id=1, source_target_pairs={{0,16},{4,20},{8,24},{12,28},{16,0},{20,4},{24,8},{28,12},{1,17},{... | collective-permute-start | bytes 786440 | tf_op jit(solution)/shard_map/ppermute | solution.py:327
  21.9 9.9 %collective-permute-start.6 = (f32[128,512]{1,0:T(8,128)S(1)}, f32[128,512]{1,0:T(8,128)S(1)}, u32[]{:S(2)}, u32[]{:S(2)}) collective-permute-start(f32[128,512]{1,0:T(8,128)S(1)} %get-tuple-element.77), channel_id=1, source_target_pairs={{0,8},{4,12},{8,0},{12,4},{16,24},{20,28},{24,16},{28,20},{1,9},{5... | collective-permute-start | bytes 786440 | tf_op jit(solution)/shard_map/ppermute | solution.py:327
  32.1 3.3 %collective-permute-start.7 = (f32[2,128,1024]{2,1,0:T(8,128)S(1)}, f32[2,128,1024]{2,1,0:T(8,128)S(1)}, u32[]{:S(2)}, u32[]{:S(2)}) collective-permute-start(f32[2,128,1024]{2,1,0:T(8,128)S(1)} %get-tuple-element.95), channel_id=1, source_target_pairs={{0,4},{4,0},{8,12},{12,8},{16,20},{20,16},{24,28},{28,24},{1,5},{5... | collective-permute-start | bytes 3145736 | tf_op jit(solution)/shard_map/ppermute | solution.py:703
  35.4 5.8 %copy-start.5 = (bf16[512,256]{1,0:T(8,128)(2,1)S(1)}, bf16[512,256]{1,0:T(8,128)(2,1)}, u32[]{:S(2)}) copy-start(bf16[512,256]{1,0:T(8,128)(2,1)} %get-tuple-element.58.factor_ref.suf_ref) | copy-start | bytes 786436
  37.5 7.5 %collective-permute-start.8 = (f32[2,128,128]{2,1,0:T(8,128)S(1)}, f32[2,128,128]{2,1,0:T(8,128)S(1)}, u32[]{:S(2)}, u32[]{:S(2)}) collective-permute-start(f32[2,128,128]{2,1,0:T(8,128)S(1)} %get-tuple-element.108), channel_id=1, source_target_pairs={{0,1},{1,2},{2,3},{3,0},{4,5},{5,6},{6,7},{7,4},{8,9},{9,10},{10,1... | collective-permute-start | bytes 393224 | tf_op jit(solution)/shard_map/ppermute | solution.py:707
  38.8 10.9 %collective-permute-start.9 = (f32[2,128,128]{2,1,0:T(8,128)S(1)}, f32[2,128,128]{2,1,0:T(8,128)S(1)}, u32[]{:S(2)}, u32[]{:S(2)}) collective-permute-start(f32[2,128,128]{2,1,0:T(8,128)S(1)} %get-tuple-element.109), channel_id=1, source_target_pairs={{0,2},{1,3},{2,0},{3,1},{4,6},{5,7},{6,4},{7,5},{8,10},{9,11},{10,... | collective-permute-start | bytes 393224 | tf_op jit(solution)/shard_map/ppermute | solution.py:707
  39.9 12.3 %collective-permute-start.10 = (f32[2,128,128]{2,1,0:T(8,128)S(1)}, f32[2,128,128]{2,1,0:T(8,128)S(1)}, u32[]{:S(2)}, u32[]{:S(2)}) collective-permute-start(f32[2,128,128]{2,1,0:T(8,128)S(1)} %get-tuple-element.110), channel_id=1, source_target_pairs={{0,3},{1,0},{2,1},{3,2},{4,7},{5,4},{6,5},{7,6},{8,11},{9,8},{10,9... | collective-permute-start | bytes 393224 | tf_op jit(solution)/shard_map/ppermute | solution.py:707

commit v13 on v12

--- a/solution.py
+++ b/solution.py
@@ -208,19 +208,20 @@
     )(x, dy, b, c, decays)
 
 
-def own_kernel(heads, count, x_ref, dy_ref, b_ref, c_ref, factor_ref, out_ref, bt_ref, ct_ref):
+def own_kernel(heads, count, x_ref, dy_ref, b_ref, c_ref, decays_ref, out_ref, bt_ref, ct_ref, factor_ref):
     step = pl.program_id(0)
 
     @pl.when(step == 0)
     def _():
         bt_ref[...] = transposed(b_ref[...])
         ct_ref[...] = transposed(c_ref[...])
+        device_factors(decays_ref[...], factor_ref)
 
     first = (place(CORE) * count + step) * (x_ref.shape[1] // P_SIZE)
     tile_totals(heads, first, x_ref[...], dy_ref[...], bt_ref, ct_ref, factor_ref, out_ref)
 
 
-def own_totals(x, dy, b, c, factors):
+def own_totals(x, dy, b, c, decays):
     local, width = x.shape
     tile = min(WIDE, width // 2)
     count = width // 2 // tile
@@ -229,14 +230,18 @@
     return pl.pallas_call(
         functools.partial(own_kernel, width // P_SIZE, count),
         grid=(count,),
-        in_specs=[column, column, whole(b), whole(c), whole(factors)],
+        in_specs=[column, column, whole(b), whole(c), whole(decays)],
         out_specs=pl.BlockSpec((2, N + EXTRA, tile), lambda j: (0, 0, j)),
-        scratch_shapes=[pltpu.VMEM((N, local), BF16), pltpu.VMEM((N, local), BF16)],
+        scratch_shapes=[
+            pltpu.VMEM((N, local), BF16),
+            pltpu.VMEM((N, local), BF16),
+            pltpu.VMEM((local, 2 * LANES), BF16),
+        ],
         out_shape=jax.ShapeDtypeStruct((2, N + EXTRA, width // 2), F32),
         compiler_params=PARAMS,
         name="own_totals",
         cost_estimate=pl.CostEstimate(flops=8 * local * N * width // 2, bytes_accessed=4 * local * width, transcendentals=0),
-    )(x, dy, b, c, factors)
+    )(x, dy, b, c, decays)
 
 
 def ordered(core, mine, recv):
@@ -713,7 +718,7 @@
     args = mixer_input, output_grad, input_map, output_map
     sent, factors = other_totals(*args, decays)
     recv = swap_cores(sent, length)
-    mine = own_totals(*args, factors)
+    mine = own_totals(*args, decays)
     tiles = mixer_input.shape[1] // WIDE
     if chips == 4:
         ahead = tiles // 2

time: 53.4 us -> 53 us (level)
  local copies, waits for them, and re-layouts: 0.97 us -> 0.02 us
    unnamed x14 -> x12, local copies, waits for them, and re-layouts: 0.97 us -> 0.02 us
  transfers between devices with their start and end apart: 11 -> 11, of which waited for: 4 -> 4; matrix products, arithmetic and copies ran while one was open for 0% -> 0% of each run, Pallas kernels for 43% -> 44%
where the time goes in v13:
time: 53 us; the launch traced here: 52.2 us
  Pallas kernels  31.6 us (60%)
  starting transfers between devices  11.4 us (22%)
  waiting for transfers between devices  8.48 us (16%)
  between operations  0.81 us (2%)
    pallas_call x2, Pallas kernels, local_part(): pl.pallas_call(functools.partial(local_kernel, first_tile, before is not...  14.8 us
    ppermute x3, waiting for transfers between devices, turned(): lax.ppermute(v, axis, [(i, (i + by) % length) for i in range(length)])  7.22 us
    ppermute x6, starting transfers between devices, crossed(): return lax.ppermute(v, 'seq', [(i, i ^ bit) for i in range(length)])  5.49 us
    pallas_call x1, Pallas kernels, other_totals(): pl.pallas_call(functools.partial(other_kernel, width // P_SIZE), grid=(1,...  5.1 us
    pallas_call x2, Pallas kernels, map_terms(): pl.pallas_call(functools.partial(map_kernel, count, ranks), grid=(count,)...  3.99 us
    ppermute x3, starting transfers between devices, turned(): lax.ppermute(v, axis, [(i, (i + by) % length) for i in range(length)])  3.83 us
    pallas_call x1, Pallas kernels, input_terms(): pl.pallas_call(functools.partial(input_kernel, width // P_SIZE, count), g...  3.69 us
    pallas_call x1, Pallas kernels, own_totals(): pl.pallas_call(functools.partial(own_kernel, width // P_SIZE, count), gri...  2.6 us
  transfers between devices with their start and end apart: 11, of which 4 were waited for; matrix products, arithmetic and copies ran while one was open for 0% of the time, Pallas kernels for 44%

profile of v13, /device:TPU:11, one launch (start us, length us, event | category | flops | bytes accessed | tf_op | source)
XLA Modules:
  0.0 52.2 jit_solution(14057674085480819222)
XLA Ops:
  0.7 5.1 %other_totals.1 = (f32[2,136,1024]{2,1,0:T(8,128)}, bf16[512,256]{1,0:T(8,128)(2,1)}) custom-call(bf16[512,2048]{1,0:T(8,128)(2,1)} %refs_0_.3, bf16[512,2048]{1,0:T(8,128)(2,1)} %refs_1_.3, bf16[512,128]{1,0:T(8,128)(2,1)} %b_ref.5, bf16[512,128]{1,0:T(8,128)(2,1)} %refs_3_.3, f32[32,512]{1,0:T(8,128)} %refs_4_.3), custom_call_target="tpu_custom_call" | custom-call | flops 536870912 | bytes 4194304 | tf_op jit(solution)/shard_map/other_totals/pallas_call | solution.py:186
  5.8 0.7 %collective-permute-start = (f32[2,136,1024]{2,1,0:T(8,128)}, f32[2,136,1024]{2,1,0:T(8,128)S(1)}, u32[]{:S(2)}, u32[]{:S(2)}) collective-permute-start(f32[2,136,1024]{2,1,0:T(8,128)} %get-tuple-element.58), channel_id=1, source_target_pairs={{0,4},{4,0},{8,12},{12,8},{16,20},{20,16},{24,28},{28,24},{1,5},{5... | collective-permute-start | bytes 3342344 | tf_op jit(solution)/shard_map/ppermute | solution.py:708
  6.5 2.6 %own_totals.1.mine_ref = f32[2,136,1024]{2,1,0:T(8,128)S(1)} custom-call(bf16[512,2048]{1,0:T(8,128)(2,1)S(1)} %copy-done, bf16[512,2048]{1,0:T(8,128)(2,1)S(1)} %copy-done.1, bf16[512,128]{1,0:T(8,128)(2,1)S(1)} %copy-done.2, bf16[512,128]{1,0:T(8,128)(2,1)S(1)} %copy-done.3, f32[32,512]{1,0:T(8,128)S(1)} %copy-done.4), custom_call_target="tpu_custom_call" | custom-call | flops 536870912 | bytes 4194304 | tf_op jit(solution)/shard_map/own_totals/pallas_call | solution.py:230
  9.4 0.3 collective-permute-start.1
  9.7 1.2 %collective-permute-start.2 = (f32[128,512]{1,0:T(8,128)S(1)}, f32[128,512]{1,0:T(8,128)S(1)}, u32[]{:S(2)}, u32[]{:S(2)}) collective-permute-start(f32[128,512]{1,0:T(8,128)S(1)} %get-tuple-element.60), channel_id=1, source_target_pairs={{0,16},{4,20},{8,24},{12,28},{16,0},{20,4},{24,8},{28,12},{1,17},{... | collective-permute-start | bytes 786440 | tf_op jit(solution)/shard_map/ppermute | solution.py:332
  11.0 1.1 %collective-permute-start.3 = (f32[8,512]{1,0:T(8,128)S(1)}, f32[8,512]{1,0:T(8,128)S(1)}, u32[]{:S(2)}, u32[]{:S(2)}) collective-permute-start(f32[8,512]{1,0:T(8,128)S(1)} %get-tuple-element.61), channel_id=1, source_target_pairs={{0,24},{4,28},{8,16},{12,20},{16,8},{20,12},{24,0},{28,4},{1,25},{... | collective-permute-start | bytes 49160 | tf_op jit(solution)/shard_map/ppermute | solution.py:332
  12.1 0.3 collective-permute-start.4
  12.4 7.4 %local_part.2 = (f32[512,2048]{1,0:T(8,128)S(1)}, bf16[2,2,512,2048]{3,2,1,0:T(8,128)(2,1)S(1)}, f32[512,128]{1,0:T(8,128)S(1)}, f32[512,128]{1,0:T(8,128)S(1)}) custom-call(bf16[512,2048]{1,0:T(8,128)(2,1)S(1)} %copy-done, bf16[512,2048]{1,0:T(8,128)(2,1)S(1)} %copy-done.1, bf16[512,128]{1,0:T(8,128)(2,1)S(1)} %copy-done.2, bf16[512,128]{1,0:T(8,128)(2,1)S(1)} %copy-done.3, ...), custom_call_target="tpu_custom_call" | custom-call | flops 2684354560 | bytes 4194304 | tf_op jit(solution)/shard_map/local_part/pallas_call | solution.py:600
  19.9 1.3 %collective-permute-start.5 = (f32[128,512]{1,0:T(8,128)S(1)}, f32[128,512]{1,0:T(8,128)S(1)}, u32[]{:S(2)}, u32[]{:S(2)}) collective-permute-start(f32[128,512]{1,0:T(8,128)S(1)} %get-tuple-element.75), channel_id=1, source_target_pairs={{0,16},{4,20},{8,24},{12,28},{16,0},{20,4},{24,8},{28,12},{1,17},{... | collective-permute-start | bytes 786440 | tf_op jit(solution)/shard_map/ppermute | solution.py:332
  21.2 1.2 %collective-permute-start.6 = (f32[128,512]{1,0:T(8,128)S(1)}, f32[128,512]{1,0:T(8,128)S(1)}, u32[]{:S(2)}, u32[]{:S(2)}) collective-permute-start(f32[128,512]{1,0:T(8,128)S(1)} %get-tuple-element.76), channel_id=1, source_target_pairs={{0,8},{4,12},{8,0},{12,4},{16,24},{20,28},{24,16},{28,20},{1,9},{5... | collective-permute-start | bytes 786440 | tf_op jit(solution)/shard_map/ppermute | solution.py:332
  22.4 0.9 %collective-permute-done.4.later_ref = f32[128,512]{1,0:T(8,128)S(1)} collective-permute-done((f32[128,512]{1,0:T(8,128)S(1)}, f32[128,512]{1,0:T(8,128)S(1)}, u32[]{:S(2)}, u32[]{:S(2)}) %collective-permute-start.4) | collective-permute-done | bytes 262176 | tf_op jit(solution)/shard_map/ppermute | solution.py:332
  23.4 7.4 %local_part.3 = (f32[512,2048]{1,0:T(8,128)S(1)}, bf16[2,2,512,2048]{3,2,1,0:T(8,128)(2,1)S(1)}, f32[512,128]{1,0:T(8,128)S(1)}, f32[512,128]{1,0:T(8,128)S(1)}) custom-call(bf16[512,2048]{1,0:T(8,128)(2,1)S(1)} %copy-done, bf16[512,2048]{1,0:T(8,128)(2,1)S(1)} %copy-done.1, ...), custom_call_target="tpu_custom_call", output_to_operand_aliasing={{0}: (7, {}), {1}: (8, {})} | custom-call | flops 2684354560 | bytes 4194304 | tf_op jit(solution)/shard_map/local_part/pallas_call | solution.py:600
  30.8 0.4 carried_in.1
  31.2 1.3 %collective-permute-start.7 = (f32[2,128,1024]{2,1,0:T(8,128)S(1)}, f32[2,128,1024]{2,1,0:T(8,128)S(1)}, u32[]{:S(2)}, u32[]{:S(2)}) collective-permute-start(f32[2,128,1024]{2,1,0:T(8,128)S(1)} %get-tuple-element.95), channel_id=1, source_target_pairs={{0,4},{4,0},{8,12},{12,8},{16,20},{20,16},{24,28},{28,24},{1,5},{5... | collective-permute-start | bytes 3145736 | tf_op jit(solution)/shard_map/ppermute | solution.py:708
  32.5 2.0 %map_terms.2 = (f32[512,128]{1,0:T(8,128)S(1)}, f32[512,128]{1,0:T(8,128)S(1)}) custom-call(bf16[2,2,512,2048]{3,2,1,0:T(8,128)(2,1)S(1)} %get-tuple-element.96.scaled_ref, f32[2,128,1024]{2,1,0:T(8,128)S(1)} %get-tuple-element.105.carry_ref.own_ref, f32[512,128]{1,0:T(8,128)S(1)} %get-tuple-element.97.out_before_ref, ...), custom_call_target="tpu_custom_call" | custom-call | flops 805306368 | bytes 4194304 | tf_op jit(solution)/shard_map/map_terms/pallas_call | solution.py:657
  34.5 0.3 collective-permute-done.7.carry_ref.other_ref
  34.8 2.0 %map_terms.3 = (f32[2,128,128]{2,1,0:T(8,128)S(1)}, f32[2,128,128]{2,1,0:T(8,128)S(1)}, f32[2,128,128]{2,1,0:T(8,128)S(1)}, f32[2,128,128]{2,1,0:T(8,128)S(1)}) custom-call(bf16[2,2,512,2048]{3,2,1,0:T(8,128)(2,1)S(1)} %get-tuple-element.96.scaled_ref, f32[2,128,1024]{2,1,0:T(8,128)S(1)} %collective-permute-done.7.carry_ref.other_ref, ...), custom_call_target="tpu_custom_call" | custom-call | flops 805306368 | bytes 4194304 | tf_op jit(solution)/shard_map/map_terms/pallas_call | solution.py:657
  36.8 1.4 %collective-permute-start.8 = (f32[2,128,128]{2,1,0:T(8,128)S(1)}, f32[2,128,128]{2,1,0:T(8,128)S(1)}, u32[]{:S(2)}, u32[]{:S(2)}) collective-permute-start(f32[2,128,128]{2,1,0:T(8,128)S(1)} %get-tuple-element.108), channel_id=1, source_target_pairs={{0,1},{1,2},{2,3},{3,0},{4,5},{5,6},{6,7},{7,4},{8,9},{9,10},{10,1... | collective-permute-start | bytes 393224 | tf_op jit(solution)/shard_map/ppermute | solution.py:712
  38.2 1.1 %collective-permute-start.9 = (f32[2,128,128]{2,1,0:T(8,128)S(1)}, f32[2,128,128]{2,1,0:T(8,128)S(1)}, u32[]{:S(2)}, u32[]{:S(2)}) collective-permute-start(f32[2,128,128]{2,1,0:T(8,128)S(1)} %get-tuple-element.109), channel_id=1, source_target_pairs={{0,2},{1,3},{2,0},{3,1},{4,6},{5,7},{6,4},{7,5},{8,10},{9,11},{10,... | collective-permute-start | bytes 393224 | tf_op jit(solution)/shard_map/ppermute | solution.py:712
  39.3 1.4 %collective-permute-start.10 = (f32[2,128,128]{2,1,0:T(8,128)S(1)}, f32[2,128,128]{2,1,0:T(8,128)S(1)}, u32[]{:S(2)}, u32[]{:S(2)}) collective-permute-start(f32[2,128,128]{2,1,0:T(8,128)S(1)} %get-tuple-element.110), channel_id=1, source_target_pairs={{0,3},{1,0},{2,1},{3,2},{4,7},{5,4},{6,5},{7,6},{8,11},{9,8},{10,9... | collective-permute-start | bytes 393224 | tf_op jit(solution)/shard_map/ppermute | solution.py:712
  40.6 3.7 %input_terms.1 = bf16[512,2048]{1,0:T(8,128)(2,1)} custom-call(f32[512,2048]{1,0:T(8,128)S(1)} %get-tuple-element.86.part_ref, bf16[512,256]{1,0:T(8,128)(2,1)S(1)} %copy-done.5, bf16[512,128]{1,0:T(8,128)(2,1)S(1)} %copy-done.2, f32[2,128,1024]{2,1,0:T(8,128)S(1)} %get-tuple-element.105.carry_ref.own_ref, ...), custom_call_target="tpu_custom_call" | custom-call | flops 536870912 | bytes 8388608 | tf_op jit(solution)/shard_map/input_terms/pallas_call | solution.py:689
  44.3 4.8 %collective-permute-done.9.refs_2_ = f32[2,128,128]{2,1,0:T(8,128)S(1)} collective-permute-done((f32[2,128,128]{2,1,0:T(8,128)S(1)}, f32[2,128,128]{2,1,0:T(8,128)S(1)}, u32[]{:S(2)}, u32[]{:S(2)}) %collective-permute-start.9) | collective-permute-done | bytes 131104 | tf_op jit(solution)/shard_map/ppermute | solution.py:712
  49.1 2.4 %collective-permute-done.10.refs_3_ = f32[2,128,128]{2,1,0:T(8,128)S(1)} collective-permute-done((f32[2,128,128]{2,1,0:T(8,128)S(1)}, f32[2,128,128]{2,1,0:T(8,128)S(1)}, u32[]{:S(2)}, u32[]{:S(2)}) %collective-permute-start.10) | collective-permute-done | bytes 131104 | tf_op jit(solution)/shard_map/ppermute | solution.py:712
  51.6 0.7 %head_sums.1 = (f32[128,128]{1,0:T(8,128)}, f32[128,128]{1,0:T(8,128)}) custom-call(f32[2,128,128]{2,1,0:T(8,128)S(1)} %get-tuple-element.107.refs_0_, f32[2,128,128]{2,1,0:T(8,128)S(1)} %collective-permute-done.8.refs_1_, f32[2,128,128]{2,1,0:T(8,128)S(1)} %collective-permute-done.9.refs_2_, f32[2,128,128]{2,1,0:T(8,128)S(1)} %collective-permute-done.10.refs_3_), custom_call_target="tpu_custom_call" | custom-call | flops 1048576 | bytes 524288 | tf_op jit(solution)/shard_map/head_sums/pallas_call | solution.py:319
  (21 shorter events, 0.4 us)
Async XLA Ops:
  0.6 5.9 %copy-start.2 = (bf16[512,128]{1,0:T(8,128)(2,1)S(1)}, bf16[512,128]{1,0:T(8,128)(2,1)}, u32[]{:S(2)}) copy-start(bf16[512,128]{1,0:T(8,128)(2,1)} %b_ref.5) | copy-start | bytes 393220
  0.6 5.9 %copy-start.4 = (f32[32,512]{1,0:T(8,128)S(1)}, f32[32,512]{1,0:T(8,128)}, u32[]{:S(2)}) copy-start(f32[32,512]{1,0:T(8,128)} %refs_4_.3) | copy-start | bytes 196612
  0.7 5.9 %copy-start.3 = (bf16[512,128]{1,0:T(8,128)(2,1)S(1)}, bf16[512,128]{1,0:T(8,128)(2,1)}, u32[]{:S(2)}) copy-start(bf16[512,128]{1,0:T(8,128)(2,1)} %refs_3_.3) | copy-start | bytes 393220
  0.7 5.9 %copy-start.1 = (bf16[512,2048]{1,0:T(8,128)(2,1)S(1)}, bf16[512,2048]{1,0:T(8,128)(2,1)}, u32[]{:S(2)}) copy-start(bf16[512,2048]{1,0:T(8,128)(2,1)} %refs_1_.3) | copy-start | bytes 6291460
  0.7 5.9 %copy-start = (bf16[512,2048]{1,0:T(8,128)(2,1)S(1)}, bf16[512,2048]{1,0:T(8,128)(2,1)}, u32[]{:S(2)}) copy-start(bf16[512,2048]{1,0:T(8,128)(2,1)} %refs_0_.3) | copy-start | bytes 6291460
  5.8 3.4 %collective-permute-start = (f32[2,136,1024]{2,1,0:T(8,128)}, f32[2,136,1024]{2,1,0:T(8,128)S(1)}, u32[]{:S(2)}, u32[]{:S(2)}) collective-permute-start(f32[2,136,1024]{2,1,0:T(8,128)} %get-tuple-element.58), channel_id=1, source_target_pairs={{0,4},{4,0},{8,12},{12,8},{16,20},{20,16},{24,28},{28,24},{1,5},{5... | collective-permute-start | bytes 3342344 | tf_op jit(solution)/shard_map/ppermute | solution.py:708
  9.4 10.4 %collective-permute-start.1 = (f32[136,512]{1,0:T(8,128)S(1)}, f32[136,512]{1,0:T(8,128)S(1)}, u32[]{:S(2)}, u32[]{:S(2)}) collective-permute-start(f32[136,512]{1,0:T(8,128)S(1)} %get-tuple-element.59.own_ref), channel_id=1, source_target_pairs={{0,8},{4,12},{8,0},{12,4},{16,24},{20,28},{24,16},{28,20},{1,9},{5... | collective-permute-start | bytes 835592 | tf_op jit(solution)/shard_map/ppermute | solution.py:332
  9.7 10.1 %collective-permute-start.2 = (f32[128,512]{1,0:T(8,128)S(1)}, f32[128,512]{1,0:T(8,128)S(1)}, u32[]{:S(2)}, u32[]{:S(2)}) collective-permute-start(f32[128,512]{1,0:T(8,128)S(1)} %get-tuple-element.60), channel_id=1, source_target_pairs={{0,16},{4,20},{8,24},{12,28},{16,0},{20,4},{24,8},{28,12},{1,17},{... | collective-permute-start | bytes 786440 | tf_op jit(solution)/shard_map/ppermute | solution.py:332
  11.0 8.8 %collective-permute-start.3 = (f32[8,512]{1,0:T(8,128)S(1)}, f32[8,512]{1,0:T(8,128)S(1)}, u32[]{:S(2)}, u32[]{:S(2)}) collective-permute-start(f32[8,512]{1,0:T(8,128)S(1)} %get-tuple-element.61), channel_id=1, source_target_pairs={{0,24},{4,28},{8,16},{12,20},{16,8},{20,12},{24,0},{28,4},{1,25},{... | collective-permute-start | bytes 49160 | tf_op jit(solution)/shard_map/ppermute | solution.py:332
  12.1 11.3 %collective-permute-start.4 = (f32[128,512]{1,0:T(8,128)S(1)}, f32[128,512]{1,0:T(8,128)S(1)}, u32[]{:S(2)}, u32[]{:S(2)}) collective-permute-start(f32[128,512]{1,0:T(8,128)S(1)} %get-tuple-element.73), channel_id=1, source_target_pairs={{0,8},{4,12},{8,0},{12,4},{16,24},{20,28},{24,16},{28,20},{1,9},{5... | collective-permute-start | bytes 786440 | tf_op jit(solution)/shard_map/ppermute | solution.py:332
  19.9 10.9 %collective-permute-start.5 = (f32[128,512]{1,0:T(8,128)S(1)}, f32[128,512]{1,0:T(8,128)S(1)}, u32[]{:S(2)}, u32[]{:S(2)}) collective-permute-start(f32[128,512]{1,0:T(8,128)S(1)} %get-tuple-element.75), channel_id=1, source_target_pairs={{0,16},{4,20},{8,24},{12,28},{16,0},{20,4},{24,8},{28,12},{1,17},{... | collective-permute-start | bytes 786440 | tf_op jit(solution)/shard_map/ppermute | solution.py:332
  21.2 9.6 %collective-permute-start.6 = (f32[128,512]{1,0:T(8,128)S(1)}, f32[128,512]{1,0:T(8,128)S(1)}, u32[]{:S(2)}, u32[]{:S(2)}) collective-permute-start(f32[128,512]{1,0:T(8,128)S(1)} %get-tuple-element.76), channel_id=1, source_target_pairs={{0,8},{4,12},{8,0},{12,4},{16,24},{20,28},{24,16},{28,20},{1,9},{5... | collective-permute-start | bytes 786440 | tf_op jit(solution)/shard_map/ppermute | solution.py:332
  31.2 3.6 %collective-permute-start.7 = (f32[2,128,1024]{2,1,0:T(8,128)S(1)}, f32[2,128,1024]{2,1,0:T(8,128)S(1)}, u32[]{:S(2)}, u32[]{:S(2)}) collective-permute-start(f32[2,128,1024]{2,1,0:T(8,128)S(1)} %get-tuple-element.95), channel_id=1, source_target_pairs={{0,4},{4,0},{8,12},{12,8},{16,20},{20,16},{24,28},{28,24},{1,5},{5... | collective-permute-start | bytes 3145736 | tf_op jit(solution)/shard_map/ppermute | solution.py:708
  34.8 5.9 %copy-start.5 = (bf16[512,256]{1,0:T(8,128)(2,1)S(1)}, bf16[512,256]{1,0:T(8,128)(2,1)}, u32[]{:S(2)}) copy-start(bf16[512,256]{1,0:T(8,128)(2,1)} %get-tuple-element.87.suf_ref) | copy-start | bytes 786436
  36.8 7.5 %collective-permute-start.8 = (f32[2,128,128]{2,1,0:T(8,128)S(1)}, f32[2,128,128]{2,1,0:T(8,128)S(1)}, u32[]{:S(2)}, u32[]{:S(2)}) collective-permute-start(f32[2,128,128]{2,1,0:T(8,128)S(1)} %get-tuple-element.108), channel_id=1, source_target_pairs={{0,1},{1,2},{2,3},{3,0},{4,5},{5,6},{6,7},{7,4},{8,9},{9,10},{10,1... | collective-permute-start | bytes 393224 | tf_op jit(solution)/shard_map/ppermute | solution.py:712
  38.2 10.9 %collective-permute-start.9 = (f32[2,128,128]{2,1,0:T(8,128)S(1)}, f32[2,128,128]{2,1,0:T(8,128)S(1)}, u32[]{:S(2)}, u32[]{:S(2)}) collective-permute-start(f32[2,128,128]{2,1,0:T(8,128)S(1)} %get-tuple-element.109), channel_id=1, source_target_pairs={{0,2},{1,3},{2,0},{3,1},{4,6},{5,7},{6,4},{7,5},{8,10},{9,11},{10,... | collective-permute-start | bytes 393224 | tf_op jit(solution)/shard_map/ppermute | solution.py:712
  39.3 12.3 %collective-permute-start.10 = (f32[2,128,128]{2,1,0:T(8,128)S(1)}, f32[2,128,128]{2,1,0:T(8,128)S(1)}, u32[]{:S(2)}, u32[]{:S(2)}) collective-permute-start(f32[2,128,128]{2,1,0:T(8,128)S(1)} %get-tuple-element.110), channel_id=1, source_target_pairs={{0,3},{1,0},{2,1},{3,2},{4,7},{5,4},{6,5},{7,6},{8,11},{9,8},{10,9... | collective-permute-start | bytes 393224 | tf_op jit(solution)/shard_map/ppermute | solution.py:712

commit v14 on v13

--- a/solution.py
+++ b/solution.py
@@ -164,17 +164,36 @@
     smalls[2].wait()
     bt_ref[...] = transposed(b_buf[...])
     ct_ref[...] = transposed(c_buf[...])
-    for load in loads:
+    stores = []
+
+    def store(k, part, index, rows):
+        columns = pl.ds(k * tile, tile)
+        copy = pltpu.make_async_copy(out_buf.at[k, index, rows], out_ref.at[index, rows, columns], sent.at[k, part])
+        copy.start()
+        stores.append(copy)
+
+    def factor(k, lanes):
+        return dot(factor_ref[:, lanes], spread_table(heads, (place(OTHER) * count + k) * (tile // P_SIZE), tile))
+
+    for load in loads[:PARTS]:
         load.wait()
-    stores = []
     for k in range(count):
-        first = (place(OTHER) * count + k) * (tile // P_SIZE)
-        x, dy = x_buf[:, k * tile : (k + 1) * tile], dy_buf[:, k * tile : (k + 1) * tile]
-        tile_totals(heads, first, x, dy, bt_ref, ct_ref, factor_ref, out_buf.at[k])
-        stores.append(pltpu.make_async_copy(out_buf.at[k], out_ref.at[:, :, pl.ds(k * tile, tile)], sent.at[k]))
-        stores[-1].start()
-    for store in stores:
-        store.wait()
+        scaled = x_buf[:, k * tile : (k + 1) * tile].astype(F32) * factor(k, slice(LANES, None))
+        out_buf[k, 0, :N, :] = dot12(bt_ref[...], halves(scaled))
+        store(k, 0, 0, pl.ds(0, N))
+    for load in loads[PARTS:]:
+        load.wait()
+    for k in range(count):
+        before = factor(k, slice(0, LANES))
+        ended = jnp.broadcast_to(before[local - 1 :, :], (EXTRA, tile))
+        out_buf[k, 0, N:, :] = ended
+        store(k, 1, 0, pl.ds(N, EXTRA))
+        scaled = dy_buf[:, k * tile : (k + 1) * tile].astype(F32) * before
+        out_buf[k, 1, :N, :] = dot12(ct_ref[...], halves(scaled))
+        out_buf[k, 1, N:, :] = ended
+        store(k, 2, 1, pl.ds(0, N + EXTRA))
+    for copy in stores:
+        copy.wait()
 
 
 def other_totals(x, dy, b, c, decays):
@@ -200,7 +219,7 @@
             pltpu.VMEM((N, local), BF16),
             pltpu.SemaphoreType.DMA((2, PARTS)),
             pltpu.SemaphoreType.DMA((3,)),
-            pltpu.SemaphoreType.DMA((count,)),
+            pltpu.SemaphoreType.DMA((count, 3)),
         ],
         compiler_params=FIRST,
         name="other_totals",

time: 53 us -> 53.3 us (level)
  no operation moved by 1% of the time
where the time goes in v14:
time: 53.3 us; the launch traced here: 52.6 us
  Pallas kernels  31.9 us (60%)
  starting transfers between devices  11.4 us (21%)
  waiting for transfers between devices  8.5 us (16%)
  between operations  0.81 us (2%)
    pallas_call x2, Pallas kernels, local_part(): pl.pallas_call(functools.partial(local_kernel, first_tile, before is not...  14.8 us
    ppermute x3, waiting for transfers between devices, turned(): lax.ppermute(v, axis, [(i, (i + by) % length) for i in range(length)])  7.22 us
    ppermute x6, starting transfers between devices, crossed(): return lax.ppermute(v, 'seq', [(i, i ^ bit) for i in range(length)])  5.48 us
    pallas_call x1, Pallas kernels, other_totals(): pl.pallas_call(functools.partial(other_kernel, width // P_SIZE), grid=(1,...  5.41 us
    pallas_call x2, Pallas kernels, map_terms(): pl.pallas_call(functools.partial(map_kernel, count, ranks), grid=(count,)...  3.97 us
    ppermute x3, starting transfers between devices, turned(): lax.ppermute(v, axis, [(i, (i + by) % length) for i in range(length)])  3.8 us
    pallas_call x1, Pallas kernels, input_terms(): pl.pallas_call(functools.partial(input_kernel, width // P_SIZE, count), g...  3.69 us
    pallas_call x1, Pallas kernels, own_totals(): pl.pallas_call(functools.partial(own_kernel, width // P_SIZE, count), gri...  2.6 us
  transfers between devices with their start and end apart: 11, of which 4 were waited for; matrix products, arithmetic and copies ran while one was open for 0% of the time, Pallas kernels for 44%

profile of v14, /device:TPU:11, one launch (start us, length us, event | category | flops | bytes accessed | tf_op | source)
XLA Modules:
  0.0 52.6 jit_solution(15361102297276354246)
XLA Ops:
  0.7 5.4 %other_totals.1 = (f32[2,136,1024]{2,1,0:T(8,128)}, bf16[512,256]{1,0:T(8,128)(2,1)}) custom-call(bf16[512,2048]{1,0:T(8,128)(2,1)} %refs_0_.3, bf16[512,2048]{1,0:T(8,128)(2,1)} %refs_1_.3, bf16[512,128]{1,0:T(8,128)(2,1)} %b_ref.5, bf16[512,128]{1,0:T(8,128)(2,1)} %refs_3_.3, f32[32,512]{1,0:T(8,128)} %refs_4_.3), custom_call_target="tpu_custom_call" | custom-call | flops 536870912 | bytes 4194304 | tf_op jit(solution)/shard_map/other_totals/pallas_call | solution.py:205
  6.1 0.8 %collective-permute-start = (f32[2,136,1024]{2,1,0:T(8,128)}, f32[2,136,1024]{2,1,0:T(8,128)S(1)}, u32[]{:S(2)}, u32[]{:S(2)}) collective-permute-start(f32[2,136,1024]{2,1,0:T(8,128)} %get-tuple-element.58), channel_id=1, source_target_pairs={{0,4},{4,0},{8,12},{12,8},{16,20},{20,16},{24,28},{28,24},{1,5},{5... | collective-permute-start | bytes 3342344 | tf_op jit(solution)/shard_map/ppermute | solution.py:727
  6.9 2.6 %own_totals.1.mine_ref = f32[2,136,1024]{2,1,0:T(8,128)S(1)} custom-call(bf16[512,2048]{1,0:T(8,128)(2,1)S(1)} %copy-done, bf16[512,2048]{1,0:T(8,128)(2,1)S(1)} %copy-done.1, bf16[512,128]{1,0:T(8,128)(2,1)S(1)} %copy-done.2, bf16[512,128]{1,0:T(8,128)(2,1)S(1)} %copy-done.3, f32[32,512]{1,0:T(8,128)S(1)} %copy-done.4), custom_call_target="tpu_custom_call" | custom-call | flops 536870912 | bytes 4194304 | tf_op jit(solution)/shard_map/own_totals/pallas_call | solution.py:249
  9.7 0.3 collective-permute-start.1
  10.1 1.2 %collective-permute-start.2 = (f32[128,512]{1,0:T(8,128)S(1)}, f32[128,512]{1,0:T(8,128)S(1)}, u32[]{:S(2)}, u32[]{:S(2)}) collective-permute-start(f32[128,512]{1,0:T(8,128)S(1)} %get-tuple-element.60), channel_id=1, source_target_pairs={{0,16},{4,20},{8,24},{12,28},{16,0},{20,4},{24,8},{28,12},{1,17},{... | collective-permute-start | bytes 786440 | tf_op jit(solution)/shard_map/ppermute | solution.py:351
  11.3 1.2 %collective-permute-start.3 = (f32[8,512]{1,0:T(8,128)S(1)}, f32[8,512]{1,0:T(8,128)S(1)}, u32[]{:S(2)}, u32[]{:S(2)}) collective-permute-start(f32[8,512]{1,0:T(8,128)S(1)} %get-tuple-element.61), channel_id=1, source_target_pairs={{0,24},{4,28},{8,16},{12,20},{16,8},{20,12},{24,0},{28,4},{1,25},{... | collective-permute-start | bytes 49160 | tf_op jit(solution)/shard_map/ppermute | solution.py:351
  12.5 0.2 collective-permute-start.4
  12.7 7.4 %local_part.2 = (f32[512,2048]{1,0:T(8,128)S(1)}, bf16[2,2,512,2048]{3,2,1,0:T(8,128)(2,1)S(1)}, f32[512,128]{1,0:T(8,128)S(1)}, f32[512,128]{1,0:T(8,128)S(1)}) custom-call(bf16[512,2048]{1,0:T(8,128)(2,1)S(1)} %copy-done, bf16[512,2048]{1,0:T(8,128)(2,1)S(1)} %copy-done.1, bf16[512,128]{1,0:T(8,128)(2,1)S(1)} %copy-done.2, bf16[512,128]{1,0:T(8,128)(2,1)S(1)} %copy-done.3, ...), custom_call_target="tpu_custom_call" | custom-call | flops 2684354560 | bytes 4194304 | tf_op jit(solution)/shard_map/local_part/pallas_call | solution.py:619
  20.2 1.3 %collective-permute-start.5 = (f32[128,512]{1,0:T(8,128)S(1)}, f32[128,512]{1,0:T(8,128)S(1)}, u32[]{:S(2)}, u32[]{:S(2)}) collective-permute-start(f32[128,512]{1,0:T(8,128)S(1)} %get-tuple-element.75), channel_id=1, source_target_pairs={{0,16},{4,20},{8,24},{12,28},{16,0},{20,4},{24,8},{28,12},{1,17},{... | collective-permute-start | bytes 786440 | tf_op jit(solution)/shard_map/ppermute | solution.py:351
  21.5 1.2 %collective-permute-start.6 = (f32[128,512]{1,0:T(8,128)S(1)}, f32[128,512]{1,0:T(8,128)S(1)}, u32[]{:S(2)}, u32[]{:S(2)}) collective-permute-start(f32[128,512]{1,0:T(8,128)S(1)} %get-tuple-element.76), channel_id=1, source_target_pairs={{0,8},{4,12},{8,0},{12,4},{16,24},{20,28},{24,16},{28,20},{1,9},{5... | collective-permute-start | bytes 786440 | tf_op jit(solution)/shard_map/ppermute | solution.py:351
  22.8 0.9 %collective-permute-done.4.later_ref = f32[128,512]{1,0:T(8,128)S(1)} collective-permute-done((f32[128,512]{1,0:T(8,128)S(1)}, f32[128,512]{1,0:T(8,128)S(1)}, u32[]{:S(2)}, u32[]{:S(2)}) %collective-permute-start.4) | collective-permute-done | bytes 262176 | tf_op jit(solution)/shard_map/ppermute | solution.py:351
  23.7 7.4 %local_part.3 = (f32[512,2048]{1,0:T(8,128)S(1)}, bf16[2,2,512,2048]{3,2,1,0:T(8,128)(2,1)S(1)}, f32[512,128]{1,0:T(8,128)S(1)}, f32[512,128]{1,0:T(8,128)S(1)}) custom-call(bf16[512,2048]{1,0:T(8,128)(2,1)S(1)} %copy-done, bf16[512,2048]{1,0:T(8,128)(2,1)S(1)} %copy-done.1, ...), custom_call_target="tpu_custom_call", output_to_operand_aliasing={{0}: (7, {}), {1}: (8, {})} | custom-call | flops 2684354560 | bytes 4194304 | tf_op jit(solution)/shard_map/local_part/pallas_call | solution.py:619
  31.2 0.4 carried_in.1
  31.5 1.3 %collective-permute-start.7 = (f32[2,128,1024]{2,1,0:T(8,128)S(1)}, f32[2,128,1024]{2,1,0:T(8,128)S(1)}, u32[]{:S(2)}, u32[]{:S(2)}) collective-permute-start(f32[2,128,1024]{2,1,0:T(8,128)S(1)} %get-tuple-element.95), channel_id=1, source_target_pairs={{0,4},{4,0},{8,12},{12,8},{16,20},{20,16},{24,28},{28,24},{1,5},{5... | collective-permute-start | bytes 3145736 | tf_op jit(solution)/shard_map/ppermute | solution.py:727
  32.9 2.0 %map_terms.2 = (f32[512,128]{1,0:T(8,128)S(1)}, f32[512,128]{1,0:T(8,128)S(1)}) custom-call(bf16[2,2,512,2048]{3,2,1,0:T(8,128)(2,1)S(1)} %get-tuple-element.96.scaled_ref, f32[2,128,1024]{2,1,0:T(8,128)S(1)} %get-tuple-element.105.carry_ref.own_ref, f32[512,128]{1,0:T(8,128)S(1)} %get-tuple-element.97.out_before_ref, ...), custom_call_target="tpu_custom_call" | custom-call | flops 805306368 | bytes 4194304 | tf_op jit(solution)/shard_map/map_terms/pallas_call | solution.py:676
  34.8 0.3 collective-permute-done.7.carry_ref.other_ref
  35.1 2.0 %map_terms.3 = (f32[2,128,128]{2,1,0:T(8,128)S(1)}, f32[2,128,128]{2,1,0:T(8,128)S(1)}, f32[2,128,128]{2,1,0:T(8,128)S(1)}, f32[2,128,128]{2,1,0:T(8,128)S(1)}) custom-call(bf16[2,2,512,2048]{3,2,1,0:T(8,128)(2,1)S(1)} %get-tuple-element.96.scaled_ref, f32[2,128,1024]{2,1,0:T(8,128)S(1)} %collective-permute-done.7.carry_ref.other_ref, ...), custom_call_target="tpu_custom_call" | custom-call | flops 805306368 | bytes 4194304 | tf_op jit(solution)/shard_map/map_terms/pallas_call | solution.py:676
  37.2 1.3 %collective-permute-start.8 = (f32[2,128,128]{2,1,0:T(8,128)S(1)}, f32[2,128,128]{2,1,0:T(8,128)S(1)}, u32[]{:S(2)}, u32[]{:S(2)}) collective-permute-start(f32[2,128,128]{2,1,0:T(8,128)S(1)} %get-tuple-element.108), channel_id=1, source_target_pairs={{0,1},{1,2},{2,3},{3,0},{4,5},{5,6},{6,7},{7,4},{8,9},{9,10},{10,1... | collective-permute-start | bytes 393224 | tf_op jit(solution)/shard_map/ppermute | solution.py:731
  38.5 1.1 %collective-permute-start.9 = (f32[2,128,128]{2,1,0:T(8,128)S(1)}, f32[2,128,128]{2,1,0:T(8,128)S(1)}, u32[]{:S(2)}, u32[]{:S(2)}) collective-permute-start(f32[2,128,128]{2,1,0:T(8,128)S(1)} %get-tuple-element.109), channel_id=1, source_target_pairs={{0,2},{1,3},{2,0},{3,1},{4,6},{5,7},{6,4},{7,5},{8,10},{9,11},{10,... | collective-permute-start | bytes 393224 | tf_op jit(solution)/shard_map/ppermute | solution.py:731
  39.6 1.4 %collective-permute-start.10 = (f32[2,128,128]{2,1,0:T(8,128)S(1)}, f32[2,128,128]{2,1,0:T(8,128)S(1)}, u32[]{:S(2)}, u32[]{:S(2)}) collective-permute-start(f32[2,128,128]{2,1,0:T(8,128)S(1)} %get-tuple-element.110), channel_id=1, source_target_pairs={{0,3},{1,0},{2,1},{3,2},{4,7},{5,4},{6,5},{7,6},{8,11},{9,8},{10,9... | collective-permute-start | bytes 393224 | tf_op jit(solution)/shard_map/ppermute | solution.py:731
  41.0 3.7 %input_terms.1 = bf16[512,2048]{1,0:T(8,128)(2,1)} custom-call(f32[512,2048]{1,0:T(8,128)S(1)} %get-tuple-element.86.part_ref, bf16[512,256]{1,0:T(8,128)(2,1)S(1)} %copy-done.5, bf16[512,128]{1,0:T(8,128)(2,1)S(1)} %copy-done.2, f32[2,128,1024]{2,1,0:T(8,128)S(1)} %get-tuple-element.105.carry_ref.own_ref, ...), custom_call_target="tpu_custom_call" | custom-call | flops 536870912 | bytes 8388608 | tf_op jit(solution)/shard_map/input_terms/pallas_call | solution.py:708
  44.7 4.7 %collective-permute-done.9.refs_2_ = f32[2,128,128]{2,1,0:T(8,128)S(1)} collective-permute-done((f32[2,128,128]{2,1,0:T(8,128)S(1)}, f32[2,128,128]{2,1,0:T(8,128)S(1)}, u32[]{:S(2)}, u32[]{:S(2)}) %collective-permute-start.9) | collective-permute-done | bytes 131104 | tf_op jit(solution)/shard_map/ppermute | solution.py:731
  49.4 2.5 %collective-permute-done.10.refs_3_ = f32[2,128,128]{2,1,0:T(8,128)S(1)} collective-permute-done((f32[2,128,128]{2,1,0:T(8,128)S(1)}, f32[2,128,128]{2,1,0:T(8,128)S(1)}, u32[]{:S(2)}, u32[]{:S(2)}) %collective-permute-start.10) | collective-permute-done | bytes 131104 | tf_op jit(solution)/shard_map/ppermute | solution.py:731
  51.9 0.7 %head_sums.1 = (f32[128,128]{1,0:T(8,128)}, f32[128,128]{1,0:T(8,128)}) custom-call(f32[2,128,128]{2,1,0:T(8,128)S(1)} %get-tuple-element.107.refs_0_, f32[2,128,128]{2,1,0:T(8,128)S(1)} %collective-permute-done.8.refs_1_, f32[2,128,128]{2,1,0:T(8,128)S(1)} %collective-permute-done.9.refs_2_, f32[2,128,128]{2,1,0:T(8,128)S(1)} %collective-permute-done.10.refs_3_), custom_call_target="tpu_custom_call" | custom-call | flops 1048576 | bytes 524288 | tf_op jit(solution)/shard_map/head_sums/pallas_call | solution.py:338
  (21 shorter events, 0.4 us)
Async XLA Ops:
  0.6 6.2 %copy-start.2 = (bf16[512,128]{1,0:T(8,128)(2,1)S(1)}, bf16[512,128]{1,0:T(8,128)(2,1)}, u32[]{:S(2)}) copy-start(bf16[512,128]{1,0:T(8,128)(2,1)} %b_ref.5) | copy-start | bytes 393220
  0.6 6.2 %copy-start.4 = (f32[32,512]{1,0:T(8,128)S(1)}, f32[32,512]{1,0:T(8,128)}, u32[]{:S(2)}) copy-start(f32[32,512]{1,0:T(8,128)} %refs_4_.3) | copy-start | bytes 196612
  0.7 6.2 %copy-start.3 = (bf16[512,128]{1,0:T(8,128)(2,1)S(1)}, bf16[512,128]{1,0:T(8,128)(2,1)}, u32[]{:S(2)}) copy-start(bf16[512,128]{1,0:T(8,128)(2,1)} %refs_3_.3) | copy-start | bytes 393220
  0.7 6.2 %copy-start.1 = (bf16[512,2048]{1,0:T(8,128)(2,1)S(1)}, bf16[512,2048]{1,0:T(8,128)(2,1)}, u32[]{:S(2)}) copy-start(bf16[512,2048]{1,0:T(8,128)(2,1)} %refs_1_.3) | copy-start | bytes 6291460
  0.7 6.2 %copy-start = (bf16[512,2048]{1,0:T(8,128)(2,1)S(1)}, bf16[512,2048]{1,0:T(8,128)(2,1)}, u32[]{:S(2)}) copy-start(bf16[512,2048]{1,0:T(8,128)(2,1)} %refs_0_.3) | copy-start | bytes 6291460
  6.1 3.4 %collective-permute-start = (f32[2,136,1024]{2,1,0:T(8,128)}, f32[2,136,1024]{2,1,0:T(8,128)S(1)}, u32[]{:S(2)}, u32[]{:S(2)}) collective-permute-start(f32[2,136,1024]{2,1,0:T(8,128)} %get-tuple-element.58), channel_id=1, source_target_pairs={{0,4},{4,0},{8,12},{12,8},{16,20},{20,16},{24,28},{28,24},{1,5},{5... | collective-permute-start | bytes 3342344 | tf_op jit(solution)/shard_map/ppermute | solution.py:727
  9.7 10.4 %collective-permute-start.1 = (f32[136,512]{1,0:T(8,128)S(1)}, f32[136,512]{1,0:T(8,128)S(1)}, u32[]{:S(2)}, u32[]{:S(2)}) collective-permute-start(f32[136,512]{1,0:T(8,128)S(1)} %get-tuple-element.59.own_ref), channel_id=1, source_target_pairs={{0,8},{4,12},{8,0},{12,4},{16,24},{20,28},{24,16},{28,20},{1,9},{5... | collective-permute-start | bytes 835592 | tf_op jit(solution)/shard_map/ppermute | solution.py:351
  10.1 10.1 %collective-permute-start.2 = (f32[128,512]{1,0:T(8,128)S(1)}, f32[128,512]{1,0:T(8,128)S(1)}, u32[]{:S(2)}, u32[]{:S(2)}) collective-permute-start(f32[128,512]{1,0:T(8,128)S(1)} %get-tuple-element.60), channel_id=1, source_target_pairs={{0,16},{4,20},{8,24},{12,28},{16,0},{20,4},{24,8},{28,12},{1,17},{... | collective-permute-start | bytes 786440 | tf_op jit(solution)/shard_map/ppermute | solution.py:351
  11.3 8.8 %collective-permute-start.3 = (f32[8,512]{1,0:T(8,128)S(1)}, f32[8,512]{1,0:T(8,128)S(1)}, u32[]{:S(2)}, u32[]{:S(2)}) collective-permute-start(f32[8,512]{1,0:T(8,128)S(1)} %get-tuple-element.61), channel_id=1, source_target_pairs={{0,24},{4,28},{8,16},{12,20},{16,8},{20,12},{24,0},{28,4},{1,25},{... | collective-permute-start | bytes 49160 | tf_op jit(solution)/shard_map/ppermute | solution.py:351
  12.5 11.3 %collective-permute-start.4 = (f32[128,512]{1,0:T(8,128)S(1)}, f32[128,512]{1,0:T(8,128)S(1)}, u32[]{:S(2)}, u32[]{:S(2)}) collective-permute-start(f32[128,512]{1,0:T(8,128)S(1)} %get-tuple-element.73), channel_id=1, source_target_pairs={{0,8},{4,12},{8,0},{12,4},{16,24},{20,28},{24,16},{28,20},{1,9},{5... | collective-permute-start | bytes 786440 | tf_op jit(solution)/shard_map/ppermute | solution.py:351
  20.2 10.9 %collective-permute-start.5 = (f32[128,512]{1,0:T(8,128)S(1)}, f32[128,512]{1,0:T(8,128)S(1)}, u32[]{:S(2)}, u32[]{:S(2)}) collective-permute-start(f32[128,512]{1,0:T(8,128)S(1)} %get-tuple-element.75), channel_id=1, source_target_pairs={{0,16},{4,20},{8,24},{12,28},{16,0},{20,4},{24,8},{28,12},{1,17},{... | collective-permute-start | bytes 786440 | tf_op jit(solution)/shard_map/ppermute | solution.py:351
  21.5 9.6 %collective-permute-start.6 = (f32[128,512]{1,0:T(8,128)S(1)}, f32[128,512]{1,0:T(8,128)S(1)}, u32[]{:S(2)}, u32[]{:S(2)}) collective-permute-start(f32[128,512]{1,0:T(8,128)S(1)} %get-tuple-element.76), channel_id=1, source_target_pairs={{0,8},{4,12},{8,0},{12,4},{16,24},{20,28},{24,16},{28,20},{1,9},{5... | collective-permute-start | bytes 786440 | tf_op jit(solution)/shard_map/ppermute | solution.py:351
  31.5 3.6 %collective-permute-start.7 = (f32[2,128,1024]{2,1,0:T(8,128)S(1)}, f32[2,128,1024]{2,1,0:T(8,128)S(1)}, u32[]{:S(2)}, u32[]{:S(2)}) collective-permute-start(f32[2,128,1024]{2,1,0:T(8,128)S(1)} %get-tuple-element.95), channel_id=1, source_target_pairs={{0,4},{4,0},{8,12},{12,8},{16,20},{20,16},{24,28},{28,24},{1,5},{5... | collective-permute-start | bytes 3145736 | tf_op jit(solution)/shard_map/ppermute | solution.py:727
  35.1 5.8 %copy-start.5 = (bf16[512,256]{1,0:T(8,128)(2,1)S(1)}, bf16[512,256]{1,0:T(8,128)(2,1)}, u32[]{:S(2)}) copy-start(bf16[512,256]{1,0:T(8,128)(2,1)} %get-tuple-element.87.suf_ref) | copy-start | bytes 786436
  37.2 7.5 %collective-permute-start.8 = (f32[2,128,128]{2,1,0:T(8,128)S(1)}, f32[2,128,128]{2,1,0:T(8,128)S(1)}, u32[]{:S(2)}, u32[]{:S(2)}) collective-permute-start(f32[2,128,128]{2,1,0:T(8,128)S(1)} %get-tuple-element.108), channel_id=1, source_target_pairs={{0,1},{1,2},{2,3},{3,0},{4,5},{5,6},{6,7},{7,4},{8,9},{9,10},{10,1... | collective-permute-start | bytes 393224 | tf_op jit(solution)/shard_map/ppermute | solution.py:731
  38.5 10.9 %collective-permute-start.9 = (f32[2,128,128]{2,1,0:T(8,128)S(1)}, f32[2,128,128]{2,1,0:T(8,128)S(1)}, u32[]{:S(2)}, u32[]{:S(2)}) collective-permute-start(f32[2,128,128]{2,1,0:T(8,128)S(1)} %get-tuple-element.109), channel_id=1, source_target_pairs={{0,2},{1,3},{2,0},{3,1},{4,6},{5,7},{6,4},{7,5},{8,10},{9,11},{10,... | collective-permute-start | bytes 393224 | tf_op jit(solution)/shard_map/ppermute | solution.py:731
  39.6 12.3 %collective-permute-start.10 = (f32[2,128,128]{2,1,0:T(8,128)S(1)}, f32[2,128,128]{2,1,0:T(8,128)S(1)}, u32[]{:S(2)}, u32[]{:S(2)}) collective-permute-start(f32[2,128,128]{2,1,0:T(8,128)S(1)} %get-tuple-element.110), channel_id=1, source_target_pairs={{0,3},{1,0},{2,1},{3,2},{4,7},{5,4},{6,5},{7,6},{8,11},{9,8},{10,9... | collective-permute-start | bytes 393224 | tf_op jit(solution)/shard_map/ppermute | solution.py:731

commit v15 on v13

--- a/solution.py
+++ b/solution.py
@@ -726,8 +726,9 @@
         result = local_part(0, ahead, *args, decays)
         others, result = lax.optimization_barrier((others, result))
         cross, same = second_phase(own, back, *others)
-        crossing = [crossed(cross, length, 4), crossed(same, length, 2)]
-        result, later, _, _ = lax.optimization_barrier((result, later, cross, same))
+        same = crossed(same, length, 2)
+        crossing = [crossed(cross, length, 4), same]
+        result, later, _ = lax.optimization_barrier((result, later, cross))
         result = local_part(ahead, tiles - ahead, *args, decays, result)
         others, result = lax.optimization_barrier((others + [later] + crossing, result))
         own, peer = carried4(mine, recv, *others)

time: 53 us -> 53 us (level); the launches traced: 52.2 us -> 52.9 us
  starting transfers between devices: 11.4 us -> 12 us
    ppermute x2, starting transfers between devices: 2.04 us -> 2.66 us  [swap_cores(): return lax.ppermute(v, 'seq', [(i, i ^ 1) for i in range(length)])]
where the time goes in v15:
time: 53 us; the launch traced here: 52.9 us
  Pallas kernels  31.6 us (60%)
  starting transfers between devices  12 us (23%)
  waiting for transfers between devices  8.48 us (16%)
  between operations  0.81 us (2%)
    pallas_call x2, Pallas kernels, local_part(): pl.pallas_call(functools.partial(local_kernel, first_tile, before is not...  14.8 us
    ppermute x3, waiting for transfers between devices, turned(): lax.ppermute(v, axis, [(i, (i + by) % length) for i in range(length)])  7.22 us
    ppermute x6, starting transfers between devices, crossed(): return lax.ppermute(v, 'seq', [(i, i ^ bit) for i in range(length)])  5.49 us
    pallas_call x1, Pallas kernels, other_totals(): pl.pallas_call(functools.partial(other_kernel, width // P_SIZE), grid=(1,...  5.1 us
    pallas_call x2, Pallas kernels, map_terms(): pl.pallas_call(functools.partial(map_kernel, count, ranks), grid=(count,)...  3.99 us
    ppermute x3, starting transfers between devices, turned(): lax.ppermute(v, axis, [(i, (i + by) % length) for i in range(length)])  3.83 us
    pallas_call x1, Pallas kernels, input_terms(): pl.pallas_call(functools.partial(input_kernel, width // P_SIZE, count), g...  3.69 us
    ppermute x2, starting transfers between devices, swap_cores(): return lax.ppermute(v, 'seq', [(i, i ^ 1) for i in range(length)])  2.66 us
  transfers between devices with their start and end apart: 11, of which 4 were waited for; matrix products, arithmetic and copies ran while one was open for 0% of the time, Pallas kernels for 44%

profile of v15, /device:TPU:11, one launch (start us, length us, event | category | flops | bytes accessed | tf_op | source)
XLA Modules:
  0.0 52.9 jit_solution(1830335005769665435)
XLA Ops:
  0.7 5.1 %other_totals.1 = (f32[2,136,1024]{2,1,0:T(8,128)}, bf16[512,256]{1,0:T(8,128)(2,1)}) custom-call(bf16[512,2048]{1,0:T(8,128)(2,1)} %refs_0_.3, bf16[512,2048]{1,0:T(8,128)(2,1)} %refs_1_.3, bf16[512,128]{1,0:T(8,128)(2,1)} %b_ref.5, bf16[512,128]{1,0:T(8,128)(2,1)} %refs_3_.3, f32[32,512]{1,0:T(8,128)} %refs_4_.3), custom_call_target="tpu_custom_call" | custom-call | flops 536870912 | bytes 4194304 | tf_op jit(solution)/shard_map/other_totals/pallas_call | solution.py:186
  5.8 0.7 %collective-permute-start = (f32[2,136,1024]{2,1,0:T(8,128)}, f32[2,136,1024]{2,1,0:T(8,128)S(1)}, u32[]{:S(2)}, u32[]{:S(2)}) collective-permute-start(f32[2,136,1024]{2,1,0:T(8,128)} %get-tuple-element.58), channel_id=1, source_target_pairs={{0,4},{4,0},{8,12},{12,8},{16,20},{20,16},{24,28},{28,24},{1,5},{5... | collective-permute-start | bytes 3342344 | tf_op jit(solution)/shard_map/ppermute | solution.py:708
  6.5 2.6 %own_totals.1.mine_ref = f32[2,136,1024]{2,1,0:T(8,128)S(1)} custom-call(bf16[512,2048]{1,0:T(8,128)(2,1)S(1)} %copy-done, bf16[512,2048]{1,0:T(8,128)(2,1)S(1)} %copy-done.1, bf16[512,128]{1,0:T(8,128)(2,1)S(1)} %copy-done.2, bf16[512,128]{1,0:T(8,128)(2,1)S(1)} %copy-done.3, f32[32,512]{1,0:T(8,128)S(1)} %copy-done.4), custom_call_target="tpu_custom_call" | custom-call | flops 536870912 | bytes 4194304 | tf_op jit(solution)/shard_map/own_totals/pallas_call | solution.py:230
  9.4 0.3 collective-permute-start.1
  9.7 1.2 %collective-permute-start.2 = (f32[128,512]{1,0:T(8,128)S(1)}, f32[128,512]{1,0:T(8,128)S(1)}, u32[]{:S(2)}, u32[]{:S(2)}) collective-permute-start(f32[128,512]{1,0:T(8,128)S(1)} %get-tuple-element.60), channel_id=1, source_target_pairs={{0,16},{4,20},{8,24},{12,28},{16,0},{20,4},{24,8},{28,12},{1,17},{... | collective-permute-start | bytes 786440 | tf_op jit(solution)/shard_map/ppermute | solution.py:332
  11.0 1.1 %collective-permute-start.3 = (f32[8,512]{1,0:T(8,128)S(1)}, f32[8,512]{1,0:T(8,128)S(1)}, u32[]{:S(2)}, u32[]{:S(2)}) collective-permute-start(f32[8,512]{1,0:T(8,128)S(1)} %get-tuple-element.61), channel_id=1, source_target_pairs={{0,24},{4,28},{8,16},{12,20},{16,8},{20,12},{24,0},{28,4},{1,25},{... | collective-permute-start | bytes 49160 | tf_op jit(solution)/shard_map/ppermute | solution.py:332
  12.1 0.3 collective-permute-start.4
  12.4 7.4 %local_part.2 = (f32[512,2048]{1,0:T(8,128)S(1)}, bf16[2,2,512,2048]{3,2,1,0:T(8,128)(2,1)S(1)}, f32[512,128]{1,0:T(8,128)S(1)}, f32[512,128]{1,0:T(8,128)S(1)}) custom-call(bf16[512,2048]{1,0:T(8,128)(2,1)S(1)} %copy-done, bf16[512,2048]{1,0:T(8,128)(2,1)S(1)} %copy-done.1, bf16[512,128]{1,0:T(8,128)(2,1)S(1)} %copy-done.2, bf16[512,128]{1,0:T(8,128)(2,1)S(1)} %copy-done.3, ...), custom_call_target="tpu_custom_call" | custom-call | flops 2684354560 | bytes 4194304 | tf_op jit(solution)/shard_map/local_part/pallas_call | solution.py:600
  19.9 1.3 %collective-permute-start.6 = (f32[128,512]{1,0:T(8,128)S(1)}, f32[128,512]{1,0:T(8,128)S(1)}, u32[]{:S(2)}, u32[]{:S(2)}) collective-permute-start(f32[128,512]{1,0:T(8,128)S(1)} %get-tuple-element.77), channel_id=1, source_target_pairs={{0,8},{4,12},{8,0},{12,4},{16,24},{20,28},{24,16},{28,20},{1,9},{5... | collective-permute-start | bytes 786440 | tf_op jit(solution)/shard_map/ppermute | solution.py:332
  21.2 1.2 %collective-permute-start.5 = (f32[128,512]{1,0:T(8,128)S(1)}, f32[128,512]{1,0:T(8,128)S(1)}, u32[]{:S(2)}, u32[]{:S(2)}) collective-permute-start(f32[128,512]{1,0:T(8,128)S(1)} %get-tuple-element.75), channel_id=1, source_target_pairs={{0,16},{4,20},{8,24},{12,28},{16,0},{20,4},{24,8},{28,12},{1,17},{... | collective-permute-start | bytes 786440 | tf_op jit(solution)/shard_map/ppermute | solution.py:332
  22.4 0.9 %collective-permute-done.4.later_ref = f32[128,512]{1,0:T(8,128)S(1)} collective-permute-done((f32[128,512]{1,0:T(8,128)S(1)}, f32[128,512]{1,0:T(8,128)S(1)}, u32[]{:S(2)}, u32[]{:S(2)}) %collective-permute-start.4) | collective-permute-done | bytes 262176 | tf_op jit(solution)/shard_map/ppermute | solution.py:332
  23.4 7.4 %local_part.3 = (f32[512,2048]{1,0:T(8,128)S(1)}, bf16[2,2,512,2048]{3,2,1,0:T(8,128)(2,1)S(1)}, f32[512,128]{1,0:T(8,128)S(1)}, f32[512,128]{1,0:T(8,128)S(1)}) custom-call(bf16[512,2048]{1,0:T(8,128)(2,1)S(1)} %copy-done, bf16[512,2048]{1,0:T(8,128)(2,1)S(1)} %copy-done.1, ...), custom_call_target="tpu_custom_call", output_to_operand_aliasing={{0}: (7, {}), {1}: (8, {})} | custom-call | flops 2684354560 | bytes 4194304 | tf_op jit(solution)/shard_map/local_part/pallas_call | solution.py:600
  30.8 0.4 carried_in.1
  31.2 1.9 %collective-permute-start.7 = (f32[2,128,1024]{2,1,0:T(8,128)S(1)}, f32[2,128,1024]{2,1,0:T(8,128)S(1)}, u32[]{:S(2)}, u32[]{:S(2)}) collective-permute-start(f32[2,128,1024]{2,1,0:T(8,128)S(1)} %get-tuple-element.95), channel_id=1, source_target_pairs={{0,4},{4,0},{8,12},{12,8},{16,20},{20,16},{24,28},{28,24},{1,5},{5... | collective-permute-start | bytes 3145736 | tf_op jit(solution)/shard_map/ppermute | solution.py:708
  33.1 2.0 %map_terms.2 = (f32[512,128]{1,0:T(8,128)S(1)}, f32[512,128]{1,0:T(8,128)S(1)}) custom-call(bf16[2,2,512,2048]{3,2,1,0:T(8,128)(2,1)S(1)} %get-tuple-element.96.scaled_ref, f32[2,128,1024]{2,1,0:T(8,128)S(1)} %get-tuple-element.105.carry_ref.own_ref, f32[512,128]{1,0:T(8,128)S(1)} %get-tuple-element.97.out_before_ref, ...), custom_call_target="tpu_custom_call" | custom-call | flops 805306368 | bytes 4194304 | tf_op jit(solution)/shard_map/map_terms/pallas_call | solution.py:657
  35.1 0.3 collective-permute-done.7.carry_ref.other_ref
  35.4 2.0 %map_terms.3 = (f32[2,128,128]{2,1,0:T(8,128)S(1)}, f32[2,128,128]{2,1,0:T(8,128)S(1)}, f32[2,128,128]{2,1,0:T(8,128)S(1)}, f32[2,128,128]{2,1,0:T(8,128)S(1)}) custom-call(bf16[2,2,512,2048]{3,2,1,0:T(8,128)(2,1)S(1)} %get-tuple-element.96.scaled_ref, f32[2,128,1024]{2,1,0:T(8,128)S(1)} %collective-permute-done.7.carry_ref.other_ref, ...), custom_call_target="tpu_custom_call" | custom-call | flops 805306368 | bytes 4194304 | tf_op jit(solution)/shard_map/map_terms/pallas_call | solution.py:657
  37.4 1.4 %collective-permute-start.8 = (f32[2,128,128]{2,1,0:T(8,128)S(1)}, f32[2,128,128]{2,1,0:T(8,128)S(1)}, u32[]{:S(2)}, u32[]{:S(2)}) collective-permute-start(f32[2,128,128]{2,1,0:T(8,128)S(1)} %get-tuple-element.108), channel_id=1, source_target_pairs={{0,1},{1,2},{2,3},{3,0},{4,5},{5,6},{6,7},{7,4},{8,9},{9,10},{10,1... | collective-permute-start | bytes 393224 | tf_op jit(solution)/shard_map/ppermute | solution.py:712
  38.8 1.1 %collective-permute-start.9 = (f32[2,128,128]{2,1,0:T(8,128)S(1)}, f32[2,128,128]{2,1,0:T(8,128)S(1)}, u32[]{:S(2)}, u32[]{:S(2)}) collective-permute-start(f32[2,128,128]{2,1,0:T(8,128)S(1)} %get-tuple-element.109), channel_id=1, source_target_pairs={{0,2},{1,3},{2,0},{3,1},{4,6},{5,7},{6,4},{7,5},{8,10},{9,11},{10,... | collective-permute-start | bytes 393224 | tf_op jit(solution)/shard_map/ppermute | solution.py:712
  39.9 1.4 %collective-permute-start.10 = (f32[2,128,128]{2,1,0:T(8,128)S(1)}, f32[2,128,128]{2,1,0:T(8,128)S(1)}, u32[]{:S(2)}, u32[]{:S(2)}) collective-permute-start(f32[2,128,128]{2,1,0:T(8,128)S(1)} %get-tuple-element.110), channel_id=1, source_target_pairs={{0,3},{1,0},{2,1},{3,2},{4,7},{5,4},{6,5},{7,6},{8,11},{9,8},{10,9... | collective-permute-start | bytes 393224 | tf_op jit(solution)/shard_map/ppermute | solution.py:712
  41.3 3.7 %input_terms.1 = bf16[512,2048]{1,0:T(8,128)(2,1)} custom-call(f32[512,2048]{1,0:T(8,128)S(1)} %get-tuple-element.86.part_ref, bf16[512,256]{1,0:T(8,128)(2,1)S(1)} %copy-done.5, bf16[512,128]{1,0:T(8,128)(2,1)S(1)} %copy-done.2, f32[2,128,1024]{2,1,0:T(8,128)S(1)} %get-tuple-element.105.carry_ref.own_ref, ...), custom_call_target="tpu_custom_call" | custom-call | flops 536870912 | bytes 8388608 | tf_op jit(solution)/shard_map/input_terms/pallas_call | solution.py:689
  45.0 4.7 %collective-permute-done.9.refs_2_ = f32[2,128,128]{2,1,0:T(8,128)S(1)} collective-permute-done((f32[2,128,128]{2,1,0:T(8,128)S(1)}, f32[2,128,128]{2,1,0:T(8,128)S(1)}, u32[]{:S(2)}, u32[]{:S(2)}) %collective-permute-start.9) | collective-permute-done | bytes 131104 | tf_op jit(solution)/shard_map/ppermute | solution.py:712
  49.7 2.5 %collective-permute-done.10.refs_3_ = f32[2,128,128]{2,1,0:T(8,128)S(1)} collective-permute-done((f32[2,128,128]{2,1,0:T(8,128)S(1)}, f32[2,128,128]{2,1,0:T(8,128)S(1)}, u32[]{:S(2)}, u32[]{:S(2)}) %collective-permute-start.10) | collective-permute-done | bytes 131104 | tf_op jit(solution)/shard_map/ppermute | solution.py:712
  52.2 0.7 %head_sums.1 = (f32[128,128]{1,0:T(8,128)}, f32[128,128]{1,0:T(8,128)}) custom-call(f32[2,128,128]{2,1,0:T(8,128)S(1)} %get-tuple-element.107.refs_0_, f32[2,128,128]{2,1,0:T(8,128)S(1)} %collective-permute-done.8.refs_1_, f32[2,128,128]{2,1,0:T(8,128)S(1)} %collective-permute-done.9.refs_2_, f32[2,128,128]{2,1,0:T(8,128)S(1)} %collective-permute-done.10.refs_3_), custom_call_target="tpu_custom_call" | custom-call | flops 1048576 | bytes 524288 | tf_op jit(solution)/shard_map/head_sums/pallas_call | solution.py:319
  (21 shorter events, 0.4 us)
Async XLA Ops:
  0.6 5.9 %copy-start.2 = (bf16[512,128]{1,0:T(8,128)(2,1)S(1)}, bf16[512,128]{1,0:T(8,128)(2,1)}, u32[]{:S(2)}) copy-start(bf16[512,128]{1,0:T(8,128)(2,1)} %b_ref.5) | copy-start | bytes 393220
  0.6 5.9 %copy-start.4 = (f32[32,512]{1,0:T(8,128)S(1)}, f32[32,512]{1,0:T(8,128)}, u32[]{:S(2)}) copy-start(f32[32,512]{1,0:T(8,128)} %refs_4_.3) | copy-start | bytes 196612
  0.7 5.9 %copy-start.3 = (bf16[512,128]{1,0:T(8,128)(2,1)S(1)}, bf16[512,128]{1,0:T(8,128)(2,1)}, u32[]{:S(2)}) copy-start(bf16[512,128]{1,0:T(8,128)(2,1)} %refs_3_.3) | copy-start | bytes 393220
  0.7 5.9 %copy-start.1 = (bf16[512,2048]{1,0:T(8,128)(2,1)S(1)}, bf16[512,2048]{1,0:T(8,128)(2,1)}, u32[]{:S(2)}) copy-start(bf16[512,2048]{1,0:T(8,128)(2,1)} %refs_1_.3) | copy-start | bytes 6291460
  0.7 5.9 %copy-start = (bf16[512,2048]{1,0:T(8,128)(2,1)S(1)}, bf16[512,2048]{1,0:T(8,128)(2,1)}, u32[]{:S(2)}) copy-start(bf16[512,2048]{1,0:T(8,128)(2,1)} %refs_0_.3) | copy-start | bytes 6291460
  5.8 3.4 %collective-permute-start = (f32[2,136,1024]{2,1,0:T(8,128)}, f32[2,136,1024]{2,1,0:T(8,128)S(1)}, u32[]{:S(2)}, u32[]{:S(2)}) collective-permute-start(f32[2,136,1024]{2,1,0:T(8,128)} %get-tuple-element.58), channel_id=1, source_target_pairs={{0,4},{4,0},{8,12},{12,8},{16,20},{20,16},{24,28},{28,24},{1,5},{5... | collective-permute-start | bytes 3342344 | tf_op jit(solution)/shard_map/ppermute | solution.py:708
  9.4 10.4 %collective-permute-start.1 = (f32[136,512]{1,0:T(8,128)S(1)}, f32[136,512]{1,0:T(8,128)S(1)}, u32[]{:S(2)}, u32[]{:S(2)}) collective-permute-start(f32[136,512]{1,0:T(8,128)S(1)} %get-tuple-element.59.own_ref), channel_id=1, source_target_pairs={{0,8},{4,12},{8,0},{12,4},{16,24},{20,28},{24,16},{28,20},{1,9},{5... | collective-permute-start | bytes 835592 | tf_op jit(solution)/shard_map/ppermute | solution.py:332
  9.7 10.1 %collective-permute-start.2 = (f32[128,512]{1,0:T(8,128)S(1)}, f32[128,512]{1,0:T(8,128)S(1)}, u32[]{:S(2)}, u32[]{:S(2)}) collective-permute-start(f32[128,512]{1,0:T(8,128)S(1)} %get-tuple-element.60), channel_id=1, source_target_pairs={{0,16},{4,20},{8,24},{12,28},{16,0},{20,4},{24,8},{28,12},{1,17},{... | collective-permute-start | bytes 786440 | tf_op jit(solution)/shard_map/ppermute | solution.py:332
  11.0 8.8 %collective-permute-start.3 = (f32[8,512]{1,0:T(8,128)S(1)}, f32[8,512]{1,0:T(8,128)S(1)}, u32[]{:S(2)}, u32[]{:S(2)}) collective-permute-start(f32[8,512]{1,0:T(8,128)S(1)} %get-tuple-element.61), channel_id=1, source_target_pairs={{0,24},{4,28},{8,16},{12,20},{16,8},{20,12},{24,0},{28,4},{1,25},{... | collective-permute-start | bytes 49160 | tf_op jit(solution)/shard_map/ppermute | solution.py:332
  12.1 11.3 %collective-permute-start.4 = (f32[128,512]{1,0:T(8,128)S(1)}, f32[128,512]{1,0:T(8,128)S(1)}, u32[]{:S(2)}, u32[]{:S(2)}) collective-permute-start(f32[128,512]{1,0:T(8,128)S(1)} %get-tuple-element.73), channel_id=1, source_target_pairs={{0,8},{4,12},{8,0},{12,4},{16,24},{20,28},{24,16},{28,20},{1,9},{5... | collective-permute-start | bytes 786440 | tf_op jit(solution)/shard_map/ppermute | solution.py:332
  19.9 10.9 %collective-permute-start.6 = (f32[128,512]{1,0:T(8,128)S(1)}, f32[128,512]{1,0:T(8,128)S(1)}, u32[]{:S(2)}, u32[]{:S(2)}) collective-permute-start(f32[128,512]{1,0:T(8,128)S(1)} %get-tuple-element.77), channel_id=1, source_target_pairs={{0,8},{4,12},{8,0},{12,4},{16,24},{20,28},{24,16},{28,20},{1,9},{5... | collective-permute-start | bytes 786440 | tf_op jit(solution)/shard_map/ppermute | solution.py:332
  21.2 9.6 %collective-permute-start.5 = (f32[128,512]{1,0:T(8,128)S(1)}, f32[128,512]{1,0:T(8,128)S(1)}, u32[]{:S(2)}, u32[]{:S(2)}) collective-permute-start(f32[128,512]{1,0:T(8,128)S(1)} %get-tuple-element.75), channel_id=1, source_target_pairs={{0,16},{4,20},{8,24},{12,28},{16,0},{20,4},{24,8},{28,12},{1,17},{... | collective-permute-start | bytes 786440 | tf_op jit(solution)/shard_map/ppermute | solution.py:332
  31.2 4.2 %collective-permute-start.7 = (f32[2,128,1024]{2,1,0:T(8,128)S(1)}, f32[2,128,1024]{2,1,0:T(8,128)S(1)}, u32[]{:S(2)}, u32[]{:S(2)}) collective-permute-start(f32[2,128,1024]{2,1,0:T(8,128)S(1)} %get-tuple-element.95), channel_id=1, source_target_pairs={{0,4},{4,0},{8,12},{12,8},{16,20},{20,16},{24,28},{28,24},{1,5},{5... | collective-permute-start | bytes 3145736 | tf_op jit(solution)/shard_map/ppermute | solution.py:708
  35.4 5.9 %copy-start.5 = (bf16[512,256]{1,0:T(8,128)(2,1)S(1)}, bf16[512,256]{1,0:T(8,128)(2,1)}, u32[]{:S(2)}) copy-start(bf16[512,256]{1,0:T(8,128)(2,1)} %get-tuple-element.87.suf_ref) | copy-start | bytes 786436
  37.4 7.5 %collective-permute-start.8 = (f32[2,128,128]{2,1,0:T(8,128)S(1)}, f32[2,128,128]{2,1,0:T(8,128)S(1)}, u32[]{:S(2)}, u32[]{:S(2)}) collective-permute-start(f32[2,128,128]{2,1,0:T(8,128)S(1)} %get-tuple-element.108), channel_id=1, source_target_pairs={{0,1},{1,2},{2,3},{3,0},{4,5},{5,6},{6,7},{7,4},{8,9},{9,10},{10,1... | collective-permute-start | bytes 393224 | tf_op jit(solution)/shard_map/ppermute | solution.py:712
  38.8 10.9 %collective-permute-start.9 = (f32[2,128,128]{2,1,0:T(8,128)S(1)}, f32[2,128,128]{2,1,0:T(8,128)S(1)}, u32[]{:S(2)}, u32[]{:S(2)}) collective-permute-start(f32[2,128,128]{2,1,0:T(8,128)S(1)} %get-tuple-element.109), channel_id=1, source_target_pairs={{0,2},{1,3},{2,0},{3,1},{4,6},{5,7},{6,4},{7,5},{8,10},{9,11},{10,... | collective-permute-start | bytes 393224 | tf_op jit(solution)/shard_map/ppermute | solution.py:712
  39.9 12.3 %collective-permute-start.10 = (f32[2,128,128]{2,1,0:T(8,128)S(1)}, f32[2,128,128]{2,1,0:T(8,128)S(1)}, u32[]{:S(2)}, u32[]{:S(2)}) collective-permute-start(f32[2,128,128]{2,1,0:T(8,128)S(1)} %get-tuple-element.110), channel_id=1, source_target_pairs={{0,3},{1,0},{2,1},{3,2},{4,7},{5,4},{6,5},{7,6},{8,11},{9,8},{10,9... | collective-permute-start | bytes 393224 | tf_op jit(solution)/shard_map/ppermute | solution.py:712
